TPU v7x, 32 devices: a whole 2x2x4 slice. The times are simulated.
32 devices in a mesh: groups: 1, tm: 8 (over z, y), cell: 2 (over x), sub: 2 (over core).
Axes of the slice: x: 2, y: 2, z: 4, core: 2. Of those that a mesh axis runs over, the one named last changes fastest.
Arguments:
- frames: bfloat16 [512, 128, 384], P(('groups', 'tm', 'sub'), 'cell'), may hold values from -6 to 6
- w_qkv: bfloat16 [384, 1152], P('sub'), may hold values from -1.5 to 1.5
- w_out: bfloat16 [384, 384], P('sub'), may hold values from -0.3125 to 0.3125
- w_up: bfloat16 [384, 1536], P('sub'), may hold values from -0.3125 to 0.3125
- w_down: bfloat16 [1536, 384], P('sub'), may hold values from -0.15625 to 0.15625
- temporal_weight_first: bfloat16 [1152, 768], P('sub'), may hold values from -0.1875 to 0.1875
- temporal_weight_second: bfloat16 [1152, 768], P('sub'), may hold values from -0.1875 to 0.1875
Outputs:
- features_out: bfloat16 [512, 128, 384], P(('groups', 'tm', 'sub'), 'cell')
All inputs are finite; a program needn't handle non-finite values.
Results may differ from a plain program's by a relative error of at most 0.009.
Values may be sent and summed in bfloat16 or wider, within the bound.
No kernel may reach another device: no remote copies, remote signals or barrier semaphores. Data moves between devices by JAX's collectives and lax.ppermute only.
A program may use at most 64 MiB of HBM per device.

v0:
```python
import jax
import jax.numpy as jnp
from jax import lax
from jax.sharding import PartitionSpec as P

HEAD_DIM = 64
DILATION_FIRST = 16
DILATION_SECOND = 256


def with_halo(block, sides, width):
    for axis, dim in sides:
        count = lax.axis_size(axis)
        forward = [(i, i + 1) for i in range(count - 1)]
        backward = [(target, source) for source, target in forward]
        low = lax.ppermute(
            lax.slice_in_dim(block, block.shape[dim] - width, None, axis=dim), axis, forward
        )
        high = lax.ppermute(lax.slice_in_dim(block, 0, width, axis=dim), axis, backward)
        block = jnp.concatenate([low, block, high], axis=dim)
    return block


def shifted(shard, axis, by):
    size = lax.axis_size(axis)
    pairs = [(i, i + by) for i in range(size) if 0 <= i + by < size]
    return lax.ppermute(shard, axis, pairs)


def normalize(values):
    row_mean = jnp.mean(values, axis=-1, keepdims=True)
    centred = values - row_mean
    row_var = jnp.mean(centred * centred, axis=-1, keepdims=True)
    return centred * lax.rsqrt(row_var + 1e-05)


def attend(queries, key_part, value_part):
    frame_count, q_cells, features = queries.shape
    head_count = features // HEAD_DIM
    q_heads = queries.reshape(frame_count, q_cells, head_count, HEAD_DIM)
    k_heads = key_part.reshape(frame_count, -1, head_count, HEAD_DIM)
    v_heads = value_part.reshape(frame_count, -1, head_count, HEAD_DIM)
    scores = jnp.einsum(
        "fqhd,fkhd->fhqk", q_heads, k_heads, preferred_element_type=jnp.float32
    ) * HEAD_DIM ** (-0.5)
    row_max = jnp.max(scores, axis=-1, keepdims=True)
    exp_terms = jnp.exp(scores - row_max)
    attn_probs = (exp_terms / jnp.sum(exp_terms, axis=-1, keepdims=True)).astype(jnp.bfloat16)
    mixed = jnp.einsum("fhqk,fkhd->fqhd", attn_probs, v_heads, preferred_element_type=jnp.float32)
    return mixed.astype(jnp.bfloat16).reshape(frame_count, q_cells, features)


def gated_step(center, earlier, later_frames, weight):
    features = center.shape[-1]
    stacked = jnp.concatenate([earlier, center, later_frames], axis=-1).reshape(-1, 3 * features)
    preact = jnp.dot(stacked, weight, preferred_element_type=jnp.float32)
    gated_part = jnp.tanh(preact[:, :features]) * jax.nn.sigmoid(preact[:, features:])
    return (center.astype(jnp.float32) + gated_part.reshape(center.shape)).astype(jnp.bfloat16)


def local(frames, w_qkv, w_out, w_up, w_down, temporal_weight_first, temporal_weight_second):
    frames_local, cell_rows, features = frames.shape
    whole_qkv, whole_out, whole_up, whole_down, whole_tcn_a, whole_tcn_b = (
        lax.all_gather(w_qkv, "sub", axis=0, tiled=True),
        lax.all_gather(w_out, "sub", axis=0, tiled=True),
        lax.all_gather(w_up, "sub", axis=0, tiled=True),
        lax.all_gather(w_down, "sub", axis=0, tiled=True),
        lax.all_gather(temporal_weight_first, "sub", axis=0, tiled=True),
        lax.all_gather(temporal_weight_second, "sub", axis=0, tiled=True),
    )
    working = lax.all_to_all(frames, "cell", split_axis=0, concat_axis=1, tiled=True)
    frame_count, cells_here = (working.shape[0], working.shape[1])
    residual = working.astype(jnp.float32)
    normed = normalize(residual).astype(jnp.bfloat16).reshape(-1, features)
    projected = jnp.dot(normed, whole_qkv, preferred_element_type=jnp.float32).astype(jnp.bfloat16)
    projected = projected.reshape(frame_count, cells_here, 3 * features)
    queries = projected[..., :features]
    key_vals = projected[..., features:]
    attended = attend(queries, key_vals[..., :features], key_vals[..., features:])
    out_part = jnp.dot(
        attended.reshape(-1, features), whole_out, preferred_element_type=jnp.float32
    )
    mid_state = (residual + out_part.reshape(frame_count, cells_here, features)).astype(
        jnp.bfloat16
    )
    mid_float = lax.optimization_barrier(mid_state).astype(jnp.float32)
    normed_two = normalize(mid_float).astype(jnp.bfloat16).reshape(-1, features)
    hidden = jax.nn.gelu(jnp.dot(normed_two, whole_up, preferred_element_type=jnp.float32)).astype(
        jnp.bfloat16
    )
    down_part = jnp.dot(hidden, whole_down, preferred_element_type=jnp.float32).reshape(
        frame_count, cells_here, features
    )
    sectioned_frames = (mid_float + down_part).astype(jnp.bfloat16)
    sectioned_frames = lax.all_to_all(
        sectioned_frames, "cell", split_axis=1, concat_axis=0, tiled=True
    )
    padded_frames = with_halo(sectioned_frames, ((("tm", "sub"), 0),), DILATION_FIRST)
    earlier = padded_frames[:frames_local]
    later_frames = padded_frames[2 * DILATION_FIRST : 2 * DILATION_FIRST + frames_local]
    opening_layer = gated_step(sectioned_frames, earlier, later_frames, whole_tcn_a)
    shard_step_count = DILATION_SECOND // frames_local
    far_earlier = shifted(opening_layer, ("tm", "sub"), shard_step_count)
    far_later = shifted(opening_layer, ("tm", "sub"), -shard_step_count)
    return gated_step(opening_layer, far_earlier, far_later, whole_tcn_b)


def solution(mesh):
    placed = (
        P(("groups", "tm", "sub"), "cell", None),
        P("sub", None),
        P("sub", None),
        P("sub", None),
        P("sub", None),
        P("sub", None),
        P("sub", None),
    )
    return jax.shard_map(
        local,
        mesh=mesh,
        in_specs=placed,
        out_specs=P(("groups", "tm", "sub"), "cell", None),
        check_vma=False,
    )
```

profile of v0, /device:TPU:0, one launch (start us, length us, event | category | flops | bytes accessed | tf_op | source)
XLA Modules:
  0.0 221.9 jit_solution(18040901323473818572)
XLA Ops:
  7.3 4.2 %all-to-all-start = ((bf16[32,64,384]{2,1,0:T(8,128)(2,1)}), bf16[32,64,384]{2,1,0:T(8,128)(2,1)S(1)}, u32[]{:S(2)}, u32[]{:S(2)}) async-start(bf16[32,64,384]{2,1,0:T(8,128)(2,1)} %param.7), calls=%async_computation | async-start | bytes 3145728 | tf_op jit(solution)/shard_map/all_to_all | solution.py:71
  12.2 2.0 all_gather.19
  14.2 2.4 %all_gather.18 = bf16[384,1152]{1,0:T(8,128)(2,1)S(1)} all-gather(bf16[192,1152]{1,0:T(8,128)(2,1)S(1)} %copy-done.4), channel_id=1, replica_groups=mesh['groups'=1,'tm'=8,'cell'=2,'sub'=2] {'sub'}, dimensions={0}, use_global_device_ids=true | all-gather | bytes 1327104 | tf_op jit(solution)/shard_map/all_gather | solution.py:64
  16.7 14.9 %all-to-all-done = bf16[32,64,384]{2,1,0:T(8,128)(2,1)S(1)} async-done(((bf16[32,64,384]{2,1,0:T(8,128)(2,1)}), bf16[32,64,384]{2,1,0:T(8,128)(2,1)S(1)}, u32[]{:S(2)}, u32[]{:S(2)}) %all-to-all-start) | async-done | bytes 1572896 | tf_op jit(solution)/shard_map/all_to_all | solution.py:71
  33.7 1.7 copy-done
  36.3 2.9 %convolution_convert_fusion = bf16[2048,1152]{1,0:T(8,128)(2,1)S(1)} fusion(bf16[2048,384]{1,0:T(8,128)(2,1)S(1)} %fusion.32, bf16[384,1152]{1,0:T(8,128)(2,1)S(1)} %all_gather.18), kind=kOutput, calls=%fused_computation.10 | convolution fusion | flops 1814298624 | bytes 7176192 | tf_op jit(solution)/shard_map/dot_general | solution.py:75
  39.3 2.0 fusion.49
  41.3 2.6 %copy.17 = bf16[16,128,384]{1,2,0:T(8,128)(2,1)} copy(bf16[16,128,384]{2,1,0:T(8,128)(2,1)} %get-tuple-element.6) | data formatting | bytes 3145728 | tf_op jit(solution)/shard_map/slice | solution.py:77
  43.9 1.6 copy.18
  45.5 1.6 copy.16
  47.2 6.6 %fusion.51 = (f32[16,6,128]{2,1,0:T(8,128)S(1)}, f32[16,6,128,128]{2,3,1,0:T(8,128)}) fusion(bf16[16,128,6,64]{1,3,2,0:T(8,128)(2,1)S(1)} %bitcast.76, bf16[16,128,6,64]{1,3,2,0:T(8,128)(2,1)} %bitcast.77), kind=kOutput, calls=%fused_computation.76 | convolution fusion | flops 206045312 | bytes 9486336 | tf_op jit(solution)/shard_map/sub | solution.py:47
  53.8 3.9 %fusion.39 = bf16[16,6,64,128]{3,2,1,0:T(8,128)(2,1)S(1)} fusion(bf16[16,128,6,64]{1,3,2,0:T(8,128)(2,1)S(1)} %bitcast.78, f32[16,6,128,128]{2,3,1,0:T(8,128)} %get-tuple-element.15, f32[16,6,128]{2,1,0:T(8,128)S(1)} %get-tuple-element.14), kind=kOutput, calls=%fused_computation.56 | convolution fusion | flops 205258752 | bytes 9486336 | tf_op jit(solution)/shard_map/fhqk,fkhd->fqhd/dot_general | solution.py:49
  57.7 1.2 fusion.33
  61.1 10.7 %fusion.38 = f32[2048,384]{1,0:T(8,128)} fusion(bf16[1536,384]{1,0:T(8,128)(2,1)} %all-gather.7.cloned.1.call-done, bf16[2048,384]{1,0:T(8,128)(2,1)S(1)} %bitcast.75, bf16[384,1536]{1,0:T(8,128)(2,1)} %all-gather.5.cloned.1.call-done), kind=kOutput, calls=%fused_computation.55 | convolution fusion | flops 4860149760 | bytes 7077888 | tf_op jit(solution)/shard_map/dot_general | solution.py:91
  71.8 2.3 %fusion.22 = bf16[16,128,384]{2,1,0:T(8,128)(2,1)S(1)} fusion(f32[16,128,384]{2,1,0:T(8,128)} %bitcast.74, bf16[16,128,384]{2,1,0:T(8,128)(2,1)S(1)} %fusion.33), kind=kLoop, calls=%fused_computation.29 | loop fusion | flops 2359296 | bytes 6291456 | tf_op jit(solution)/shard_map/convert_element_type | solution.py:94
  74.1 2.1 copy.21
  76.2 3.7 %all-to-all-start.1 = ((bf16[16,128,384]{2,0,1:T(8,128)(2,1)}), bf16[16,128,384]{2,0,1:T(8,128)(2,1)S(1)}, u32[]{:S(2)}, u32[]{:S(2)}) async-start(bf16[16,128,384]{2,0,1:T(8,128)(2,1)} %copy.21), calls=%async_computation.1 | async-start | bytes 3145728 | tf_op jit(solution)/shard_map/all_to_all | solution.py:95
  80.6 18.1 %all-to-all-done.1 = bf16[16,128,384]{2,0,1:T(8,128)(2,1)S(1)} async-done(((bf16[16,128,384]{2,0,1:T(8,128)(2,1)}), bf16[16,128,384]{2,0,1:T(8,128)(2,1)S(1)}, u32[]{:S(2)}, u32[]{:S(2)}) %all-to-all-start.1) | async-done | bytes 1572896 | tf_op jit(solution)/shard_map/all_to_all | solution.py:95
  99.3 1.3 collective-permute-start
  100.7 1.5 collective-permute-start.1
  102.5 4.0 %collective-permute-done.1 = bf16[16,64,384]{2,1,0:T(8,128)(2,1)S(1)} collective-permute-done((bf16[16,64,384]{2,1,0:T(8,128)(2,1)S(1)}, bf16[16,64,384]{2,1,0:T(8,128)(2,1)S(1)}, u32[]{:S(2)}, u32[]{:S(2)}) %collective-permute-start.1) | collective-permute-done | bytes 786464 | tf_op jit(solution)/shard_map/ppermute | solution.py:19
  106.5 1.5 pad_maximum_fusion.2
  108.0 6.3 %fusion.10 = f32[2048,768]{1,0:T(8,128)S(1)} fusion(bf16[1152,768]{1,0:T(8,128)(2,1)} %all-gather.9.cloned.1.call-done, bf16[2048,384]{1,0:T(8,128)(2,1)} %bitcast.80, bf16[2048,384]{1,0:T(8,128)(2,1)S(1)} %bitcast.67, bf16[2048,384]{1,0:T(8,128)(2,1)S(1)} %bitcast.79), kind=kOutput, calls=%fused_computation.18 | convolution fusion | flops 3638034432 | bytes 12779520 | tf_op jit(solution)/shard_map/dot_general | solution.py:56
  114.3 1.2 fusion.30
  116.2 13.4 %collective-permute-start.2 = (bf16[32,64,384]{2,1,0:T(8,128)(2,1)S(1)}, bf16[32,64,384]{2,1,0:T(8,128)(2,1)S(1)}, u32[]{:S(2)}, u32[]{:S(2)}) collective-permute-start(bf16[32,64,384]{2,1,0:T(8,128)(2,1)S(1)} %add_convert_fusion.1), channel_id=1, source_target_pairs={{0,16},{1,17},{4,20},{5,21},{8,24},{9,25},{12,28},{13,29},{2,18},{... | collective-permute-start | bytes 4718600 | tf_op jit(solution)/shard_map/ppermute | solution.py:27
  129.6 1.3 collective-permute-start.3
  130.9 27.9 %collective-permute-done.2 = bf16[32,64,384]{2,1,0:T(8,128)(2,1)S(1)} collective-permute-done((bf16[32,64,384]{2,1,0:T(8,128)(2,1)S(1)}, bf16[32,64,384]{2,1,0:T(8,128)(2,1)S(1)}, u32[]{:S(2)}, u32[]{:S(2)}) %collective-permute-start.2) | collective-permute-done | bytes 1572896 | tf_op jit(solution)/shard_map/ppermute | solution.py:27
  158.8 43.5 %collective-permute-done.3 = bf16[32,64,384]{2,1,0:T(8,128)(2,1)} collective-permute-done((bf16[32,64,384]{2,1,0:T(8,128)(2,1)S(1)}, bf16[32,64,384]{2,1,0:T(8,128)(2,1)}, u32[]{:S(2)}, u32[]{:S(2)}) %collective-permute-start.3) | collective-permute-done | bytes 1572896 | tf_op jit(solution)/shard_map/ppermute | solution.py:27
  202.3 3.6 %pad_maximum_fusion = bf16[32,64,1152]{2,1,0:T(8,128)(2,1)} fusion(bf16[32,64,384]{2,1,0:T(8,128)(2,1)} %collective-permute-done.3, bf16[32,64,384]{2,1,0:T(8,128)(2,1)S(1)} %add_convert_fusion.1, bf16[32,64,384]{2,1,0:T(8,128)(2,1)S(1)} %collective-permute-done.2), kind=kLoop, calls=%fused_computation.24 | loop fusion | flops 14155776 | bytes 9437184 | tf_op jit(solution)/shard_map/concatenate | solution.py:55
  205.8 6.6 %fusion.52 = f32[2048,768]{1,0:T(8,128)S(1)} fusion(bf16[2048,1152]{1,0:T(8,128)(2,1)} %bitcast.72, bf16[1152,768]{1,0:T(8,128)(2,1)} %all-gather.11.cloned.1.call-done), kind=kOutput, calls=%fused_computation.78 | convolution fusion | flops 3623878656 | bytes 12779520 | tf_op jit(solution)/shard_map/dot_general | solution.py:56
  212.5 1.2 fusion.26
  213.7 1.6 add_convert_fusion
  (41 shorter events, 9.0 us)
Async XLA Ops:
  6.5 5.7 %copy-start.5 = (bf16[192,384]{1,0:T(8,128)(2,1)S(1)}, bf16[192,384]{1,0:T(8,128)(2,1)}, u32[]{:S(2)}) copy-start(bf16[192,384]{1,0:T(8,128)(2,1)} %param.9) | copy-start | bytes 442372
  6.5 7.7 %copy-start.4 = (bf16[192,1152]{1,0:T(8,128)(2,1)S(1)}, bf16[192,1152]{1,0:T(8,128)(2,1)}, u32[]{:S(2)}) copy-start(bf16[192,1152]{1,0:T(8,128)(2,1)} %param.8) | copy-start | bytes 1327108
  6.5 54.6 %all-gather.5.cloned.1.call-start = ((), (), s32[]{:S(2)}) async-start(), calls=%async_computation.2 | async-start | bytes 1769472 | tf_op jit(solution)/shard_map/all_gather | solution.py:66
  7.3 24.4 %all-to-all-start = ((bf16[32,64,384]{2,1,0:T(8,128)(2,1)}), bf16[32,64,384]{2,1,0:T(8,128)(2,1)S(1)}, u32[]{:S(2)}, u32[]{:S(2)}) async-start(bf16[32,64,384]{2,1,0:T(8,128)(2,1)} %param.7), calls=%async_computation | async-start | bytes 3145728 | tf_op jit(solution)/shard_map/all_to_all | solution.py:71
  11.5 49.6 %all-gather.7.cloned.1.call-start = ((), (), s32[]{:S(2)}) async-start(), calls=%async_computation.3 | async-start | bytes 1769472 | tf_op jit(solution)/shard_map/all_gather | solution.py:67
  33.7 1.7 copy-start
  45.5 1.6 copy-start.2
  47.2 6.6 %copy-start.3 = (bf16[16,128,384]{1,2,0:T(8,128)(2,1)S(1)}, bf16[16,128,384]{1,2,0:T(8,128)(2,1)}, u32[]{:S(2)}) copy-start(bf16[16,128,384]{1,2,0:T(8,128)(2,1)} %copy.16) | copy-start | bytes 4718596
  53.8 3.9 %copy-start.1 = (f32[2,16,64,384]{3,2,0,1:T(8,128)S(1)}, f32[2,16,64,384]{3,2,0,1:T(8,128)}, u32[]{:S(2)}) copy-start(f32[2,16,64,384]{3,2,0,1:T(8,128)} %copy-done) | copy-start | bytes 9437188
  76.2 22.6 %all-to-all-start.1 = ((bf16[16,128,384]{2,0,1:T(8,128)(2,1)}), bf16[16,128,384]{2,0,1:T(8,128)(2,1)S(1)}, u32[]{:S(2)}, u32[]{:S(2)}) async-start(bf16[16,128,384]{2,0,1:T(8,128)(2,1)} %copy.21), calls=%async_computation.1 | async-start | bytes 3145728 | tf_op jit(solution)/shard_map/all_to_all | solution.py:95
  79.8 28.1 %all-gather.9.cloned.1.call-start = ((), (), s32[]{:S(2)}) async-start(), calls=%async_computation.4 | async-start | bytes 2654208 | tf_op jit(solution)/shard_map/all_gather | solution.py:68
  80.6 125.3 %all-gather.11.cloned.1.call-start = ((), (), s32[]{:S(2)}) async-start(), calls=%async_computation.5 | async-start | bytes 2654208 | tf_op jit(solution)/shard_map/all_gather | solution.py:69
  99.3 3.2 %collective-permute-start = (bf16[16,64,384]{2,1,0:T(8,128)(2,1)S(1)}, bf16[16,64,384]{2,1,0:T(8,128)(2,1)S(1)}, u32[]{:S(2)}, u32[]{:S(2)}) collective-permute-start(bf16[16,64,384]{2,1,0:T(8,128)(2,1)S(1)} %get-tuple-element.10), channel_id=1, source_target_pairs={{0,1},{1,4},{4,5},{5,8},{8,9},{9,12},{12,13},{13,16},{16,17},{17,2... | collective-permute-start | bytes 2359304 | tf_op jit(solution)/shard_map/ppermute | solution.py:16
  100.7 5.8 %collective-permute-start.1 = (bf16[16,64,384]{2,1,0:T(8,128)(2,1)S(1)}, bf16[16,64,384]{2,1,0:T(8,128)(2,1)S(1)}, u32[]{:S(2)}, u32[]{:S(2)}) collective-permute-start(bf16[16,64,384]{2,1,0:T(8,128)(2,1)S(1)} %get-tuple-element.11), channel_id=1, source_target_pairs={{1,0},{4,1},{5,4},{8,5},{9,8},{12,9},{13,12},{16,13},{17,16},{20,1... | collective-permute-start | bytes 2359304 | tf_op jit(solution)/shard_map/ppermute | solution.py:19
  116.2 42.6 %collective-permute-start.2 = (bf16[32,64,384]{2,1,0:T(8,128)(2,1)S(1)}, bf16[32,64,384]{2,1,0:T(8,128)(2,1)S(1)}, u32[]{:S(2)}, u32[]{:S(2)}) collective-permute-start(bf16[32,64,384]{2,1,0:T(8,128)(2,1)S(1)} %add_convert_fusion.1), channel_id=1, source_target_pairs={{0,16},{1,17},{4,20},{5,21},{8,24},{9,25},{12,28},{13,29},{2,18},{... | collective-permute-start | bytes 4718600 | tf_op jit(solution)/shard_map/ppermute | solution.py:27
  129.6 72.7 %collective-permute-start.3 = (bf16[32,64,384]{2,1,0:T(8,128)(2,1)S(1)}, bf16[32,64,384]{2,1,0:T(8,128)(2,1)}, u32[]{:S(2)}, u32[]{:S(2)}) collective-permute-start(bf16[32,64,384]{2,1,0:T(8,128)(2,1)S(1)} %add_convert_fusion.1), channel_id=1, source_target_pairs={{16,0},{17,1},{20,4},{21,5},{24,8},{25,9},{28,12},{29,13},{18,2},{... | collective-permute-start | bytes 4718600 | tf_op jit(solution)/shard_map/ppermute | solution.py:27
Sparse Core Ops, SparseCore 0:
  8.9 11.9 all-gather.4
  22.4 10.3 all-gather.6
  82.2 12.0 all-gather.8
  131.0 17.2 all-gather.10
where the time goes:
time: 223 us; the launch traced here: 222 us
  waiting for transfers between devices  111 us (50%)
  matrix products  38.2 us (17%)
  starting transfers between devices  25.5 us (11%)
  other arithmetic  16.7 us (7%)
  between operations  13.4 us (6%)
  local copies, waits for them, and re-layouts  12.7 us (6%)
  blocking collectives  4.44 us (2%)
    ppermute x2, waiting for transfers between devices, shifted(): return lax.ppermute(shard, axis, pairs)  71.4 us
    all_to_all x1, waiting for transfers between devices, local(): lax.all_to_all(sectioned_frames, 'cell', split_axis=1, concat_axis=0, til...  18.1 us
    all_to_all x1, waiting for transfers between devices, local(): lax.all_to_all(frames, 'cell', split_axis=0, concat_axis=1, tiled=True)  14.9 us
    ppermute x2, starting transfers between devices, shifted(): return lax.ppermute(shard, axis, pairs)  14.7 us
    dot_general x2, matrix products, gated_step(): preact = jnp.dot(stacked, weight, preferred_element_type=jnp.float32)  12.9 us
    dot_general x1, matrix products, local(): jnp.dot(hidden, whole_down, preferred_element_type=jnp.float32)  10.7 us
    sub x1, matrix products, attend(): exp_terms = jnp.exp(scores - row_max)  6.6 us
  transfers between devices with their start and end apart: 10, of which 6 were waited for; matrix products, arithmetic and copies ran while one was open for 15% of the time, Pallas kernels for 0%

commit v1 on v0

--- a/solution.py
+++ b/solution.py
@@ -1,11 +1,18 @@
+import functools
+import math
+
 import jax
 import jax.numpy as jnp
 from jax import lax
+from jax.experimental import pallas as pl
+from jax.experimental.pallas import tpu as pltpu
 from jax.sharding import PartitionSpec as P
 
 HEAD_DIM = 64
 DILATION_FIRST = 16
 DILATION_SECOND = 256
+CHUNKS = (1, 1, 1, 1)
+VMEM_LIMIT = 40 * 1024 * 1024
 
 
 def with_halo(block, sides, width):
@@ -58,15 +65,11 @@
     return (center.astype(jnp.float32) + gated_part.reshape(center.shape)).astype(jnp.bfloat16)
 
 
-def local(frames, w_qkv, w_out, w_up, w_down, temporal_weight_first, temporal_weight_second):
+def general(frames, w_qkv, w_out, w_up, w_down, temporal_weight_first, temporal_weight_second):
     frames_local, cell_rows, features = frames.shape
     whole_qkv, whole_out, whole_up, whole_down, whole_tcn_a, whole_tcn_b = (
-        lax.all_gather(w_qkv, "sub", axis=0, tiled=True),
-        lax.all_gather(w_out, "sub", axis=0, tiled=True),
-        lax.all_gather(w_up, "sub", axis=0, tiled=True),
-        lax.all_gather(w_down, "sub", axis=0, tiled=True),
-        lax.all_gather(temporal_weight_first, "sub", axis=0, tiled=True),
-        lax.all_gather(temporal_weight_second, "sub", axis=0, tiled=True),
+        lax.all_gather(w, "sub", axis=0, tiled=True)
+        for w in (w_qkv, w_out, w_up, w_down, temporal_weight_first, temporal_weight_second)
     )
     working = lax.all_to_all(frames, "cell", split_axis=0, concat_axis=1, tiled=True)
     frame_count, cells_here = (working.shape[0], working.shape[1])
@@ -74,9 +77,11 @@
     normed = normalize(residual).astype(jnp.bfloat16).reshape(-1, features)
     projected = jnp.dot(normed, whole_qkv, preferred_element_type=jnp.float32).astype(jnp.bfloat16)
     projected = projected.reshape(frame_count, cells_here, 3 * features)
-    queries = projected[..., :features]
-    key_vals = projected[..., features:]
-    attended = attend(queries, key_vals[..., :features], key_vals[..., features:])
+    attended = attend(
+        projected[..., :features],
+        projected[..., features : 2 * features],
+        projected[..., 2 * features :],
+    )
     out_part = jnp.dot(
         attended.reshape(-1, features), whole_out, preferred_element_type=jnp.float32
     )
@@ -105,16 +110,388 @@
     return gated_step(opening_layer, far_earlier, far_later, whole_tcn_b)
 
 
+def load_halves(core, pairs, scratches, sems):
+    copies = []
+    for index, ((mine, other), scratch) in enumerate(zip(pairs, scratches)):
+        rows = mine.shape[0]
+        here = pl.multiple_of(core * rows, 16)
+        there = pl.multiple_of((1 - core) * rows, 16)
+        copies.append(
+            (
+                pltpu.make_async_copy(mine, scratch.at[pl.ds(here, rows)], sems.at[index, 0]),
+                pltpu.make_async_copy(other, scratch.at[pl.ds(there, rows)], sems.at[index, 1]),
+            )
+        )
+    return copies
+
+
+def start_all(copies):
+    for pair in copies:
+        for copy in pair:
+            copy.start()
+
+
+def wait_pair(pair):
+    for copy in pair:
+        copy.wait()
+
+
+def section_kernel(
+    place,
+    own,
+    near_cells,
+    far_own,
+    far_cells,
+    qkv_a,
+    qkv_b,
+    out_a,
+    out_b,
+    up_a,
+    up_b,
+    down_a,
+    down_b,
+    even_ref,
+    odd_ref,
+    w_qkv,
+    w_out,
+    w_up,
+    w_down,
+    sems,
+):
+    core = place[0]
+    copies = load_halves(
+        core,
+        ((qkv_a, qkv_b), (out_a, out_b), (up_a, up_b), (down_a, down_b)),
+        (w_qkv, w_out, w_up, w_down),
+        sems,
+    )
+    first = pl.program_id(0) == 0
+
+    @pl.when(first)
+    def _():
+        start_all(copies)
+
+    features = own.shape[-1]
+    cells = 2 * own.shape[2]
+    parts = []
+    for mine, other in ((own, near_cells), (far_own, far_cells)):
+        for slot in range(2):
+            parts += [mine[slot, 0], other[slot, 0]]
+    residual = jnp.concatenate(parts, axis=0).astype(jnp.float32)
+    frame_count = 4
+    normed = normalize(residual).astype(jnp.bfloat16)
+
+    @pl.when(first)
+    def _():
+        wait_pair(copies[0])
+
+    projected = jnp.dot(normed, w_qkv[...], preferred_element_type=jnp.float32).astype(jnp.bfloat16)
+    pair_width = 2 * HEAD_DIM
+    low = lax.broadcasted_iota(jnp.int32, (cells, pair_width), 1) < HEAD_DIM
+    low_one = low.astype(jnp.bfloat16)
+    high_one = 1 - low_one
+    scale = HEAD_DIM ** (-0.5) * math.log2(math.e)
+    rows = []
+    for frame in range(frame_count):
+        block = projected[frame * cells : (frame + 1) * cells]
+        columns = []
+        for pair in range(features // pair_width):
+            at = pair * pair_width
+            queries = block[:, at : at + pair_width]
+            keys = block[:, features + at : features + at + pair_width]
+            values = block[:, 2 * features + at : 2 * features + at + pair_width]
+            split_keys = jnp.concatenate([keys * low_one, keys * high_one], axis=0)
+            scores = lax.dot_general(
+                queries, split_keys, (((1,), (1,)), ((), ())), preferred_element_type=jnp.float32
+            )
+            terms = []
+            for head in range(2):
+                own_scores = scores[:, head * cells : (head + 1) * cells]
+                row_max = jnp.max(own_scores, axis=-1, keepdims=True)
+                terms.append(jnp.exp2((own_scores - row_max) * scale).astype(jnp.bfloat16))
+            split_values = jnp.concatenate(
+                [
+                    jnp.concatenate([values * low_one, low_one], axis=1),
+                    jnp.concatenate([values * high_one, high_one], axis=1),
+                ],
+                axis=0,
+            )
+            mixed = jnp.dot(
+                jnp.concatenate(terms, axis=1), split_values, preferred_element_type=jnp.float32
+            )
+            columns.append((mixed[:, :pair_width] / mixed[:, pair_width:]).astype(jnp.bfloat16))
+        rows.append(jnp.concatenate(columns, axis=1))
+    attended = jnp.concatenate(rows, axis=0)
+
+    @pl.when(first)
+    def _():
+        wait_pair(copies[1])
+        wait_pair(copies[2])
+        wait_pair(copies[3])
+
+    mid_state = (
+        residual + jnp.dot(attended, w_out[...], preferred_element_type=jnp.float32)
+    ).astype(jnp.bfloat16)
+    mid_float = mid_state.astype(jnp.float32)
+    normed_two = normalize(mid_float).astype(jnp.bfloat16)
+    total = mid_float
+    width = features
+    for at in range(0, w_up.shape[1], width):
+        lifted = jnp.dot(normed_two, w_up[:, at : at + width], preferred_element_type=jnp.float32)
+        inner = lifted * (
+            math.sqrt(2 / math.pi) + (math.sqrt(2 / math.pi) * 0.044715) * (lifted * lifted)
+        )
+        halved = 0.5 * lifted
+        hidden = (halved + halved * jnp.tanh(inner)).astype(jnp.bfloat16)
+        total = total + jnp.dot(hidden, w_down[at : at + width], preferred_element_type=jnp.float32)
+    sectioned = total.astype(jnp.bfloat16)
+    for block in range(2):
+        even_ref[block, 0] = sectioned[(2 * block) * cells : (2 * block + 1) * cells]
+        odd_ref[block, 0] = sectioned[(2 * block + 1) * cells : (2 * block + 2) * cells]
+
+
+def gate(center, preact):
+    features = center.shape[-1]
+    gated = jnp.tanh(preact[:, :features]) * (
+        0.5 + 0.5 * jnp.tanh(0.5 * preact[:, features:])
+    )
+    return (center.astype(jnp.float32) + gated).astype(jnp.bfloat16)
+
+
+def temporal_kernel(
+    place,
+    even,
+    odd,
+    left_odd,
+    right_even,
+    first_a,
+    first_b,
+    second_a,
+    second_b,
+    out0,
+    out1,
+    out2,
+    out3,
+    w_first,
+    w_second,
+    sems,
+):
+    core, near, is_first, is_last = place[0], place[1], place[2], place[3]
+    copies = load_halves(
+        core, ((first_a, first_b), (second_a, second_b)), (w_first, w_second), sems
+    )
+    starting = pl.program_id(0) == 0
+
+    @pl.when(starting)
+    def _():
+        start_all(copies)
+        wait_pair(copies[0])
+
+    far = 1 - near
+    features = even.shape[-1]
+    cells = even.shape[2]
+    zero = jnp.zeros((cells, features), even.dtype)
+    even_n, odd_n, even_f, odd_f = even[near, 0], odd[near, 0], even[far, 0], odd[far, 0]
+    left_n = jnp.where(is_first == 1, zero, left_odd[near, 0])
+    left_f = left_odd[jnp.where(is_first == 1, near, far), 0]
+    right_n = right_even[jnp.where(is_last == 1, far, near), 0]
+    right_f = jnp.where(is_last == 1, zero, right_even[far, 0])
+    center = jnp.concatenate([even_n, odd_n, even_f, odd_f], axis=0)
+    stacked = jnp.concatenate(
+        [
+            jnp.concatenate([left_n, even_n, left_f, even_f], axis=0),
+            center,
+            jnp.concatenate([odd_n, right_n, odd_f, right_f], axis=0),
+        ],
+        axis=1,
+    )
+    opening = gate(center, jnp.dot(stacked, w_first[...], preferred_element_type=jnp.float32))
+
+    @pl.when(starting)
+    def _():
+        wait_pair(copies[1])
+
+    rows = 2 * cells
+    near_part, far_part = opening[:rows], opening[rows:]
+    both = jnp.concatenate([near_part, far_part], axis=1)
+    result_n = gate(
+        near_part, jnp.dot(both, w_second[features:], preferred_element_type=jnp.float32)
+    )
+    result_f = gate(
+        far_part, jnp.dot(both, w_second[: 2 * features], preferred_element_type=jnp.float32)
+    )
+    same = jnp.where(near == 0, result_n, result_f)
+    other = jnp.where(near == 0, result_f, result_n)
+    half = cells // 2
+    for slot in range(2):
+        at = slot * cells
+        out0[slot, 0] = same[at : at + half]
+        out1[slot, 0] = same[at + half : at + cells]
+        out2[slot, 0] = other[at : at + half]
+        out3[slot, 0] = other[at + half : at + cells]
+
+
+ANYWHERE = pl.BlockSpec(memory_space=pl.ANY)
+SCALARS = pl.BlockSpec(memory_space=pltpu.SMEM)
+
+
+def run_section(place, pieces, weights):
+    slots, count, cells, features = pieces[0].shape
+    ff = weights[2][0].shape[1]
+    block_in = pl.BlockSpec((slots, 1, cells, features), lambda i: (0, i, 0, 0))
+    block_out = pl.BlockSpec((2, 1, 2 * cells, features), lambda i: (0, i, 0, 0))
+    shape = jax.ShapeDtypeStruct((2, count, 2 * cells, features), jnp.bfloat16)
+    tokens = 2 * slots * count * 2 * cells
+    macs = tokens * (features * (4 * features + 2 * ff) + 4 * cells * features)
+    flat = [half for pair in weights for half in pair]
+    return pl.pallas_call(
+        section_kernel,
+        grid=(count,),
+        out_shape=(shape, shape),
+        in_specs=[SCALARS] + [block_in] * 4 + [ANYWHERE] * 8,
+        out_specs=(block_out, block_out),
+        scratch_shapes=[
+            pltpu.VMEM((2 * mine.shape[0], mine.shape[1]), mine.dtype) for mine, _ in weights
+        ]
+        + [pltpu.SemaphoreType.DMA((4, 2))],
+        compiler_params=pltpu.CompilerParams(vmem_limit_bytes=VMEM_LIMIT),
+        cost_estimate=pl.CostEstimate(
+            flops=2 * macs, bytes_accessed=8 * tokens * features, transcendentals=tokens * ff
+        ),
+        name="section",
+    )(place, *pieces, *flat)
+
+
+def run_temporal(place, even, odd, left_odd, right_even, weights):
+    blocks, count, cells, features = even.shape
+    block_in = pl.BlockSpec((blocks, 1, cells, features), lambda i: (0, i, 0, 0))
+    block_out = pl.BlockSpec((2, 1, cells // 2, features), lambda i: (0, i, 0, 0))
+    shape = jax.ShapeDtypeStruct((2, count, cells // 2, features), jnp.bfloat16)
+    tokens = 2 * blocks * count * cells
+    flat = [half for pair in weights for half in pair]
+    return pl.pallas_call(
+        temporal_kernel,
+        grid=(count,),
+        out_shape=(shape,) * 4,
+        in_specs=[SCALARS] + [block_in] * 4 + [ANYWHERE] * 4,
+        out_specs=(block_out,) * 4,
+        scratch_shapes=[
+            pltpu.VMEM((2 * mine.shape[0], mine.shape[1]), mine.dtype) for mine, _ in weights
+        ]
+        + [pltpu.SemaphoreType.DMA((2, 2))],
+        compiler_params=pltpu.CompilerParams(vmem_limit_bytes=VMEM_LIMIT),
+        cost_estimate=pl.CostEstimate(
+            flops=20 * tokens * features * features,
+            bytes_accessed=8 * tokens * features,
+            transcendentals=4 * tokens * features,
+        ),
+        name="temporal",
+    )(place, even, odd, left_odd, right_even, *flat)
+
+
+AXES = ("tm", "cell", "sub")
+
+
+def permutation(sizes, target):
+    tm_size, cell_size, sub_size = sizes
+    pairs = []
+    for tm in range(tm_size):
+        for cell in range(cell_size):
+            for sub in range(sub_size):
+                to_tm, to_cell, to_sub = target(tm, cell, sub)
+                pairs.append(
+                    (
+                        (tm * cell_size + cell) * sub_size + sub,
+                        (to_tm * cell_size + to_cell) * sub_size + to_sub,
+                    )
+                )
+    return pairs
+
+
+def paired(frames, w_qkv, w_out, w_up, w_down, temporal_weight_first, temporal_weight_second):
+    frames_local, cells, features = frames.shape
+    sizes = tuple(lax.axis_size(axis) for axis in AXES)
+    half = sizes[0] // 2
+    subs = sizes[2]
+    tm, cell, sub = (lax.axis_index(axis) for axis in AXES)
+    side = tm // half
+    quarter = 2 * side + cell
+    position = (tm % half) * subs + sub
+    place = jnp.stack(
+        [sub, side, (position == 0).astype(jnp.int32), (position == half * subs - 1).astype(jnp.int32)]
+    ).astype(jnp.int32)
+
+    def partner(delta):
+        def target(at_tm, at_cell, at_sub):
+            return (at_tm + half * (delta // 2)) % (2 * half), at_cell ^ (delta % 2), at_sub
+
+        return permutation(sizes, target)
+
+    def ring(step):
+        def target(at_tm, at_cell, at_sub):
+            spot = ((at_tm % half) * subs + at_sub + step) % (half * subs)
+            return (at_tm // half) * half + spot // subs, at_cell, spot % subs
+
+        return permutation(sizes, target)
+
+    slots = frames_local // DILATION_FIRST
+    grouped = frames.reshape(slots, DILATION_FIRST, cells, features)
+
+    starts = []
+    at = 0
+    for count in CHUNKS:
+        starts.append(at)
+        at += 4 * count
+    pieces = []
+    for begin, count in zip(starts, CHUNKS):
+        cut = [
+            lax.dynamic_slice_in_dim(grouped, begin + (quarter ^ delta) * count, count, axis=1)
+            for delta in range(4)
+        ]
+        pieces.append([cut[0]] + [lax.ppermute(cut[d], AXES, partner(d)) for d in (1, 2, 3)])
+
+    def swap_core(weight):
+        return weight, lax.ppermute(
+            weight, AXES, permutation(sizes, lambda a, b, c: (a, b, (c + 1) % subs))
+        )
+
+    section_weights = [swap_core(w) for w in (w_qkv, w_out, w_up, w_down)]
+    temporal_weights = [swap_core(w) for w in (temporal_weight_first, temporal_weight_second)]
+
+    result = jnp.zeros_like(grouped)
+    for begin, count, chunk in zip(starts, CHUNKS, pieces):
+        even, odd = run_section(place, chunk, section_weights)
+        left_odd = lax.ppermute(odd, AXES, ring(1))
+        right_even = lax.ppermute(even, AXES, ring(-1))
+        outs = run_temporal(place, even, odd, left_odd, right_even, temporal_weights)
+        for delta in range(4):
+            back = outs[delta]
+            if delta:
+                back = lax.ppermute(back, AXES, partner(delta))
+            result = lax.dynamic_update_slice_in_dim(
+                result, back, begin + (quarter ^ delta) * count, axis=1
+            )
+    return result.reshape(frames.shape)
+
+
+def local(frames, *weights):
+    frames_local, cells, features = frames.shape
+    tm_size, cell_size, sub_size = (lax.axis_size(axis) for axis in AXES)
+    video = frames_local * tm_size * sub_size
+    fits = (
+        video == 2 * DILATION_SECOND
+        and frames_local == 2 * DILATION_FIRST
+        and tm_size % 2 == 0
+        and cell_size == 2
+        and sub_size == 2
+        and cells % 16 == 0
+        and DILATION_FIRST == 4 * sum(CHUNKS)
+    )
+    return (paired if fits else general)(frames, *weights)
+
+
 def solution(mesh):
-    placed = (
-        P(("groups", "tm", "sub"), "cell", None),
-        P("sub", None),
-        P("sub", None),
-        P("sub", None),
-        P("sub", None),
-        P("sub", None),
-        P("sub", None),
-    )
+    placed = (P(("groups", "tm", "sub"), "cell", None),) + (P("sub", None),) * 6
     return jax.shard_map(
         local,
         mesh=mesh,

time: 223 us -> 137 us (0.61)
  waiting for transfers between devices: 111 us -> 32.9 us
  Pallas kernels: 0 us -> 44.6 us
  matrix products: 38.2 us -> 0 us
  starting transfers between devices: 25.5 us -> 42.8 us
  other arithmetic: 16.7 us -> 0.08 us
  between operations: 13.4 us -> 0.47 us
  blocking collectives: 4.44 us -> 0 us
  local copies, waits for them, and re-layouts: 12.7 us -> 15.4 us
    pallas_call x0 -> x8, Pallas kernels: none -> 44.6 us  [the longest x4 25.6 us: run_section(): pl.pallas_call(section_kernel, grid=(count,), out_shape=(shape, shape), i...]
    ppermute x4 -> x38, waiting for transfers between devices: 75.7 us -> 32.9 us  [the longest x12 20.3 us: paired(): lax.ppermute(cut[d], AXES, partner(d))]
    all_to_all x2 -> x0, waiting for transfers between devices: 33.1 us -> none  [the longest x1 18.1 us: local(): lax.all_to_all(sectioned_frames, 'cell', split_axis=1, concat_axis=0, til...]
    dot_general x6 -> x0, matrix products: 31.6 us -> none  [the longest x2 12.9 us: gated_step(): preact = jnp.dot(stacked, weight, preferred_element_type=jnp.float32)]
    ppermute x4 -> x38, starting transfers between devices: 17.5 us -> 42.8 us  [the longest x12 17.9 us: paired(): back = lax.ppermute(back, AXES, partner(delta))]
    unnamed x12 -> x56, local copies, waits for them, and re-layouts: 1.72 us -> 12.3 us
    slice x5 -> x0, local copies, waits for them, and re-layouts: 8.04 us -> none  [the longest x2 3.67 us: local(): key_vals[..., :features]]
    all_to_all x2 -> x0, starting transfers between devices: 7.89 us -> none  [the longest x1 4.22 us: local(): lax.all_to_all(frames, 'cell', split_axis=0, concat_axis=1, tiled=True)]
  transfers between devices with their start and end apart: 10 -> 38, of which waited for: 6 -> 10; matrix products, arithmetic and copies ran while one was open for 15% -> 2% of each run, Pallas kernels for 0% -> 33%
where the time goes in v1:
time: 137 us; the launch traced here: 136 us
  Pallas kernels  44.6 us (33%)
  starting transfers between devices  42.8 us (31%)
  waiting for transfers between devices  32.9 us (24%)
  local copies, waits for them, and re-layouts  15.4 us (11%)
    pallas_call x4, Pallas kernels, run_section(): pl.pallas_call(section_kernel, grid=(count,), out_shape=(shape, shape), i...  25.6 us
    ppermute x12, waiting for transfers between devices, paired(): lax.ppermute(cut[d], AXES, partner(d))  20.3 us
    pallas_call x4, Pallas kernels, run_temporal(): pl.pallas_call(temporal_kernel, grid=(count,), out_shape=(shape,) * 4, in...  19 us
    ppermute x12, starting transfers between devices, paired(): back = lax.ppermute(back, AXES, partner(delta))  17.9 us
    ppermute x12, starting transfers between devices, paired(): lax.ppermute(cut[d], AXES, partner(d))  15.4 us
    ppermute x12, waiting for transfers between devices, paired(): back = lax.ppermute(back, AXES, partner(delta))  12.6 us
    unnamed x56, local copies, waits for them, and re-layouts  12.3 us
    ppermute x4, starting transfers between devices, paired(): right_even = lax.ppermute(even, AXES, ring(-1))  8.3 us
  transfers between devices with their start and end apart: 38, of which 10 were waited for; matrix products, arithmetic and copies ran while one was open for 2% of the time, Pallas kernels for 33%

profile of v1, /device:TPU:0, one launch (start us, length us, event | category | flops | bytes accessed | tf_op | source)
XLA Modules:
  0.0 136.3 jit_solution(15002291827988061217)
XLA Ops:
  0.5 2.6 %constant_dynamic-slice_fusion = (bf16[2,1,64,384]{3,2,1,0:T(8,128)(2,1)S(1)}, bf16[2,1,64,384]{3,2,1,0:T(8,128)(2,1)S(1)}, bf16[2,1,64,384]{3,2,1,0:T(8,128)(2,...) fusion(bf16[2,16,64,384]{3,2,1,0:T(8,128)(2,1)} %bitcast.6, ...), kind=kLoop, calls=%fused_computation.4 | loop fusion | bytes 3145792 | tf_op jit(solution)/shard_map/dynamic_slice | solution.py:448
  3.1 3.0 %collective-permute-start.30 = (bf16[2,1,64,384]{3,2,1,0:T(8,128)(2,1)S(1)}, bf16[2,1,64,384]{3,2,1,0:T(8,128)(2,1)S(1)}, u32[]{:S(2)}, u32[]{:S(2)}) collective-permute-start(bf16[2,1,64,384]{3,2,1,0:T(8,128)(2,1)S(1)} %get-tuple-element.55), channel_id=1, source_target_pairs={{0,2},{1,3},{2,0},{3,1},{4,6},{5,7},{6,4},{7,5},{8,10},{9,11},{10,... | collective-permute-start | bytes 294920 | tf_op jit(solution)/shard_map/ppermute | solution.py:451
  6.1 2.6 %collective-permute-start.31 = (bf16[2,1,64,384]{3,2,1,0:T(8,128)(2,1)S(1)}, bf16[2,1,64,384]{3,2,1,0:T(8,128)(2,1)S(1)}, u32[]{:S(2)}, u32[]{:S(2)}) collective-permute-start(bf16[2,1,64,384]{3,2,1,0:T(8,128)(2,1)S(1)} %get-tuple-element.54), channel_id=1, source_target_pairs={{0,16},{1,17},{2,18},{3,19},{4,20},{5,21},{6,22},{7,23},{8,24},{9,... | collective-permute-start | bytes 294920 | tf_op jit(solution)/shard_map/ppermute | solution.py:451
  9.7 6.8 %collective-permute-done.31.far_own = bf16[2,1,64,384]{3,2,1,0:T(8,128)(2,1)S(1)} collective-permute-done((bf16[2,1,64,384]{3,2,1,0:T(8,128)(2,1)S(1)}, bf16[2,1,64,384]{3,2,1,0:T(8,128)(2,1)S(1)}, u32[]{:S(2)}, u32[]{:S(2)}) %collective-permute-start.31) | collective-permute-done | bytes 98336 | tf_op jit(solution)/shard_map/ppermute | solution.py:451
  18.3 3.5 %collective-permute-done.near_cells = bf16[2,1,64,384]{3,2,1,0:T(8,128)(2,1)S(1)} collective-permute-done((bf16[2,1,64,384]{3,2,1,0:T(8,128)(2,1)S(1)}, bf16[2,1,64,384]{3,2,1,0:T(8,128)(2,1)S(1)}, u32[]{:S(2)}, u32[]{:S(2)}) %collective-permute-start) | collective-permute-done | bytes 98336 | tf_op jit(solution)/shard_map/ppermute | solution.py:451
  22.5 3.4 %collective-permute-done.1.far_own = bf16[2,1,64,384]{3,2,1,0:T(8,128)(2,1)S(1)} collective-permute-done((bf16[2,1,64,384]{3,2,1,0:T(8,128)(2,1)S(1)}, bf16[2,1,64,384]{3,2,1,0:T(8,128)(2,1)S(1)}, u32[]{:S(2)}, u32[]{:S(2)}) %collective-permute-start.1) | collective-permute-done | bytes 98336 | tf_op jit(solution)/shard_map/ppermute | solution.py:451
  27.0 6.0 %collective-permute-done.2.far_cells = bf16[2,1,64,384]{3,2,1,0:T(8,128)(2,1)S(1)} collective-permute-done((bf16[2,1,64,384]{3,2,1,0:T(8,128)(2,1)S(1)}, bf16[2,1,64,384]{3,2,1,0:T(8,128)(2,1)S(1)}, u32[]{:S(2)}, u32[]{:S(2)}) %collective-permute-start.2) | collective-permute-done | bytes 98336 | tf_op jit(solution)/shard_map/ppermute | solution.py:451
  36.4 2.9 %collective-permute-start.24 = (bf16[2,1,64,384]{3,2,1,0:T(8,128)(2,1)}, bf16[2,1,64,384]{3,2,1,0:T(8,128)(2,1)S(1)}, u32[]{:S(2)}, u32[]{:S(2)}) collective-permute-start(bf16[2,1,64,384]{3,2,1,0:T(8,128)(2,1)} %get-tuple-element.57), channel_id=1, source_target_pairs={{0,18},{1,19},{2,16},{3,17},{4,22},{5,23},{6,20},{7,21},{8,26},{9,... | collective-permute-start | bytes 294920 | tf_op jit(solution)/shard_map/ppermute | solution.py:451
  46.0 6.4 %section.4 = (bf16[2,1,128,384]{3,2,1,0:T(8,128)(2,1)S(1)}, bf16[2,1,128,384]{3,2,1,0:T(8,128)(2,1)S(1)}) custom-call(s32[4]{0:T(128)S(1)} %pad_add_fusion.place, bf16[2,1,64,384]{3,2,1,0:T(8,128)(2,1)S(1)} %get-tuple-element.68.own, bf16[2,1,64,384]{3,2,1,0:T(8,128)(2,1)S(1)} %copy-done.19, bf16[2,1,64,384]{3,2,1,0:T(8,128)(2,1)S(1)} %copy-done.21, ...), custom_call_target="tpu_custom_call" | custom-call | flops 1912602624 | bytes 1572864 | tf_op jit(solution)/shard_map/section/pallas_call | solution.py:347
  52.5 1.6 %collective-permute-start.14 = (bf16[2,1,64,384]{3,2,1,0:T(8,128)(2,1)S(1)}, bf16[2,1,64,384]{3,2,1,0:T(8,128)(2,1)S(1)}, u32[]{:S(2)}, u32[]{:S(2)}) collective-permute-start(bf16[2,1,64,384]{3,2,1,0:T(8,128)(2,1)S(1)} %copy-done.27), channel_id=1, source_target_pairs={{0,2},{1,3},{2,0},{3,1},{4,6},{5,7},{6,4},{7,5},{8,10},{9,11},{10,... | collective-permute-start | bytes 294920 | tf_op jit(solution)/shard_map/ppermute | solution.py:451
  54.2 6.4 %section.7 = (bf16[2,1,128,384]{3,2,1,0:T(8,128)(2,1)S(1)}, bf16[2,1,128,384]{3,2,1,0:T(8,128)(2,1)S(1)}) custom-call(s32[4]{0:T(128)S(1)} %pad_add_fusion.place, bf16[2,1,64,384]{3,2,1,0:T(8,128)(2,1)S(1)} %get-tuple-element.56.own, bf16[2,1,64,384]{3,2,1,0:T(8,128)(2,1)S(1)} %copy-done.13, bf16[2,1,64,384]{3,2,1,0:T(8,128)(2,1)S(1)} %copy-done.15, ...), custom_call_target="tpu_custom_call" | custom-call | flops 1912602624 | bytes 1572864 | tf_op jit(solution)/shard_map/section/pallas_call | solution.py:347
  60.6 2.9 %collective-permute-start.16 = (bf16[2,1,64,384]{3,2,1,0:T(8,128)(2,1)S(1)}, bf16[2,1,64,384]{3,2,1,0:T(8,128)(2,1)S(1)}, u32[]{:S(2)}, u32[]{:S(2)}) collective-permute-start(bf16[2,1,64,384]{3,2,1,0:T(8,128)(2,1)S(1)} %copy-done.25), channel_id=1, source_target_pairs={{0,18},{1,19},{2,16},{3,17},{4,22},{5,23},{6,20},{7,21},{8,26},{9,... | collective-permute-start | bytes 294920 | tf_op jit(solution)/shard_map/ppermute | solution.py:451
  63.5 2.3 %collective-permute-start.8 = (bf16[2,1,128,384]{3,2,1,0:T(8,128)(2,1)S(1)}, bf16[2,1,128,384]{3,2,1,0:T(8,128)(2,1)S(1)}, u32[]{:S(2)}, u32[]{:S(2)}) collective-permute-start(bf16[2,1,128,384]{3,2,1,0:T(8,128)(2,1)S(1)} %get-tuple-element.29.even), channel_id=1, source_target_pairs={{0,13},{1,0},{2,15},{3,2},{4,1},{5,4},{6,3},{7,6},{8,5},{9,8},{10,... | collective-permute-start | bytes 589832 | tf_op jit(solution)/shard_map/ppermute | solution.py:465
  65.8 6.4 %section.6 = (bf16[2,1,128,384]{3,2,1,0:T(8,128)(2,1)S(1)}, bf16[2,1,128,384]{3,2,1,0:T(8,128)(2,1)S(1)}) custom-call(s32[4]{0:T(128)S(1)} %pad_add_fusion.place, bf16[2,1,64,384]{3,2,1,0:T(8,128)(2,1)S(1)} %get-tuple-element.60.own, bf16[2,1,64,384]{3,2,1,0:T(8,128)(2,1)S(1)} %collective-permute-done.22.near_cells, ...), custom_call_target="tpu_custom_call" | custom-call | flops 1912602624 | bytes 1572864 | tf_op jit(solution)/shard_map/section/pallas_call | solution.py:347
  72.3 2.6 %collective-permute-start.34 = (bf16[2,1,128,384]{3,2,1,0:T(8,128)(2,1)S(1)}, bf16[2,1,128,384]{3,2,1,0:T(8,128)(2,1)S(1)}, u32[]{:S(2)}, u32[]{:S(2)}) collective-permute-start(bf16[2,1,128,384]{3,2,1,0:T(8,128)(2,1)S(1)} %get-tuple-element.47.even), channel_id=1, source_target_pairs={{0,13},{1,0},{2,15},{3,2},{4,1},{5,4},{6,3},{7,6},{8,5},{9,8},{10,... | collective-permute-start | bytes 589832 | tf_op jit(solution)/shard_map/ppermute | solution.py:465
  75.0 6.4 %section.5 = (bf16[2,1,128,384]{3,2,1,0:T(8,128)(2,1)S(1)}, bf16[2,1,128,384]{3,2,1,0:T(8,128)(2,1)S(1)}) custom-call(s32[4]{0:T(128)S(1)} %pad_add_fusion.place, bf16[2,1,64,384]{3,2,1,0:T(8,128)(2,1)S(1)} %get-tuple-element.64.own, bf16[2,1,64,384]{3,2,1,0:T(8,128)(2,1)S(1)} %collective-permute-done.14.near_cells, ...), custom_call_target="tpu_custom_call" | custom-call | flops 1912602624 | bytes 1572864 | tf_op jit(solution)/shard_map/section/pallas_call | solution.py:347
  81.5 2.6 %collective-permute-start.18 = (bf16[2,1,128,384]{3,2,1,0:T(8,128)(2,1)S(1)}, bf16[2,1,128,384]{3,2,1,0:T(8,128)(2,1)S(1)}, u32[]{:S(2)}, u32[]{:S(2)}) collective-permute-start(bf16[2,1,128,384]{3,2,1,0:T(8,128)(2,1)S(1)} %get-tuple-element.35.even), channel_id=1, source_target_pairs={{0,13},{1,0},{2,15},{3,2},{4,1},{5,4},{6,3},{7,6},{8,5},{9,8},{10,... | collective-permute-start | bytes 589832 | tf_op jit(solution)/shard_map/ppermute | solution.py:465
  84.2 4.7 %temporal.4 = (bf16[2,1,64,384]{3,2,1,0:T(8,128)(2,1)S(1)}, bf16[2,1,64,384]{3,2,1,0:T(8,128)(2,1)S(1)}, bf16[2,1,64,384]{3,2,1,0:T(8,128)(2,1)S(1)}, bf16[2,1,64,384]{3,2,1,0:T(8,128)(2,1)S(1)}) custom-call(s32[4]{0:T(128)S(1)} %pad_add_fusion.place, bf16[2,1,128,384]{3,2,1,0:T(8,128)(2,1)S(1)} %get-tuple-element.29.even, ...), custom_call_target="tpu_custom_call" | custom-call | flops 1509949440 | bytes 1572864 | tf_op jit(solution)/shard_map/temporal/pallas_call | solution.py:372
  91.1 4.7 %temporal.7 = (bf16[2,1,64,384]{3,2,1,0:T(8,128)(2,1)S(1)}, bf16[2,1,64,384]{3,2,1,0:T(8,128)(2,1)S(1)}, bf16[2,1,64,384]{3,2,1,0:T(8,128)(2,1)S(1)}, bf16[2,1,64,384]{3,2,1,0:T(8,128)(2,1)S(1)}) custom-call(s32[4]{0:T(128)S(1)} %pad_add_fusion.place, bf16[2,1,128,384]{3,2,1,0:T(8,128)(2,1)S(1)} %get-tuple-element.47.even, ...), custom_call_target="tpu_custom_call" | custom-call | flops 1509949440 | bytes 1572864 | tf_op jit(solution)/shard_map/temporal/pallas_call | solution.py:372
  96.0 2.8 %collective-permute-start.13 = (bf16[2,1,64,384]{3,2,1,0:T(8,128)(2,1)S(1)}, bf16[2,1,64,384]{3,2,1,0:T(8,128)(2,1)S(1)}, u32[]{:S(2)}, u32[]{:S(2)}) collective-permute-start(bf16[2,1,64,384]{3,2,1,0:T(8,128)(2,1)S(1)} %get-tuple-element.34), channel_id=1, source_target_pairs={{0,18},{1,19},{2,16},{3,17},{4,22},{5,23},{6,20},{7,21},{8,26},{9,... | collective-permute-start | bytes 294920 | tf_op jit(solution)/shard_map/ppermute | solution.py:470
  98.8 4.7 %temporal.5 = (bf16[2,1,64,384]{3,2,1,0:T(8,128)(2,1)S(1)}, bf16[2,1,64,384]{3,2,1,0:T(8,128)(2,1)S(1)}, bf16[2,1,64,384]{3,2,1,0:T(8,128)(2,1)S(1)}, bf16[2,1,64,384]{3,2,1,0:T(8,128)(2,1)S(1)}) custom-call(s32[4]{0:T(128)S(1)} %pad_add_fusion.place, bf16[2,1,128,384]{3,2,1,0:T(8,128)(2,1)S(1)} %get-tuple-element.35.even, ...), custom_call_target="tpu_custom_call" | custom-call | flops 1509949440 | bytes 1572864 | tf_op jit(solution)/shard_map/temporal/pallas_call | solution.py:372
  103.6 1.6 %collective-permute-start.19 = (bf16[2,1,64,384]{3,2,1,0:T(8,128)(2,1)S(1)}, bf16[2,1,64,384]{3,2,1,0:T(8,128)(2,1)S(1)}, u32[]{:S(2)}, u32[]{:S(2)}) collective-permute-start(bf16[2,1,64,384]{3,2,1,0:T(8,128)(2,1)S(1)} %get-tuple-element.38), channel_id=1, source_target_pairs={{0,2},{1,3},{2,0},{3,1},{4,6},{5,7},{6,4},{7,5},{8,10},{9,11},{10,... | collective-permute-start | bytes 294920 | tf_op jit(solution)/shard_map/ppermute | solution.py:470
  105.3 4.7 %temporal.6 = (bf16[2,1,64,384]{3,2,1,0:T(8,128)(2,1)S(1)}, bf16[2,1,64,384]{3,2,1,0:T(8,128)(2,1)S(1)}, bf16[2,1,64,384]{3,2,1,0:T(8,128)(2,1)S(1)}, bf16[2,1,64,384]{3,2,1,0:T(8,128)(2,1)S(1)}) custom-call(s32[4]{0:T(128)S(1)} %pad_add_fusion.place, bf16[2,1,128,384]{3,2,1,0:T(8,128)(2,1)S(1)} %get-tuple-element.41.even, ...), custom_call_target="tpu_custom_call" | custom-call | flops 1509949440 | bytes 1572864 | tf_op jit(solution)/shard_map/temporal/pallas_call | solution.py:372
  110.3 2.9 %collective-permute-start.21 = (bf16[2,1,64,384]{3,2,1,0:T(8,128)(2,1)S(1)}, bf16[2,1,64,384]{3,2,1,0:T(8,128)(2,1)S(1)}, u32[]{:S(2)}, u32[]{:S(2)}) collective-permute-start(bf16[2,1,64,384]{3,2,1,0:T(8,128)(2,1)S(1)} %get-tuple-element.40), channel_id=1, source_target_pairs={{0,18},{1,19},{2,16},{3,17},{4,22},{5,23},{6,20},{7,21},{8,26},{9,... | collective-permute-start | bytes 294920 | tf_op jit(solution)/shard_map/ppermute | solution.py:470
  113.2 1.6 %collective-permute-start.27 = (bf16[2,1,64,384]{3,2,1,0:T(8,128)(2,1)S(1)}, bf16[2,1,64,384]{3,2,1,0:T(8,128)(2,1)S(1)}, u32[]{:S(2)}, u32[]{:S(2)}) collective-permute-start(bf16[2,1,64,384]{3,2,1,0:T(8,128)(2,1)S(1)} %get-tuple-element.44), channel_id=1, source_target_pairs={{0,2},{1,3},{2,0},{3,1},{4,6},{5,7},{6,4},{7,5},{8,10},{9,11},{10,... | collective-permute-start | bytes 294920 | tf_op jit(solution)/shard_map/ppermute | solution.py:470
  115.0 2.9 %collective-permute-start.29 = (bf16[2,1,64,384]{3,2,1,0:T(8,128)(2,1)S(1)}, bf16[2,1,64,384]{3,2,1,0:T(8,128)(2,1)S(1)}, u32[]{:S(2)}, u32[]{:S(2)}) collective-permute-start(bf16[2,1,64,384]{3,2,1,0:T(8,128)(2,1)S(1)} %get-tuple-element.46), channel_id=1, source_target_pairs={{0,18},{1,19},{2,16},{3,17},{4,22},{5,23},{6,20},{7,21},{8,26},{9,... | collective-permute-start | bytes 294920 | tf_op jit(solution)/shard_map/ppermute | solution.py:470
  117.9 1.6 %collective-permute-start.35 = (bf16[2,1,64,384]{3,2,1,0:T(8,128)(2,1)S(1)}, bf16[2,1,64,384]{3,2,1,0:T(8,128)(2,1)S(1)}, u32[]{:S(2)}, u32[]{:S(2)}) collective-permute-start(bf16[2,1,64,384]{3,2,1,0:T(8,128)(2,1)S(1)} %get-tuple-element.50), channel_id=1, source_target_pairs={{0,2},{1,3},{2,0},{3,1},{4,6},{5,7},{6,4},{7,5},{8,10},{9,11},{10,... | collective-permute-start | bytes 294920 | tf_op jit(solution)/shard_map/ppermute | solution.py:470
  119.5 6.1 %collective-permute-done.21 = bf16[2,1,64,384]{3,2,1,0:T(8,128)(2,1)S(1)} collective-permute-done((bf16[2,1,64,384]{3,2,1,0:T(8,128)(2,1)S(1)}, bf16[2,1,64,384]{3,2,1,0:T(8,128)(2,1)S(1)}, u32[]{:S(2)}, u32[]{:S(2)}) %collective-permute-start.21) | collective-permute-done | bytes 98336 | tf_op jit(solution)/shard_map/ppermute | solution.py:470
  125.6 2.8 %collective-permute-start.37 = (bf16[2,1,64,384]{3,2,1,0:T(8,128)(2,1)S(1)}, bf16[2,1,64,384]{3,2,1,0:T(8,128)(2,1)S(1)}, u32[]{:S(2)}, u32[]{:S(2)}) collective-permute-start(bf16[2,1,64,384]{3,2,1,0:T(8,128)(2,1)S(1)} %get-tuple-element.52), channel_id=1, source_target_pairs={{0,18},{1,19},{2,16},{3,17},{4,22},{5,23},{6,20},{7,21},{8,26},{9,... | collective-permute-start | bytes 294920 | tf_op jit(solution)/shard_map/ppermute | solution.py:470
  128.5 2.3 %collective-permute-done.29 = bf16[2,1,64,384]{3,2,1,0:T(8,128)(2,1)S(1)} collective-permute-done((bf16[2,1,64,384]{3,2,1,0:T(8,128)(2,1)S(1)}, bf16[2,1,64,384]{3,2,1,0:T(8,128)(2,1)S(1)}, u32[]{:S(2)}, u32[]{:S(2)}) %collective-permute-start.29) | collective-permute-done | bytes 98336 | tf_op jit(solution)/shard_map/ppermute | solution.py:470
  130.9 2.3 %collective-permute-done.36 = bf16[2,1,64,384]{3,2,1,0:T(8,128)(2,1)S(1)} collective-permute-done((bf16[2,1,64,384]{3,2,1,0:T(8,128)(2,1)S(1)}, bf16[2,1,64,384]{3,2,1,0:T(8,128)(2,1)S(1)}, u32[]{:S(2)}, u32[]{:S(2)}) %collective-permute-start.36) | collective-permute-done | bytes 98336 | tf_op jit(solution)/shard_map/ppermute | solution.py:470
  133.3 1.9 %collective-permute-done.37 = bf16[2,1,64,384]{3,2,1,0:T(8,128)(2,1)S(1)} collective-permute-done((bf16[2,1,64,384]{3,2,1,0:T(8,128)(2,1)S(1)}, bf16[2,1,64,384]{3,2,1,0:T(8,128)(2,1)S(1)}, u32[]{:S(2)}, u32[]{:S(2)}) %collective-permute-start.37) | collective-permute-done | bytes 98336 | tf_op jit(solution)/shard_map/ppermute | solution.py:470
  (127 shorter events, 19.7 us)
Async XLA Ops:
  0.0 36.4 %collective-permute-start.5 = (bf16[192,1536]{1,0:T(8,128)(2,1)}, bf16[192,1536]{1,0:T(8,128)(2,1)}, u32[]{:S(2)}, u32[]{:S(2)}) collective-permute-start(bf16[192,1536]{1,0:T(8,128)(2,1)} %up_a.7), channel_id=1, source_target_pairs={{0,1},{1,0},{2,3},{3,2},{4,5},{5,4},{6,7},{7,6},{8,9},{9,8},{10,11... | collective-permute-start | bytes 1769480 | tf_op jit(solution)/shard_map/ppermute | solution.py:454
  0.5 36.0 %collective-permute-start.6 = (bf16[768,384]{1,0:T(8,128)(2,1)}, bf16[768,384]{1,0:T(8,128)(2,1)}, u32[]{:S(2)}, u32[]{:S(2)}) collective-permute-start(bf16[768,384]{1,0:T(8,128)(2,1)} %down_a.7), channel_id=1, source_target_pairs={{0,1},{1,0},{2,3},{3,2},{4,5},{5,4},{6,7},{7,6},{8,9},{9,8},{10,11... | collective-permute-start | bytes 1769480 | tf_op jit(solution)/shard_map/ppermute | solution.py:454
  6.1 10.4 %collective-permute-start.31 = (bf16[2,1,64,384]{3,2,1,0:T(8,128)(2,1)S(1)}, bf16[2,1,64,384]{3,2,1,0:T(8,128)(2,1)S(1)}, u32[]{:S(2)}, u32[]{:S(2)}) collective-permute-start(bf16[2,1,64,384]{3,2,1,0:T(8,128)(2,1)S(1)} %get-tuple-element.54), channel_id=1, source_target_pairs={{0,16},{1,17},{2,18},{3,19},{4,20},{5,21},{6,22},{7,23},{8,24},{9,... | collective-permute-start | bytes 294920 | tf_op jit(solution)/shard_map/ppermute | solution.py:451
  8.7 9.0 %collective-permute-start.32 = (bf16[2,1,64,384]{3,2,1,0:T(8,128)(2,1)S(1)}, bf16[2,1,64,384]{3,2,1,0:T(8,128)(2,1)S(1)}, u32[]{:S(2)}, u32[]{:S(2)}) collective-permute-start(bf16[2,1,64,384]{3,2,1,0:T(8,128)(2,1)S(1)} %get-tuple-element.53), channel_id=1, source_target_pairs={{0,18},{1,19},{2,16},{3,17},{4,22},{5,23},{6,20},{7,21},{8,26},{9,... | collective-permute-start | bytes 294920 | tf_op jit(solution)/shard_map/ppermute | solution.py:451
  9.7 25.2 %collective-permute-start.3 = (bf16[192,1152]{1,0:T(8,128)(2,1)S(1)}, bf16[192,1152]{1,0:T(8,128)(2,1)}, u32[]{:S(2)}, u32[]{:S(2)}) collective-permute-start(bf16[192,1152]{1,0:T(8,128)(2,1)S(1)} %copy-done.6), channel_id=1, source_target_pairs={{0,1},{1,0},{2,3},{3,2},{4,5},{5,4},{6,7},{7,6},{8,9},{9,8},{10,11... | collective-permute-start | bytes 1327112 | tf_op jit(solution)/shard_map/ppermute | solution.py:454
  22.4 11.2 %collective-permute-start.4 = (bf16[192,384]{1,0:T(8,128)(2,1)S(1)}, bf16[192,384]{1,0:T(8,128)(2,1)S(1)}, u32[]{:S(2)}, u32[]{:S(2)}) collective-permute-start(bf16[192,384]{1,0:T(8,128)(2,1)S(1)} %copy-done.7), channel_id=1, source_target_pairs={{0,1},{1,0},{2,3},{3,2},{4,5},{5,4},{6,7},{7,6},{8,9},{9,8},{10,11... | collective-permute-start | bytes 442376 | tf_op jit(solution)/shard_map/ppermute | solution.py:454
  33.7 47.8 %collective-permute-start.10 = (bf16[576,768]{1,0:T(8,128)(2,1)S(1)}, bf16[576,768]{1,0:T(8,128)(2,1)S(1)}, u32[]{:S(2)}, u32[]{:S(2)}) collective-permute-start(bf16[576,768]{1,0:T(8,128)(2,1)S(1)} %copy-done.1), channel_id=1, source_target_pairs={{0,1},{1,0},{2,3},{3,2},{4,5},{5,4},{6,7},{7,6},{8,9},{9,8},{10,11... | collective-permute-start | bytes 2654216 | tf_op jit(solution)/shard_map/ppermute | solution.py:454
  34.3 47.2 %collective-permute-start.9 = (bf16[576,768]{1,0:T(8,128)(2,1)S(1)}, bf16[576,768]{1,0:T(8,128)(2,1)}, u32[]{:S(2)}, u32[]{:S(2)}) collective-permute-start(bf16[576,768]{1,0:T(8,128)(2,1)S(1)} %copy-done), channel_id=1, source_target_pairs={{0,1},{1,0},{2,3},{3,2},{4,5},{5,4},{6,7},{7,6},{8,9},{9,8},{10,11... | collective-permute-start | bytes 2654216 | tf_op jit(solution)/shard_map/ppermute | solution.py:454
  34.9 17.5 %collective-permute-start.22 = (bf16[2,1,64,384]{3,2,1,0:T(8,128)(2,1)}, bf16[2,1,64,384]{3,2,1,0:T(8,128)(2,1)S(1)}, u32[]{:S(2)}, u32[]{:S(2)}) collective-permute-start(bf16[2,1,64,384]{3,2,1,0:T(8,128)(2,1)} %get-tuple-element.59), channel_id=1, source_target_pairs={{0,2},{1,3},{2,0},{3,1},{4,6},{5,7},{6,4},{7,5},{8,10},{9,11},{10,... | collective-permute-start | bytes 294920 | tf_op jit(solution)/shard_map/ppermute | solution.py:451
  36.4 17.6 %collective-permute-start.23 = (bf16[2,1,64,384]{3,2,1,0:T(8,128)(2,1)}, bf16[2,1,64,384]{3,2,1,0:T(8,128)(2,1)S(1)}, u32[]{:S(2)}, u32[]{:S(2)}) collective-permute-start(bf16[2,1,64,384]{3,2,1,0:T(8,128)(2,1)} %get-tuple-element.58), channel_id=1, source_target_pairs={{0,16},{1,17},{2,18},{3,19},{4,20},{5,21},{6,22},{7,23},{8,24},{9,... | collective-permute-start | bytes 294920 | tf_op jit(solution)/shard_map/ppermute | solution.py:451
  36.4 17.6 %collective-permute-start.24 = (bf16[2,1,64,384]{3,2,1,0:T(8,128)(2,1)}, bf16[2,1,64,384]{3,2,1,0:T(8,128)(2,1)S(1)}, u32[]{:S(2)}, u32[]{:S(2)}) collective-permute-start(bf16[2,1,64,384]{3,2,1,0:T(8,128)(2,1)} %get-tuple-element.57), channel_id=1, source_target_pairs={{0,18},{1,19},{2,16},{3,17},{4,22},{5,23},{6,20},{7,21},{8,26},{9,... | collective-permute-start | bytes 294920 | tf_op jit(solution)/shard_map/ppermute | solution.py:451
  54.0 9.5 %collective-permute-start.15 = (bf16[2,1,64,384]{3,2,1,0:T(8,128)(2,1)S(1)}, bf16[2,1,64,384]{3,2,1,0:T(8,128)(2,1)S(1)}, u32[]{:S(2)}, u32[]{:S(2)}) collective-permute-start(bf16[2,1,64,384]{3,2,1,0:T(8,128)(2,1)S(1)} %copy-done.26), channel_id=1, source_target_pairs={{0,16},{1,17},{2,18},{3,19},{4,20},{5,21},{6,22},{7,23},{8,24},{9,... | collective-permute-start | bytes 294920 | tf_op jit(solution)/shard_map/ppermute | solution.py:451
  54.1 18.2 %collective-permute-start.7 = (bf16[2,1,128,384]{3,2,1,0:T(8,128)(2,1)S(1)}, bf16[2,1,128,384]{3,2,1,0:T(8,128)(2,1)S(1)}, u32[]{:S(2)}, u32[]{:S(2)}) collective-permute-start(bf16[2,1,128,384]{3,2,1,0:T(8,128)(2,1)S(1)} %get-tuple-element.30.odd), channel_id=1, source_target_pairs={{0,1},{1,4},{2,3},{3,6},{4,5},{5,8},{6,7},{7,10},{8,9},{9,12},{10,... | collective-permute-start | bytes 589832 | tf_op jit(solution)/shard_map/ppermute | solution.py:464
  60.6 11.6 %collective-permute-start.16 = (bf16[2,1,64,384]{3,2,1,0:T(8,128)(2,1)S(1)}, bf16[2,1,64,384]{3,2,1,0:T(8,128)(2,1)S(1)}, u32[]{:S(2)}, u32[]{:S(2)}) collective-permute-start(bf16[2,1,64,384]{3,2,1,0:T(8,128)(2,1)S(1)} %copy-done.25), channel_id=1, source_target_pairs={{0,18},{1,19},{2,16},{3,17},{4,22},{5,23},{6,20},{7,21},{8,26},{9,... | collective-permute-start | bytes 294920 | tf_op jit(solution)/shard_map/ppermute | solution.py:451
  63.5 17.9 %collective-permute-start.8 = (bf16[2,1,128,384]{3,2,1,0:T(8,128)(2,1)S(1)}, bf16[2,1,128,384]{3,2,1,0:T(8,128)(2,1)S(1)}, u32[]{:S(2)}, u32[]{:S(2)}) collective-permute-start(bf16[2,1,128,384]{3,2,1,0:T(8,128)(2,1)S(1)} %get-tuple-element.29.even), channel_id=1, source_target_pairs={{0,13},{1,0},{2,15},{3,2},{4,1},{5,4},{6,3},{7,6},{8,5},{9,8},{10,... | collective-permute-start | bytes 589832 | tf_op jit(solution)/shard_map/ppermute | solution.py:465
  72.3 16.6 %collective-permute-start.33 = (bf16[2,1,128,384]{3,2,1,0:T(8,128)(2,1)S(1)}, bf16[2,1,128,384]{3,2,1,0:T(8,128)(2,1)S(1)}, u32[]{:S(2)}, u32[]{:S(2)}) collective-permute-start(bf16[2,1,128,384]{3,2,1,0:T(8,128)(2,1)S(1)} %get-tuple-element.48.odd), channel_id=1, source_target_pairs={{0,1},{1,4},{2,3},{3,6},{4,5},{5,8},{6,7},{7,10},{8,9},{9,12},{10,... | collective-permute-start | bytes 589832 | tf_op jit(solution)/shard_map/ppermute | solution.py:464
  72.3 17.3 %collective-permute-start.34 = (bf16[2,1,128,384]{3,2,1,0:T(8,128)(2,1)S(1)}, bf16[2,1,128,384]{3,2,1,0:T(8,128)(2,1)S(1)}, u32[]{:S(2)}, u32[]{:S(2)}) collective-permute-start(bf16[2,1,128,384]{3,2,1,0:T(8,128)(2,1)S(1)} %get-tuple-element.47.even), channel_id=1, source_target_pairs={{0,13},{1,0},{2,15},{3,2},{4,1},{5,4},{6,3},{7,6},{8,5},{9,8},{10,... | collective-permute-start | bytes 589832 | tf_op jit(solution)/shard_map/ppermute | solution.py:465
  81.4 22.2 %collective-permute-start.25 = (bf16[2,1,128,384]{3,2,1,0:T(8,128)(2,1)S(1)}, bf16[2,1,128,384]{3,2,1,0:T(8,128)(2,1)S(1)}, u32[]{:S(2)}, u32[]{:S(2)}) collective-permute-start(bf16[2,1,128,384]{3,2,1,0:T(8,128)(2,1)S(1)} %get-tuple-element.42.odd), channel_id=1, source_target_pairs={{0,1},{1,4},{2,3},{3,6},{4,5},{5,8},{6,7},{7,10},{8,9},{9,12},{10,... | collective-permute-start | bytes 589832 | tf_op jit(solution)/shard_map/ppermute | solution.py:464
  81.5 14.4 %collective-permute-start.17 = (bf16[2,1,128,384]{3,2,1,0:T(8,128)(2,1)S(1)}, bf16[2,1,128,384]{3,2,1,0:T(8,128)(2,1)S(1)}, u32[]{:S(2)}, u32[]{:S(2)}) collective-permute-start(bf16[2,1,128,384]{3,2,1,0:T(8,128)(2,1)S(1)} %get-tuple-element.36.odd), channel_id=1, source_target_pairs={{0,1},{1,4},{2,3},{3,6},{4,5},{5,8},{6,7},{7,10},{8,9},{9,12},{10,... | collective-permute-start | bytes 589832 | tf_op jit(solution)/shard_map/ppermute | solution.py:464
  81.5 14.5 %collective-permute-start.18 = (bf16[2,1,128,384]{3,2,1,0:T(8,128)(2,1)S(1)}, bf16[2,1,128,384]{3,2,1,0:T(8,128)(2,1)S(1)}, u32[]{:S(2)}, u32[]{:S(2)}) collective-permute-start(bf16[2,1,128,384]{3,2,1,0:T(8,128)(2,1)S(1)} %get-tuple-element.35.even), channel_id=1, source_target_pairs={{0,13},{1,0},{2,15},{3,2},{4,1},{5,4},{6,3},{7,6},{8,5},{9,8},{10,... | collective-permute-start | bytes 589832 | tf_op jit(solution)/shard_map/ppermute | solution.py:465
  88.9 16.3 %collective-permute-start.26 = (bf16[2,1,128,384]{3,2,1,0:T(8,128)(2,1)S(1)}, bf16[2,1,128,384]{3,2,1,0:T(8,128)(2,1)S(1)}, u32[]{:S(2)}, u32[]{:S(2)}) collective-permute-start(bf16[2,1,128,384]{3,2,1,0:T(8,128)(2,1)S(1)} %get-tuple-element.41.even), channel_id=1, source_target_pairs={{0,13},{1,0},{2,15},{3,2},{4,1},{5,4},{6,3},{7,6},{8,5},{9,8},{10,... | collective-permute-start | bytes 589832 | tf_op jit(solution)/shard_map/ppermute | solution.py:465
  89.6 20.6 %collective-permute-start.11 = (bf16[2,1,64,384]{3,2,1,0:T(8,128)(2,1)S(1)}, bf16[2,1,64,384]{3,2,1,0:T(8,128)(2,1)S(1)}, u32[]{:S(2)}, u32[]{:S(2)}) collective-permute-start(bf16[2,1,64,384]{3,2,1,0:T(8,128)(2,1)S(1)} %get-tuple-element.32), channel_id=1, source_target_pairs={{0,2},{1,3},{2,0},{3,1},{4,6},{5,7},{6,4},{7,5},{8,10},{9,11},{10,... | collective-permute-start | bytes 294920 | tf_op jit(solution)/shard_map/ppermute | solution.py:470
  95.9 17.3 %collective-permute-start.12 = (bf16[2,1,64,384]{3,2,1,0:T(8,128)(2,1)S(1)}, bf16[2,1,64,384]{3,2,1,0:T(8,128)(2,1)S(1)}, u32[]{:S(2)}, u32[]{:S(2)}) collective-permute-start(bf16[2,1,64,384]{3,2,1,0:T(8,128)(2,1)S(1)} %get-tuple-element.33), channel_id=1, source_target_pairs={{0,16},{1,17},{2,18},{3,19},{4,20},{5,21},{6,22},{7,23},{8,24},{9,... | collective-permute-start | bytes 294920 | tf_op jit(solution)/shard_map/ppermute | solution.py:470
  96.0 18.8 %collective-permute-start.13 = (bf16[2,1,64,384]{3,2,1,0:T(8,128)(2,1)S(1)}, bf16[2,1,64,384]{3,2,1,0:T(8,128)(2,1)S(1)}, u32[]{:S(2)}, u32[]{:S(2)}) collective-permute-start(bf16[2,1,64,384]{3,2,1,0:T(8,128)(2,1)S(1)} %get-tuple-element.34), channel_id=1, source_target_pairs={{0,18},{1,19},{2,16},{3,17},{4,22},{5,23},{6,20},{7,21},{8,26},{9,... | collective-permute-start | bytes 294920 | tf_op jit(solution)/shard_map/ppermute | solution.py:470
  103.6 11.4 %collective-permute-start.19 = (bf16[2,1,64,384]{3,2,1,0:T(8,128)(2,1)S(1)}, bf16[2,1,64,384]{3,2,1,0:T(8,128)(2,1)S(1)}, u32[]{:S(2)}, u32[]{:S(2)}) collective-permute-start(bf16[2,1,64,384]{3,2,1,0:T(8,128)(2,1)S(1)} %get-tuple-element.38), channel_id=1, source_target_pairs={{0,2},{1,3},{2,0},{3,1},{4,6},{5,7},{6,4},{7,5},{8,10},{9,11},{10,... | collective-permute-start | bytes 294920 | tf_op jit(solution)/shard_map/ppermute | solution.py:470
  105.2 12.7 %collective-permute-start.20 = (bf16[2,1,64,384]{3,2,1,0:T(8,128)(2,1)S(1)}, bf16[2,1,64,384]{3,2,1,0:T(8,128)(2,1)S(1)}, u32[]{:S(2)}, u32[]{:S(2)}) collective-permute-start(bf16[2,1,64,384]{3,2,1,0:T(8,128)(2,1)S(1)} %get-tuple-element.39), channel_id=1, source_target_pairs={{0,16},{1,17},{2,18},{3,19},{4,20},{5,21},{6,22},{7,23},{8,24},{9,... | collective-permute-start | bytes 294920 | tf_op jit(solution)/shard_map/ppermute | solution.py:470
  110.3 15.3 %collective-permute-start.21 = (bf16[2,1,64,384]{3,2,1,0:T(8,128)(2,1)S(1)}, bf16[2,1,64,384]{3,2,1,0:T(8,128)(2,1)S(1)}, u32[]{:S(2)}, u32[]{:S(2)}) collective-permute-start(bf16[2,1,64,384]{3,2,1,0:T(8,128)(2,1)S(1)} %get-tuple-element.40), channel_id=1, source_target_pairs={{0,18},{1,19},{2,16},{3,17},{4,22},{5,23},{6,20},{7,21},{8,26},{9,... | collective-permute-start | bytes 294920 | tf_op jit(solution)/shard_map/ppermute | solution.py:470
  113.2 12.4 %collective-permute-start.27 = (bf16[2,1,64,384]{3,2,1,0:T(8,128)(2,1)S(1)}, bf16[2,1,64,384]{3,2,1,0:T(8,128)(2,1)S(1)}, u32[]{:S(2)}, u32[]{:S(2)}) collective-permute-start(bf16[2,1,64,384]{3,2,1,0:T(8,128)(2,1)S(1)} %get-tuple-element.44), channel_id=1, source_target_pairs={{0,2},{1,3},{2,0},{3,1},{4,6},{5,7},{6,4},{7,5},{8,10},{9,11},{10,... | collective-permute-start | bytes 294920 | tf_op jit(solution)/shard_map/ppermute | solution.py:470
  114.8 13.7 %collective-permute-start.28 = (bf16[2,1,64,384]{3,2,1,0:T(8,128)(2,1)S(1)}, bf16[2,1,64,384]{3,2,1,0:T(8,128)(2,1)S(1)}, u32[]{:S(2)}, u32[]{:S(2)}) collective-permute-start(bf16[2,1,64,384]{3,2,1,0:T(8,128)(2,1)S(1)} %get-tuple-element.45), channel_id=1, source_target_pairs={{0,16},{1,17},{2,18},{3,19},{4,20},{5,21},{6,22},{7,23},{8,24},{9,... | collective-permute-start | bytes 294920 | tf_op jit(solution)/shard_map/ppermute | solution.py:470
  115.0 15.8 %collective-permute-start.29 = (bf16[2,1,64,384]{3,2,1,0:T(8,128)(2,1)S(1)}, bf16[2,1,64,384]{3,2,1,0:T(8,128)(2,1)S(1)}, u32[]{:S(2)}, u32[]{:S(2)}) collective-permute-start(bf16[2,1,64,384]{3,2,1,0:T(8,128)(2,1)S(1)} %get-tuple-element.46), channel_id=1, source_target_pairs={{0,18},{1,19},{2,16},{3,17},{4,22},{5,23},{6,20},{7,21},{8,26},{9,... | collective-permute-start | bytes 294920 | tf_op jit(solution)/shard_map/ppermute | solution.py:470
  117.9 13.0 %collective-permute-start.35 = (bf16[2,1,64,384]{3,2,1,0:T(8,128)(2,1)S(1)}, bf16[2,1,64,384]{3,2,1,0:T(8,128)(2,1)S(1)}, u32[]{:S(2)}, u32[]{:S(2)}) collective-permute-start(bf16[2,1,64,384]{3,2,1,0:T(8,128)(2,1)S(1)} %get-tuple-element.50), channel_id=1, source_target_pairs={{0,2},{1,3},{2,0},{3,1},{4,6},{5,7},{6,4},{7,5},{8,10},{9,11},{10,... | collective-permute-start | bytes 294920 | tf_op jit(solution)/shard_map/ppermute | solution.py:470
  125.6 9.5 %collective-permute-start.37 = (bf16[2,1,64,384]{3,2,1,0:T(8,128)(2,1)S(1)}, bf16[2,1,64,384]{3,2,1,0:T(8,128)(2,1)S(1)}, u32[]{:S(2)}, u32[]{:S(2)}) collective-permute-start(bf16[2,1,64,384]{3,2,1,0:T(8,128)(2,1)S(1)} %get-tuple-element.52), channel_id=1, source_target_pairs={{0,18},{1,19},{2,16},{3,17},{4,22},{5,23},{6,20},{7,21},{8,26},{9,... | collective-permute-start | bytes 294920 | tf_op jit(solution)/shard_map/ppermute | solution.py:470
  (34 other events, 220.6 us)

commit v2 on v1

--- a/solution.py
+++ b/solution.py
@@ -11,8 +11,9 @@
 HEAD_DIM = 64
 DILATION_FIRST = 16
 DILATION_SECOND = 256
-CHUNKS = (1, 1, 1, 1)
-VMEM_LIMIT = 40 * 1024 * 1024
+CHUNKS = (1, 2, 1)
+ORDER = (("s", 0), ("t", 0), ("s", 1), ("s", 2), ("t", 1), ("t", 2))
+VMEM_LIMIT = 24 * 1024 * 1024
 
 
 def with_halo(block, sides, width):
@@ -138,10 +139,8 @@
 
 def section_kernel(
     place,
-    own,
-    near_cells,
-    far_own,
-    far_cells,
+    before,
+    arrived,
     qkv_a,
     qkv_b,
     out_a,
@@ -171,12 +170,12 @@
     def _():
         start_all(copies)
 
-    features = own.shape[-1]
-    cells = 2 * own.shape[2]
+    features = arrived.shape[-1]
+    cells = 2 * arrived.shape[3]
     parts = []
-    for mine, other in ((own, near_cells), (far_own, far_cells)):
+    for block in range(2):
         for slot in range(2):
-            parts += [mine[slot, 0], other[slot, 0]]
+            parts += [arrived[2 * block, slot, 0], arrived[2 * block + 1, slot, 0]]
     residual = jnp.concatenate(parts, axis=0).astype(jnp.float32)
     frame_count = 4
     normed = normalize(residual).astype(jnp.bfloat16)
@@ -260,6 +259,7 @@
 
 def temporal_kernel(
     place,
+    before,
     even,
     odd,
     left_odd,
@@ -268,15 +268,12 @@
     first_b,
     second_a,
     second_b,
-    out0,
-    out1,
-    out2,
-    out3,
+    out,
     w_first,
     w_second,
     sems,
 ):
-    core, near, is_first, is_last = place[0], place[1], place[2], place[3]
+    core, is_first, is_last = place[0], place[1], place[2]
     copies = load_halves(
         core, ((first_a, first_b), (second_a, second_b)), (w_first, w_second), sems
     )
@@ -287,7 +284,7 @@
         start_all(copies)
         wait_pair(copies[0])
 
-    far = 1 - near
+    near, far = 0, 1
     features = even.shape[-1]
     cells = even.shape[2]
     zero = jnp.zeros((cells, features), even.dtype)
@@ -320,35 +317,32 @@
     result_f = gate(
         far_part, jnp.dot(both, w_second[: 2 * features], preferred_element_type=jnp.float32)
     )
-    same = jnp.where(near == 0, result_n, result_f)
-    other = jnp.where(near == 0, result_f, result_n)
     half = cells // 2
-    for slot in range(2):
-        at = slot * cells
-        out0[slot, 0] = same[at : at + half]
-        out1[slot, 0] = same[at + half : at + cells]
-        out2[slot, 0] = other[at : at + half]
-        out3[slot, 0] = other[at + half : at + cells]
-
-
-ANYWHERE = pl.BlockSpec(memory_space=pl.ANY)
+    for block, result in enumerate((result_n, result_f)):
+        for slot in range(2):
+            at = slot * cells
+            out[2 * block, slot, 0] = result[at : at + half]
+            out[2 * block + 1, slot, 0] = result[at + half : at + cells]
+
+
+PINNED = pl.BlockSpec(memory_space=pl.ANY)
 SCALARS = pl.BlockSpec(memory_space=pltpu.SMEM)
 
 
-def run_section(place, pieces, weights):
-    slots, count, cells, features = pieces[0].shape
+def run_section(place, before, arrived, weights):
+    parts, slots, count, cells, features = arrived.shape
     ff = weights[2][0].shape[1]
-    block_in = pl.BlockSpec((slots, 1, cells, features), lambda i: (0, i, 0, 0))
+    block_in = pl.BlockSpec((parts, slots, 1, cells, features), lambda i: (0, 0, i, 0, 0))
     block_out = pl.BlockSpec((2, 1, 2 * cells, features), lambda i: (0, i, 0, 0))
     shape = jax.ShapeDtypeStruct((2, count, 2 * cells, features), jnp.bfloat16)
-    tokens = 2 * slots * count * 2 * cells
+    tokens = parts * slots * count * cells
     macs = tokens * (features * (4 * features + 2 * ff) + 4 * cells * features)
     flat = [half for pair in weights for half in pair]
     return pl.pallas_call(
         section_kernel,
         grid=(count,),
         out_shape=(shape, shape),
-        in_specs=[SCALARS] + [block_in] * 4 + [ANYWHERE] * 8,
+        in_specs=[SCALARS, PINNED, block_in] + [PINNED] * 8,
         out_specs=(block_out, block_out),
         scratch_shapes=[
             pltpu.VMEM((2 * mine.shape[0], mine.shape[1]), mine.dtype) for mine, _ in weights
@@ -356,146 +350,144 @@
         + [pltpu.SemaphoreType.DMA((4, 2))],
         compiler_params=pltpu.CompilerParams(vmem_limit_bytes=VMEM_LIMIT),
         cost_estimate=pl.CostEstimate(
-            flops=2 * macs, bytes_accessed=8 * tokens * features, transcendentals=tokens * ff
+            flops=6 * macs, bytes_accessed=8 * tokens * features, transcendentals=tokens * ff
         ),
         name="section",
-    )(place, *pieces, *flat)
-
-
-def run_temporal(place, even, odd, left_odd, right_even, weights):
+    )(place, before, arrived, *flat)
+
+
+def run_temporal(place, before, even, odd, left_odd, right_even, weights):
     blocks, count, cells, features = even.shape
     block_in = pl.BlockSpec((blocks, 1, cells, features), lambda i: (0, i, 0, 0))
-    block_out = pl.BlockSpec((2, 1, cells // 2, features), lambda i: (0, i, 0, 0))
-    shape = jax.ShapeDtypeStruct((2, count, cells // 2, features), jnp.bfloat16)
+    parts, slots = 2 * blocks, 2
+    block_out = pl.BlockSpec((parts, slots, 1, cells // 2, features), lambda i: (0, 0, i, 0, 0))
+    shape = jax.ShapeDtypeStruct((parts, slots, count, cells // 2, features), jnp.bfloat16)
     tokens = 2 * blocks * count * cells
     flat = [half for pair in weights for half in pair]
     return pl.pallas_call(
         temporal_kernel,
         grid=(count,),
-        out_shape=(shape,) * 4,
-        in_specs=[SCALARS] + [block_in] * 4 + [ANYWHERE] * 4,
-        out_specs=(block_out,) * 4,
+        out_shape=shape,
+        in_specs=[SCALARS, PINNED] + [block_in] * 4 + [PINNED] * 4,
+        out_specs=block_out,
         scratch_shapes=[
             pltpu.VMEM((2 * mine.shape[0], mine.shape[1]), mine.dtype) for mine, _ in weights
         ]
         + [pltpu.SemaphoreType.DMA((2, 2))],
         compiler_params=pltpu.CompilerParams(vmem_limit_bytes=VMEM_LIMIT),
         cost_estimate=pl.CostEstimate(
-            flops=20 * tokens * features * features,
+            flops=60 * tokens * features * features,
             bytes_accessed=8 * tokens * features,
             transcendentals=4 * tokens * features,
         ),
         name="temporal",
-    )(place, even, odd, left_odd, right_even, *flat)
-
-
-AXES = ("tm", "cell", "sub")
-
-
-def permutation(sizes, target):
-    tm_size, cell_size, sub_size = sizes
-    pairs = []
-    for tm in range(tm_size):
-        for cell in range(cell_size):
-            for sub in range(sub_size):
-                to_tm, to_cell, to_sub = target(tm, cell, sub)
-                pairs.append(
-                    (
-                        (tm * cell_size + cell) * sub_size + sub,
-                        (to_tm * cell_size + to_cell) * sub_size + to_sub,
-                    )
-                )
-    return pairs
+    )(place, before, even, odd, left_odd, right_even, *flat)
+
+
+def pack_kernel(begin, count, before, frames, packed, sems):
+    copies = []
+    for part in range(packed.shape[0]):
+        for slot in range(packed.shape[1]):
+            source = frames.at[slot, begin + part * count : begin + (part + 1) * count]
+            copies.append(
+                pltpu.make_async_copy(source, packed.at[part, slot], sems.at[part, slot])
+            )
+    for copy in copies:
+        copy.start()
+    for copy in copies:
+        copy.wait()
+
+
+def run_pack(before, grouped, begin, count, parts):
+    slots, _, cells, features = grouped.shape
+    return pl.pallas_call(
+        functools.partial(pack_kernel, begin, count),
+        out_shape=jax.ShapeDtypeStruct((parts, slots, count, cells, features), grouped.dtype),
+        in_specs=[PINNED, PINNED],
+        out_specs=PINNED,
+        scratch_shapes=[pltpu.SemaphoreType.DMA((parts, slots))],
+        cost_estimate=pl.CostEstimate(
+            flops=0,
+            bytes_accessed=4 * parts * slots * count * cells * features,
+            transcendentals=0,
+        ),
+        name="pack",
+    )(before, grouped)
 
 
 def paired(frames, w_qkv, w_out, w_up, w_down, temporal_weight_first, temporal_weight_second):
     frames_local, cells, features = frames.shape
-    sizes = tuple(lax.axis_size(axis) for axis in AXES)
-    half = sizes[0] // 2
-    subs = sizes[2]
-    tm, cell, sub = (lax.axis_index(axis) for axis in AXES)
-    side = tm // half
-    quarter = 2 * side + cell
-    position = (tm % half) * subs + sub
-    place = jnp.stack(
-        [sub, side, (position == 0).astype(jnp.int32), (position == half * subs - 1).astype(jnp.int32)]
-    ).astype(jnp.int32)
-
-    def partner(delta):
-        def target(at_tm, at_cell, at_sub):
-            return (at_tm + half * (delta // 2)) % (2 * half), at_cell ^ (delta % 2), at_sub
-
-        return permutation(sizes, target)
-
-    def ring(step):
-        def target(at_tm, at_cell, at_sub):
-            spot = ((at_tm % half) * subs + at_sub + step) % (half * subs)
-            return (at_tm // half) * half + spot // subs, at_cell, spot % subs
-
-        return permutation(sizes, target)
-
+    near_size, subs = lax.axis_size("near"), lax.axis_size("sub")
+    sub = lax.axis_index("sub")
+    ring = near_size * subs
+    position = lax.axis_index("near") * subs + sub
+    place = jnp.stack([sub, position == 0, position == ring - 1]).astype(jnp.int32)
+    rightward = [(i, (i + 1) % ring) for i in range(ring)]
+    leftward = [(target, source) for source, target in rightward]
     slots = frames_local // DILATION_FIRST
     grouped = frames.reshape(slots, DILATION_FIRST, cells, features)
 
-    starts = []
-    at = 0
+    arrived = []
+    begin = 0
+    before = place
     for count in CHUNKS:
-        starts.append(at)
-        at += 4 * count
-    pieces = []
-    for begin, count in zip(starts, CHUNKS):
-        cut = [
-            lax.dynamic_slice_in_dim(grouped, begin + (quarter ^ delta) * count, count, axis=1)
-            for delta in range(4)
-        ]
-        pieces.append([cut[0]] + [lax.ppermute(cut[d], AXES, partner(d)) for d in (1, 2, 3)])
+        before = run_pack(before, grouped, begin, count, 4)
+        arrived.append(lax.all_to_all(before, ("far", "cell"), 0, 0))
+        begin += 4 * count
 
     def swap_core(weight):
-        return weight, lax.ppermute(
-            weight, AXES, permutation(sizes, lambda a, b, c: (a, b, (c + 1) % subs))
-        )
+        return weight, lax.ppermute(weight, "sub", [(0, 1), (1, 0)])
 
     section_weights = [swap_core(w) for w in (w_qkv, w_out, w_up, w_down)]
     temporal_weights = [swap_core(w) for w in (temporal_weight_first, temporal_weight_second)]
 
-    result = jnp.zeros_like(grouped)
-    for begin, count, chunk in zip(starts, CHUNKS, pieces):
-        even, odd = run_section(place, chunk, section_weights)
-        left_odd = lax.ppermute(odd, AXES, ring(1))
-        right_even = lax.ppermute(even, AXES, ring(-1))
-        outs = run_temporal(place, even, odd, left_odd, right_even, temporal_weights)
-        for delta in range(4):
-            back = outs[delta]
-            if delta:
-                back = lax.ppermute(back, AXES, partner(delta))
-            result = lax.dynamic_update_slice_in_dim(
-                result, back, begin + (quarter ^ delta) * count, axis=1
-            )
-    return result.reshape(frames.shape)
-
-
-def local(frames, *weights):
-    frames_local, cells, features = frames.shape
-    tm_size, cell_size, sub_size = (lax.axis_size(axis) for axis in AXES)
-    video = frames_local * tm_size * sub_size
-    fits = (
-        video == 2 * DILATION_SECOND
-        and frames_local == 2 * DILATION_FIRST
-        and tm_size % 2 == 0
-        and cell_size == 2
-        and sub_size == 2
-        and cells % 16 == 0
-        and DILATION_FIRST == 4 * sum(CHUNKS)
-    )
-    return (paired if fits else general)(frames, *weights)
+    waiting, backs = {}, {}
+    before = place
+    for kind, index in ORDER:
+        if kind == "s":
+            even, odd = run_section(place, before, arrived[index], section_weights)
+            left_odd = lax.ppermute(odd, ("near", "sub"), rightward)
+            right_even = lax.ppermute(even, ("near", "sub"), leftward)
+            waiting[index] = (even, odd, left_odd, right_even)
+            before = even
+        else:
+            before = run_temporal(place, before, *waiting[index], temporal_weights)
+            backs[index] = lax.all_to_all(before, ("far", "cell"), 0, 0)
+    results = [
+        backs[index].swapaxes(0, 1).reshape(slots, 4 * count, cells, features)
+        for index, count in enumerate(CHUNKS)
+    ]
+    return jnp.concatenate(results, axis=1).reshape(frames.shape)
 
 
 def solution(mesh):
-    placed = (P(("groups", "tm", "sub"), "cell", None),) + (P("sub", None),) * 6
-    return jax.shard_map(
-        local,
-        mesh=mesh,
-        in_specs=placed,
-        out_specs=P(("groups", "tm", "sub"), "cell", None),
-        check_vma=False,
-    )
+    groups, tm, cell, sub = (mesh.shape[axis] for axis in ("groups", "tm", "cell", "sub"))
+
+    def run(frames, *weights):
+        frame_total, cells, _ = frames.shape
+        video = frame_total // groups
+        frames_local = video // (tm * sub)
+        fits = (
+            video == 2 * DILATION_SECOND
+            and frames_local == 2 * DILATION_FIRST
+            and tm % 2 == 0
+            and cell == 2
+            and sub == 2
+            and (cells // cell) % 16 == 0
+            and DILATION_FIRST == 4 * sum(CHUNKS)
+        )
+        if fits:
+            devices = mesh.devices.reshape(groups, 2, tm // 2, cell, sub)
+            axes = ("groups", "far", "near", "cell", "sub")
+            used, split, body = jax.sharding.Mesh(devices, axes), ("groups", "far", "near", "sub"), paired
+        else:
+            used, split, body = mesh, ("groups", "tm", "sub"), general
+        return jax.shard_map(
+            body,
+            mesh=used,
+            in_specs=(P(split, "cell", None),) + (P("sub", None),) * 6,
+            out_specs=P(split, "cell", None),
+            check_vma=False,
+        )(frames, *weights)
+
+    return run

time: 137 us -> 176 us (1.28)
  Pallas kernels: 44.6 us -> 96.9 us
  waiting for transfers between devices: 32.9 us -> 22.2 us
  starting transfers between devices: 42.8 us -> 39.2 us
  other arithmetic: 0.08 us -> 2.89 us
  local copies, waits for them, and re-layouts: 15.4 us -> 13.1 us
    pallas_call x4 -> x6, Pallas kernels: 19 us -> 71.4 us  [the longest x3 51.2 us: run_pack(): pl.pallas_call(functools.partial(pack_kernel, begin, count), out_shape=ja...]
    ppermute x38 -> x12, starting transfers between devices: 42.8 us -> 8.82 us  [the longest x3 7.3 us: paired(): right_even = lax.ppermute(even, ('near', 'sub'), leftward)]
    all_to_all x0 -> x6, starting transfers between devices: none -> 30.4 us  [the longest x3 16.2 us: paired(): arrived.append(lax.all_to_all(before, ('far', 'cell'), 0, 0))]
    ppermute x38 -> x12, waiting for transfers between devices: 32.9 us -> 7.73 us  [the longest x3 3.46 us: paired(): left_odd = lax.ppermute(odd, ('near', 'sub'), rightward)]
    all_to_all x0 -> x6, waiting for transfers between devices: none -> 14.5 us  [the longest x3 14.5 us: paired(): backs[index] = lax.all_to_all(before, ('far', 'cell'), 0, 0)]
    dynamic_slice x1 -> x0, local copies, waits for them, and re-layouts: 2.61 us -> none  [paired(): lax.dynamic_slice_in_dim(grouped, begin + (quarter ^ delta) * count, coun...]
    concatenate x0 -> x1, other arithmetic: none -> 2.3 us  [paired(): return jnp.concatenate(results, axis=1).reshape(frames.shape)]
    unnamed x56 -> x44, local copies, waits for them, and re-layouts: 12.3 us -> 13 us
  transfers between devices with their start and end apart: 38 -> 18, of which waited for: 10 -> 5; matrix products, arithmetic and copies ran while one was open for 2% -> 0% of each run, Pallas kernels for 33% -> 48%
where the time goes in v2:
time: 176 us; the launch traced here: 175 us
  Pallas kernels  96.9 us (55%)
  starting transfers between devices  39.2 us (22%)
  waiting for transfers between devices  22.2 us (13%)
  local copies, waits for them, and re-layouts  13.1 us (7%)
  other arithmetic  2.89 us (2%)
    pallas_call x3, Pallas kernels, run_pack(): pl.pallas_call(functools.partial(pack_kernel, begin, count), out_shape=ja...  51.2 us
    pallas_call x3, Pallas kernels, run_section(): pl.pallas_call(section_kernel, grid=(count,), out_shape=(shape, shape), i...  25.6 us
    pallas_call x3, Pallas kernels, run_temporal(): pl.pallas_call(temporal_kernel, grid=(count,), out_shape=shape, in_specs=...  20.2 us
    all_to_all x3, starting transfers between devices, paired(): arrived.append(lax.all_to_all(before, ('far', 'cell'), 0, 0))  16.2 us
    all_to_all x3, waiting for transfers between devices, paired(): backs[index] = lax.all_to_all(before, ('far', 'cell'), 0, 0)  14.5 us
    all_to_all x3, starting transfers between devices, paired(): backs[index] = lax.all_to_all(before, ('far', 'cell'), 0, 0)  14.2 us
    unnamed x44, local copies, waits for them, and re-layouts  13 us
    ppermute x3, starting transfers between devices, paired(): right_even = lax.ppermute(even, ('near', 'sub'), leftward)  7.3 us
  transfers between devices with their start and end apart: 18, of which 5 were waited for; matrix products, arithmetic and copies ran while one was open for 0% of the time, Pallas kernels for 48%

profile of v2, /device:TPU:0, one launch (start us, length us, event | category | flops | bytes accessed | tf_op | source)
XLA Modules:
  0.0 174.6 jit_solution(8756439990106683494)
XLA Ops:
  0.6 13.1 %pack.3.before = bf16[4,2,1,64,384]{4,3,2,1,0:T(8,128)(2,1)} custom-call(s32[3]{0:T(128)} %pad_add_fusion.before.place, bf16[2,16,64,384]{3,2,1,0:T(8,128)(2,1)} %bitcast.19), custom_call_target="tpu_custom_call" | custom-call | bytes 786432 | tf_op jit(solution)/shard_map/pack/pallas_call | solution.py:403
  13.7 6.3 %all-to-all-start = ((bf16[4,2,1,64,384]{4,3,2,1,0:T(8,128)(2,1)}), bf16[4,2,1,64,384]{4,3,2,1,0:T(8,128)(2,1)S(1)}, u32[]{:S(2)}, u32[]{:S(2)}) async-start(bf16[4,2,1,64,384]{4,3,2,1,0:T(8,128)(2,1)} %pack.3.before), calls=%async_computation | async-start | bytes 786432 | tf_op jit(solution)/shard_map/all_to_all | solution.py:435
  21.1 2.0 %collective-permute-done.1.out_b = bf16[192,384]{1,0:T(8,128)(2,1)S(1)} collective-permute-done((bf16[192,384]{1,0:T(8,128)(2,1)S(1)}, bf16[192,384]{1,0:T(8,128)(2,1)S(1)}, u32[]{:S(2)}, u32[]{:S(2)}) %collective-permute-start.1) | collective-permute-done | bytes 147488 | tf_op jit(solution)/shard_map/ppermute | solution.py:439
  23.4 25.0 %pack.4.before = bf16[4,2,2,64,384]{4,3,2,1,0:T(8,128)(2,1)} custom-call(bf16[4,2,1,64,384]{4,3,2,1,0:T(8,128)(2,1)} %pack.3.before, bf16[2,16,64,384]{3,2,1,0:T(8,128)(2,1)} %bitcast.20), custom_call_target="tpu_custom_call" | custom-call | bytes 1572864 | tf_op jit(solution)/shard_map/pack/pallas_call | solution.py:403
  48.5 5.1 %all-to-all-start.2 = ((bf16[4,2,2,64,384]{4,3,2,1,0:T(8,128)(2,1)}), bf16[4,2,2,64,384]{4,3,2,1,0:T(8,128)(2,1)S(1)}, u32[]{:S(2)}, u32[]{:S(2)}) async-start(bf16[4,2,2,64,384]{4,3,2,1,0:T(8,128)(2,1)} %pack.4.before), calls=%async_computation.2 | async-start | bytes 1572864 | tf_op jit(solution)/shard_map/all_to_all | solution.py:435
  53.6 1.1 copy-done.4
  54.7 1.0 copy-done.7
  55.7 0.9 copy-done.15
  56.6 0.9 copy-done.19
  57.5 7.1 %section.3 = (bf16[2,1,128,384]{3,2,1,0:T(8,128)(2,1)}, bf16[2,1,128,384]{3,2,1,0:T(8,128)(2,1)}) custom-call(s32[3]{0:T(128)S(1)} %copy-done, s32[3]{0:T(128)S(1)} %copy-done, bf16[4,2,1,64,384]{4,3,2,1,0:T(8,128)(2,1)S(1)} %all-to-all-done.arrived, bf16[192,1152]{1,0:T(8,128)(2,1)S(1)} %copy-done.7, bf16[192,1152]{1,0:T(8,128)(2,1)} %collective-permute-done.qkv_b, ...), custom_call_target="tpu_custom_call" | custom-call | flops 5737807872 | bytes 1572864 | tf_op jit(solution)/shard_map/section/pallas_call | solution.py:341
  64.6 2.0 %collective-permute-start.5 = (bf16[2,1,128,384]{3,2,1,0:T(8,128)(2,1)}, bf16[2,1,128,384]{3,2,1,0:T(8,128)(2,1)S(1)}, u32[]{:S(2)}, u32[]{:S(2)}) collective-permute-start(bf16[2,1,128,384]{3,2,1,0:T(8,128)(2,1)} %get-tuple-element.11.before.even), channel_id=1, source_target_pairs={{1,0},{4,1},{5,4},{8,5},{9,8},{12,9},{13,12},{0,13},{3,2},{6,3},{7... | collective-permute-start | bytes 589832 | tf_op jit(solution)/shard_map/ppermute | solution.py:450
  66.7 13.1 %pack.5 = bf16[4,2,1,64,384]{4,3,2,1,0:T(8,128)(2,1)} custom-call(bf16[4,2,2,64,384]{4,3,2,1,0:T(8,128)(2,1)} %pack.4.before, bf16[2,16,64,384]{3,2,1,0:T(8,128)(2,1)} %bitcast.21), custom_call_target="tpu_custom_call" | custom-call | bytes 786432 | tf_op jit(solution)/shard_map/pack/pallas_call | solution.py:403
  79.8 6.0 %temporal.3.before = bf16[4,2,1,64,384]{4,3,2,1,0:T(8,128)(2,1)} custom-call(s32[3]{0:T(128)S(1)} %copy-done, bf16[2,1,128,384]{3,2,1,0:T(8,128)(2,1)} %get-tuple-element.11.before.even, bf16[2,1,128,384]{3,2,1,0:T(8,128)(2,1)} %get-tuple-element.11.before.even, bf16[2,1,128,384]{3,2,1,0:T(8,128)(2,1)} %get-tuple-element.12.odd, ...), custom_call_target="tpu_custom_call" | custom-call | flops 4529848320 | bytes 1572864 | tf_op jit(solution)/shard_map/temporal/pallas_call | solution.py:367
  85.8 4.8 %all-to-all-start.3 = ((bf16[4,2,1,64,384]{4,3,2,1,0:T(8,128)(2,1)}), bf16[4,2,1,64,384]{4,3,2,1,0:T(8,128)(2,1)S(1)}, u32[]{:S(2)}, u32[]{:S(2)}) async-start(bf16[4,2,1,64,384]{4,3,2,1,0:T(8,128)(2,1)} %pack.5), calls=%async_computation.3 | async-start | bytes 786432 | tf_op jit(solution)/shard_map/all_to_all | solution.py:435
  90.6 1.1 copy-done.5
  91.7 1.0 copy-done.8
  94.5 12.0 %section.4 = (bf16[2,2,128,384]{3,2,1,0:T(8,128)(2,1)}, bf16[2,2,128,384]{3,2,1,0:T(8,128)(2,1)}) custom-call(s32[3]{0:T(128)S(1)} %copy-done, bf16[4,2,1,64,384]{4,3,2,1,0:T(8,128)(2,1)} %temporal.3.before, bf16[4,2,2,64,384]{4,3,2,1,0:T(8,128)(2,1)S(1)} %all-to-all-done.2.arrived, bf16[192,1152]{1,0:T(8,128)(2,1)S(1)} %copy-done.8, ...), custom_call_target="tpu_custom_call" | custom-call | flops 11475615744 | bytes 3145728 | tf_op jit(solution)/shard_map/section/pallas_call | solution.py:341
  106.6 2.6 %collective-permute-start.9 = (bf16[2,2,128,384]{3,2,1,0:T(8,128)(2,1)}, bf16[2,2,128,384]{3,2,1,0:T(8,128)(2,1)S(1)}, u32[]{:S(2)}, u32[]{:S(2)}) collective-permute-start(bf16[2,2,128,384]{3,2,1,0:T(8,128)(2,1)} %get-tuple-element.13.before.even), channel_id=1, source_target_pairs={{1,0},{4,1},{5,4},{8,5},{9,8},{12,9},{13,12},{0,13},{3,2},{6,3},{7... | collective-permute-start | bytes 1179656 | tf_op jit(solution)/shard_map/ppermute | solution.py:450
  109.2 5.1 %all-to-all-start.1 = ((bf16[4,2,1,64,384]{4,3,2,1,0:T(8,128)(2,1)}), bf16[4,2,1,64,384]{4,3,2,1,0:T(8,128)(2,1)}, u32[]{:S(2)}, u32[]{:S(2)}) async-start(bf16[4,2,1,64,384]{4,3,2,1,0:T(8,128)(2,1)} %temporal.3.before), calls=%async_computation.1 | async-start | bytes 786432 | tf_op jit(solution)/shard_map/all_to_all | solution.py:455
  114.3 1.1 copy-done.6
  115.4 1.0 copy-done.9
  118.2 6.4 %section.5 = (bf16[2,1,128,384]{3,2,1,0:T(8,128)(2,1)S(1)}, bf16[2,1,128,384]{3,2,1,0:T(8,128)(2,1)S(1)}) custom-call(s32[3]{0:T(128)S(1)} %copy-done, bf16[2,2,128,384]{3,2,1,0:T(8,128)(2,1)} %get-tuple-element.13.before.even, bf16[4,2,1,64,384]{4,3,2,1,0:T(8,128)(2,1)S(1)} %all-to-all-done.3.arrived, bf16[192,1152]{1,0:T(8,128)(2,1)S(1)} %copy-done.9, ...), custom_call_target="tpu_custom_call" | custom-call | flops 5737807872 | bytes 1572864 | tf_op jit(solution)/shard_map/section/pallas_call | solution.py:341
  125.3 8.8 %temporal.4.before = bf16[4,2,2,64,384]{4,3,2,1,0:T(8,128)(2,1)} custom-call(s32[3]{0:T(128)S(1)} %copy-done, bf16[2,1,128,384]{3,2,1,0:T(8,128)(2,1)S(1)} %get-tuple-element.14.before.even, bf16[2,2,128,384]{3,2,1,0:T(8,128)(2,1)} %get-tuple-element.13.before.even, bf16[2,2,128,384]{3,2,1,0:T(8,128)(2,1)} %get-tuple-element.15.odd, ...), custom_call_target="tpu_custom_call" | custom-call | flops 9059696640 | bytes 3145728 | tf_op jit(solution)/shard_map/temporal/pallas_call | solution.py:367
  134.8 5.2 %all-to-all-start.4 = ((bf16[4,2,2,64,384]{4,3,2,1,0:T(8,128)(2,1)}), bf16[4,2,2,64,384]{4,3,2,1,0:T(8,128)(2,1)S(1)}, u32[]{:S(2)}, u32[]{:S(2)}) async-start(bf16[4,2,2,64,384]{4,3,2,1,0:T(8,128)(2,1)} %temporal.4.before), calls=%async_computation.4 | async-start | bytes 1572864 | tf_op jit(solution)/shard_map/all_to_all | solution.py:455
  140.0 2.6 %collective-permute-start.11 = (bf16[2,1,128,384]{3,2,1,0:T(8,128)(2,1)S(1)}, bf16[2,1,128,384]{3,2,1,0:T(8,128)(2,1)S(1)}, u32[]{:S(2)}, u32[]{:S(2)}) collective-permute-start(bf16[2,1,128,384]{3,2,1,0:T(8,128)(2,1)S(1)} %copy-done.11), channel_id=1, source_target_pairs={{1,0},{4,1},{5,4},{8,5},{9,8},{12,9},{13,12},{0,13},{3,2},{6,3},{7... | collective-permute-start | bytes 589832 | tf_op jit(solution)/shard_map/ppermute | solution.py:450
  142.7 3.5 %collective-permute-done.10.left_odd = bf16[2,1,128,384]{3,2,1,0:T(8,128)(2,1)S(1)} collective-permute-done((bf16[2,1,128,384]{3,2,1,0:T(8,128)(2,1)S(1)}, bf16[2,1,128,384]{3,2,1,0:T(8,128)(2,1)S(1)}, u32[]{:S(2)}, u32[]{:S(2)}) %collective-permute-start.10) | collective-permute-done | bytes 196640 | tf_op jit(solution)/shard_map/ppermute | solution.py:449
  146.1 2.2 %collective-permute-done.11.right_even = bf16[2,1,128,384]{3,2,1,0:T(8,128)(2,1)S(1)} collective-permute-done((bf16[2,1,128,384]{3,2,1,0:T(8,128)(2,1)S(1)}, bf16[2,1,128,384]{3,2,1,0:T(8,128)(2,1)S(1)}, u32[]{:S(2)}, u32[]{:S(2)}) %collective-permute-start.11) | collective-permute-done | bytes 196640 | tf_op jit(solution)/shard_map/ppermute | solution.py:450
  148.4 5.5 %temporal.5 = bf16[4,2,1,64,384]{4,3,2,1,0:T(8,128)(2,1)} custom-call(s32[3]{0:T(128)S(1)} %copy-done, bf16[4,2,2,64,384]{4,3,2,1,0:T(8,128)(2,1)} %temporal.4.before, bf16[2,1,128,384]{3,2,1,0:T(8,128)(2,1)S(1)} %copy-done.11, bf16[2,1,128,384]{3,2,1,0:T(8,128)(2,1)S(1)} %copy-done.13, bf16[2,1,128,384]{3,2,1,0:T(8,128)(2,1)S(1)} %collective-permute-done.10.left_odd, ...), custom_call_target="tpu_custom_call" | custom-call | flops 4529848320 | bytes 1572864 | tf_op jit(solution)/shard_map/temporal/pallas_call | solution.py:367
  153.8 3.8 %all-to-all-done.4 = bf16[4,2,2,64,384]{4,3,2,1,0:T(8,128)(2,1)S(1)} async-done(((bf16[4,2,2,64,384]{4,3,2,1,0:T(8,128)(2,1)}), bf16[4,2,2,64,384]{4,3,2,1,0:T(8,128)(2,1)S(1)}, u32[]{:S(2)}, u32[]{:S(2)}) %all-to-all-start.4) | async-done | bytes 786464 | tf_op jit(solution)/shard_map/all_to_all | solution.py:455
  157.7 3.9 %all-to-all-start.5 = ((bf16[4,2,1,64,384]{4,3,2,1,0:T(8,128)(2,1)}), bf16[4,2,1,64,384]{4,3,2,1,0:T(8,128)(2,1)S(1)}, u32[]{:S(2)}, u32[]{:S(2)}) async-start(bf16[4,2,1,64,384]{4,3,2,1,0:T(8,128)(2,1)} %temporal.5), calls=%async_computation.5 | async-start | bytes 786432 | tf_op jit(solution)/shard_map/all_to_all | solution.py:455
  161.6 10.7 %all-to-all-done.5 = bf16[4,2,1,64,384]{4,3,2,1,0:T(8,128)(2,1)S(1)} async-done(((bf16[4,2,1,64,384]{4,3,2,1,0:T(8,128)(2,1)}), bf16[4,2,1,64,384]{4,3,2,1,0:T(8,128)(2,1)S(1)}, u32[]{:S(2)}, u32[]{:S(2)}) %all-to-all-start.5) | async-done | bytes 393248 | tf_op jit(solution)/shard_map/all_to_all | solution.py:455
  172.3 2.3 %pad_maximum_fusion = bf16[2,16,64,384]{3,2,1,0:T(8,128)(2,1)} fusion(bf16[2,8,64,384]{3,2,1,0:T(8,128)(2,1)S(1)} %bitcast.23, bf16[4,2,1,64,384]{4,3,2,1,0:T(8,128)(2,1)} %all-to-all-done.1, bf16[4,2,1,64,384]{4,3,2,1,0:T(8,128)(2,1)S(1)} %all-to-all-done.5), kind=kLoop, calls=%fused_computation | loop fusion | flops 4718592 | bytes 3145728 | tf_op jit(solution)/shard_map/concatenate | solution.py:460
  (60 shorter events, 7.2 us)
Async XLA Ops:
  0.0 19.9 %copy-start.3 = (bf16[192,1536]{1,0:T(8,128)(2,1)S(1)}, bf16[192,1536]{1,0:T(8,128)(2,1)}, u32[]{:S(2)}) copy-start(bf16[192,1536]{1,0:T(8,128)(2,1)} %up_a.5) | copy-start | bytes 1769476
  0.0 20.5 %copy-start.14 = (bf16[192,384]{1,0:T(8,128)(2,1)S(1)}, bf16[192,384]{1,0:T(8,128)(2,1)}, u32[]{:S(2)}) copy-start(bf16[192,384]{1,0:T(8,128)(2,1)} %out_a.5) | copy-start | bytes 442372
  0.0 21.0 %copy-start.1 = (bf16[576,768]{1,0:T(8,128)(2,1)S(1)}, bf16[576,768]{1,0:T(8,128)(2,1)}, u32[]{:S(2)}) copy-start(bf16[576,768]{1,0:T(8,128)(2,1)} %first_a.5) | copy-start | bytes 2654212
  0.0 23.1 %copy-start.2 = (bf16[576,768]{1,0:T(8,128)(2,1)S(1)}, bf16[576,768]{1,0:T(8,128)(2,1)}, u32[]{:S(2)}) copy-start(bf16[576,768]{1,0:T(8,128)(2,1)} %second_a.5) | copy-start | bytes 2654212
  13.7 34.8 %all-to-all-start = ((bf16[4,2,1,64,384]{4,3,2,1,0:T(8,128)(2,1)}), bf16[4,2,1,64,384]{4,3,2,1,0:T(8,128)(2,1)S(1)}, u32[]{:S(2)}, u32[]{:S(2)}) async-start(bf16[4,2,1,64,384]{4,3,2,1,0:T(8,128)(2,1)} %pack.3.before), calls=%async_computation | async-start | bytes 786432 | tf_op jit(solution)/shard_map/all_to_all | solution.py:435
  20.0 33.6 %copy-start = (s32[3]{0:T(128)S(1)}, s32[3]{0:T(128)}, u32[]{:S(2)}) copy-start(s32[3]{0:T(128)} %pad_add_fusion.before.place) | copy-start | bytes 40
  20.0 33.6 %collective-permute-start.2 = (bf16[192,1536]{1,0:T(8,128)(2,1)S(1)}, bf16[192,1536]{1,0:T(8,128)(2,1)}, u32[]{:S(2)}, u32[]{:S(2)}) collective-permute-start(bf16[192,1536]{1,0:T(8,128)(2,1)S(1)} %copy-done.3), channel_id=1, source_target_pairs={{0,1},{1,0},{2,3},{3,2},{4,5},{5,4},{6,7},{7,6},{8,9},{9,8},{10,11... | collective-permute-start | bytes 1769480 | tf_op jit(solution)/shard_map/ppermute | solution.py:439
  20.0 33.6 %collective-permute-start.3 = (bf16[768,384]{1,0:T(8,128)(2,1)}, bf16[768,384]{1,0:T(8,128)(2,1)}, u32[]{:S(2)}, u32[]{:S(2)}) collective-permute-start(bf16[768,384]{1,0:T(8,128)(2,1)} %down_a.5), channel_id=1, source_target_pairs={{0,1},{1,0},{2,3},{3,2},{4,5},{5,4},{6,7},{7,6},{8,9},{9,8},{10,11... | collective-permute-start | bytes 1769480 | tf_op jit(solution)/shard_map/ppermute | solution.py:439
  20.5 33.1 %collective-permute-start = (bf16[192,1152]{1,0:T(8,128)(2,1)}, bf16[192,1152]{1,0:T(8,128)(2,1)}, u32[]{:S(2)}, u32[]{:S(2)}) collective-permute-start(bf16[192,1152]{1,0:T(8,128)(2,1)} %qkv_a.5), channel_id=1, source_target_pairs={{0,1},{1,0},{2,3},{3,2},{4,5},{5,4},{6,7},{7,6},{8,9},{9,8},{10,11... | collective-permute-start | bytes 1327112 | tf_op jit(solution)/shard_map/ppermute | solution.py:439
  20.5 2.5 %collective-permute-start.1 = (bf16[192,384]{1,0:T(8,128)(2,1)S(1)}, bf16[192,384]{1,0:T(8,128)(2,1)S(1)}, u32[]{:S(2)}, u32[]{:S(2)}) collective-permute-start(bf16[192,384]{1,0:T(8,128)(2,1)S(1)} %copy-done.14), channel_id=1, source_target_pairs={{0,1},{1,0},{2,3},{3,2},{4,5},{5,4},{6,7},{7,6},{8,9},{9,8},{10,11... | collective-permute-start | bytes 442376 | tf_op jit(solution)/shard_map/ppermute | solution.py:439
  21.0 58.8 %collective-permute-start.6 = (bf16[576,768]{1,0:T(8,128)(2,1)S(1)}, bf16[576,768]{1,0:T(8,128)(2,1)}, u32[]{:S(2)}, u32[]{:S(2)}) collective-permute-start(bf16[576,768]{1,0:T(8,128)(2,1)S(1)} %copy-done.1), channel_id=1, source_target_pairs={{0,1},{1,0},{2,3},{3,2},{4,5},{5,4},{6,7},{7,6},{8,9},{9,8},{10,11... | collective-permute-start | bytes 2654216 | tf_op jit(solution)/shard_map/ppermute | solution.py:439
  23.1 25.4 %copy-start.18 = (bf16[192,384]{1,0:T(8,128)(2,1)}, bf16[192,384]{1,0:T(8,128)(2,1)S(1)}, u32[]{:S(2)}) copy-start(bf16[192,384]{1,0:T(8,128)(2,1)S(1)} %collective-permute-done.1.out_b) | copy-start | bytes 442372
  23.1 56.7 %collective-permute-start.7 = (bf16[576,768]{1,0:T(8,128)(2,1)S(1)}, bf16[576,768]{1,0:T(8,128)(2,1)}, u32[]{:S(2)}, u32[]{:S(2)}) collective-permute-start(bf16[576,768]{1,0:T(8,128)(2,1)S(1)} %copy-done.2), channel_id=1, source_target_pairs={{0,1},{1,0},{2,3},{3,2},{4,5},{5,4},{6,7},{7,6},{8,9},{9,8},{10,11... | collective-permute-start | bytes 2654216 | tf_op jit(solution)/shard_map/ppermute | solution.py:439
  48.5 37.3 %all-to-all-start.2 = ((bf16[4,2,2,64,384]{4,3,2,1,0:T(8,128)(2,1)}), bf16[4,2,2,64,384]{4,3,2,1,0:T(8,128)(2,1)S(1)}, u32[]{:S(2)}, u32[]{:S(2)}) async-start(bf16[4,2,2,64,384]{4,3,2,1,0:T(8,128)(2,1)} %pack.4.before), calls=%async_computation.2 | async-start | bytes 1572864 | tf_op jit(solution)/shard_map/all_to_all | solution.py:435
  53.6 1.1 copy-start.4
  54.7 1.0 copy-start.7
  64.6 15.1 %collective-permute-start.5 = (bf16[2,1,128,384]{3,2,1,0:T(8,128)(2,1)}, bf16[2,1,128,384]{3,2,1,0:T(8,128)(2,1)S(1)}, u32[]{:S(2)}, u32[]{:S(2)}) collective-permute-start(bf16[2,1,128,384]{3,2,1,0:T(8,128)(2,1)} %get-tuple-element.11.before.even), channel_id=1, source_target_pairs={{1,0},{4,1},{5,4},{8,5},{9,8},{12,9},{13,12},{0,13},{3,2},{6,3},{7... | collective-permute-start | bytes 589832 | tf_op jit(solution)/shard_map/ppermute | solution.py:450
  66.7 13.1 %collective-permute-start.4 = (bf16[2,1,128,384]{3,2,1,0:T(8,128)(2,1)}, bf16[2,1,128,384]{3,2,1,0:T(8,128)(2,1)S(1)}, u32[]{:S(2)}, u32[]{:S(2)}) collective-permute-start(bf16[2,1,128,384]{3,2,1,0:T(8,128)(2,1)} %get-tuple-element.12.odd), channel_id=1, source_target_pairs={{0,1},{1,4},{4,5},{5,8},{8,9},{9,12},{12,13},{13,0},{2,3},{3,6},{6... | collective-permute-start | bytes 589832 | tf_op jit(solution)/shard_map/ppermute | solution.py:449
  85.8 23.5 %all-to-all-start.3 = ((bf16[4,2,1,64,384]{4,3,2,1,0:T(8,128)(2,1)}), bf16[4,2,1,64,384]{4,3,2,1,0:T(8,128)(2,1)S(1)}, u32[]{:S(2)}, u32[]{:S(2)}) async-start(bf16[4,2,1,64,384]{4,3,2,1,0:T(8,128)(2,1)} %pack.5), calls=%async_computation.3 | async-start | bytes 786432 | tf_op jit(solution)/shard_map/all_to_all | solution.py:435
  90.6 1.1 copy-start.5
  91.7 1.0 copy-start.8
  106.5 18.8 %collective-permute-start.8 = (bf16[2,2,128,384]{3,2,1,0:T(8,128)(2,1)}, bf16[2,2,128,384]{3,2,1,0:T(8,128)(2,1)S(1)}, u32[]{:S(2)}, u32[]{:S(2)}) collective-permute-start(bf16[2,2,128,384]{3,2,1,0:T(8,128)(2,1)} %get-tuple-element.15.odd), channel_id=1, source_target_pairs={{0,1},{1,4},{4,5},{5,8},{8,9},{9,12},{12,13},{13,0},{2,3},{3,6},{6... | collective-permute-start | bytes 1179656 | tf_op jit(solution)/shard_map/ppermute | solution.py:449
  106.6 18.7 %collective-permute-start.9 = (bf16[2,2,128,384]{3,2,1,0:T(8,128)(2,1)}, bf16[2,2,128,384]{3,2,1,0:T(8,128)(2,1)S(1)}, u32[]{:S(2)}, u32[]{:S(2)}) collective-permute-start(bf16[2,2,128,384]{3,2,1,0:T(8,128)(2,1)} %get-tuple-element.13.before.even), channel_id=1, source_target_pairs={{1,0},{4,1},{5,4},{8,5},{9,8},{12,9},{13,12},{0,13},{3,2},{6,3},{7... | collective-permute-start | bytes 1179656 | tf_op jit(solution)/shard_map/ppermute | solution.py:450
  109.2 25.6 %all-to-all-start.1 = ((bf16[4,2,1,64,384]{4,3,2,1,0:T(8,128)(2,1)}), bf16[4,2,1,64,384]{4,3,2,1,0:T(8,128)(2,1)}, u32[]{:S(2)}, u32[]{:S(2)}) async-start(bf16[4,2,1,64,384]{4,3,2,1,0:T(8,128)(2,1)} %temporal.3.before), calls=%async_computation.1 | async-start | bytes 786432 | tf_op jit(solution)/shard_map/all_to_all | solution.py:455
  114.3 1.1 copy-start.6
  115.4 1.0 copy-start.9
  134.8 5.2 %copy-start.13 = (bf16[2,1,128,384]{3,2,1,0:T(8,128)(2,1)S(1)}, bf16[2,1,128,384]{3,2,1,0:T(8,128)(2,1)}, u32[]{:S(2)}) copy-start(bf16[2,1,128,384]{3,2,1,0:T(8,128)(2,1)} %copy-done.12) | copy-start | bytes 589828
  134.8 5.2 %copy-start.11 = (bf16[2,1,128,384]{3,2,1,0:T(8,128)(2,1)S(1)}, bf16[2,1,128,384]{3,2,1,0:T(8,128)(2,1)}, u32[]{:S(2)}) copy-start(bf16[2,1,128,384]{3,2,1,0:T(8,128)(2,1)} %copy-done.10) | copy-start | bytes 589828
  134.8 22.9 %all-to-all-start.4 = ((bf16[4,2,2,64,384]{4,3,2,1,0:T(8,128)(2,1)}), bf16[4,2,2,64,384]{4,3,2,1,0:T(8,128)(2,1)S(1)}, u32[]{:S(2)}, u32[]{:S(2)}) async-start(bf16[4,2,2,64,384]{4,3,2,1,0:T(8,128)(2,1)} %temporal.4.before), calls=%async_computation.4 | async-start | bytes 1572864 | tf_op jit(solution)/shard_map/all_to_all | solution.py:455
  140.0 6.1 %collective-permute-start.10 = (bf16[2,1,128,384]{3,2,1,0:T(8,128)(2,1)S(1)}, bf16[2,1,128,384]{3,2,1,0:T(8,128)(2,1)S(1)}, u32[]{:S(2)}, u32[]{:S(2)}) collective-permute-start(bf16[2,1,128,384]{3,2,1,0:T(8,128)(2,1)S(1)} %copy-done.13), channel_id=1, source_target_pairs={{0,1},{1,4},{4,5},{5,8},{8,9},{9,12},{12,13},{13,0},{2,3},{3,6},{6... | collective-permute-start | bytes 589832 | tf_op jit(solution)/shard_map/ppermute | solution.py:449
  140.0 8.3 %collective-permute-start.11 = (bf16[2,1,128,384]{3,2,1,0:T(8,128)(2,1)S(1)}, bf16[2,1,128,384]{3,2,1,0:T(8,128)(2,1)S(1)}, u32[]{:S(2)}, u32[]{:S(2)}) collective-permute-start(bf16[2,1,128,384]{3,2,1,0:T(8,128)(2,1)S(1)} %copy-done.11), channel_id=1, source_target_pairs={{1,0},{4,1},{5,4},{8,5},{9,8},{12,9},{13,12},{0,13},{3,2},{6,3},{7... | collective-permute-start | bytes 589832 | tf_op jit(solution)/shard_map/ppermute | solution.py:450
  157.7 14.6 %all-to-all-start.5 = ((bf16[4,2,1,64,384]{4,3,2,1,0:T(8,128)(2,1)}), bf16[4,2,1,64,384]{4,3,2,1,0:T(8,128)(2,1)S(1)}, u32[]{:S(2)}, u32[]{:S(2)}) async-start(bf16[4,2,1,64,384]{4,3,2,1,0:T(8,128)(2,1)} %temporal.5), calls=%async_computation.5 | async-start | bytes 786432 | tf_op jit(solution)/shard_map/all_to_all | solution.py:455
  (8 other events, 6.8 us)

commit v3 on v2

--- a/solution.py
+++ b/solution.py
@@ -1,4 +1,3 @@
-import functools
 import math
 
 import jax
@@ -11,8 +10,8 @@
 HEAD_DIM = 64
 DILATION_FIRST = 16
 DILATION_SECOND = 256
-CHUNKS = (1, 2, 1)
-ORDER = (("s", 0), ("t", 0), ("s", 1), ("s", 2), ("t", 1), ("t", 2))
+CHUNKS = (1, 1, 1, 1)
+ORDER = (("s", 0), ("s", 1), ("t", 0), ("s", 2), ("t", 1), ("s", 3), ("t", 2), ("t", 3))
 VMEM_LIMIT = 24 * 1024 * 1024
 
 
@@ -111,79 +110,120 @@
     return gated_step(opening_layer, far_earlier, far_later, whole_tcn_b)
 
 
-def load_halves(core, pairs, scratches, sems):
-    copies = []
-    for index, ((mine, other), scratch) in enumerate(zip(pairs, scratches)):
-        rows = mine.shape[0]
-        here = pl.multiple_of(core * rows, 16)
-        there = pl.multiple_of((1 - core) * rows, 16)
-        copies.append(
-            (
-                pltpu.make_async_copy(mine, scratch.at[pl.ds(here, rows)], sems.at[index, 0]),
-                pltpu.make_async_copy(other, scratch.at[pl.ds(there, rows)], sems.at[index, 1]),
-            )
+ANYWHERE = pl.BlockSpec(memory_space=pl.ANY)
+RESIDENT = pl.BlockSpec(memory_space=pltpu.VMEM)
+SCALARS = pl.BlockSpec(memory_space=pltpu.SMEM)
+
+
+def params():
+    return pltpu.CompilerParams(vmem_limit_bytes=VMEM_LIMIT)
+
+
+def moved(count):
+    return pl.CostEstimate(flops=0, bytes_accessed=4 * count, transcendentals=0)
+
+
+def pack_weights_kernel(before, *refs):
+    *sources, packed = refs
+    width = packed.shape[1]
+    at = 0
+    for source in sources:
+        rows = source.shape[0]
+        for column in range(0, source.shape[1], width):
+            packed[at : at + rows] = source[:, column : column + width]
+            at += rows
+
+
+def pack_weights(before, weights, width):
+    rows = sum(w.size for w in weights) // width
+    return pl.pallas_call(
+        pack_weights_kernel,
+        out_shape=jax.ShapeDtypeStruct((rows, width), weights[0].dtype),
+        in_specs=[ANYWHERE] + [RESIDENT] * len(weights),
+        out_specs=RESIDENT,
+        compiler_params=params(),
+        cost_estimate=moved(rows * width),
+        name="pack_weights",
+    )(before, *weights)
+
+
+def join_weights_kernel(place, before, mine, other, *wholes):
+    width = mine.shape[1]
+    for source, index in ((mine, place[0]), (other, 1 - place[0])):
+        at = 0
+        for whole in wholes:
+            rows = whole.shape[0] // 2
+            spot = pl.ds(pl.multiple_of(index * rows, 16), rows)
+            for column in range(0, whole.shape[1], width):
+                whole[spot, column : column + width] = source[at : at + rows]
+                at += rows
+
+
+def join_weights(place, before, mine, other, halves):
+    return pl.pallas_call(
+        join_weights_kernel,
+        out_shape=[jax.ShapeDtypeStruct((2 * w.shape[0], w.shape[1]), w.dtype) for w in halves],
+        in_specs=[SCALARS, ANYWHERE, RESIDENT, RESIDENT],
+        out_specs=[RESIDENT] * len(halves),
+        compiler_params=params(),
+        cost_estimate=moved(2 * mine.size),
+        name="join_weights",
+    )(place, before, mine, other)
+
+
+def pack_kernel(place, before, *refs):
+    half = len(refs) // 2
+    for source, packed in zip(refs[:half], refs[half:]):
+        packed[...] = source[...]
+
+
+def run_pack(place, before, grouped, begin, count):
+    slots, _, cells, features = grouped.shape
+    shape = (slots, 1, cells, features)
+
+    def source(delta):
+        return pl.BlockSpec(
+            shape, lambda i, at: (0, begin + (at[4] ^ delta) * count + i, 0, 0)
         )
-    return copies
-
-
-def start_all(copies):
-    for pair in copies:
-        for copy in pair:
-            copy.start()
-
-
-def wait_pair(pair):
-    for copy in pair:
-        copy.wait()
+
+    return pl.pallas_call(
+        pack_kernel,
+        grid_spec=pltpu.PrefetchScalarGridSpec(
+            num_scalar_prefetch=1,
+            grid=(count,),
+            in_specs=[ANYWHERE] + [source(delta) for delta in (1, 2, 3)],
+            out_specs=[pl.BlockSpec(shape, lambda i, at: (0, i, 0, 0))] * 3,
+        ),
+        out_shape=[jax.ShapeDtypeStruct((slots, count, cells, features), grouped.dtype)] * 3,
+        compiler_params=params(),
+        cost_estimate=moved(3 * slots * count * cells * features),
+        name="pack",
+    )(place, before, grouped, grouped, grouped)
 
 
 def section_kernel(
     place,
     before,
-    arrived,
-    qkv_a,
-    qkv_b,
-    out_a,
-    out_b,
-    up_a,
-    up_b,
-    down_a,
-    down_b,
-    even_ref,
-    odd_ref,
+    own,
+    near_cells,
+    far_own,
+    far_cells,
     w_qkv,
     w_out,
     w_up,
     w_down,
-    sems,
+    even_ref,
+    odd_ref,
 ):
-    core = place[0]
-    copies = load_halves(
-        core,
-        ((qkv_a, qkv_b), (out_a, out_b), (up_a, up_b), (down_a, down_b)),
-        (w_qkv, w_out, w_up, w_down),
-        sems,
-    )
-    first = pl.program_id(0) == 0
-
-    @pl.when(first)
-    def _():
-        start_all(copies)
-
-    features = arrived.shape[-1]
-    cells = 2 * arrived.shape[3]
+    features = own.shape[-1]
+    cells = 2 * own.shape[2]
     parts = []
-    for block in range(2):
+    for mine, other in ((own, near_cells), (far_own, far_cells)):
         for slot in range(2):
-            parts += [arrived[2 * block, slot, 0], arrived[2 * block + 1, slot, 0]]
+            parts += [mine[slot, 0], other[slot, 0]]
     residual = jnp.concatenate(parts, axis=0).astype(jnp.float32)
     frame_count = 4
     normed = normalize(residual).astype(jnp.bfloat16)
-
-    @pl.when(first)
-    def _():
-        wait_pair(copies[0])
-
     projected = jnp.dot(normed, w_qkv[...], preferred_element_type=jnp.float32).astype(jnp.bfloat16)
     pair_width = 2 * HEAD_DIM
     low = lax.broadcasted_iota(jnp.int32, (cells, pair_width), 1) < HEAD_DIM
@@ -222,12 +262,6 @@
         rows.append(jnp.concatenate(columns, axis=1))
     attended = jnp.concatenate(rows, axis=0)
 
-    @pl.when(first)
-    def _():
-        wait_pair(copies[1])
-        wait_pair(copies[2])
-        wait_pair(copies[3])
-
     mid_state = (
         residual + jnp.dot(attended, w_out[...], preferred_element_type=jnp.float32)
     ).astype(jnp.bfloat16)
@@ -264,27 +298,15 @@
     odd,
     left_odd,
     right_even,
-    first_a,
-    first_b,
-    second_a,
-    second_b,
-    out,
     w_first,
     w_second,
-    sems,
+    out0,
+    out1,
+    out2,
+    out3,
 ):
-    core, is_first, is_last = place[0], place[1], place[2]
-    copies = load_halves(
-        core, ((first_a, first_b), (second_a, second_b)), (w_first, w_second), sems
-    )
-    starting = pl.program_id(0) == 0
-
-    @pl.when(starting)
-    def _():
-        start_all(copies)
-        wait_pair(copies[0])
-
-    near, far = 0, 1
+    near, is_first, is_last = place[1], place[2], place[3]
+    far = 1 - near
     features = even.shape[-1]
     cells = even.shape[2]
     zero = jnp.zeros((cells, features), even.dtype)
@@ -303,11 +325,6 @@
         axis=1,
     )
     opening = gate(center, jnp.dot(stacked, w_first[...], preferred_element_type=jnp.float32))
-
-    @pl.when(starting)
-    def _():
-        wait_pair(copies[1])
-
     rows = 2 * cells
     near_part, far_part = opening[:rows], opening[rows:]
     both = jnp.concatenate([near_part, far_part], axis=1)
@@ -317,147 +334,136 @@
     result_f = gate(
         far_part, jnp.dot(both, w_second[: 2 * features], preferred_element_type=jnp.float32)
     )
+    same = jnp.where(near == 0, result_n, result_f)
+    other = jnp.where(near == 0, result_f, result_n)
     half = cells // 2
-    for block, result in enumerate((result_n, result_f)):
-        for slot in range(2):
-            at = slot * cells
-            out[2 * block, slot, 0] = result[at : at + half]
-            out[2 * block + 1, slot, 0] = result[at + half : at + cells]
-
-
-PINNED = pl.BlockSpec(memory_space=pl.ANY)
-SCALARS = pl.BlockSpec(memory_space=pltpu.SMEM)
-
-
-def run_section(place, before, arrived, weights):
-    parts, slots, count, cells, features = arrived.shape
-    ff = weights[2][0].shape[1]
-    block_in = pl.BlockSpec((parts, slots, 1, cells, features), lambda i: (0, 0, i, 0, 0))
-    block_out = pl.BlockSpec((2, 1, 2 * cells, features), lambda i: (0, i, 0, 0))
+    for slot in range(2):
+        at = slot * cells
+        out0[slot, 0] = same[at : at + half]
+        out1[slot, 0] = same[at + half : at + cells]
+        out2[slot, 0] = other[at : at + half]
+        out3[slot, 0] = other[at + half : at + cells]
+
+
+def run_section(place, before, grouped, begin, pieces, weights):
+    slots, count, cells, features = pieces[0].shape
+    ff = weights[2].shape[1]
+    shape_in = (slots, 1, cells, features)
+    own = pl.BlockSpec(shape_in, lambda i, at: (0, begin + at[4] * count + i, 0, 0))
+    block_in = pl.BlockSpec(shape_in, lambda i, at: (0, i, 0, 0))
+    block_out = pl.BlockSpec((2, 1, 2 * cells, features), lambda i, at: (0, i, 0, 0))
     shape = jax.ShapeDtypeStruct((2, count, 2 * cells, features), jnp.bfloat16)
-    tokens = parts * slots * count * cells
+    tokens = 2 * slots * count * 2 * cells
     macs = tokens * (features * (4 * features + 2 * ff) + 4 * cells * features)
-    flat = [half for pair in weights for half in pair]
     return pl.pallas_call(
         section_kernel,
-        grid=(count,),
-        out_shape=(shape, shape),
-        in_specs=[SCALARS, PINNED, block_in] + [PINNED] * 8,
-        out_specs=(block_out, block_out),
-        scratch_shapes=[
-            pltpu.VMEM((2 * mine.shape[0], mine.shape[1]), mine.dtype) for mine, _ in weights
-        ]
-        + [pltpu.SemaphoreType.DMA((4, 2))],
-        compiler_params=pltpu.CompilerParams(vmem_limit_bytes=VMEM_LIMIT),
+        grid_spec=pltpu.PrefetchScalarGridSpec(
+            num_scalar_prefetch=1,
+            grid=(count,),
+            in_specs=[ANYWHERE, own] + [block_in] * 3 + [RESIDENT] * 4,
+            out_specs=[block_out, block_out],
+        ),
+        out_shape=[shape, shape],
+        compiler_params=params(),
         cost_estimate=pl.CostEstimate(
             flops=6 * macs, bytes_accessed=8 * tokens * features, transcendentals=tokens * ff
         ),
         name="section",
-    )(place, before, arrived, *flat)
+    )(place, before, grouped, *pieces, *weights)
 
 
 def run_temporal(place, before, even, odd, left_odd, right_even, weights):
     blocks, count, cells, features = even.shape
-    block_in = pl.BlockSpec((blocks, 1, cells, features), lambda i: (0, i, 0, 0))
-    parts, slots = 2 * blocks, 2
-    block_out = pl.BlockSpec((parts, slots, 1, cells // 2, features), lambda i: (0, 0, i, 0, 0))
-    shape = jax.ShapeDtypeStruct((parts, slots, count, cells // 2, features), jnp.bfloat16)
+    block_in = pl.BlockSpec((blocks, 1, cells, features), lambda i, at: (0, i, 0, 0))
+    block_out = pl.BlockSpec((2, 1, cells // 2, features), lambda i, at: (0, i, 0, 0))
+    shape = jax.ShapeDtypeStruct((2, count, cells // 2, features), jnp.bfloat16)
     tokens = 2 * blocks * count * cells
-    flat = [half for pair in weights for half in pair]
     return pl.pallas_call(
         temporal_kernel,
-        grid=(count,),
-        out_shape=shape,
-        in_specs=[SCALARS, PINNED] + [block_in] * 4 + [PINNED] * 4,
-        out_specs=block_out,
-        scratch_shapes=[
-            pltpu.VMEM((2 * mine.shape[0], mine.shape[1]), mine.dtype) for mine, _ in weights
-        ]
-        + [pltpu.SemaphoreType.DMA((2, 2))],
-        compiler_params=pltpu.CompilerParams(vmem_limit_bytes=VMEM_LIMIT),
+        grid_spec=pltpu.PrefetchScalarGridSpec(
+            num_scalar_prefetch=1,
+            grid=(count,),
+            in_specs=[ANYWHERE] + [block_in] * 4 + [RESIDENT] * 2,
+            out_specs=[block_out] * 4,
+        ),
+        out_shape=[shape] * 4,
+        compiler_params=params(),
         cost_estimate=pl.CostEstimate(
             flops=60 * tokens * features * features,
             bytes_accessed=8 * tokens * features,
             transcendentals=4 * tokens * features,
         ),
         name="temporal",
-    )(place, before, even, odd, left_odd, right_even, *flat)
-
-
-def pack_kernel(begin, count, before, frames, packed, sems):
-    copies = []
-    for part in range(packed.shape[0]):
-        for slot in range(packed.shape[1]):
-            source = frames.at[slot, begin + part * count : begin + (part + 1) * count]
-            copies.append(
-                pltpu.make_async_copy(source, packed.at[part, slot], sems.at[part, slot])
-            )
-    for copy in copies:
-        copy.start()
-    for copy in copies:
-        copy.wait()
-
-
-def run_pack(before, grouped, begin, count, parts):
-    slots, _, cells, features = grouped.shape
-    return pl.pallas_call(
-        functools.partial(pack_kernel, begin, count),
-        out_shape=jax.ShapeDtypeStruct((parts, slots, count, cells, features), grouped.dtype),
-        in_specs=[PINNED, PINNED],
-        out_specs=PINNED,
-        scratch_shapes=[pltpu.SemaphoreType.DMA((parts, slots))],
-        cost_estimate=pl.CostEstimate(
-            flops=0,
-            bytes_accessed=4 * parts * slots * count * cells * features,
-            transcendentals=0,
-        ),
-        name="pack",
-    )(before, grouped)
+    )(place, before, even, odd, left_odd, right_even, *weights)
+
+
+GROUP = ("far", "cell")
+RING = ("near", "sub")
 
 
 def paired(frames, w_qkv, w_out, w_up, w_down, temporal_weight_first, temporal_weight_second):
     frames_local, cells, features = frames.shape
     near_size, subs = lax.axis_size("near"), lax.axis_size("sub")
-    sub = lax.axis_index("sub")
+    sub, side = lax.axis_index("sub"), lax.axis_index("far")
+    quarter = 2 * side + lax.axis_index("cell")
     ring = near_size * subs
     position = lax.axis_index("near") * subs + sub
-    place = jnp.stack([sub, position == 0, position == ring - 1]).astype(jnp.int32)
+    place = jnp.stack([sub, side, position == 0, position == ring - 1, quarter]).astype(jnp.int32)
     rightward = [(i, (i + 1) % ring) for i in range(ring)]
     leftward = [(target, source) for source, target in rightward]
     slots = frames_local // DILATION_FIRST
     grouped = frames.reshape(slots, DILATION_FIRST, cells, features)
-
-    arrived = []
-    begin = 0
-    before = place
-    for count in CHUNKS:
-        before = run_pack(before, grouped, begin, count, 4)
-        arrived.append(lax.all_to_all(before, ("far", "cell"), 0, 0))
-        begin += 4 * count
-
-    def swap_core(weight):
-        return weight, lax.ppermute(weight, "sub", [(0, 1), (1, 0)])
-
-    section_weights = [swap_core(w) for w in (w_qkv, w_out, w_up, w_down)]
-    temporal_weights = [swap_core(w) for w in (temporal_weight_first, temporal_weight_second)]
-
-    waiting, backs = {}, {}
+    begins = [4 * sum(CHUNKS[:index]) for index in range(len(CHUNKS))]
+
+    def exchange(piece, delta):
+        return lax.ppermute(piece, GROUP, [(i, i ^ delta) for i in range(4)])
+
+    def send(before, index):
+        cut = run_pack(place, before, grouped, begins[index], CHUNKS[index])
+        return cut[0], [exchange(piece, delta) for delta, piece in zip((1, 2, 3), cut)]
+
+    def swap_core(packed):
+        return lax.ppermute(packed, "sub", [(0, 1), (1, 0)])
+
+    section_halves = (w_qkv, w_out, w_up, w_down)
+    temporal_halves = (temporal_weight_first, temporal_weight_second)
+    arrived = {}
+    before, arrived[0] = send(place, 0)
+    section_mine = pack_weights(before, section_halves, features)
+    section_weights = join_weights(
+        place, before, section_mine, swap_core(section_mine), section_halves
+    )
+    before, arrived[1] = send(section_weights[0], 1)
+    temporal_mine = pack_weights(before, temporal_halves, features)
+    temporal_weights = join_weights(
+        place, before, temporal_mine, swap_core(temporal_mine), temporal_halves
+    )
+    before = temporal_weights[0]
+    for index in range(2, len(CHUNKS)):
+        before, arrived[index] = send(before, index)
+
+    waiting, outs = {}, {}
     before = place
     for kind, index in ORDER:
         if kind == "s":
-            even, odd = run_section(place, before, arrived[index], section_weights)
-            left_odd = lax.ppermute(odd, ("near", "sub"), rightward)
-            right_even = lax.ppermute(even, ("near", "sub"), leftward)
+            even, odd = run_section(
+                place, before, grouped, begins[index], arrived[index], section_weights
+            )
+            left_odd = lax.ppermute(odd, RING, rightward)
+            right_even = lax.ppermute(even, RING, leftward)
             waiting[index] = (even, odd, left_odd, right_even)
             before = even
         else:
-            before = run_temporal(place, before, *waiting[index], temporal_weights)
-            backs[index] = lax.all_to_all(before, ("far", "cell"), 0, 0)
-    results = [
-        backs[index].swapaxes(0, 1).reshape(slots, 4 * count, cells, features)
-        for index, count in enumerate(CHUNKS)
-    ]
-    return jnp.concatenate(results, axis=1).reshape(frames.shape)
+            sent = run_temporal(place, before, *waiting[index], temporal_weights)
+            outs[index] = [sent[0]] + [exchange(sent[delta], delta) for delta in (1, 2, 3)]
+            before = sent[0]
+    result = jnp.zeros_like(grouped)
+    for index, count in enumerate(CHUNKS):
+        for delta in range(4):
+            result = lax.dynamic_update_slice_in_dim(
+                result, outs[index][delta], begins[index] + (quarter ^ delta) * count, axis=1
+            )
+    return result.reshape(frames.shape)
 
 
 def solution(mesh):

time: 176 us -> 133 us (0.76)
  Pallas kernels: 96.9 us -> 40.4 us
  starting transfers between devices: 39.2 us -> 49.7 us
  waiting for transfers between devices: 22.2 us -> 30 us
  other arithmetic: 2.89 us -> 0 us
  local copies, waits for them, and re-layouts: 13.1 us -> 10.4 us
    pallas_call x9 -> x16, Pallas kernels: 96.9 us -> 40.4 us  [the longest x4 21.6 us: run_section(): pl.pallas_call(section_kernel, grid_spec=pltpu.PrefetchScalarGridSpec(num...]
    ppermute x12 -> x34, starting transfers between devices: 8.82 us -> 49.7 us  [the longest x24 39.8 us: exchange(): return lax.ppermute(piece, GROUP, [(i, i ^ delta) for i in range(4)])]
    all_to_all x6 -> x0, starting transfers between devices: 30.4 us -> none  [the longest x3 16.2 us: paired(): arrived.append(lax.all_to_all(before, ('far', 'cell'), 0, 0))]
    ppermute x12 -> x34, waiting for transfers between devices: 7.73 us -> 30 us  [the longest x24 26.6 us: exchange(): return lax.ppermute(piece, GROUP, [(i, i ^ delta) for i in range(4)])]
    all_to_all x6 -> x0, waiting for transfers between devices: 14.5 us -> none  [the longest x3 14.5 us: paired(): backs[index] = lax.all_to_all(before, ('far', 'cell'), 0, 0)]
    unnamed x44 -> x46, local copies, waits for them, and re-layouts: 13 us -> 9.78 us
    concatenate x1 -> x0, other arithmetic: 2.3 us -> none  [paired(): return jnp.concatenate(results, axis=1).reshape(frames.shape)]
  transfers between devices with their start and end apart: 18 -> 34, of which waited for: 5 -> 11; matrix products, arithmetic and copies ran while one was open for 0% -> 0% of each run, Pallas kernels for 48% -> 29%
where the time goes in v3:
time: 133 us; the launch traced here: 131 us
  starting transfers between devices  49.7 us (37%)
  Pallas kernels  40.4 us (30%)
  waiting for transfers between devices  30 us (23%)
  local copies, waits for them, and re-layouts  10.4 us (8%)
    ppermute x24, starting transfers between devices, exchange(): return lax.ppermute(piece, GROUP, [(i, i ^ delta) for i in range(4)])  39.8 us
    ppermute x24, waiting for transfers between devices, exchange(): return lax.ppermute(piece, GROUP, [(i, i ^ delta) for i in range(4)])  26.6 us
    pallas_call x4, Pallas kernels, run_section(): pl.pallas_call(section_kernel, grid_spec=pltpu.PrefetchScalarGridSpec(num...  21.6 us
    pallas_call x4, Pallas kernels, run_temporal(): pl.pallas_call(temporal_kernel, grid_spec=pltpu.PrefetchScalarGridSpec(nu...  12.8 us
    unnamed x46, local copies, waits for them, and re-layouts  9.78 us
    ppermute x4, starting transfers between devices, paired(): right_even = lax.ppermute(even, RING, leftward)  8.73 us
    ppermute x2, waiting for transfers between devices, swap_core(): return lax.ppermute(packed, 'sub', [(0, 1), (1, 0)])  3.32 us
    pallas_call x4, Pallas kernels, run_pack(): pl.pallas_call(pack_kernel, grid_spec=pltpu.PrefetchScalarGridSpec(num_sc...  3.04 us
  transfers between devices with their start and end apart: 34, of which 11 were waited for; matrix products, arithmetic and copies ran while one was open for 0% of the time, Pallas kernels for 29%

profile of v3, /device:TPU:0, one launch (start us, length us, event | category | flops | bytes accessed | tf_op | source)
XLA Modules:
  0.0 130.9 jit_solution(4346607960606416540)
XLA Ops:
  3.6 3.3 %collective-permute-done.3.other = bf16[2304,384]{1,0:T(8,128)(2,1)S(1)} collective-permute-done((bf16[2304,384]{1,0:T(8,128)(2,1)S(1)}, bf16[2304,384]{1,0:T(8,128)(2,1)S(1)}, u32[]{:S(2)}, u32[]{:S(2)}) %collective-permute-start.3) | collective-permute-done | bytes 1769504 | tf_op jit(solution)/shard_map/ppermute | solution.py:426
  11.4 2.6 %collective-permute-start = (bf16[2,1,64,384]{3,2,1,0:T(8,128)(2,1)S(1)}, bf16[2,1,64,384]{3,2,1,0:T(8,128)(2,1)}, u32[]{:S(2)}, u32[]{:S(2)}) collective-permute-start(bf16[2,1,64,384]{3,2,1,0:T(8,128)(2,1)S(1)} %get-tuple-element.47.before), channel_id=1, source_target_pairs={{0,2},{2,0},{16,18},{18,16},{1,3},{3,1},{17,19},{19,17},{4,6},{6,4... | collective-permute-start | bytes 294920 | tf_op jit(solution)/shard_map/ppermute | solution.py:419
  14.1 2.6 %collective-permute-start.1 = (bf16[2,1,64,384]{3,2,1,0:T(8,128)(2,1)}, bf16[2,1,64,384]{3,2,1,0:T(8,128)(2,1)}, u32[]{:S(2)}, u32[]{:S(2)}) collective-permute-start(bf16[2,1,64,384]{3,2,1,0:T(8,128)(2,1)} %get-tuple-element.48), channel_id=1, source_target_pairs={{0,16},{2,18},{16,0},{18,2},{1,17},{3,19},{17,1},{19,3},{4,20},{6,... | collective-permute-start | bytes 294920 | tf_op jit(solution)/shard_map/ppermute | solution.py:419
  16.7 1.8 %collective-permute-start.4 = (bf16[2,1,64,384]{3,2,1,0:T(8,128)(2,1)S(1)}, bf16[2,1,64,384]{3,2,1,0:T(8,128)(2,1)S(1)}, u32[]{:S(2)}, u32[]{:S(2)}) collective-permute-start(bf16[2,1,64,384]{3,2,1,0:T(8,128)(2,1)S(1)} %get-tuple-element.55.before), channel_id=1, source_target_pairs={{0,2},{2,0},{16,18},{18,16},{1,3},{3,1},{17,19},{19,17},{4,6},{6,4... | collective-permute-start | bytes 294920 | tf_op jit(solution)/shard_map/ppermute | solution.py:419
  18.5 2.6 %collective-permute-start.5 = (bf16[2,1,64,384]{3,2,1,0:T(8,128)(2,1)}, bf16[2,1,64,384]{3,2,1,0:T(8,128)(2,1)S(1)}, u32[]{:S(2)}, u32[]{:S(2)}) collective-permute-start(bf16[2,1,64,384]{3,2,1,0:T(8,128)(2,1)} %copy-done.21), channel_id=1, source_target_pairs={{0,16},{2,18},{16,0},{18,2},{1,17},{3,19},{17,1},{19,3},{4,20},{6,... | collective-permute-start | bytes 294920 | tf_op jit(solution)/shard_map/ppermute | solution.py:419
  21.0 6.2 %collective-permute-done.1.far_own = bf16[2,1,64,384]{3,2,1,0:T(8,128)(2,1)} collective-permute-done((bf16[2,1,64,384]{3,2,1,0:T(8,128)(2,1)}, bf16[2,1,64,384]{3,2,1,0:T(8,128)(2,1)}, u32[]{:S(2)}, u32[]{:S(2)}) %collective-permute-start.1) | collective-permute-done | bytes 98336 | tf_op jit(solution)/shard_map/ppermute | solution.py:419
  27.3 1.7 %collective-permute-done.2.far_cells = bf16[2,1,64,384]{3,2,1,0:T(8,128)(2,1)} collective-permute-done((bf16[2,1,64,384]{3,2,1,0:T(8,128)(2,1)}, bf16[2,1,64,384]{3,2,1,0:T(8,128)(2,1)}, u32[]{:S(2)}, u32[]{:S(2)}) %collective-permute-start.2) | collective-permute-done | bytes 98336 | tf_op jit(solution)/shard_map/ppermute | solution.py:419
  33.6 6.1 %section.4 = (bf16[2,1,128,384]{3,2,1,0:T(8,128)(2,1)S(1)}, bf16[2,1,128,384]{3,2,1,0:T(8,128)(2,1)S(1)}) custom-call(s32[5]{0:T(128)S(1)} %stack.31.place.before, s32[5]{0:T(128)S(1)} %stack.31.place.before, bf16[2,16,64,384]{3,2,1,0:T(8,128)(2,1)S(1)} %bitcast.13, bf16[2,1,64,384]{3,2,1,0:T(8,128)(2,1)} %collective-permute-done.near_cells, ...), custom_call_target="tpu_custom_call" | custom-call | flops 5737807872 | bytes 1572864 | tf_op jit(solution)/shard_map/section/pallas_call | solution.py:358
  39.9 2.9 %collective-permute-start.8 = (bf16[2,1,128,384]{3,2,1,0:T(8,128)(2,1)S(1)}, bf16[2,1,128,384]{3,2,1,0:T(8,128)(2,1)S(1)}, u32[]{:S(2)}, u32[]{:S(2)}) collective-permute-start(bf16[2,1,128,384]{3,2,1,0:T(8,128)(2,1)S(1)} %get-tuple-element.54.before.even), channel_id=1, source_target_pairs={{1,0},{4,1},{5,4},{8,5},{9,8},{12,9},{13,12},{0,13},{3,2},{6,3},{7... | collective-permute-start | bytes 589832 | tf_op jit(solution)/shard_map/ppermute | solution.py:453
  42.7 5.2 %section.5 = (bf16[2,1,128,384]{3,2,1,0:T(8,128)(2,1)S(1)}, bf16[2,1,128,384]{3,2,1,0:T(8,128)(2,1)S(1)}) custom-call(s32[5]{0:T(128)S(1)} %stack.31.place.before, bf16[2,1,128,384]{3,2,1,0:T(8,128)(2,1)S(1)} %get-tuple-element.54.before.even, bf16[2,16,64,384]{3,2,1,0:T(8,128)(2,1)S(1)} %bitcast.14, ...), custom_call_target="tpu_custom_call" | custom-call | flops 5737807872 | bytes 1572864 | tf_op jit(solution)/shard_map/section/pallas_call | solution.py:358
  47.9 2.6 %collective-permute-start.17 = (bf16[2,1,128,384]{3,2,1,0:T(8,128)(2,1)S(1)}, bf16[2,1,128,384]{3,2,1,0:T(8,128)(2,1)S(1)}, u32[]{:S(2)}, u32[]{:S(2)}) collective-permute-start(bf16[2,1,128,384]{3,2,1,0:T(8,128)(2,1)S(1)} %get-tuple-element.58.before.even), channel_id=1, source_target_pairs={{1,0},{4,1},{5,4},{8,5},{9,8},{12,9},{13,12},{0,13},{3,2},{6,3},{7... | collective-permute-start | bytes 589832 | tf_op jit(solution)/shard_map/ppermute | solution.py:453
  50.6 1.8 %join_weights.3 = (bf16[1152,768]{1,0:T(8,128)(2,1)S(1)}, bf16[1152,768]{1,0:T(8,128)(2,1)S(1)}) custom-call(s32[5]{0:T(128)S(1)} %stack.31.place.before, bf16[2,1,64,384]{3,2,1,0:T(8,128)(2,1)S(1)} %get-tuple-element.55.before, bf16[2304,384]{1,0:T(8,128)(2,1)S(1)} %pack_weights.3.mine, bf16[2304,384]{1,0:T(8,128)(2,1)} %collective-permute-done.9.other), custom_call_target="tpu_custom_call" | custom-call | bytes 7077888 | tf_op jit(solution)/shard_map/join_weights/pallas_call | solution.py:163
  55.3 2.3 %collective-permute-start.14 = (bf16[2,1,64,384]{3,2,1,0:T(8,128)(2,1)S(1)}, bf16[2,1,64,384]{3,2,1,0:T(8,128)(2,1)S(1)}, u32[]{:S(2)}, u32[]{:S(2)}) collective-permute-start(bf16[2,1,64,384]{3,2,1,0:T(8,128)(2,1)S(1)} %get-tuple-element.67), channel_id=1, source_target_pairs={{0,16},{2,18},{16,0},{18,2},{1,17},{3,19},{17,1},{19,3},{4,20},{6,... | collective-permute-start | bytes 294920 | tf_op jit(solution)/shard_map/ppermute | solution.py:419
  58.1 3.2 %temporal.4 = (bf16[2,1,64,384]{3,2,1,0:T(8,128)(2,1)S(1)}, bf16[2,1,64,384]{3,2,1,0:T(8,128)(2,1)S(1)}, bf16[2,1,64,384]{3,2,1,0:T(8,128)(2,1)S(1)}, bf16[2,1,64,384]{3,2,1,0:T(8,128)(2,1)S(1)}) custom-call(s32[5]{0:T(128)S(1)} %stack.31.place.before, bf16[2,1,128,384]{3,2,1,0:T(8,128)(2,1)S(1)} %get-tuple-element.58.before.even, ...), custom_call_target="tpu_custom_call" | custom-call | flops 4529848320 | bytes 1572864 | tf_op jit(solution)/shard_map/temporal/pallas_call | solution.py:381
  65.6 3.0 %collective-permute-done.15.far_cells = bf16[2,1,64,384]{3,2,1,0:T(8,128)(2,1)S(1)} collective-permute-done((bf16[2,1,64,384]{3,2,1,0:T(8,128)(2,1)S(1)}, bf16[2,1,64,384]{3,2,1,0:T(8,128)(2,1)S(1)}, u32[]{:S(2)}, u32[]{:S(2)}) %collective-permute-start.15) | collective-permute-done | bytes 98336 | tf_op jit(solution)/shard_map/ppermute | solution.py:419
  68.6 5.2 %section.6 = (bf16[2,1,128,384]{3,2,1,0:T(8,128)(2,1)S(1)}, bf16[2,1,128,384]{3,2,1,0:T(8,128)(2,1)S(1)}) custom-call(s32[5]{0:T(128)S(1)} %stack.31.place.before, bf16[2,1,64,384]{3,2,1,0:T(8,128)(2,1)S(1)} %get-tuple-element.62.before, bf16[2,16,64,384]{3,2,1,0:T(8,128)(2,1)S(1)} %bitcast.21, ...), custom_call_target="tpu_custom_call" | custom-call | flops 5737807872 | bytes 1572864 | tf_op jit(solution)/shard_map/section/pallas_call | solution.py:358
  74.9 3.3 %collective-permute-start.11 = (bf16[2,1,64,384]{3,2,1,0:T(8,128)(2,1)S(1)}, bf16[2,1,64,384]{3,2,1,0:T(8,128)(2,1)S(1)}, u32[]{:S(2)}, u32[]{:S(2)}) collective-permute-start(bf16[2,1,64,384]{3,2,1,0:T(8,128)(2,1)S(1)} %get-tuple-element.64), channel_id=1, source_target_pairs={{0,16},{2,18},{16,0},{18,2},{1,17},{3,19},{17,1},{19,3},{4,20},{6,... | collective-permute-start | bytes 294920 | tf_op jit(solution)/shard_map/ppermute | solution.py:419
  78.2 3.2 %temporal.5 = (bf16[2,1,64,384]{3,2,1,0:T(8,128)(2,1)S(1)}, bf16[2,1,64,384]{3,2,1,0:T(8,128)(2,1)S(1)}, bf16[2,1,64,384]{3,2,1,0:T(8,128)(2,1)S(1)}, bf16[2,1,64,384]{3,2,1,0:T(8,128)(2,1)S(1)}) custom-call(s32[5]{0:T(128)S(1)} %stack.31.place.before, bf16[2,1,128,384]{3,2,1,0:T(8,128)(2,1)S(1)} %get-tuple-element.69.before.even, ...), custom_call_target="tpu_custom_call" | custom-call | flops 4529848320 | bytes 1572864 | tf_op jit(solution)/shard_map/temporal/pallas_call | solution.py:381
  82.5 5.2 %section.7 = (bf16[2,1,128,384]{3,2,1,0:T(8,128)(2,1)S(1)}, bf16[2,1,128,384]{3,2,1,0:T(8,128)(2,1)S(1)}) custom-call(s32[5]{0:T(128)S(1)} %stack.31.place.before, bf16[2,1,64,384]{3,2,1,0:T(8,128)(2,1)S(1)} %get-tuple-element.71.before, bf16[2,16,64,384]{3,2,1,0:T(8,128)(2,1)S(1)} %bitcast.22, ...), custom_call_target="tpu_custom_call" | custom-call | flops 5737807872 | bytes 1572864 | tf_op jit(solution)/shard_map/section/pallas_call | solution.py:358
  87.8 2.7 %collective-permute-start.30 = (bf16[2,1,128,384]{3,2,1,0:T(8,128)(2,1)S(1)}, bf16[2,1,128,384]{3,2,1,0:T(8,128)(2,1)S(1)}, u32[]{:S(2)}, u32[]{:S(2)}) collective-permute-start(bf16[2,1,128,384]{3,2,1,0:T(8,128)(2,1)S(1)} %get-tuple-element.78.before.even), channel_id=1, source_target_pairs={{1,0},{4,1},{5,4},{8,5},{9,8},{12,9},{13,12},{0,13},{3,2},{6,3},{7... | collective-permute-start | bytes 589832 | tf_op jit(solution)/shard_map/ppermute | solution.py:453
  90.5 2.0 %collective-permute-start.18 = (bf16[2,1,64,384]{3,2,1,0:T(8,128)(2,1)S(1)}, bf16[2,1,64,384]{3,2,1,0:T(8,128)(2,1)S(1)}, u32[]{:S(2)}, u32[]{:S(2)}) collective-permute-start(bf16[2,1,64,384]{3,2,1,0:T(8,128)(2,1)S(1)} %get-tuple-element.72), channel_id=1, source_target_pairs={{0,2},{2,0},{16,18},{18,16},{1,3},{3,1},{17,19},{19,17},{4,6},{6,4... | collective-permute-start | bytes 294920 | tf_op jit(solution)/shard_map/ppermute | solution.py:419
  92.6 2.6 %collective-permute-done.18 = bf16[2,1,64,384]{3,2,1,0:T(8,128)(2,1)S(1)} collective-permute-done((bf16[2,1,64,384]{3,2,1,0:T(8,128)(2,1)S(1)}, bf16[2,1,64,384]{3,2,1,0:T(8,128)(2,1)S(1)}, u32[]{:S(2)}, u32[]{:S(2)}) %collective-permute-start.18) | collective-permute-done | bytes 98336 | tf_op jit(solution)/shard_map/ppermute | solution.py:419
  95.2 2.9 %collective-permute-start.19 = (bf16[2,1,64,384]{3,2,1,0:T(8,128)(2,1)S(1)}, bf16[2,1,64,384]{3,2,1,0:T(8,128)(2,1)S(1)}, u32[]{:S(2)}, u32[]{:S(2)}) collective-permute-start(bf16[2,1,64,384]{3,2,1,0:T(8,128)(2,1)S(1)} %get-tuple-element.73), channel_id=1, source_target_pairs={{0,16},{2,18},{16,0},{18,2},{1,17},{3,19},{17,1},{19,3},{4,20},{6,... | collective-permute-start | bytes 294920 | tf_op jit(solution)/shard_map/ppermute | solution.py:419
  98.1 3.2 %collective-permute-done.19 = bf16[2,1,64,384]{3,2,1,0:T(8,128)(2,1)S(1)} collective-permute-done((bf16[2,1,64,384]{3,2,1,0:T(8,128)(2,1)S(1)}, bf16[2,1,64,384]{3,2,1,0:T(8,128)(2,1)S(1)}, u32[]{:S(2)}, u32[]{:S(2)}) %collective-permute-start.19) | collective-permute-done | bytes 98336 | tf_op jit(solution)/shard_map/ppermute | solution.py:419
  101.3 2.9 %collective-permute-start.20 = (bf16[2,1,64,384]{3,2,1,0:T(8,128)(2,1)S(1)}, bf16[2,1,64,384]{3,2,1,0:T(8,128)(2,1)S(1)}, u32[]{:S(2)}, u32[]{:S(2)}) collective-permute-start(bf16[2,1,64,384]{3,2,1,0:T(8,128)(2,1)S(1)} %get-tuple-element.74), channel_id=1, source_target_pairs={{0,18},{2,16},{16,2},{18,0},{1,19},{3,17},{17,3},{19,1},{4,22},{6,... | collective-permute-start | bytes 294920 | tf_op jit(solution)/shard_map/ppermute | solution.py:419
  104.2 3.5 %collective-permute-done.20 = bf16[2,1,64,384]{3,2,1,0:T(8,128)(2,1)S(1)} collective-permute-done((bf16[2,1,64,384]{3,2,1,0:T(8,128)(2,1)S(1)}, bf16[2,1,64,384]{3,2,1,0:T(8,128)(2,1)S(1)}, u32[]{:S(2)}, u32[]{:S(2)}) %collective-permute-start.20) | collective-permute-done | bytes 98336 | tf_op jit(solution)/shard_map/ppermute | solution.py:419
  107.7 3.2 %temporal.6 = (bf16[2,1,64,384]{3,2,1,0:T(8,128)(2,1)S(1)}, bf16[2,1,64,384]{3,2,1,0:T(8,128)(2,1)S(1)}, bf16[2,1,64,384]{3,2,1,0:T(8,128)(2,1)S(1)}, bf16[2,1,64,384]{3,2,1,0:T(8,128)(2,1)S(1)}) custom-call(s32[5]{0:T(128)S(1)} %stack.31.place.before, bf16[2,1,128,384]{3,2,1,0:T(8,128)(2,1)S(1)} %get-tuple-element.78.before.even, ...), custom_call_target="tpu_custom_call" | custom-call | flops 4529848320 | bytes 1572864 | tf_op jit(solution)/shard_map/temporal/pallas_call | solution.py:381
  110.9 2.6 %collective-permute-start.26 = (bf16[2,1,64,384]{3,2,1,0:T(8,128)(2,1)S(1)}, bf16[2,1,64,384]{3,2,1,0:T(8,128)(2,1)S(1)}, u32[]{:S(2)}, u32[]{:S(2)}) collective-permute-start(bf16[2,1,64,384]{3,2,1,0:T(8,128)(2,1)S(1)} %get-tuple-element.81), channel_id=1, source_target_pairs={{0,2},{2,0},{16,18},{18,16},{1,3},{3,1},{17,19},{19,17},{4,6},{6,4... | collective-permute-start | bytes 294920 | tf_op jit(solution)/shard_map/ppermute | solution.py:419
  115.9 3.2 %temporal.7 = (bf16[2,1,64,384]{3,2,1,0:T(8,128)(2,1)S(1)}, bf16[2,1,64,384]{3,2,1,0:T(8,128)(2,1)S(1)}, bf16[2,1,64,384]{3,2,1,0:T(8,128)(2,1)S(1)}, bf16[2,1,64,384]{3,2,1,0:T(8,128)(2,1)S(1)}) custom-call(s32[5]{0:T(128)S(1)} %stack.31.place.before, bf16[2,1,64,384]{3,2,1,0:T(8,128)(2,1)S(1)} %get-tuple-element.80.before, ...), custom_call_target="tpu_custom_call" | custom-call | flops 4529848320 | bytes 1572864 | tf_op jit(solution)/shard_map/temporal/pallas_call | solution.py:381
  119.1 2.0 %collective-permute-start.31 = (bf16[2,1,64,384]{3,2,1,0:T(8,128)(2,1)S(1)}, bf16[2,1,64,384]{3,2,1,0:T(8,128)(2,1)S(1)}, u32[]{:S(2)}, u32[]{:S(2)}) collective-permute-start(bf16[2,1,64,384]{3,2,1,0:T(8,128)(2,1)S(1)} %get-tuple-element.86), channel_id=1, source_target_pairs={{0,2},{2,0},{16,18},{18,16},{1,3},{3,1},{17,19},{19,17},{4,6},{6,4... | collective-permute-start | bytes 294920 | tf_op jit(solution)/shard_map/ppermute | solution.py:419
  123.8 2.1 %collective-permute-done.28 = bf16[2,1,64,384]{3,2,1,0:T(8,128)(2,1)S(1)} collective-permute-done((bf16[2,1,64,384]{3,2,1,0:T(8,128)(2,1)S(1)}, bf16[2,1,64,384]{3,2,1,0:T(8,128)(2,1)S(1)}, u32[]{:S(2)}, u32[]{:S(2)}) %collective-permute-start.28) | collective-permute-done | bytes 98336 | tf_op jit(solution)/shard_map/ppermute | solution.py:419
  126.8 2.8 %collective-permute-done.33 = bf16[2,1,64,384]{3,2,1,0:T(8,128)(2,1)S(1)} collective-permute-done((bf16[2,1,64,384]{3,2,1,0:T(8,128)(2,1)S(1)}, bf16[2,1,64,384]{3,2,1,0:T(8,128)(2,1)S(1)}, u32[]{:S(2)}, u32[]{:S(2)}) %collective-permute-start.33) | collective-permute-done | bytes 98336 | tf_op jit(solution)/shard_map/ppermute | solution.py:419
  (116 shorter events, 29.9 us)
Async XLA Ops:
  11.0 39.6 %collective-permute-start.9 = (bf16[2304,384]{1,0:T(8,128)(2,1)S(1)}, bf16[2304,384]{1,0:T(8,128)(2,1)}, u32[]{:S(2)}, u32[]{:S(2)}) collective-permute-start(bf16[2304,384]{1,0:T(8,128)(2,1)S(1)} %pack_weights.3.mine), channel_id=1, source_target_pairs={{0,1},{1,0},{2,3},{3,2},{4,5},{5,4},{6,7},{7,6},{8,9},{9,8},{10,11... | collective-permute-start | bytes 5308424 | tf_op jit(solution)/shard_map/ppermute | solution.py:426
  11.4 7.0 %collective-permute-start = (bf16[2,1,64,384]{3,2,1,0:T(8,128)(2,1)S(1)}, bf16[2,1,64,384]{3,2,1,0:T(8,128)(2,1)}, u32[]{:S(2)}, u32[]{:S(2)}) collective-permute-start(bf16[2,1,64,384]{3,2,1,0:T(8,128)(2,1)S(1)} %get-tuple-element.47.before), channel_id=1, source_target_pairs={{0,2},{2,0},{16,18},{18,16},{1,3},{3,1},{17,19},{19,17},{4,6},{6,4... | collective-permute-start | bytes 294920 | tf_op jit(solution)/shard_map/ppermute | solution.py:419
  14.1 13.2 %collective-permute-start.1 = (bf16[2,1,64,384]{3,2,1,0:T(8,128)(2,1)}, bf16[2,1,64,384]{3,2,1,0:T(8,128)(2,1)}, u32[]{:S(2)}, u32[]{:S(2)}) collective-permute-start(bf16[2,1,64,384]{3,2,1,0:T(8,128)(2,1)} %get-tuple-element.48), channel_id=1, source_target_pairs={{0,16},{2,18},{16,0},{18,2},{1,17},{3,19},{17,1},{19,3},{4,20},{6,... | collective-permute-start | bytes 294920 | tf_op jit(solution)/shard_map/ppermute | solution.py:419
  16.7 12.3 %collective-permute-start.2 = (bf16[2,1,64,384]{3,2,1,0:T(8,128)(2,1)}, bf16[2,1,64,384]{3,2,1,0:T(8,128)(2,1)}, u32[]{:S(2)}, u32[]{:S(2)}) collective-permute-start(bf16[2,1,64,384]{3,2,1,0:T(8,128)(2,1)} %get-tuple-element.49), channel_id=1, source_target_pairs={{0,18},{2,16},{16,2},{18,0},{1,19},{3,17},{17,3},{19,1},{4,22},{6,... | collective-permute-start | bytes 294920 | tf_op jit(solution)/shard_map/ppermute | solution.py:419
  16.7 23.2 %collective-permute-start.4 = (bf16[2,1,64,384]{3,2,1,0:T(8,128)(2,1)S(1)}, bf16[2,1,64,384]{3,2,1,0:T(8,128)(2,1)S(1)}, u32[]{:S(2)}, u32[]{:S(2)}) collective-permute-start(bf16[2,1,64,384]{3,2,1,0:T(8,128)(2,1)S(1)} %get-tuple-element.55.before), channel_id=1, source_target_pairs={{0,2},{2,0},{16,18},{18,16},{1,3},{3,1},{17,19},{19,17},{4,6},{6,4... | collective-permute-start | bytes 294920 | tf_op jit(solution)/shard_map/ppermute | solution.py:419
  18.5 24.3 %collective-permute-start.5 = (bf16[2,1,64,384]{3,2,1,0:T(8,128)(2,1)}, bf16[2,1,64,384]{3,2,1,0:T(8,128)(2,1)S(1)}, u32[]{:S(2)}, u32[]{:S(2)}) collective-permute-start(bf16[2,1,64,384]{3,2,1,0:T(8,128)(2,1)} %copy-done.21), channel_id=1, source_target_pairs={{0,16},{2,18},{16,0},{18,2},{1,17},{3,19},{17,1},{19,3},{4,20},{6,... | collective-permute-start | bytes 294920 | tf_op jit(solution)/shard_map/ppermute | solution.py:419
  27.3 15.5 %collective-permute-start.6 = (bf16[2,1,64,384]{3,2,1,0:T(8,128)(2,1)}, bf16[2,1,64,384]{3,2,1,0:T(8,128)(2,1)S(1)}, u32[]{:S(2)}, u32[]{:S(2)}) collective-permute-start(bf16[2,1,64,384]{3,2,1,0:T(8,128)(2,1)} %copy-done.20), channel_id=1, source_target_pairs={{0,18},{2,16},{16,2},{18,0},{1,19},{3,17},{17,3},{19,1},{4,22},{6,... | collective-permute-start | bytes 294920 | tf_op jit(solution)/shard_map/ppermute | solution.py:419
  39.8 15.5 %collective-permute-start.7 = (bf16[2,1,128,384]{3,2,1,0:T(8,128)(2,1)S(1)}, bf16[2,1,128,384]{3,2,1,0:T(8,128)(2,1)S(1)}, u32[]{:S(2)}, u32[]{:S(2)}) collective-permute-start(bf16[2,1,128,384]{3,2,1,0:T(8,128)(2,1)S(1)} %get-tuple-element.59.odd), channel_id=1, source_target_pairs={{0,1},{1,4},{4,5},{5,8},{8,9},{9,12},{12,13},{13,0},{2,3},{3,6},{6... | collective-permute-start | bytes 589832 | tf_op jit(solution)/shard_map/ppermute | solution.py:452
  39.9 17.8 %collective-permute-start.8 = (bf16[2,1,128,384]{3,2,1,0:T(8,128)(2,1)S(1)}, bf16[2,1,128,384]{3,2,1,0:T(8,128)(2,1)S(1)}, u32[]{:S(2)}, u32[]{:S(2)}) collective-permute-start(bf16[2,1,128,384]{3,2,1,0:T(8,128)(2,1)S(1)} %get-tuple-element.54.before.even), channel_id=1, source_target_pairs={{1,0},{4,1},{5,4},{8,5},{9,8},{12,9},{13,12},{0,13},{3,2},{6,3},{7... | collective-permute-start | bytes 589832 | tf_op jit(solution)/shard_map/ppermute | solution.py:453
  47.9 25.9 %collective-permute-start.16 = (bf16[2,1,128,384]{3,2,1,0:T(8,128)(2,1)S(1)}, bf16[2,1,128,384]{3,2,1,0:T(8,128)(2,1)S(1)}, u32[]{:S(2)}, u32[]{:S(2)}) collective-permute-start(bf16[2,1,128,384]{3,2,1,0:T(8,128)(2,1)S(1)} %get-tuple-element.70.odd), channel_id=1, source_target_pairs={{0,1},{1,4},{4,5},{5,8},{8,9},{9,12},{12,13},{13,0},{2,3},{3,6},{6... | collective-permute-start | bytes 589832 | tf_op jit(solution)/shard_map/ppermute | solution.py:452
  47.9 26.9 %collective-permute-start.17 = (bf16[2,1,128,384]{3,2,1,0:T(8,128)(2,1)S(1)}, bf16[2,1,128,384]{3,2,1,0:T(8,128)(2,1)S(1)}, u32[]{:S(2)}, u32[]{:S(2)}) collective-permute-start(bf16[2,1,128,384]{3,2,1,0:T(8,128)(2,1)S(1)} %get-tuple-element.58.before.even), channel_id=1, source_target_pairs={{1,0},{4,1},{5,4},{8,5},{9,8},{12,9},{13,12},{0,13},{3,2},{6,3},{7... | collective-permute-start | bytes 589832 | tf_op jit(solution)/shard_map/ppermute | solution.py:453
  53.0 8.6 %collective-permute-start.13 = (bf16[2,1,64,384]{3,2,1,0:T(8,128)(2,1)S(1)}, bf16[2,1,64,384]{3,2,1,0:T(8,128)(2,1)S(1)}, u32[]{:S(2)}, u32[]{:S(2)}) collective-permute-start(bf16[2,1,64,384]{3,2,1,0:T(8,128)(2,1)S(1)} %get-tuple-element.66.before), channel_id=1, source_target_pairs={{0,2},{2,0},{16,18},{18,16},{1,3},{3,1},{17,19},{19,17},{4,6},{6,4... | collective-permute-start | bytes 294920 | tf_op jit(solution)/shard_map/ppermute | solution.py:419
  55.3 8.6 %collective-permute-start.14 = (bf16[2,1,64,384]{3,2,1,0:T(8,128)(2,1)S(1)}, bf16[2,1,64,384]{3,2,1,0:T(8,128)(2,1)S(1)}, u32[]{:S(2)}, u32[]{:S(2)}) collective-permute-start(bf16[2,1,64,384]{3,2,1,0:T(8,128)(2,1)S(1)} %get-tuple-element.67), channel_id=1, source_target_pairs={{0,16},{2,18},{16,0},{18,2},{1,17},{3,19},{17,1},{19,3},{4,20},{6,... | collective-permute-start | bytes 294920 | tf_op jit(solution)/shard_map/ppermute | solution.py:419
  57.6 10.9 %collective-permute-start.15 = (bf16[2,1,64,384]{3,2,1,0:T(8,128)(2,1)S(1)}, bf16[2,1,64,384]{3,2,1,0:T(8,128)(2,1)S(1)}, u32[]{:S(2)}, u32[]{:S(2)}) collective-permute-start(bf16[2,1,64,384]{3,2,1,0:T(8,128)(2,1)S(1)} %get-tuple-element.68), channel_id=1, source_target_pairs={{0,18},{2,16},{16,2},{18,0},{1,19},{3,17},{17,3},{19,1},{4,22},{6,... | collective-permute-start | bytes 294920 | tf_op jit(solution)/shard_map/ppermute | solution.py:419
  61.6 19.8 %collective-permute-start.21 = (bf16[2,1,64,384]{3,2,1,0:T(8,128)(2,1)S(1)}, bf16[2,1,64,384]{3,2,1,0:T(8,128)(2,1)S(1)}, u32[]{:S(2)}, u32[]{:S(2)}) collective-permute-start(bf16[2,1,64,384]{3,2,1,0:T(8,128)(2,1)S(1)} %get-tuple-element.75), channel_id=1, source_target_pairs={{0,2},{2,0},{16,18},{18,16},{1,3},{3,1},{17,19},{19,17},{4,6},{6,4... | collective-permute-start | bytes 294920 | tf_op jit(solution)/shard_map/ppermute | solution.py:419
  63.9 18.0 %collective-permute-start.22 = (bf16[2,1,64,384]{3,2,1,0:T(8,128)(2,1)S(1)}, bf16[2,1,64,384]{3,2,1,0:T(8,128)(2,1)S(1)}, u32[]{:S(2)}, u32[]{:S(2)}) collective-permute-start(bf16[2,1,64,384]{3,2,1,0:T(8,128)(2,1)S(1)} %get-tuple-element.76), channel_id=1, source_target_pairs={{0,16},{2,18},{16,0},{18,2},{1,17},{3,19},{17,1},{19,3},{4,20},{6,... | collective-permute-start | bytes 294920 | tf_op jit(solution)/shard_map/ppermute | solution.py:419
  68.6 13.9 %collective-permute-start.23 = (bf16[2,1,64,384]{3,2,1,0:T(8,128)(2,1)S(1)}, bf16[2,1,64,384]{3,2,1,0:T(8,128)(2,1)S(1)}, u32[]{:S(2)}, u32[]{:S(2)}) collective-permute-start(bf16[2,1,64,384]{3,2,1,0:T(8,128)(2,1)S(1)} %get-tuple-element.77), channel_id=1, source_target_pairs={{0,18},{2,16},{16,2},{18,0},{1,19},{3,17},{17,3},{19,1},{4,22},{6,... | collective-permute-start | bytes 294920 | tf_op jit(solution)/shard_map/ppermute | solution.py:419
  73.8 13.9 %collective-permute-start.10 = (bf16[2,1,64,384]{3,2,1,0:T(8,128)(2,1)S(1)}, bf16[2,1,64,384]{3,2,1,0:T(8,128)(2,1)S(1)}, u32[]{:S(2)}, u32[]{:S(2)}) collective-permute-start(bf16[2,1,64,384]{3,2,1,0:T(8,128)(2,1)S(1)} %get-tuple-element.63), channel_id=1, source_target_pairs={{0,2},{2,0},{16,18},{18,16},{1,3},{3,1},{17,19},{19,17},{4,6},{6,4... | collective-permute-start | bytes 294920 | tf_op jit(solution)/shard_map/ppermute | solution.py:419
  74.9 12.9 %collective-permute-start.11 = (bf16[2,1,64,384]{3,2,1,0:T(8,128)(2,1)S(1)}, bf16[2,1,64,384]{3,2,1,0:T(8,128)(2,1)S(1)}, u32[]{:S(2)}, u32[]{:S(2)}) collective-permute-start(bf16[2,1,64,384]{3,2,1,0:T(8,128)(2,1)S(1)} %get-tuple-element.64), channel_id=1, source_target_pairs={{0,16},{2,18},{16,0},{18,2},{1,17},{3,19},{17,1},{19,3},{4,20},{6,... | collective-permute-start | bytes 294920 | tf_op jit(solution)/shard_map/ppermute | solution.py:419
  81.4 9.1 %collective-permute-start.12 = (bf16[2,1,64,384]{3,2,1,0:T(8,128)(2,1)S(1)}, bf16[2,1,64,384]{3,2,1,0:T(8,128)(2,1)S(1)}, u32[]{:S(2)}, u32[]{:S(2)}) collective-permute-start(bf16[2,1,64,384]{3,2,1,0:T(8,128)(2,1)S(1)} %get-tuple-element.65), channel_id=1, source_target_pairs={{0,18},{2,16},{16,2},{18,0},{1,19},{3,17},{17,3},{19,1},{4,22},{6,... | collective-permute-start | bytes 294920 | tf_op jit(solution)/shard_map/ppermute | solution.py:419
  82.0 25.8 %collective-permute-start.25 = (bf16[2,1,128,384]{3,2,1,0:T(8,128)(2,1)S(1)}, bf16[2,1,128,384]{3,2,1,0:T(8,128)(2,1)S(1)}, u32[]{:S(2)}, u32[]{:S(2)}) collective-permute-start(bf16[2,1,128,384]{3,2,1,0:T(8,128)(2,1)S(1)} %get-tuple-element.69.before.even), channel_id=1, source_target_pairs={{1,0},{4,1},{5,4},{8,5},{9,8},{12,9},{13,12},{0,13},{3,2},{6,3},{7... | collective-permute-start | bytes 589832 | tf_op jit(solution)/shard_map/ppermute | solution.py:453
  82.5 25.2 %collective-permute-start.24 = (bf16[2,1,128,384]{3,2,1,0:T(8,128)(2,1)S(1)}, bf16[2,1,128,384]{3,2,1,0:T(8,128)(2,1)S(1)}, u32[]{:S(2)}, u32[]{:S(2)}) collective-permute-start(bf16[2,1,128,384]{3,2,1,0:T(8,128)(2,1)S(1)} %get-tuple-element.79.odd), channel_id=1, source_target_pairs={{0,1},{1,4},{4,5},{5,8},{8,9},{9,12},{12,13},{13,0},{2,3},{3,6},{6... | collective-permute-start | bytes 589832 | tf_op jit(solution)/shard_map/ppermute | solution.py:452
  87.7 28.3 %collective-permute-start.29 = (bf16[2,1,128,384]{3,2,1,0:T(8,128)(2,1)S(1)}, bf16[2,1,128,384]{3,2,1,0:T(8,128)(2,1)S(1)}, u32[]{:S(2)}, u32[]{:S(2)}) collective-permute-start(bf16[2,1,128,384]{3,2,1,0:T(8,128)(2,1)S(1)} %get-tuple-element.84.odd), channel_id=1, source_target_pairs={{0,1},{1,4},{4,5},{5,8},{8,9},{9,12},{12,13},{13,0},{2,3},{3,6},{6... | collective-permute-start | bytes 589832 | tf_op jit(solution)/shard_map/ppermute | solution.py:452
  87.8 28.2 %collective-permute-start.30 = (bf16[2,1,128,384]{3,2,1,0:T(8,128)(2,1)S(1)}, bf16[2,1,128,384]{3,2,1,0:T(8,128)(2,1)S(1)}, u32[]{:S(2)}, u32[]{:S(2)}) collective-permute-start(bf16[2,1,128,384]{3,2,1,0:T(8,128)(2,1)S(1)} %get-tuple-element.78.before.even), channel_id=1, source_target_pairs={{1,0},{4,1},{5,4},{8,5},{9,8},{12,9},{13,12},{0,13},{3,2},{6,3},{7... | collective-permute-start | bytes 589832 | tf_op jit(solution)/shard_map/ppermute | solution.py:453
  95.2 6.1 %collective-permute-start.19 = (bf16[2,1,64,384]{3,2,1,0:T(8,128)(2,1)S(1)}, bf16[2,1,64,384]{3,2,1,0:T(8,128)(2,1)S(1)}, u32[]{:S(2)}, u32[]{:S(2)}) collective-permute-start(bf16[2,1,64,384]{3,2,1,0:T(8,128)(2,1)S(1)} %get-tuple-element.73), channel_id=1, source_target_pairs={{0,16},{2,18},{16,0},{18,2},{1,17},{3,19},{17,1},{19,3},{4,20},{6,... | collective-permute-start | bytes 294920 | tf_op jit(solution)/shard_map/ppermute | solution.py:419
  101.3 6.4 %collective-permute-start.20 = (bf16[2,1,64,384]{3,2,1,0:T(8,128)(2,1)S(1)}, bf16[2,1,64,384]{3,2,1,0:T(8,128)(2,1)S(1)}, u32[]{:S(2)}, u32[]{:S(2)}) collective-permute-start(bf16[2,1,64,384]{3,2,1,0:T(8,128)(2,1)S(1)} %get-tuple-element.74), channel_id=1, source_target_pairs={{0,18},{2,16},{16,2},{18,0},{1,19},{3,17},{17,3},{19,1},{4,22},{6,... | collective-permute-start | bytes 294920 | tf_op jit(solution)/shard_map/ppermute | solution.py:419
  110.9 11.2 %collective-permute-start.26 = (bf16[2,1,64,384]{3,2,1,0:T(8,128)(2,1)S(1)}, bf16[2,1,64,384]{3,2,1,0:T(8,128)(2,1)S(1)}, u32[]{:S(2)}, u32[]{:S(2)}) collective-permute-start(bf16[2,1,64,384]{3,2,1,0:T(8,128)(2,1)S(1)} %get-tuple-element.81), channel_id=1, source_target_pairs={{0,2},{2,0},{16,18},{18,16},{1,3},{3,1},{17,19},{19,17},{4,6},{6,4... | collective-permute-start | bytes 294920 | tf_op jit(solution)/shard_map/ppermute | solution.py:419
  113.5 10.2 %collective-permute-start.27 = (bf16[2,1,64,384]{3,2,1,0:T(8,128)(2,1)S(1)}, bf16[2,1,64,384]{3,2,1,0:T(8,128)(2,1)S(1)}, u32[]{:S(2)}, u32[]{:S(2)}) collective-permute-start(bf16[2,1,64,384]{3,2,1,0:T(8,128)(2,1)S(1)} %get-tuple-element.82), channel_id=1, source_target_pairs={{0,16},{2,18},{16,0},{18,2},{1,17},{3,19},{17,1},{19,3},{4,20},{6,... | collective-permute-start | bytes 294920 | tf_op jit(solution)/shard_map/ppermute | solution.py:419
  114.5 11.4 %collective-permute-start.28 = (bf16[2,1,64,384]{3,2,1,0:T(8,128)(2,1)S(1)}, bf16[2,1,64,384]{3,2,1,0:T(8,128)(2,1)S(1)}, u32[]{:S(2)}, u32[]{:S(2)}) collective-permute-start(bf16[2,1,64,384]{3,2,1,0:T(8,128)(2,1)S(1)} %get-tuple-element.83), channel_id=1, source_target_pairs={{0,18},{2,16},{16,2},{18,0},{1,19},{3,17},{17,3},{19,1},{4,22},{6,... | collective-permute-start | bytes 294920 | tf_op jit(solution)/shard_map/ppermute | solution.py:419
  119.1 6.8 %collective-permute-start.31 = (bf16[2,1,64,384]{3,2,1,0:T(8,128)(2,1)S(1)}, bf16[2,1,64,384]{3,2,1,0:T(8,128)(2,1)S(1)}, u32[]{:S(2)}, u32[]{:S(2)}) collective-permute-start(bf16[2,1,64,384]{3,2,1,0:T(8,128)(2,1)S(1)} %get-tuple-element.86), channel_id=1, source_target_pairs={{0,2},{2,0},{16,18},{18,16},{1,3},{3,1},{17,19},{19,17},{4,6},{6,4... | collective-permute-start | bytes 294920 | tf_op jit(solution)/shard_map/ppermute | solution.py:419
  121.2 5.7 %collective-permute-start.32 = (bf16[2,1,64,384]{3,2,1,0:T(8,128)(2,1)S(1)}, bf16[2,1,64,384]{3,2,1,0:T(8,128)(2,1)S(1)}, u32[]{:S(2)}, u32[]{:S(2)}) collective-permute-start(bf16[2,1,64,384]{3,2,1,0:T(8,128)(2,1)S(1)} %get-tuple-element.87), channel_id=1, source_target_pairs={{0,16},{2,18},{16,0},{18,2},{1,17},{3,19},{17,1},{19,3},{4,20},{6,... | collective-permute-start | bytes 294920 | tf_op jit(solution)/shard_map/ppermute | solution.py:419
  122.2 7.5 %collective-permute-start.33 = (bf16[2,1,64,384]{3,2,1,0:T(8,128)(2,1)S(1)}, bf16[2,1,64,384]{3,2,1,0:T(8,128)(2,1)S(1)}, u32[]{:S(2)}, u32[]{:S(2)}) collective-permute-start(bf16[2,1,64,384]{3,2,1,0:T(8,128)(2,1)S(1)} %get-tuple-element.88), channel_id=1, source_target_pairs={{0,18},{2,16},{16,2},{18,0},{1,19},{3,17},{17,3},{19,1},{4,22},{6,... | collective-permute-start | bytes 294920 | tf_op jit(solution)/shard_map/ppermute | solution.py:419
  (25 other events, 74.1 us)

commit v4 on v3

--- a/solution.py
+++ b/solution.py
@@ -10,9 +10,11 @@
 HEAD_DIM = 64
 DILATION_FIRST = 16
 DILATION_SECOND = 256
-CHUNKS = (1, 1, 1, 1)
-ORDER = (("s", 0), ("s", 1), ("t", 0), ("s", 2), ("t", 1), ("s", 3), ("t", 2), ("t", 3))
-VMEM_LIMIT = 24 * 1024 * 1024
+GROUPS = ((0, 1), (2,), (3,))
+ORDER = (("s", 0), ("s", 1), ("t", 0), ("s", 2), ("s", 3), ("t", 1), ("t", 2))
+MIB = 1024 * 1024
+SECTION_MIB = 14
+TEMPORAL_MIB = 14
 
 
 def with_halo(block, sides, width):
@@ -115,8 +117,8 @@
 SCALARS = pl.BlockSpec(memory_space=pltpu.SMEM)
 
 
-def params():
-    return pltpu.CompilerParams(vmem_limit_bytes=VMEM_LIMIT)
+def params(mib):
+    return pltpu.CompilerParams(vmem_limit_bytes=mib * MIB)
 
 
 def moved(count):
@@ -141,7 +143,7 @@
         out_shape=jax.ShapeDtypeStruct((rows, width), weights[0].dtype),
         in_specs=[ANYWHERE] + [RESIDENT] * len(weights),
         out_specs=RESIDENT,
-        compiler_params=params(),
+        compiler_params=params(8),
         cost_estimate=moved(rows * width),
         name="pack_weights",
     )(before, *weights)
@@ -165,62 +167,67 @@
         out_shape=[jax.ShapeDtypeStruct((2 * w.shape[0], w.shape[1]), w.dtype) for w in halves],
         in_specs=[SCALARS, ANYWHERE, RESIDENT, RESIDENT],
         out_specs=[RESIDENT] * len(halves),
-        compiler_params=params(),
+        compiler_params=params(8),
         cost_estimate=moved(2 * mine.size),
         name="join_weights",
     )(place, before, mine, other)
 
 
-def pack_kernel(place, before, *refs):
-    half = len(refs) // 2
-    for source, packed in zip(refs[:half], refs[half:]):
-        packed[...] = source[...]
-
-
-def run_pack(place, before, grouped, begin, count):
+def pack_kernel(before, source, packed):
+    for part in range(packed.shape[0]):
+        packed[part] = source[:, part]
+
+
+def run_pack(before, grouped, unit, parts):
     slots, _, cells, features = grouped.shape
-    shape = (slots, 1, cells, features)
-
-    def source(delta):
-        return pl.BlockSpec(
-            shape, lambda i, at: (0, begin + (at[4] ^ delta) * count + i, 0, 0)
-        )
-
     return pl.pallas_call(
         pack_kernel,
-        grid_spec=pltpu.PrefetchScalarGridSpec(
-            num_scalar_prefetch=1,
-            grid=(count,),
-            in_specs=[ANYWHERE] + [source(delta) for delta in (1, 2, 3)],
-            out_specs=[pl.BlockSpec(shape, lambda i, at: (0, i, 0, 0))] * 3,
+        grid=(1,),
+        in_specs=[
+            ANYWHERE,
+            pl.BlockSpec((slots, parts, cells, features), lambda i: (0, unit, 0, 0)),
+        ],
+        out_specs=pl.BlockSpec((parts, slots, cells, features), lambda i: (0, 0, 0, 0)),
+        out_shape=jax.ShapeDtypeStruct((parts, slots, cells, features), grouped.dtype),
+        compiler_params=params(4),
+        cost_estimate=moved(parts * slots * cells * features),
+        name="pack",
+    )(before, grouped)
+
+
+def unpack_kernel(before, buffer, received, result):
+    for unit in range(received.shape[2]):
+
+        @pl.when(pl.program_id(0) == unit)
+        def _():
+            for part in range(received.shape[0]):
+                result[:, part] = received[part, :, unit]
+
+
+def run_unpack(before, buffer, received, first_unit, shape):
+    parts, slots, count, cells, features = received.shape
+    return pl.pallas_call(
+        unpack_kernel,
+        grid=(count,),
+        in_specs=[ANYWHERE, ANYWHERE, RESIDENT],
+        out_specs=pl.BlockSpec(
+            (slots, parts, cells, features), lambda i: (0, first_unit + i, 0, 0)
         ),
-        out_shape=[jax.ShapeDtypeStruct((slots, count, cells, features), grouped.dtype)] * 3,
-        compiler_params=params(),
-        cost_estimate=moved(3 * slots * count * cells * features),
-        name="pack",
-    )(place, before, grouped, grouped, grouped)
-
-
-def section_kernel(
-    place,
-    before,
-    own,
-    near_cells,
-    far_own,
-    far_cells,
-    w_qkv,
-    w_out,
-    w_up,
-    w_down,
-    even_ref,
-    odd_ref,
-):
-    features = own.shape[-1]
-    cells = 2 * own.shape[2]
+        out_shape=pltpu.HBM(shape, received.dtype),
+        input_output_aliases={} if buffer is before else {1: 0},
+        compiler_params=params(4),
+        cost_estimate=moved(received.size),
+        name="unpack",
+    )(before, buffer, received)
+
+
+def section_kernel(before, arrived, w_qkv, w_out, w_up, w_down, even_ref, odd_ref):
+    features = arrived.shape[-1]
+    cells = 2 * arrived.shape[2]
     parts = []
-    for mine, other in ((own, near_cells), (far_own, far_cells)):
+    for block in range(2):
         for slot in range(2):
-            parts += [mine[slot, 0], other[slot, 0]]
+            parts += [arrived[2 * block, slot], arrived[2 * block + 1, slot]]
     residual = jnp.concatenate(parts, axis=0).astype(jnp.float32)
     frame_count = 4
     normed = normalize(residual).astype(jnp.bfloat16)
@@ -279,8 +286,8 @@
         total = total + jnp.dot(hidden, w_down[at : at + width], preferred_element_type=jnp.float32)
     sectioned = total.astype(jnp.bfloat16)
     for block in range(2):
-        even_ref[block, 0] = sectioned[(2 * block) * cells : (2 * block + 1) * cells]
-        odd_ref[block, 0] = sectioned[(2 * block + 1) * cells : (2 * block + 2) * cells]
+        even_ref[block] = sectioned[(2 * block) * cells : (2 * block + 1) * cells]
+        odd_ref[block] = sectioned[(2 * block + 1) * cells : (2 * block + 2) * cells]
 
 
 def gate(center, preact):
@@ -291,110 +298,82 @@
     return (center.astype(jnp.float32) + gated).astype(jnp.bfloat16)
 
 
-def temporal_kernel(
-    place,
-    before,
-    even,
-    odd,
-    left_odd,
-    right_even,
-    w_first,
-    w_second,
-    out0,
-    out1,
-    out2,
-    out3,
-):
-    near, is_first, is_last = place[1], place[2], place[3]
-    far = 1 - near
-    features = even.shape[-1]
-    cells = even.shape[2]
-    zero = jnp.zeros((cells, features), even.dtype)
-    even_n, odd_n, even_f, odd_f = even[near, 0], odd[near, 0], even[far, 0], odd[far, 0]
-    left_n = jnp.where(is_first == 1, zero, left_odd[near, 0])
-    left_f = left_odd[jnp.where(is_first == 1, near, far), 0]
-    right_n = right_even[jnp.where(is_last == 1, far, near), 0]
-    right_f = jnp.where(is_last == 1, zero, right_even[far, 0])
-    center = jnp.concatenate([even_n, odd_n, even_f, odd_f], axis=0)
-    stacked = jnp.concatenate(
-        [
-            jnp.concatenate([left_n, even_n, left_f, even_f], axis=0),
-            center,
-            jnp.concatenate([odd_n, right_n, odd_f, right_f], axis=0),
-        ],
-        axis=1,
-    )
-    opening = gate(center, jnp.dot(stacked, w_first[...], preferred_element_type=jnp.float32))
-    rows = 2 * cells
-    near_part, far_part = opening[:rows], opening[rows:]
-    both = jnp.concatenate([near_part, far_part], axis=1)
-    result_n = gate(
-        near_part, jnp.dot(both, w_second[features:], preferred_element_type=jnp.float32)
-    )
-    result_f = gate(
-        far_part, jnp.dot(both, w_second[: 2 * features], preferred_element_type=jnp.float32)
-    )
-    same = jnp.where(near == 0, result_n, result_f)
-    other = jnp.where(near == 0, result_f, result_n)
-    half = cells // 2
-    for slot in range(2):
-        at = slot * cells
-        out0[slot, 0] = same[at : at + half]
-        out1[slot, 0] = same[at + half : at + cells]
-        out2[slot, 0] = other[at : at + half]
-        out3[slot, 0] = other[at + half : at + cells]
-
-
-def run_section(place, before, grouped, begin, pieces, weights):
-    slots, count, cells, features = pieces[0].shape
+def temporal_kernel(place, before, *refs):
+    *inputs, w_first, w_second, out = refs
+    is_first, is_last = place[1], place[2]
+    for unit in range(len(inputs) // 4):
+        even, odd, left_odd, right_even = inputs[4 * unit : 4 * unit + 4]
+        _, cells, features = even.shape
+        zero = jnp.zeros((cells, features), even.dtype)
+        even_n, odd_n, even_f, odd_f = even[0], odd[0], even[1], odd[1]
+        left_n = jnp.where(is_first == 1, zero, left_odd[0])
+        left_f = left_odd[jnp.where(is_first == 1, 0, 1)]
+        right_n = right_even[jnp.where(is_last == 1, 1, 0)]
+        right_f = jnp.where(is_last == 1, zero, right_even[1])
+        center = jnp.concatenate([even_n, odd_n, even_f, odd_f], axis=0)
+        stacked = jnp.concatenate(
+            [
+                jnp.concatenate([left_n, even_n, left_f, even_f], axis=0),
+                center,
+                jnp.concatenate([odd_n, right_n, odd_f, right_f], axis=0),
+            ],
+            axis=1,
+        )
+        opening = gate(center, jnp.dot(stacked, w_first[...], preferred_element_type=jnp.float32))
+        rows = 2 * cells
+        near_part, far_part = opening[:rows], opening[rows:]
+        both = jnp.concatenate([near_part, far_part], axis=1)
+        result_n = gate(
+            near_part, jnp.dot(both, w_second[features:], preferred_element_type=jnp.float32)
+        )
+        result_f = gate(
+            far_part, jnp.dot(both, w_second[: 2 * features], preferred_element_type=jnp.float32)
+        )
+        half = cells // 2
+        for block, result in enumerate((result_n, result_f)):
+            for slot in range(2):
+                at = slot * cells
+                out[2 * block, slot, unit] = result[at : at + half]
+                out[2 * block + 1, slot, unit] = result[at + half : at + cells]
+
+
+def run_section(before, arrived, weights):
+    parts, slots, cells, features = arrived.shape
     ff = weights[2].shape[1]
-    shape_in = (slots, 1, cells, features)
-    own = pl.BlockSpec(shape_in, lambda i, at: (0, begin + at[4] * count + i, 0, 0))
-    block_in = pl.BlockSpec(shape_in, lambda i, at: (0, i, 0, 0))
-    block_out = pl.BlockSpec((2, 1, 2 * cells, features), lambda i, at: (0, i, 0, 0))
-    shape = jax.ShapeDtypeStruct((2, count, 2 * cells, features), jnp.bfloat16)
-    tokens = 2 * slots * count * 2 * cells
+    shape = jax.ShapeDtypeStruct((2, 2 * cells, features), jnp.bfloat16)
+    tokens = parts * slots * cells
     macs = tokens * (features * (4 * features + 2 * ff) + 4 * cells * features)
     return pl.pallas_call(
         section_kernel,
-        grid_spec=pltpu.PrefetchScalarGridSpec(
-            num_scalar_prefetch=1,
-            grid=(count,),
-            in_specs=[ANYWHERE, own] + [block_in] * 3 + [RESIDENT] * 4,
-            out_specs=[block_out, block_out],
-        ),
+        in_specs=[ANYWHERE] + [RESIDENT] * 5,
+        out_specs=[RESIDENT] * 2,
         out_shape=[shape, shape],
-        compiler_params=params(),
+        compiler_params=params(SECTION_MIB),
         cost_estimate=pl.CostEstimate(
             flops=6 * macs, bytes_accessed=8 * tokens * features, transcendentals=tokens * ff
         ),
         name="section",
-    )(place, before, grouped, *pieces, *weights)
-
-
-def run_temporal(place, before, even, odd, left_odd, right_even, weights):
-    blocks, count, cells, features = even.shape
-    block_in = pl.BlockSpec((blocks, 1, cells, features), lambda i, at: (0, i, 0, 0))
-    block_out = pl.BlockSpec((2, 1, cells // 2, features), lambda i, at: (0, i, 0, 0))
-    shape = jax.ShapeDtypeStruct((2, count, cells // 2, features), jnp.bfloat16)
+    )(before, arrived, *weights)
+
+
+def run_temporal(place, before, units, weights):
+    blocks, cells, features = units[0][0].shape
+    count = len(units)
+    shape = jax.ShapeDtypeStruct((2 * blocks, 2, count, cells // 2, features), jnp.bfloat16)
     tokens = 2 * blocks * count * cells
     return pl.pallas_call(
         temporal_kernel,
-        grid_spec=pltpu.PrefetchScalarGridSpec(
-            num_scalar_prefetch=1,
-            grid=(count,),
-            in_specs=[ANYWHERE] + [block_in] * 4 + [RESIDENT] * 2,
-            out_specs=[block_out] * 4,
-        ),
-        out_shape=[shape] * 4,
-        compiler_params=params(),
+        in_specs=[SCALARS, ANYWHERE] + [RESIDENT] * (4 * count + 2),
+        out_specs=RESIDENT,
+        out_shape=shape,
+        compiler_params=params(TEMPORAL_MIB),
         cost_estimate=pl.CostEstimate(
             flops=60 * tokens * features * features,
             bytes_accessed=8 * tokens * features,
             transcendentals=4 * tokens * features,
         ),
         name="temporal",
-    )(place, before, even, odd, left_odd, right_even, *weights)
+    )(place, before, *[part for unit in units for part in unit], *weights)
 
 
 GROUP = ("far", "cell")
@@ -404,23 +383,20 @@
 def paired(frames, w_qkv, w_out, w_up, w_down, temporal_weight_first, temporal_weight_second):
     frames_local, cells, features = frames.shape
     near_size, subs = lax.axis_size("near"), lax.axis_size("sub")
-    sub, side = lax.axis_index("sub"), lax.axis_index("far")
-    quarter = 2 * side + lax.axis_index("cell")
+    sub = lax.axis_index("sub")
     ring = near_size * subs
     position = lax.axis_index("near") * subs + sub
-    place = jnp.stack([sub, side, position == 0, position == ring - 1, quarter]).astype(jnp.int32)
+    place = jnp.stack([sub, position == 0, position == ring - 1]).astype(jnp.int32)
     rightward = [(i, (i + 1) % ring) for i in range(ring)]
     leftward = [(target, source) for source, target in rightward]
     slots = frames_local // DILATION_FIRST
+    parts = 4
     grouped = frames.reshape(slots, DILATION_FIRST, cells, features)
-    begins = [4 * sum(CHUNKS[:index]) for index in range(len(CHUNKS))]
-
-    def exchange(piece, delta):
-        return lax.ppermute(piece, GROUP, [(i, i ^ delta) for i in range(4)])
-
-    def send(before, index):
-        cut = run_pack(place, before, grouped, begins[index], CHUNKS[index])
-        return cut[0], [exchange(piece, delta) for delta, piece in zip((1, 2, 3), cut)]
+    pinned = pltpu.with_memory_space_constraint(grouped, pltpu.HBM)
+
+    def send(before, unit):
+        cut = run_pack(before, pinned, unit, parts)
+        return cut, lax.all_to_all(cut, GROUP, 0, 0)
 
     def swap_core(packed):
         return lax.ppermute(packed, "sub", [(0, 1), (1, 0)])
@@ -430,39 +406,32 @@
     arrived = {}
     before, arrived[0] = send(place, 0)
     section_mine = pack_weights(before, section_halves, features)
+    before, arrived[1] = send(section_mine, 1)
+    temporal_mine = pack_weights(before, temporal_halves, features)
+    before, arrived[2] = send(temporal_mine, 2)
+    before, arrived[3] = send(before, 3)
     section_weights = join_weights(
         place, before, section_mine, swap_core(section_mine), section_halves
     )
-    before, arrived[1] = send(section_weights[0], 1)
-    temporal_mine = pack_weights(before, temporal_halves, features)
     temporal_weights = join_weights(
-        place, before, temporal_mine, swap_core(temporal_mine), temporal_halves
-    )
+        place, section_weights[0], temporal_mine, swap_core(temporal_mine), temporal_halves
+    )
+    waiting, backs = {}, {}
     before = temporal_weights[0]
-    for index in range(2, len(CHUNKS)):
-        before, arrived[index] = send(before, index)
-
-    waiting, outs = {}, {}
-    before = place
     for kind, index in ORDER:
         if kind == "s":
-            even, odd = run_section(
-                place, before, grouped, begins[index], arrived[index], section_weights
-            )
+            even, odd = run_section(before, arrived[index], section_weights)
             left_odd = lax.ppermute(odd, RING, rightward)
             right_even = lax.ppermute(even, RING, leftward)
             waiting[index] = (even, odd, left_odd, right_even)
             before = even
         else:
-            sent = run_temporal(place, before, *waiting[index], temporal_weights)
-            outs[index] = [sent[0]] + [exchange(sent[delta], delta) for delta in (1, 2, 3)]
-            before = sent[0]
-    result = jnp.zeros_like(grouped)
-    for index, count in enumerate(CHUNKS):
-        for delta in range(4):
-            result = lax.dynamic_update_slice_in_dim(
-                result, outs[index][delta], begins[index] + (quarter ^ delta) * count, axis=1
-            )
+            units = [waiting[unit] for unit in GROUPS[index]]
+            before = run_temporal(place, before, units, temporal_weights)
+            backs[index] = lax.all_to_all(before, GROUP, 0, 0)
+    result = before
+    for index, group in enumerate(GROUPS):
+        result = run_unpack(before, result, backs[index], group[0], grouped.shape)
     return result.reshape(frames.shape)
 
 
@@ -480,7 +449,7 @@
             and cell == 2
             and sub == 2
             and (cells // cell) % 16 == 0
-            and DILATION_FIRST == 4 * sum(CHUNKS)
+            and DILATION_FIRST == 4 * sum(len(group) for group in GROUPS)
         )
         if fits:
             devices = mesh.devices.reshape(groups, 2, tm // 2, cell, sub)

time: 133 us -> 153 us (1.15)
  blocking collectives: 0 us -> 34.4 us
  waiting for transfers between devices: 30 us -> 14.3 us
  starting transfers between devices: 49.7 us -> 35.8 us
  local copies, waits for them, and re-layouts: 10.4 us -> 18.6 us
  Pallas kernels: 40.4 us -> 47.5 us
    ppermute x24 -> x0, starting transfers between devices: 39.8 us -> none  [exchange(): return lax.ppermute(piece, GROUP, [(i, i ^ delta) for i in range(4)])]
    all_to_all x0 -> x2, blocking collectives: none -> 34.4 us  [the longest x1 18.6 us: send(): return (cut, lax.all_to_all(cut, GROUP, 0, 0))]
    ppermute x24 -> x0, waiting for transfers between devices: 26.6 us -> none  [exchange(): return lax.ppermute(piece, GROUP, [(i, i ^ delta) for i in range(4)])]
    all_to_all x0 -> x5, starting transfers between devices: none -> 24.2 us  [the longest x3 14.3 us: send(): return (cut, lax.all_to_all(cut, GROUP, 0, 0))]
    unnamed x46 -> x78, local copies, waits for them, and re-layouts: 9.78 us -> 18.6 us
    all_to_all x0 -> x5, waiting for transfers between devices: none -> 5.81 us  [the longest x2 5.8 us: paired(): backs[index] = lax.all_to_all(before, GROUP, 0, 0)]
    pallas_call x12 -> x14, Pallas kernels: 37.4 us -> 42.4 us  [the longest x4 20 us: run_section(): pl.pallas_call(section_kernel, in_specs=[ANYWHERE] + [RESIDENT] * 5, out_...]
    ppermute x4, waiting for transfers between devices: 0.01 us -> 4.3 us  [paired(): right_even = lax.ppermute(even, RING, leftward)]
  transfers between devices with their start and end apart: 34 -> 15, of which waited for: 11 -> 4; matrix products, arithmetic and copies ran while one was open for 0% -> 0% of each run, Pallas kernels for 29% -> 28%
where the time goes in v4:
time: 153 us; the launch traced here: 151 us
  Pallas kernels  47.5 us (31%)
  starting transfers between devices  35.8 us (23%)
  blocking collectives  34.4 us (22%)
  local copies, waits for them, and re-layouts  18.6 us (12%)
  waiting for transfers between devices  14.3 us (9%)
    pallas_call x4, Pallas kernels, run_section(): pl.pallas_call(section_kernel, in_specs=[ANYWHERE] + [RESIDENT] * 5, out_...  20 us
    unnamed x78, local copies, waits for them, and re-layouts  18.6 us
    all_to_all x1, blocking collectives, send(): return (cut, lax.all_to_all(cut, GROUP, 0, 0))  18.6 us
    all_to_all x1, blocking collectives, paired(): backs[index] = lax.all_to_all(before, GROUP, 0, 0)  15.8 us
    all_to_all x3, starting transfers between devices, send(): return (cut, lax.all_to_all(cut, GROUP, 0, 0))  14.3 us
    pallas_call x3, Pallas kernels, run_temporal(): pl.pallas_call(temporal_kernel, in_specs=[SCALARS, ANYWHERE] + [RESIDENT]...  14.1 us
    all_to_all x2, starting transfers between devices, paired(): backs[index] = lax.all_to_all(before, GROUP, 0, 0)  9.94 us
    ppermute x4, starting transfers between devices, paired(): right_even = lax.ppermute(even, RING, leftward)  8.74 us
  transfers between devices with their start and end apart: 15, of which 4 were waited for; matrix products, arithmetic and copies ran while one was open for 0% of the time, Pallas kernels for 28%

profile of v4, /device:TPU:0, one launch (start us, length us, event | category | flops | bytes accessed | tf_op | source)
XLA Modules:
  0.0 151.1 jit_solution(8439563808196989355)
XLA Ops:
  4.4 18.6 %all_to_all.35.arrived = bf16[4,2,64,384]{3,2,1,0:T(8,128)(2,1)} all-to-all(bf16[4,2,64,384]{3,2,1,0:T(8,128)(2,1)S(1)} %pack.4.before), channel_id=1, replica_groups=mesh['groups'=1,'far'=2,'near'=4,'cell'=2,'sub'=2] {'far','cell'}, dimensions={0} | all-to-all | bytes 786432 | tf_op jit(solution)/shard_map/all_to_all | solution.py:399
  23.0 4.1 %all-to-all-start.1 = ((bf16[4,2,64,384]{3,2,1,0:T(8,128)(2,1)}), bf16[4,2,64,384]{3,2,1,0:T(8,128)(2,1)}, u32[]{:S(2)}, u32[]{:S(2)}) async-start(bf16[4,2,64,384]{3,2,1,0:T(8,128)(2,1)} %copy-done), calls=%async_computation.1 | async-start | bytes 786432 | tf_op jit(solution)/shard_map/all_to_all | solution.py:399
  27.2 1.8 %pack.6.before = bf16[4,2,64,384]{3,2,1,0:T(8,128)(2,1)} custom-call(bf16[2304,384]{1,0:T(8,128)(2,1)S(1)} %pack_weights.3.before.mine, bf16[2,16,64,384]{3,2,1,0:T(8,128)(2,1)} %bitcast.7), custom_call_target="tpu_custom_call" | custom-call | bytes 786432 | tf_op jit(solution)/shard_map/pack/pallas_call | solution.py:183
  29.0 1.8 %pack.7.before = bf16[4,2,64,384]{3,2,1,0:T(8,128)(2,1)} custom-call(bf16[4,2,64,384]{3,2,1,0:T(8,128)(2,1)} %pack.6.before, bf16[2,16,64,384]{3,2,1,0:T(8,128)(2,1)} %bitcast.8), custom_call_target="tpu_custom_call" | custom-call | bytes 786432 | tf_op jit(solution)/shard_map/pack/pallas_call | solution.py:183
  30.8 1.8 %join_weights.2 = (bf16[384,1152]{1,0:T(8,128)(2,1)S(1)}, bf16[384,384]{1,0:T(8,128)(2,1)S(1)}, bf16[384,1536]{1,0:T(8,128)(2,1)S(1)}, bf16[1536,384]{1,0:T(8,128)(2,1)S(1)}) custom-call(s32[3]{0:T(128)S(1)} %pad_add_fusion.before.place, bf16[4,2,64,384]{3,2,1,0:T(8,128)(2,1)} %pack.7.before, bf16[2304,384]{1,0:T(8,128)(2,1)S(1)} %pack_weights.2.before.mine, ...), custom_call_target="tpu_custom_call" | custom-call | bytes 7077888 | tf_op jit(solution)/shard_map/join_weights/pallas_call | solution.py:165
  32.6 3.1 %join_weights.3 = (bf16[1152,768]{1,0:T(8,128)(2,1)S(1)}, bf16[1152,768]{1,0:T(8,128)(2,1)S(1)}) custom-call(s32[3]{0:T(128)S(1)} %pad_add_fusion.before.place, bf16[384,1152]{1,0:T(8,128)(2,1)S(1)} %get-tuple-element.19.before.w_qkv, bf16[2304,384]{1,0:T(8,128)(2,1)S(1)} %pack_weights.3.before.mine, bf16[2304,384]{1,0:T(8,128)(2,1)} %collective-permute-done.1.other), custom_call_target="tpu_custom_call" | custom-call | bytes 7077888 | tf_op jit(solution)/shard_map/join_weights/pallas_call | solution.py:165
  35.7 1.2 copy-done.11
  37.0 4.6 %section.4 = (bf16[2,128,384]{2,1,0:T(8,128)(2,1)S(1)}, bf16[2,128,384]{2,1,0:T(8,128)(2,1)S(1)}) custom-call(bf16[1152,768]{1,0:T(8,128)(2,1)S(1)} %get-tuple-element.20.before.refs_8_.refs_4_, bf16[4,2,64,384]{3,2,1,0:T(8,128)(2,1)S(1)} %copy-done.9, bf16[384,1152]{1,0:T(8,128)(2,1)S(1)} %get-tuple-element.19.before.w_qkv, ...), custom_call_target="tpu_custom_call" | custom-call | flops 5737807872 | bytes 1572864 | tf_op jit(solution)/shard_map/section/pallas_call | solution.py:346
  41.6 5.0 %all-to-all-start.2 = ((bf16[4,2,64,384]{3,2,1,0:T(8,128)(2,1)}), bf16[4,2,64,384]{3,2,1,0:T(8,128)(2,1)S(1)}, u32[]{:S(2)}, u32[]{:S(2)}) async-start(bf16[4,2,64,384]{3,2,1,0:T(8,128)(2,1)} %pack.6.before), calls=%async_computation.2 | async-start | bytes 786432 | tf_op jit(solution)/shard_map/all_to_all | solution.py:399
  47.8 1.3 copy-done.16
  49.1 1.3 copy-done.20
  51.3 5.6 %section.5 = (bf16[2,128,384]{2,1,0:T(8,128)(2,1)S(1)}, bf16[2,128,384]{2,1,0:T(8,128)(2,1)S(1)}) custom-call(bf16[2,128,384]{2,1,0:T(8,128)(2,1)S(1)} %get-tuple-element.24.before.refs_0_, bf16[4,2,64,384]{3,2,1,0:T(8,128)(2,1)} %all-to-all-done.1.arrived, bf16[384,1152]{1,0:T(8,128)(2,1)S(1)} %copy-done.2, bf16[384,384]{1,0:T(8,128)(2,1)S(1)} %copy-done.24, ...), custom_call_target="tpu_custom_call" | custom-call | flops 5737807872 | bytes 1572864 | tf_op jit(solution)/shard_map/section/pallas_call | solution.py:346
  57.0 2.6 %collective-permute-start.5 = (bf16[2,128,384]{2,1,0:T(8,128)(2,1)S(1)}, bf16[2,128,384]{2,1,0:T(8,128)(2,1)}, u32[]{:S(2)}, u32[]{:S(2)}) collective-permute-start(bf16[2,128,384]{2,1,0:T(8,128)(2,1)S(1)} %get-tuple-element.25.before.refs_4_), channel_id=1, source_target_pairs={{1,0},{4,1},{5,4},{8,5},{9,8},{12,9},{13,12},{0,13},{3,2},{6,3},{7... | collective-permute-start | bytes 589832 | tf_op jit(solution)/shard_map/ppermute | solution.py:425
  59.6 2.6 %collective-permute-start.3 = (bf16[2,128,384]{2,1,0:T(8,128)(2,1)S(1)}, bf16[2,128,384]{2,1,0:T(8,128)(2,1)}, u32[]{:S(2)}, u32[]{:S(2)}) collective-permute-start(bf16[2,128,384]{2,1,0:T(8,128)(2,1)S(1)} %get-tuple-element.24.before.refs_0_), channel_id=1, source_target_pairs={{1,0},{4,1},{5,4},{8,5},{9,8},{12,9},{13,12},{0,13},{3,2},{6,3},{7... | collective-permute-start | bytes 589832 | tf_op jit(solution)/shard_map/ppermute | solution.py:425
  62.3 5.1 %all-to-all-start.3 = ((bf16[4,2,64,384]{3,2,1,0:T(8,128)(2,1)}), bf16[4,2,64,384]{3,2,1,0:T(8,128)(2,1)S(1)}, u32[]{:S(2)}, u32[]{:S(2)}) async-start(bf16[4,2,64,384]{3,2,1,0:T(8,128)(2,1)} %pack.7.before), calls=%async_computation.3 | async-start | bytes 786432 | tf_op jit(solution)/shard_map/all_to_all | solution.py:399
  67.4 1.5 copy-done.12
  72.6 6.3 %temporal.3.before = bf16[4,2,2,64,384]{4,3,2,1,0:T(8,128)(2,1)} custom-call(s32[3]{0:T(128)S(1)} %pad_add_fusion.before.place, bf16[2,128,384]{2,1,0:T(8,128)(2,1)S(1)} %copy-done.32, bf16[2,128,384]{2,1,0:T(8,128)(2,1)S(1)} %copy-done.28, bf16[2,128,384]{2,1,0:T(8,128)(2,1)S(1)} %copy-done.30, bf16[2,128,384]{2,1,0:T(8,128)(2,1)} %collective-permute-done.2.refs_2_, ...), custom_call_target="tpu_custom_call" | custom-call | flops 9059696640 | bytes 3145728 | tf_op jit(solution)/shard_map/temporal/pallas_call | solution.py:364
  78.9 5.3 %section.6 = (bf16[2,128,384]{2,1,0:T(8,128)(2,1)}, bf16[2,128,384]{2,1,0:T(8,128)(2,1)}) custom-call(bf16[4,2,2,64,384]{4,3,2,1,0:T(8,128)(2,1)} %temporal.3.before, bf16[4,2,64,384]{3,2,1,0:T(8,128)(2,1)S(1)} %all-to-all-done.2.arrived, bf16[384,1152]{1,0:T(8,128)(2,1)S(1)} %copy-done.3, bf16[384,384]{1,0:T(8,128)(2,1)S(1)} %copy-done.25, ...), custom_call_target="tpu_custom_call" | custom-call | flops 5737807872 | bytes 1572864 | tf_op jit(solution)/shard_map/section/pallas_call | solution.py:346
  84.2 1.8 %collective-permute-start.6 = (bf16[2,128,384]{2,1,0:T(8,128)(2,1)}, bf16[2,128,384]{2,1,0:T(8,128)(2,1)}, u32[]{:S(2)}, u32[]{:S(2)}) collective-permute-start(bf16[2,128,384]{2,1,0:T(8,128)(2,1)} %get-tuple-element.31.refs_1_), channel_id=1, source_target_pairs={{0,1},{1,4},{4,5},{5,8},{8,9},{9,12},{12,13},{13,0},{2,3},{3,6},{6... | collective-permute-start | bytes 589832 | tf_op jit(solution)/shard_map/ppermute | solution.py:424
  86.9 1.3 copy-done.18
  88.1 1.3 copy-done.22
  90.4 4.6 %section.7 = (bf16[2,128,384]{2,1,0:T(8,128)(2,1)S(1)}, bf16[2,128,384]{2,1,0:T(8,128)(2,1)S(1)}) custom-call(bf16[2,128,384]{2,1,0:T(8,128)(2,1)} %get-tuple-element.29.before.refs_0_, bf16[4,2,64,384]{3,2,1,0:T(8,128)(2,1)S(1)} %all-to-all-done.3.arrived, bf16[384,1152]{1,0:T(8,128)(2,1)S(1)} %copy-done.3, bf16[384,384]{1,0:T(8,128)(2,1)S(1)} %copy-done.26, ...), custom_call_target="tpu_custom_call" | custom-call | flops 5737807872 | bytes 1572864 | tf_op jit(solution)/shard_map/section/pallas_call | solution.py:346
  95.7 3.9 %temporal.4.before = bf16[4,2,1,64,384]{4,3,2,1,0:T(8,128)(2,1)S(1)} custom-call(s32[3]{0:T(128)S(1)} %pad_add_fusion.before.place, bf16[2,128,384]{2,1,0:T(8,128)(2,1)S(1)} %get-tuple-element.30.before.refs_0_, bf16[2,128,384]{2,1,0:T(8,128)(2,1)} %get-tuple-element.29.before.refs_0_, bf16[2,128,384]{2,1,0:T(8,128)(2,1)} %get-tuple-element.31.refs_1_, ...), custom_call_target="tpu_custom_call" | custom-call | flops 4529848320 | bytes 1572864 | tf_op jit(solution)/shard_map/temporal/pallas_call | solution.py:364
  99.6 15.8 %all_to_all.36.received = bf16[4,2,1,64,384]{4,3,2,1,0:T(8,128)(2,1)S(1)} all-to-all(bf16[4,2,1,64,384]{4,3,2,1,0:T(8,128)(2,1)S(1)} %temporal.4.before), channel_id=1, replica_groups=mesh['groups'=1,'far'=2,'near'=4,'cell'=2,'sub'=2] {'far','cell'}, dimensions={0} | all-to-all | bytes 786432 | tf_op jit(solution)/shard_map/all_to_all | solution.py:431
  115.4 3.5 %all-to-all-start.4 = ((bf16[4,2,2,64,384]{4,3,2,1,0:T(8,128)(2,1)}), bf16[4,2,2,64,384]{4,3,2,1,0:T(8,128)(2,1)S(1)}, u32[]{:S(2)}, u32[]{:S(2)}) async-start(bf16[4,2,2,64,384]{4,3,2,1,0:T(8,128)(2,1)} %temporal.3.before), calls=%async_computation.4 | async-start | bytes 1572864 | tf_op jit(solution)/shard_map/all_to_all | solution.py:431
  119.0 2.6 %collective-permute-start.9 = (bf16[2,128,384]{2,1,0:T(8,128)(2,1)S(1)}, bf16[2,128,384]{2,1,0:T(8,128)(2,1)S(1)}, u32[]{:S(2)}, u32[]{:S(2)}) collective-permute-start(bf16[2,128,384]{2,1,0:T(8,128)(2,1)S(1)} %copy-done.36), channel_id=1, source_target_pairs={{1,0},{4,1},{5,4},{8,5},{9,8},{12,9},{13,12},{0,13},{3,2},{6,3},{7... | collective-permute-start | bytes 589832 | tf_op jit(solution)/shard_map/ppermute | solution.py:425
  121.6 4.1 %collective-permute-done.8.refs_2_ = bf16[2,128,384]{2,1,0:T(8,128)(2,1)S(1)} collective-permute-done((bf16[2,128,384]{2,1,0:T(8,128)(2,1)}, bf16[2,128,384]{2,1,0:T(8,128)(2,1)S(1)}, u32[]{:S(2)}, u32[]{:S(2)}) %collective-permute-start.8) | collective-permute-done | bytes 196640 | tf_op jit(solution)/shard_map/ppermute | solution.py:424
  125.7 4.3 %collective-permute-done.9.refs_3_ = bf16[2,128,384]{2,1,0:T(8,128)(2,1)S(1)} collective-permute-done((bf16[2,128,384]{2,1,0:T(8,128)(2,1)S(1)}, bf16[2,128,384]{2,1,0:T(8,128)(2,1)S(1)}, u32[]{:S(2)}, u32[]{:S(2)}) %collective-permute-start.9) | collective-permute-done | bytes 196640 | tf_op jit(solution)/shard_map/ppermute | solution.py:425
  130.0 1.5 copy-done.14
  132.4 3.9 %temporal.5.before.buffer = bf16[4,2,1,64,384]{4,3,2,1,0:T(8,128)(2,1)} custom-call(s32[3]{0:T(128)S(1)} %pad_add_fusion.before.place, bf16[4,2,1,64,384]{4,3,2,1,0:T(8,128)(2,1)S(1)} %temporal.4.before, bf16[2,128,384]{2,1,0:T(8,128)(2,1)S(1)} %copy-done.36, bf16[2,128,384]{2,1,0:T(8,128)(2,1)S(1)} %copy-done.38, ...), custom_call_target="tpu_custom_call" | custom-call | flops 4529848320 | bytes 1572864 | tf_op jit(solution)/shard_map/temporal/pallas_call | solution.py:364
  136.6 6.4 %all-to-all-start.6 = ((bf16[4,2,1,64,384]{4,3,2,1,0:T(8,128)(2,1)}), bf16[4,2,1,64,384]{4,3,2,1,0:T(8,128)(2,1)S(1)}, u32[]{:S(2)}, u32[]{:S(2)}) async-start(bf16[4,2,1,64,384]{4,3,2,1,0:T(8,128)(2,1)} %temporal.5.before.buffer), calls=%async_computation.6 | async-start | bytes 786432 | tf_op jit(solution)/shard_map/all_to_all | solution.py:431
  144.8 5.5 %all-to-all-done.6.received = bf16[4,2,1,64,384]{4,3,2,1,0:T(8,128)(2,1)S(1)} async-done(((bf16[4,2,1,64,384]{4,3,2,1,0:T(8,128)(2,1)}), bf16[4,2,1,64,384]{4,3,2,1,0:T(8,128)(2,1)S(1)}, u32[]{:S(2)}, u32[]{:S(2)}) %all-to-all-start.6) | async-done | bytes 393248 | tf_op jit(solution)/shard_map/all_to_all | solution.py:431
  (97 shorter events, 16.6 us)
Async XLA Ops:
  1.7 1.6 %copy-start.4 = (bf16[576,768]{1,0:T(8,128)(2,1)S(1)}, bf16[576,768]{1,0:T(8,128)(2,1)}, u32[]{:S(2)}) copy-start(bf16[576,768]{1,0:T(8,128)(2,1)} %refs_0_.3) | copy-start | bytes 2654212
  1.7 1.6 %copy-start.5 = (bf16[576,768]{1,0:T(8,128)(2,1)S(1)}, bf16[576,768]{1,0:T(8,128)(2,1)}, u32[]{:S(2)}) copy-start(bf16[576,768]{1,0:T(8,128)(2,1)} %refs_1_.3) | copy-start | bytes 2654212
  1.7 29.1 %collective-permute-start = (bf16[2304,384]{1,0:T(8,128)(2,1)S(1)}, bf16[2304,384]{1,0:T(8,128)(2,1)}, u32[]{:S(2)}, u32[]{:S(2)}) collective-permute-start(bf16[2304,384]{1,0:T(8,128)(2,1)S(1)} %pack_weights.2.before.mine), channel_id=1, source_target_pairs={{0,1},{1,0},{2,3},{3,2},{4,5},{5,4},{6,7},{7,6},{8,9},{9,8},{10,11... | collective-permute-start | bytes 5308424 | tf_op jit(solution)/shard_map/ppermute | solution.py:402
  4.0 28.6 %collective-permute-start.1 = (bf16[2304,384]{1,0:T(8,128)(2,1)S(1)}, bf16[2304,384]{1,0:T(8,128)(2,1)}, u32[]{:S(2)}, u32[]{:S(2)}) collective-permute-start(bf16[2304,384]{1,0:T(8,128)(2,1)S(1)} %pack_weights.3.before.mine), channel_id=1, source_target_pairs={{0,1},{1,0},{2,3},{3,2},{4,5},{5,4},{6,7},{7,6},{8,9},{9,8},{10,11... | collective-permute-start | bytes 5308424 | tf_op jit(solution)/shard_map/ppermute | solution.py:402
  23.0 18.5 %all-to-all-start.1 = ((bf16[4,2,64,384]{3,2,1,0:T(8,128)(2,1)}), bf16[4,2,64,384]{3,2,1,0:T(8,128)(2,1)}, u32[]{:S(2)}, u32[]{:S(2)}) async-start(bf16[4,2,64,384]{3,2,1,0:T(8,128)(2,1)} %copy-done), calls=%async_computation.1 | async-start | bytes 786432 | tf_op jit(solution)/shard_map/all_to_all | solution.py:399
  32.6 4.4 %copy-start.1 = (bf16[384,1152]{1,0:T(8,128)(2,1)}, bf16[384,1152]{1,0:T(8,128)(2,1)S(1)}, u32[]{:S(2)}) copy-start(bf16[384,1152]{1,0:T(8,128)(2,1)S(1)} %get-tuple-element.19.before.w_qkv) | copy-start | bytes 2654212
  32.6 4.4 %copy-start.15 = (bf16[384,1536]{1,0:T(8,128)(2,1)}, bf16[384,1536]{1,0:T(8,128)(2,1)S(1)}, u32[]{:S(2)}) copy-start(bf16[384,1536]{1,0:T(8,128)(2,1)S(1)} %get-tuple-element.22.w_up) | copy-start | bytes 3538948
  32.6 4.4 %copy-start.19 = (bf16[1536,384]{1,0:T(8,128)(2,1)}, bf16[1536,384]{1,0:T(8,128)(2,1)S(1)}, u32[]{:S(2)}) copy-start(bf16[1536,384]{1,0:T(8,128)(2,1)S(1)} %get-tuple-element.23.w_down) | copy-start | bytes 3538948
  32.6 4.4 %copy-start.23 = (bf16[384,384]{1,0:T(8,128)(2,1)}, bf16[384,384]{1,0:T(8,128)(2,1)S(1)}, u32[]{:S(2)}) copy-start(bf16[384,384]{1,0:T(8,128)(2,1)S(1)} %get-tuple-element.21.w_out) | copy-start | bytes 884740
  32.6 4.3 %copy-start.9 = (bf16[4,2,64,384]{3,2,1,0:T(8,128)(2,1)S(1)}, bf16[4,2,64,384]{3,2,1,0:T(8,128)(2,1)}, u32[]{:S(2)}) copy-start(bf16[4,2,64,384]{3,2,1,0:T(8,128)(2,1)} %all_to_all.35.arrived) | copy-start | bytes 1179652
  41.6 18.1 %copy-start.29 = (bf16[2,128,384]{2,1,0:T(8,128)(2,1)}, bf16[2,128,384]{2,1,0:T(8,128)(2,1)S(1)}, u32[]{:S(2)}) copy-start(bf16[2,128,384]{2,1,0:T(8,128)(2,1)S(1)} %get-tuple-element.26.refs_1_) | copy-start | bytes 589828
  41.6 18.1 %copy-start.27 = (bf16[2,128,384]{2,1,0:T(8,128)(2,1)}, bf16[2,128,384]{2,1,0:T(8,128)(2,1)S(1)}, u32[]{:S(2)}) copy-start(bf16[2,128,384]{2,1,0:T(8,128)(2,1)S(1)} %get-tuple-element.24.before.refs_0_) | copy-start | bytes 589828
  41.6 20.7 %all-to-all-start.2 = ((bf16[4,2,64,384]{3,2,1,0:T(8,128)(2,1)}), bf16[4,2,64,384]{3,2,1,0:T(8,128)(2,1)S(1)}, u32[]{:S(2)}, u32[]{:S(2)}) async-start(bf16[4,2,64,384]{3,2,1,0:T(8,128)(2,1)} %pack.6.before), calls=%async_computation.2 | async-start | bytes 786432 | tf_op jit(solution)/shard_map/all_to_all | solution.py:399
  56.9 10.5 %copy-start.31 = (bf16[2,128,384]{2,1,0:T(8,128)(2,1)}, bf16[2,128,384]{2,1,0:T(8,128)(2,1)S(1)}, u32[]{:S(2)}) copy-start(bf16[2,128,384]{2,1,0:T(8,128)(2,1)S(1)} %get-tuple-element.25.before.refs_4_) | copy-start | bytes 589828
  56.9 10.5 %copy-start.33 = (bf16[2,128,384]{2,1,0:T(8,128)(2,1)}, bf16[2,128,384]{2,1,0:T(8,128)(2,1)S(1)}, u32[]{:S(2)}) copy-start(bf16[2,128,384]{2,1,0:T(8,128)(2,1)S(1)} %get-tuple-element.27.refs_5_) | copy-start | bytes 589828
  56.9 10.4 %collective-permute-start.4 = (bf16[2,128,384]{2,1,0:T(8,128)(2,1)S(1)}, bf16[2,128,384]{2,1,0:T(8,128)(2,1)}, u32[]{:S(2)}, u32[]{:S(2)}) collective-permute-start(bf16[2,128,384]{2,1,0:T(8,128)(2,1)S(1)} %get-tuple-element.27.refs_5_), channel_id=1, source_target_pairs={{0,1},{1,4},{4,5},{5,8},{8,9},{9,12},{12,13},{13,0},{2,3},{3,6},{6... | collective-permute-start | bytes 589832 | tf_op jit(solution)/shard_map/ppermute | solution.py:424
  57.0 10.4 %collective-permute-start.5 = (bf16[2,128,384]{2,1,0:T(8,128)(2,1)S(1)}, bf16[2,128,384]{2,1,0:T(8,128)(2,1)}, u32[]{:S(2)}, u32[]{:S(2)}) collective-permute-start(bf16[2,128,384]{2,1,0:T(8,128)(2,1)S(1)} %get-tuple-element.25.before.refs_4_), channel_id=1, source_target_pairs={{1,0},{4,1},{5,4},{8,5},{9,8},{12,9},{13,12},{0,13},{3,2},{6,3},{7... | collective-permute-start | bytes 589832 | tf_op jit(solution)/shard_map/ppermute | solution.py:425
  59.6 7.8 %collective-permute-start.2 = (bf16[2,128,384]{2,1,0:T(8,128)(2,1)S(1)}, bf16[2,128,384]{2,1,0:T(8,128)(2,1)}, u32[]{:S(2)}, u32[]{:S(2)}) collective-permute-start(bf16[2,128,384]{2,1,0:T(8,128)(2,1)S(1)} %get-tuple-element.26.refs_1_), channel_id=1, source_target_pairs={{0,1},{1,4},{4,5},{5,8},{8,9},{9,12},{12,13},{13,0},{2,3},{3,6},{6... | collective-permute-start | bytes 589832 | tf_op jit(solution)/shard_map/ppermute | solution.py:424
  59.6 7.8 %collective-permute-start.3 = (bf16[2,128,384]{2,1,0:T(8,128)(2,1)S(1)}, bf16[2,128,384]{2,1,0:T(8,128)(2,1)}, u32[]{:S(2)}, u32[]{:S(2)}) collective-permute-start(bf16[2,128,384]{2,1,0:T(8,128)(2,1)S(1)} %get-tuple-element.24.before.refs_0_), channel_id=1, source_target_pairs={{1,0},{4,1},{5,4},{8,5},{9,8},{12,9},{13,12},{0,13},{3,2},{6,3},{7... | collective-permute-start | bytes 589832 | tf_op jit(solution)/shard_map/ppermute | solution.py:425
  62.3 24.6 %all-to-all-start.3 = ((bf16[4,2,64,384]{3,2,1,0:T(8,128)(2,1)}), bf16[4,2,64,384]{3,2,1,0:T(8,128)(2,1)S(1)}, u32[]{:S(2)}, u32[]{:S(2)}) async-start(bf16[4,2,64,384]{3,2,1,0:T(8,128)(2,1)} %pack.7.before), calls=%async_computation.3 | async-start | bytes 786432 | tf_op jit(solution)/shard_map/all_to_all | solution.py:399
  72.6 6.3 %copy-start.3 = (bf16[384,1152]{1,0:T(8,128)(2,1)S(1)}, bf16[384,1152]{1,0:T(8,128)(2,1)}, u32[]{:S(2)}) copy-start(bf16[384,1152]{1,0:T(8,128)(2,1)} %copy-done.1) | copy-start | bytes 2654212
  72.6 6.3 %copy-start.17 = (bf16[384,1536]{1,0:T(8,128)(2,1)S(1)}, bf16[384,1536]{1,0:T(8,128)(2,1)}, u32[]{:S(2)}) copy-start(bf16[384,1536]{1,0:T(8,128)(2,1)} %copy-done.15) | copy-start | bytes 3538948
  72.6 6.3 %copy-start.21 = (bf16[1536,384]{1,0:T(8,128)(2,1)S(1)}, bf16[1536,384]{1,0:T(8,128)(2,1)}, u32[]{:S(2)}) copy-start(bf16[1536,384]{1,0:T(8,128)(2,1)} %copy-done.19) | copy-start | bytes 3538948
  72.6 6.3 %copy-start.25 = (bf16[384,384]{1,0:T(8,128)(2,1)S(1)}, bf16[384,384]{1,0:T(8,128)(2,1)}, u32[]{:S(2)}) copy-start(bf16[384,384]{1,0:T(8,128)(2,1)} %copy-done.23) | copy-start | bytes 884740
  84.2 10.8 %collective-permute-start.6 = (bf16[2,128,384]{2,1,0:T(8,128)(2,1)}, bf16[2,128,384]{2,1,0:T(8,128)(2,1)}, u32[]{:S(2)}, u32[]{:S(2)}) collective-permute-start(bf16[2,128,384]{2,1,0:T(8,128)(2,1)} %get-tuple-element.31.refs_1_), channel_id=1, source_target_pairs={{0,1},{1,4},{4,5},{5,8},{8,9},{9,12},{12,13},{13,0},{2,3},{3,6},{6... | collective-permute-start | bytes 589832 | tf_op jit(solution)/shard_map/ppermute | solution.py:424
  86.0 9.0 %collective-permute-start.7 = (bf16[2,128,384]{2,1,0:T(8,128)(2,1)}, bf16[2,128,384]{2,1,0:T(8,128)(2,1)}, u32[]{:S(2)}, u32[]{:S(2)}) collective-permute-start(bf16[2,128,384]{2,1,0:T(8,128)(2,1)} %get-tuple-element.29.before.refs_0_), channel_id=1, source_target_pairs={{1,0},{4,1},{5,4},{8,5},{9,8},{12,9},{13,12},{0,13},{3,2},{6,3},{7... | collective-permute-start | bytes 589832 | tf_op jit(solution)/shard_map/ppermute | solution.py:425
  90.4 5.3 %copy-start.13 = (bf16[1152,768]{1,0:T(8,128)(2,1)S(1)}, bf16[1152,768]{1,0:T(8,128)(2,1)}, u32[]{:S(2)}) copy-start(bf16[1152,768]{1,0:T(8,128)(2,1)} %copy-done.11) | copy-start | bytes 5308420
  99.6 19.4 %copy-start.36 = (bf16[2,128,384]{2,1,0:T(8,128)(2,1)S(1)}, bf16[2,128,384]{2,1,0:T(8,128)(2,1)}, u32[]{:S(2)}) copy-start(bf16[2,128,384]{2,1,0:T(8,128)(2,1)} %copy-done.35) | copy-start | bytes 589828
  115.4 21.2 %all-to-all-start.4 = ((bf16[4,2,2,64,384]{4,3,2,1,0:T(8,128)(2,1)}), bf16[4,2,2,64,384]{4,3,2,1,0:T(8,128)(2,1)S(1)}, u32[]{:S(2)}, u32[]{:S(2)}) async-start(bf16[4,2,2,64,384]{4,3,2,1,0:T(8,128)(2,1)} %temporal.3.before), calls=%async_computation.4 | async-start | bytes 1572864 | tf_op jit(solution)/shard_map/all_to_all | solution.py:431
  118.9 6.8 %collective-permute-start.8 = (bf16[2,128,384]{2,1,0:T(8,128)(2,1)}, bf16[2,128,384]{2,1,0:T(8,128)(2,1)S(1)}, u32[]{:S(2)}, u32[]{:S(2)}) collective-permute-start(bf16[2,128,384]{2,1,0:T(8,128)(2,1)} %copy-done.37), channel_id=1, source_target_pairs={{0,1},{1,4},{4,5},{5,8},{8,9},{9,12},{12,13},{13,0},{2,3},{3,6},{6... | collective-permute-start | bytes 589832 | tf_op jit(solution)/shard_map/ppermute | solution.py:424
  119.0 11.1 %collective-permute-start.9 = (bf16[2,128,384]{2,1,0:T(8,128)(2,1)S(1)}, bf16[2,128,384]{2,1,0:T(8,128)(2,1)S(1)}, u32[]{:S(2)}, u32[]{:S(2)}) collective-permute-start(bf16[2,128,384]{2,1,0:T(8,128)(2,1)S(1)} %copy-done.36), channel_id=1, source_target_pairs={{1,0},{4,1},{5,4},{8,5},{9,8},{12,9},{13,12},{0,13},{3,2},{6,3},{7... | collective-permute-start | bytes 589832 | tf_op jit(solution)/shard_map/ppermute | solution.py:425
  136.6 13.7 %all-to-all-start.6 = ((bf16[4,2,1,64,384]{4,3,2,1,0:T(8,128)(2,1)}), bf16[4,2,1,64,384]{4,3,2,1,0:T(8,128)(2,1)S(1)}, u32[]{:S(2)}, u32[]{:S(2)}) async-start(bf16[4,2,1,64,384]{4,3,2,1,0:T(8,128)(2,1)} %temporal.5.before.buffer), calls=%async_computation.6 | async-start | bytes 786432 | tf_op jit(solution)/shard_map/all_to_all | solution.py:431
  (22 other events, 24.8 us)

commit v5 on v3

--- a/solution.py
+++ b/solution.py
@@ -1,3 +1,4 @@
+import functools
 import math
 
 import jax
@@ -10,9 +11,9 @@
 HEAD_DIM = 64
 DILATION_FIRST = 16
 DILATION_SECOND = 256
-CHUNKS = (1, 1, 1, 1)
-ORDER = (("s", 0), ("s", 1), ("t", 0), ("s", 2), ("t", 1), ("s", 3), ("t", 2), ("t", 3))
-VMEM_LIMIT = 24 * 1024 * 1024
+CHUNKS = (2, 2)
+ORDER = (("s", 0), ("s", 1), ("t", 0), ("t", 1))
+MIB = 1024 * 1024
 
 
 def with_halo(block, sides, width):
@@ -115,60 +116,68 @@
 SCALARS = pl.BlockSpec(memory_space=pltpu.SMEM)
 
 
-def params():
-    return pltpu.CompilerParams(vmem_limit_bytes=VMEM_LIMIT)
+def params(mib):
+    return pltpu.CompilerParams(vmem_limit_bytes=mib * MIB)
 
 
 def moved(count):
-    return pl.CostEstimate(flops=0, bytes_accessed=4 * count, transcendentals=0)
-
-
-def pack_weights_kernel(before, *refs):
-    *sources, packed = refs
-    width = packed.shape[1]
-    at = 0
-    for source in sources:
-        rows = source.shape[0]
-        for column in range(0, source.shape[1], width):
-            packed[at : at + rows] = source[:, column : column + width]
-            at += rows
-
-
-def pack_weights(before, weights, width):
-    rows = sum(w.size for w in weights) // width
+    return pl.CostEstimate(flops=0, bytes_accessed=count, transcendentals=0)
+
+
+def pack_weights_kernel(counts, before, *refs):
+    sources, packed = refs[: sum(counts)], refs[sum(counts) :]
+    for count, target in zip(counts, packed):
+        group, sources = sources[:count], sources[count:]
+        width = target.shape[1]
+        at = 0
+        for source in group:
+            rows = source.shape[0]
+            for column in range(0, source.shape[1], width):
+                target[at : at + rows] = source[:, column : column + width]
+                at += rows
+
+
+def pack_weights(before, groups, width):
+    flat = [w for group in groups for w in group]
+    rows = [sum(w.size for w in group) // width for group in groups]
     return pl.pallas_call(
-        pack_weights_kernel,
-        out_shape=jax.ShapeDtypeStruct((rows, width), weights[0].dtype),
-        in_specs=[ANYWHERE] + [RESIDENT] * len(weights),
-        out_specs=RESIDENT,
-        compiler_params=params(),
-        cost_estimate=moved(rows * width),
+        functools.partial(pack_weights_kernel, tuple(len(group) for group in groups)),
+        out_shape=[jax.ShapeDtypeStruct((count, width), flat[0].dtype) for count in rows],
+        in_specs=[ANYWHERE] + [RESIDENT] * len(flat),
+        out_specs=[RESIDENT] * len(groups),
+        compiler_params=params(8),
+        cost_estimate=moved(sum(rows) * width),
         name="pack_weights",
-    )(before, *weights)
-
-
-def join_weights_kernel(place, before, mine, other, *wholes):
-    width = mine.shape[1]
-    for source, index in ((mine, place[0]), (other, 1 - place[0])):
-        at = 0
-        for whole in wholes:
-            rows = whole.shape[0] // 2
-            spot = pl.ds(pl.multiple_of(index * rows, 16), rows)
-            for column in range(0, whole.shape[1], width):
-                whole[spot, column : column + width] = source[at : at + rows]
-                at += rows
-
-
-def join_weights(place, before, mine, other, halves):
+    )(before, *flat)
+
+
+def join_weights_kernel(counts, place, before, *refs):
+    packed, wholes = refs[: 2 * len(counts)], refs[2 * len(counts) :]
+    for index, count in enumerate(counts):
+        group, wholes = wholes[:count], wholes[count:]
+        mine, other = packed[2 * index : 2 * index + 2]
+        width = mine.shape[1]
+        for source, core in ((mine, place[0]), (other, 1 - place[0])):
+            at = 0
+            for whole in group:
+                rows = whole.shape[0] // 2
+                spot = pl.ds(pl.multiple_of(core * rows, 16), rows)
+                for column in range(0, whole.shape[1], width):
+                    whole[spot, column : column + width] = source[at : at + rows]
+                    at += rows
+
+
+def join_weights(place, before, packed, groups):
+    flat = [w for group in groups for w in group]
     return pl.pallas_call(
-        join_weights_kernel,
-        out_shape=[jax.ShapeDtypeStruct((2 * w.shape[0], w.shape[1]), w.dtype) for w in halves],
-        in_specs=[SCALARS, ANYWHERE, RESIDENT, RESIDENT],
-        out_specs=[RESIDENT] * len(halves),
-        compiler_params=params(),
-        cost_estimate=moved(2 * mine.size),
+        functools.partial(join_weights_kernel, tuple(len(group) for group in groups)),
+        out_shape=[jax.ShapeDtypeStruct((2 * w.shape[0], w.shape[1]), w.dtype) for w in flat],
+        in_specs=[SCALARS, ANYWHERE] + [RESIDENT] * (2 * len(groups)),
+        out_specs=[RESIDENT] * len(flat),
+        compiler_params=params(8),
+        cost_estimate=moved(sum(w.size for w in flat)),
         name="join_weights",
-    )(place, before, mine, other)
+    )(place, before, *[half for pair in packed for half in pair])
 
 
 def pack_kernel(place, before, *refs):
@@ -195,7 +204,7 @@
             out_specs=[pl.BlockSpec(shape, lambda i, at: (0, i, 0, 0))] * 3,
         ),
         out_shape=[jax.ShapeDtypeStruct((slots, count, cells, features), grouped.dtype)] * 3,
-        compiler_params=params(),
+        compiler_params=params(4),
         cost_estimate=moved(3 * slots * count * cells * features),
         name="pack",
     )(place, before, grouped, grouped, grouped)
@@ -364,9 +373,9 @@
             out_specs=[block_out, block_out],
         ),
         out_shape=[shape, shape],
-        compiler_params=params(),
+        compiler_params=params(16),
         cost_estimate=pl.CostEstimate(
-            flops=6 * macs, bytes_accessed=8 * tokens * features, transcendentals=tokens * ff
+            flops=macs // 8, bytes_accessed=tokens * features, transcendentals=0
         ),
         name="section",
     )(place, before, grouped, *pieces, *weights)
@@ -387,11 +396,11 @@
             out_specs=[block_out] * 4,
         ),
         out_shape=[shape] * 4,
-        compiler_params=params(),
+        compiler_params=params(16),
         cost_estimate=pl.CostEstimate(
-            flops=60 * tokens * features * features,
-            bytes_accessed=8 * tokens * features,
-            transcendentals=4 * tokens * features,
+            flops=tokens * features * features // 4,
+            bytes_accessed=tokens * features,
+            transcendentals=0,
         ),
         name="temporal",
     )(place, before, even, odd, left_odd, right_even, *weights)
@@ -418,36 +427,33 @@
     def exchange(piece, delta):
         return lax.ppermute(piece, GROUP, [(i, i ^ delta) for i in range(4)])
 
+    pinned = pltpu.with_memory_space_constraint(grouped, pltpu.HBM)
+
     def send(before, index):
-        cut = run_pack(place, before, grouped, begins[index], CHUNKS[index])
+        cut = run_pack(place, before, pinned, begins[index], CHUNKS[index])
         return cut[0], [exchange(piece, delta) for delta, piece in zip((1, 2, 3), cut)]
 
     def swap_core(packed):
-        return lax.ppermute(packed, "sub", [(0, 1), (1, 0)])
+        return packed, lax.ppermute(packed, "sub", [(0, 1), (1, 0)])
 
     section_halves = (w_qkv, w_out, w_up, w_down)
     temporal_halves = (temporal_weight_first, temporal_weight_second)
+    halves = (section_halves, temporal_halves)
     arrived = {}
     before, arrived[0] = send(place, 0)
-    section_mine = pack_weights(before, section_halves, features)
-    section_weights = join_weights(
-        place, before, section_mine, swap_core(section_mine), section_halves
-    )
-    before, arrived[1] = send(section_weights[0], 1)
-    temporal_mine = pack_weights(before, temporal_halves, features)
-    temporal_weights = join_weights(
-        place, before, temporal_mine, swap_core(temporal_mine), temporal_halves
-    )
-    before = temporal_weights[0]
-    for index in range(2, len(CHUNKS)):
+    packed = pack_weights(before, halves, features)
+    before = packed[0]
+    for index in range(1, len(CHUNKS)):
         before, arrived[index] = send(before, index)
+    joined = join_weights(place, before, [swap_core(w) for w in packed], halves)
+    section_weights, temporal_weights = joined[:4], joined[4:]
 
     waiting, outs = {}, {}
-    before = place
+    before = joined[0]
     for kind, index in ORDER:
         if kind == "s":
             even, odd = run_section(
-                place, before, grouped, begins[index], arrived[index], section_weights
+                place, before, pinned, begins[index], arrived[index], section_weights
             )
             left_odd = lax.ppermute(odd, RING, rightward)
             right_even = lax.ppermute(even, RING, leftward)

time: 133 us -> 110 us (0.83); the launches traced: 131 us -> 110 us
  starting transfers between devices: 49.7 us -> 24.7 us
  waiting for transfers between devices: 30 us -> 37.7 us
  local copies, waits for them, and re-layouts: 10.4 us -> 5.64 us
    ppermute x24 -> x12, starting transfers between devices: 39.8 us -> 18.8 us  [exchange(): return lax.ppermute(piece, GROUP, [(i, i ^ delta) for i in range(4)])]
    ppermute x24 -> x12, waiting for transfers between devices: 26.6 us -> 37.7 us  [exchange(): return lax.ppermute(piece, GROUP, [(i, i ^ delta) for i in range(4)])]
    unnamed x46 -> x22, local copies, waits for them, and re-layouts: 9.78 us -> 4.13 us
    ppermute x4 -> x2, starting transfers between devices: 8.73 us -> 5.27 us  [paired(): right_even = lax.ppermute(even, RING, leftward)]
    ppermute x2, waiting for transfers between devices: 3.32 us -> 0.01 us  [swap_core(): return (packed, lax.ppermute(packed, 'sub', [(0, 1), (1, 0)]))]
    pallas_call x4 -> x2, Pallas kernels: 2.95 us -> 1.46 us  [the longest x1 1.15 us: join_weights(): pl.pallas_call(functools.partial(join_weights_kernel, tuple((len(group) f...]
    pallas_call x4 -> x2, Pallas kernels: 12.8 us -> 14 us  [run_temporal(): pl.pallas_call(temporal_kernel, grid_spec=pltpu.PrefetchScalarGridSpec(nu...]
    pallas_call x4 -> x2, Pallas kernels: 3.04 us -> 3.92 us  [run_pack(): pl.pallas_call(pack_kernel, grid_spec=pltpu.PrefetchScalarGridSpec(num_sc...]
  transfers between devices with their start and end apart: 34 -> 18, of which waited for: 11 -> 7; matrix products, arithmetic and copies ran while one was open for 0% -> 1% of each run, Pallas kernels for 29% -> 36%
where the time goes in v5:
time: 110 us
  Pallas kernels  41.7 us (38%)
  waiting for transfers between devices  37.7 us (34%)
  starting transfers between devices  24.7 us (22%)
  local copies, waits for them, and re-layouts  5.64 us (5%)
    ppermute x12, waiting for transfers between devices, exchange(): return lax.ppermute(piece, GROUP, [(i, i ^ delta) for i in range(4)])  37.7 us
    pallas_call x2, Pallas kernels, run_section(): pl.pallas_call(section_kernel, grid_spec=pltpu.PrefetchScalarGridSpec(num...  22.3 us
    ppermute x12, starting transfers between devices, exchange(): return lax.ppermute(piece, GROUP, [(i, i ^ delta) for i in range(4)])  18.8 us
    pallas_call x2, Pallas kernels, run_temporal(): pl.pallas_call(temporal_kernel, grid_spec=pltpu.PrefetchScalarGridSpec(nu...  14 us
    ppermute x2, starting transfers between devices, paired(): right_even = lax.ppermute(even, RING, leftward)  5.27 us
    unnamed x22, local copies, waits for them, and re-layouts  4.13 us
    pallas_call x2, Pallas kernels, run_pack(): pl.pallas_call(pack_kernel, grid_spec=pltpu.PrefetchScalarGridSpec(num_sc...  3.92 us
  transfers between devices with their start and end apart: 18, of which 7 were waited for; matrix products, arithmetic and copies ran while one was open for 1% of the time, Pallas kernels for 36%

profile of v5, /device:TPU:0, one launch (start us, length us, event | category | flops | bytes accessed | tf_op | source)
XLA Modules:
  0.0 109.9 jit_solution(8531582147303176747)
XLA Ops:
  0.1 2.1 %pack.2 = (bf16[2,2,64,384]{3,2,1,0:T(8,128)(2,1)S(1)}, bf16[2,2,64,384]{3,2,1,0:T(8,128)(2,1)S(1)}, bf16[2,2,64,384]{3,2,1,0:T(8,128)(2,1)S(1)}) custom-call(s32[5]{0:T(128)S(1)} %stack.31.place.before, s32[5]{0:T(128)S(1)} %stack.31.place.before, bf16[2,16,64,384]{3,2,1,0:T(8,128)(2,1)} %bitcast.7, bf16[2,16,64,384]{3,2,1,0:T(8,128)(2,1)} %bitcast.8, ...), custom_call_target="tpu_custom_call" | custom-call | bytes 294912 | tf_op jit(solution)/shard_map/pack/pallas_call | solution.py:198
  3.2 2.9 %collective-permute-start.2 = (bf16[2,2,64,384]{3,2,1,0:T(8,128)(2,1)S(1)}, bf16[2,2,64,384]{3,2,1,0:T(8,128)(2,1)S(1)}, u32[]{:S(2)}, u32[]{:S(2)}) collective-permute-start(bf16[2,2,64,384]{3,2,1,0:T(8,128)(2,1)S(1)} %get-tuple-element.31.before), channel_id=1, source_target_pairs={{0,2},{2,0},{16,18},{18,16},{1,3},{3,1},{17,19},{19,17},{4,6},{6,4... | collective-permute-start | bytes 589832 | tf_op jit(solution)/shard_map/ppermute | solution.py:428
  6.1 2.6 %collective-permute-start.3 = (bf16[2,2,64,384]{3,2,1,0:T(8,128)(2,1)S(1)}, bf16[2,2,64,384]{3,2,1,0:T(8,128)(2,1)S(1)}, u32[]{:S(2)}, u32[]{:S(2)}) collective-permute-start(bf16[2,2,64,384]{3,2,1,0:T(8,128)(2,1)S(1)} %get-tuple-element.36), channel_id=1, source_target_pairs={{0,16},{2,18},{16,0},{18,2},{1,17},{3,19},{17,1},{19,3},{4,20},{6,... | collective-permute-start | bytes 589832 | tf_op jit(solution)/shard_map/ppermute | solution.py:428
  8.7 1.8 %pack.3 = (bf16[2,2,64,384]{3,2,1,0:T(8,128)(2,1)S(1)}, bf16[2,2,64,384]{3,2,1,0:T(8,128)(2,1)S(1)}, bf16[2,2,64,384]{3,2,1,0:T(8,128)(2,1)S(1)}) custom-call(s32[5]{0:T(128)S(1)} %stack.31.place.before, bf16[2304,384]{1,0:T(8,128)(2,1)S(1)} %get-tuple-element.32.before.refs_0_, bf16[2,16,64,384]{3,2,1,0:T(8,128)(2,1)} %bitcast.10, ...), custom_call_target="tpu_custom_call" | custom-call | bytes 294912 | tf_op jit(solution)/shard_map/pack/pallas_call | solution.py:198
  10.5 0.7 collective-permute-done.2.near_cells
  11.3 1.7 %collective-permute-start.5 = (bf16[2,2,64,384]{3,2,1,0:T(8,128)(2,1)S(1)}, bf16[2,2,64,384]{3,2,1,0:T(8,128)(2,1)S(1)}, u32[]{:S(2)}, u32[]{:S(2)}) collective-permute-start(bf16[2,2,64,384]{3,2,1,0:T(8,128)(2,1)S(1)} %get-tuple-element.33.before), channel_id=1, source_target_pairs={{0,2},{2,0},{16,18},{18,16},{1,3},{3,1},{17,19},{19,17},{4,6},{6,4... | collective-permute-start | bytes 589832 | tf_op jit(solution)/shard_map/ppermute | solution.py:428
  13.0 2.6 %collective-permute-start.6 = (bf16[2,2,64,384]{3,2,1,0:T(8,128)(2,1)S(1)}, bf16[2,2,64,384]{3,2,1,0:T(8,128)(2,1)S(1)}, u32[]{:S(2)}, u32[]{:S(2)}) collective-permute-start(bf16[2,2,64,384]{3,2,1,0:T(8,128)(2,1)S(1)} %get-tuple-element.42), channel_id=1, source_target_pairs={{0,16},{2,18},{16,0},{18,2},{1,17},{3,19},{17,1},{19,3},{4,20},{6,... | collective-permute-start | bytes 589832 | tf_op jit(solution)/shard_map/ppermute | solution.py:428
  15.7 1.2 %join_weights.1 = (bf16[384,1152]{1,0:T(8,128)(2,1)S(1)}, bf16[384,384]{1,0:T(8,128)(2,1)S(1)}, bf16[384,1536]{1,0:T(8,128)(2,1)S(1)}, bf16[1536,384]{1,0:T(8,12...) custom-call(s32[5]{0:T(128)S(1)} %stack.31.place.before, ...), custom_call_target="tpu_custom_call" | custom-call | bytes 1769472 | tf_op jit(solution)/shard_map/join_weights/pallas_call | solution.py:172
  16.8 14.8 %collective-permute-done.3.far_own = bf16[2,2,64,384]{3,2,1,0:T(8,128)(2,1)S(1)} collective-permute-done((bf16[2,2,64,384]{3,2,1,0:T(8,128)(2,1)S(1)}, bf16[2,2,64,384]{3,2,1,0:T(8,128)(2,1)S(1)}, u32[]{:S(2)}, u32[]{:S(2)}) %collective-permute-start.3) | collective-permute-done | bytes 196640 | tf_op jit(solution)/shard_map/ppermute | solution.py:428
  31.6 3.9 %collective-permute-done.4.far_cells = bf16[2,2,64,384]{3,2,1,0:T(8,128)(2,1)S(1)} collective-permute-done((bf16[2,2,64,384]{3,2,1,0:T(8,128)(2,1)S(1)}, bf16[2,2,64,384]{3,2,1,0:T(8,128)(2,1)S(1)}, u32[]{:S(2)}, u32[]{:S(2)}) %collective-permute-start.4) | collective-permute-done | bytes 196640 | tf_op jit(solution)/shard_map/ppermute | solution.py:428
  35.5 10.8 %section.2 = (bf16[2,2,128,384]{3,2,1,0:T(8,128)(2,1)S(1)}, bf16[2,2,128,384]{3,2,1,0:T(8,128)(2,1)S(1)}) custom-call(s32[5]{0:T(128)S(1)} %stack.31.place.before, bf16[384,1152]{1,0:T(8,128)(2,1)S(1)} %get-tuple-element.35.before.w_qkv, bf16[2,16,64,384]{3,2,1,0:T(8,128)(2,1)} %bitcast.13, bf16[2,2,64,384]{3,2,1,0:T(8,128)(2,1)S(1)} %collective-permute-done.2.near_cells, ...), custom_call_target="tpu_custom_call" | custom-call | flops 239075328 | bytes 393216 | tf_op jit(solution)/shard_map/section/pallas_call | solution.py:367
  46.4 2.6 %collective-permute-start.9 = (bf16[2,2,128,384]{3,2,1,0:T(8,128)(2,1)S(1)}, bf16[2,2,128,384]{3,2,1,0:T(8,128)(2,1)S(1)}, u32[]{:S(2)}, u32[]{:S(2)}) collective-permute-start(bf16[2,2,128,384]{3,2,1,0:T(8,128)(2,1)S(1)} %get-tuple-element.41.before.even), channel_id=1, source_target_pairs={{1,0},{4,1},{5,4},{8,5},{9,8},{12,9},{13,12},{0,13},{3,2},{6,3},{7... | collective-permute-start | bytes 1179656 | tf_op jit(solution)/shard_map/ppermute | solution.py:459
  49.0 11.5 %section.3 = (bf16[2,2,128,384]{3,2,1,0:T(8,128)(2,1)}, bf16[2,2,128,384]{3,2,1,0:T(8,128)(2,1)}) custom-call(s32[5]{0:T(128)S(1)} %stack.31.place.before, bf16[2,2,128,384]{3,2,1,0:T(8,128)(2,1)S(1)} %get-tuple-element.41.before.even, bf16[2,16,64,384]{3,2,1,0:T(8,128)(2,1)} %bitcast.14, bf16[2,2,64,384]{3,2,1,0:T(8,128)(2,1)S(1)} %collective-permute-done.5.near_cells, ...), custom_call_target="tpu_custom_call" | custom-call | flops 239075328 | bytes 393216 | tf_op jit(solution)/shard_map/section/pallas_call | solution.py:367
  60.5 2.6 %collective-permute-start.14 = (bf16[2,2,128,384]{3,2,1,0:T(8,128)(2,1)}, bf16[2,2,128,384]{3,2,1,0:T(8,128)(2,1)}, u32[]{:S(2)}, u32[]{:S(2)}) collective-permute-start(bf16[2,2,128,384]{3,2,1,0:T(8,128)(2,1)} %get-tuple-element.44.before.even), channel_id=1, source_target_pairs={{1,0},{4,1},{5,4},{8,5},{9,8},{12,9},{13,12},{0,13},{3,2},{6,3},{7... | collective-permute-start | bytes 1179656 | tf_op jit(solution)/shard_map/ppermute | solution.py:459
  63.1 6.8 %temporal.2 = (bf16[2,2,64,384]{3,2,1,0:T(8,128)(2,1)S(1)}, bf16[2,2,64,384]{3,2,1,0:T(8,128)(2,1)}, bf16[2,2,64,384]{3,2,1,0:T(8,128)(2,1)S(1)}, bf16[2,2,64,384]{3,2,1,0:T(8,128)(2,1)S(1)}) custom-call(s32[5]{0:T(128)S(1)} %stack.31.place.before, bf16[2,2,128,384]{3,2,1,0:T(8,128)(2,1)} %get-tuple-element.44.before.even, ...), custom_call_target="tpu_custom_call" | custom-call | flops 37748736 | bytes 393216 | tf_op jit(solution)/shard_map/temporal/pallas_call | solution.py:390
  69.9 0.7 copy-done.2
  70.6 0.7 copy-done.8
  71.3 0.7 copy-done.9
  72.0 1.8 %collective-permute-start.10 = (bf16[2,2,64,384]{3,2,1,0:T(8,128)(2,1)}, bf16[2,2,64,384]{3,2,1,0:T(8,128)(2,1)}, u32[]{:S(2)}, u32[]{:S(2)}) collective-permute-start(bf16[2,2,64,384]{3,2,1,0:T(8,128)(2,1)} %get-tuple-element.49), channel_id=1, source_target_pairs={{0,2},{2,0},{16,18},{18,16},{1,3},{3,1},{17,19},{19,17},{4,6},{6,4... | collective-permute-start | bytes 589832 | tf_op jit(solution)/shard_map/ppermute | solution.py:428
  73.8 0.9 collective-permute-start.11
  74.7 1.7 %collective-permute-start.12 = (bf16[2,2,64,384]{3,2,1,0:T(8,128)(2,1)}, bf16[2,2,64,384]{3,2,1,0:T(8,128)(2,1)S(1)}, u32[]{:S(2)}, u32[]{:S(2)}) collective-permute-start(bf16[2,2,64,384]{3,2,1,0:T(8,128)(2,1)} %copy-done.8), channel_id=1, source_target_pairs={{0,18},{2,16},{16,2},{18,0},{1,19},{3,17},{17,3},{19,1},{4,22},{6,... | collective-permute-start | bytes 589832 | tf_op jit(solution)/shard_map/ppermute | solution.py:428
  76.4 0.9 copy-done.3
  77.3 7.2 %temporal.3 = (bf16[2,2,64,384]{3,2,1,0:T(8,128)(2,1)S(1)}, bf16[2,2,64,384]{3,2,1,0:T(8,128)(2,1)S(1)}, bf16[2,2,64,384]{3,2,1,0:T(8,128)(2,1)S(1)}, bf16[2,2,64,384]{3,2,1,0:T(8,128)(2,1)S(1)}) custom-call(s32[5]{0:T(128)S(1)} %stack.31.place.before, bf16[2,2,64,384]{3,2,1,0:T(8,128)(2,1)S(1)} %copy-done.3, ...), custom_call_target="tpu_custom_call" | custom-call | flops 37748736 | bytes 393216 | tf_op jit(solution)/shard_map/temporal/pallas_call | solution.py:390
  84.5 1.9 %collective-permute-start.15 = (bf16[2,2,64,384]{3,2,1,0:T(8,128)(2,1)S(1)}, bf16[2,2,64,384]{3,2,1,0:T(8,128)(2,1)S(1)}, u32[]{:S(2)}, u32[]{:S(2)}) collective-permute-start(bf16[2,2,64,384]{3,2,1,0:T(8,128)(2,1)S(1)} %get-tuple-element.54), channel_id=1, source_target_pairs={{0,2},{2,0},{16,18},{18,16},{1,3},{3,1},{17,19},{19,17},{4,6},{6,4... | collective-permute-start | bytes 589832 | tf_op jit(solution)/shard_map/ppermute | solution.py:428
  86.4 0.9 collective-permute-start.16
  87.6 1.7 %collective-permute-start.17 = (bf16[2,2,64,384]{3,2,1,0:T(8,128)(2,1)S(1)}, bf16[2,2,64,384]{3,2,1,0:T(8,128)(2,1)S(1)}, u32[]{:S(2)}, u32[]{:S(2)}) collective-permute-start(bf16[2,2,64,384]{3,2,1,0:T(8,128)(2,1)S(1)} %get-tuple-element.56), channel_id=1, source_target_pairs={{0,18},{2,16},{16,2},{18,0},{1,19},{3,17},{17,3},{19,1},{4,22},{6,... | collective-permute-start | bytes 589832 | tf_op jit(solution)/shard_map/ppermute | solution.py:428
  89.3 1.0 constant_dynamic-update-slice_fusion.6
  90.3 6.1 %collective-permute-done.11 = bf16[2,2,64,384]{3,2,1,0:T(8,128)(2,1)S(1)} collective-permute-done((bf16[2,2,64,384]{3,2,1,0:T(8,128)(2,1)}, bf16[2,2,64,384]{3,2,1,0:T(8,128)(2,1)S(1)}, u32[]{:S(2)}, u32[]{:S(2)}) %collective-permute-start.11) | collective-permute-done | bytes 196640 | tf_op jit(solution)/shard_map/ppermute | solution.py:428
  96.4 4.8 %collective-permute-done.12 = bf16[2,2,64,384]{3,2,1,0:T(8,128)(2,1)S(1)} collective-permute-done((bf16[2,2,64,384]{3,2,1,0:T(8,128)(2,1)}, bf16[2,2,64,384]{3,2,1,0:T(8,128)(2,1)S(1)}, u32[]{:S(2)}, u32[]{:S(2)}) %collective-permute-start.12) | collective-permute-done | bytes 196640 | tf_op jit(solution)/shard_map/ppermute | solution.py:428
  101.4 3.4 %collective-permute-done.16 = bf16[2,2,64,384]{3,2,1,0:T(8,128)(2,1)S(1)} collective-permute-done((bf16[2,2,64,384]{3,2,1,0:T(8,128)(2,1)S(1)}, bf16[2,2,64,384]{3,2,1,0:T(8,128)(2,1)S(1)}, u32[]{:S(2)}, u32[]{:S(2)}) %collective-permute-start.16) | collective-permute-done | bytes 196640 | tf_op jit(solution)/shard_map/ppermute | solution.py:428
  104.8 3.9 %collective-permute-done.17 = bf16[2,2,64,384]{3,2,1,0:T(8,128)(2,1)S(1)} collective-permute-done((bf16[2,2,64,384]{3,2,1,0:T(8,128)(2,1)S(1)}, bf16[2,2,64,384]{3,2,1,0:T(8,128)(2,1)S(1)}, u32[]{:S(2)}, u32[]{:S(2)}) %collective-permute-start.17) | collective-permute-done | bytes 196640 | tf_op jit(solution)/shard_map/ppermute | solution.py:428
  108.8 1.1 %copy-done.10 = bf16[2,16,64,384]{3,2,1,0:T(8,128)(2,1)} copy-done((bf16[2,16,64,384]{3,2,1,0:T(8,128)(2,1)}, bf16[2,16,64,384]{3,2,1,0:T(8,128)(2,1)S(1)}, u32[]{:S(2)}) %copy-start.10) | copy-done | bytes 1572888
  (44 shorter events, 1.6 us)
Async XLA Ops:
  0.1 2.2 %copy-start = (bf16[576,768]{1,0:T(8,128)(2,1)S(1)}, bf16[576,768]{1,0:T(8,128)(2,1)}, u32[]{:S(2)}) copy-start(bf16[576,768]{1,0:T(8,128)(2,1)} %refs_4_.1) | copy-start | bytes 2654212
  0.1 2.2 %copy-start.1 = (bf16[576,768]{1,0:T(8,128)(2,1)S(1)}, bf16[576,768]{1,0:T(8,128)(2,1)}, u32[]{:S(2)}) copy-start(bf16[576,768]{1,0:T(8,128)(2,1)} %refs_5_.1) | copy-start | bytes 2654212
  0.1 2.2 %copy-start.4 = (bf16[192,1536]{1,0:T(8,128)(2,1)S(1)}, bf16[192,1536]{1,0:T(8,128)(2,1)}, u32[]{:S(2)}) copy-start(bf16[192,1536]{1,0:T(8,128)(2,1)} %refs_2_.1) | copy-start | bytes 1769476
  0.1 2.2 %copy-start.5 = (bf16[768,384]{1,0:T(8,128)(2,1)S(1)}, bf16[768,384]{1,0:T(8,128)(2,1)}, u32[]{:S(2)}) copy-start(bf16[768,384]{1,0:T(8,128)(2,1)} %refs_3_.1) | copy-start | bytes 1769476
  0.1 2.2 %copy-start.6 = (bf16[192,1152]{1,0:T(8,128)(2,1)S(1)}, bf16[192,1152]{1,0:T(8,128)(2,1)}, u32[]{:S(2)}) copy-start(bf16[192,1152]{1,0:T(8,128)(2,1)} %refs_0_.1) | copy-start | bytes 1327108
  0.1 2.2 %copy-start.7 = (bf16[192,384]{1,0:T(8,128)(2,1)S(1)}, bf16[192,384]{1,0:T(8,128)(2,1)}, u32[]{:S(2)}) copy-start(bf16[192,384]{1,0:T(8,128)(2,1)} %refs_1_.1) | copy-start | bytes 442372
  2.6 10.4 %collective-permute-start = (bf16[2304,384]{1,0:T(8,128)(2,1)S(1)}, bf16[2304,384]{1,0:T(8,128)(2,1)S(1)}, u32[]{:S(2)}, u32[]{:S(2)}) collective-permute-start(bf16[2304,384]{1,0:T(8,128)(2,1)S(1)} %get-tuple-element.32.before.refs_0_), channel_id=1, source_target_pairs={{0,1},{1,0},{2,3},{3,2},{4,5},{5,4},{6,7},{7,6},{8,9},{9,8},{10,11... | collective-permute-start | bytes 5308424 | tf_op jit(solution)/shard_map/ppermute | solution.py:437
  3.1 12.5 %collective-permute-start.1 = (bf16[2304,384]{1,0:T(8,128)(2,1)S(1)}, bf16[2304,384]{1,0:T(8,128)(2,1)S(1)}, u32[]{:S(2)}, u32[]{:S(2)}) collective-permute-start(bf16[2304,384]{1,0:T(8,128)(2,1)S(1)} %get-tuple-element.34.refs_2_), channel_id=1, source_target_pairs={{0,1},{1,0},{2,3},{3,2},{4,5},{5,4},{6,7},{7,6},{8,9},{9,8},{10,11... | collective-permute-start | bytes 5308424 | tf_op jit(solution)/shard_map/ppermute | solution.py:437
  3.2 8.1 %collective-permute-start.2 = (bf16[2,2,64,384]{3,2,1,0:T(8,128)(2,1)S(1)}, bf16[2,2,64,384]{3,2,1,0:T(8,128)(2,1)S(1)}, u32[]{:S(2)}, u32[]{:S(2)}) collective-permute-start(bf16[2,2,64,384]{3,2,1,0:T(8,128)(2,1)S(1)} %get-tuple-element.31.before), channel_id=1, source_target_pairs={{0,2},{2,0},{16,18},{18,16},{1,3},{3,1},{17,19},{19,17},{4,6},{6,4... | collective-permute-start | bytes 589832 | tf_op jit(solution)/shard_map/ppermute | solution.py:428
  6.1 25.5 %collective-permute-start.3 = (bf16[2,2,64,384]{3,2,1,0:T(8,128)(2,1)S(1)}, bf16[2,2,64,384]{3,2,1,0:T(8,128)(2,1)S(1)}, u32[]{:S(2)}, u32[]{:S(2)}) collective-permute-start(bf16[2,2,64,384]{3,2,1,0:T(8,128)(2,1)S(1)} %get-tuple-element.36), channel_id=1, source_target_pairs={{0,16},{2,18},{16,0},{18,2},{1,17},{3,19},{17,1},{19,3},{4,20},{6,... | collective-permute-start | bytes 589832 | tf_op jit(solution)/shard_map/ppermute | solution.py:428
  8.7 26.8 %collective-permute-start.4 = (bf16[2,2,64,384]{3,2,1,0:T(8,128)(2,1)S(1)}, bf16[2,2,64,384]{3,2,1,0:T(8,128)(2,1)S(1)}, u32[]{:S(2)}, u32[]{:S(2)}) collective-permute-start(bf16[2,2,64,384]{3,2,1,0:T(8,128)(2,1)S(1)} %get-tuple-element.37), channel_id=1, source_target_pairs={{0,18},{2,16},{16,2},{18,0},{1,19},{3,17},{17,3},{19,1},{4,22},{6,... | collective-permute-start | bytes 589832 | tf_op jit(solution)/shard_map/ppermute | solution.py:428
  11.3 37.7 %collective-permute-start.5 = (bf16[2,2,64,384]{3,2,1,0:T(8,128)(2,1)S(1)}, bf16[2,2,64,384]{3,2,1,0:T(8,128)(2,1)S(1)}, u32[]{:S(2)}, u32[]{:S(2)}) collective-permute-start(bf16[2,2,64,384]{3,2,1,0:T(8,128)(2,1)S(1)} %get-tuple-element.33.before), channel_id=1, source_target_pairs={{0,2},{2,0},{16,18},{18,16},{1,3},{3,1},{17,19},{19,17},{4,6},{6,4... | collective-permute-start | bytes 589832 | tf_op jit(solution)/shard_map/ppermute | solution.py:428
  13.0 36.0 %collective-permute-start.6 = (bf16[2,2,64,384]{3,2,1,0:T(8,128)(2,1)S(1)}, bf16[2,2,64,384]{3,2,1,0:T(8,128)(2,1)S(1)}, u32[]{:S(2)}, u32[]{:S(2)}) collective-permute-start(bf16[2,2,64,384]{3,2,1,0:T(8,128)(2,1)S(1)} %get-tuple-element.42), channel_id=1, source_target_pairs={{0,16},{2,18},{16,0},{18,2},{1,17},{3,19},{17,1},{19,3},{4,20},{6,... | collective-permute-start | bytes 589832 | tf_op jit(solution)/shard_map/ppermute | solution.py:428
  15.6 33.4 %collective-permute-start.7 = (bf16[2,2,64,384]{3,2,1,0:T(8,128)(2,1)S(1)}, bf16[2,2,64,384]{3,2,1,0:T(8,128)(2,1)S(1)}, u32[]{:S(2)}, u32[]{:S(2)}) collective-permute-start(bf16[2,2,64,384]{3,2,1,0:T(8,128)(2,1)S(1)} %get-tuple-element.43), channel_id=1, source_target_pairs={{0,18},{2,16},{16,2},{18,0},{1,19},{3,17},{17,3},{19,1},{4,22},{6,... | collective-permute-start | bytes 589832 | tf_op jit(solution)/shard_map/ppermute | solution.py:428
  46.3 16.9 %collective-permute-start.8 = (bf16[2,2,128,384]{3,2,1,0:T(8,128)(2,1)S(1)}, bf16[2,2,128,384]{3,2,1,0:T(8,128)(2,1)S(1)}, u32[]{:S(2)}, u32[]{:S(2)}) collective-permute-start(bf16[2,2,128,384]{3,2,1,0:T(8,128)(2,1)S(1)} %get-tuple-element.45.odd), channel_id=1, source_target_pairs={{0,1},{1,4},{4,5},{5,8},{8,9},{9,12},{12,13},{13,0},{2,3},{3,6},{6... | collective-permute-start | bytes 1179656 | tf_op jit(solution)/shard_map/ppermute | solution.py:458
  46.4 16.8 %collective-permute-start.9 = (bf16[2,2,128,384]{3,2,1,0:T(8,128)(2,1)S(1)}, bf16[2,2,128,384]{3,2,1,0:T(8,128)(2,1)S(1)}, u32[]{:S(2)}, u32[]{:S(2)}) collective-permute-start(bf16[2,2,128,384]{3,2,1,0:T(8,128)(2,1)S(1)} %get-tuple-element.41.before.even), channel_id=1, source_target_pairs={{1,0},{4,1},{5,4},{8,5},{9,8},{12,9},{13,12},{0,13},{3,2},{6,3},{7... | collective-permute-start | bytes 1179656 | tf_op jit(solution)/shard_map/ppermute | solution.py:459
  60.5 15.9 %collective-permute-start.13 = (bf16[2,2,128,384]{3,2,1,0:T(8,128)(2,1)}, bf16[2,2,128,384]{3,2,1,0:T(8,128)(2,1)}, u32[]{:S(2)}, u32[]{:S(2)}) collective-permute-start(bf16[2,2,128,384]{3,2,1,0:T(8,128)(2,1)} %get-tuple-element.52.odd), channel_id=1, source_target_pairs={{0,1},{1,4},{4,5},{5,8},{8,9},{9,12},{12,13},{13,0},{2,3},{3,6},{6... | collective-permute-start | bytes 1179656 | tf_op jit(solution)/shard_map/ppermute | solution.py:458
  60.5 15.9 %collective-permute-start.14 = (bf16[2,2,128,384]{3,2,1,0:T(8,128)(2,1)}, bf16[2,2,128,384]{3,2,1,0:T(8,128)(2,1)}, u32[]{:S(2)}, u32[]{:S(2)}) collective-permute-start(bf16[2,2,128,384]{3,2,1,0:T(8,128)(2,1)} %get-tuple-element.44.before.even), channel_id=1, source_target_pairs={{1,0},{4,1},{5,4},{8,5},{9,8},{12,9},{13,12},{0,13},{3,2},{6,3},{7... | collective-permute-start | bytes 1179656 | tf_op jit(solution)/shard_map/ppermute | solution.py:459
  69.9 0.7 copy-start.2
  70.6 0.7 copy-start.8
  71.3 0.7 copy-start.9
  72.0 15.6 %collective-permute-start.10 = (bf16[2,2,64,384]{3,2,1,0:T(8,128)(2,1)}, bf16[2,2,64,384]{3,2,1,0:T(8,128)(2,1)}, u32[]{:S(2)}, u32[]{:S(2)}) collective-permute-start(bf16[2,2,64,384]{3,2,1,0:T(8,128)(2,1)} %get-tuple-element.49), channel_id=1, source_target_pairs={{0,2},{2,0},{16,18},{18,16},{1,3},{3,1},{17,19},{19,17},{4,6},{6,4... | collective-permute-start | bytes 589832 | tf_op jit(solution)/shard_map/ppermute | solution.py:428
  73.8 22.6 %collective-permute-start.11 = (bf16[2,2,64,384]{3,2,1,0:T(8,128)(2,1)}, bf16[2,2,64,384]{3,2,1,0:T(8,128)(2,1)S(1)}, u32[]{:S(2)}, u32[]{:S(2)}) collective-permute-start(bf16[2,2,64,384]{3,2,1,0:T(8,128)(2,1)} %copy-done.9), channel_id=1, source_target_pairs={{0,16},{2,18},{16,0},{18,2},{1,17},{3,19},{17,1},{19,3},{4,20},{6,... | collective-permute-start | bytes 589832 | tf_op jit(solution)/shard_map/ppermute | solution.py:428
  74.7 26.6 %collective-permute-start.12 = (bf16[2,2,64,384]{3,2,1,0:T(8,128)(2,1)}, bf16[2,2,64,384]{3,2,1,0:T(8,128)(2,1)S(1)}, u32[]{:S(2)}, u32[]{:S(2)}) collective-permute-start(bf16[2,2,64,384]{3,2,1,0:T(8,128)(2,1)} %copy-done.8), channel_id=1, source_target_pairs={{0,18},{2,16},{16,2},{18,0},{1,19},{3,17},{17,3},{19,1},{4,22},{6,... | collective-permute-start | bytes 589832 | tf_op jit(solution)/shard_map/ppermute | solution.py:428
  76.4 0.9 copy-start.3
  84.5 16.8 %collective-permute-start.15 = (bf16[2,2,64,384]{3,2,1,0:T(8,128)(2,1)S(1)}, bf16[2,2,64,384]{3,2,1,0:T(8,128)(2,1)S(1)}, u32[]{:S(2)}, u32[]{:S(2)}) collective-permute-start(bf16[2,2,64,384]{3,2,1,0:T(8,128)(2,1)S(1)} %get-tuple-element.54), channel_id=1, source_target_pairs={{0,2},{2,0},{16,18},{18,16},{1,3},{3,1},{17,19},{19,17},{4,6},{6,4... | collective-permute-start | bytes 589832 | tf_op jit(solution)/shard_map/ppermute | solution.py:428
  86.4 18.4 %collective-permute-start.16 = (bf16[2,2,64,384]{3,2,1,0:T(8,128)(2,1)S(1)}, bf16[2,2,64,384]{3,2,1,0:T(8,128)(2,1)S(1)}, u32[]{:S(2)}, u32[]{:S(2)}) collective-permute-start(bf16[2,2,64,384]{3,2,1,0:T(8,128)(2,1)S(1)} %get-tuple-element.55), channel_id=1, source_target_pairs={{0,16},{2,18},{16,0},{18,2},{1,17},{3,19},{17,1},{19,3},{4,20},{6,... | collective-permute-start | bytes 589832 | tf_op jit(solution)/shard_map/ppermute | solution.py:428
  87.6 21.2 %collective-permute-start.17 = (bf16[2,2,64,384]{3,2,1,0:T(8,128)(2,1)S(1)}, bf16[2,2,64,384]{3,2,1,0:T(8,128)(2,1)S(1)}, u32[]{:S(2)}, u32[]{:S(2)}) collective-permute-start(bf16[2,2,64,384]{3,2,1,0:T(8,128)(2,1)S(1)} %get-tuple-element.56), channel_id=1, source_target_pairs={{0,18},{2,16},{16,2},{18,0},{1,19},{3,17},{17,3},{19,1},{4,22},{6,... | collective-permute-start | bytes 589832 | tf_op jit(solution)/shard_map/ppermute | solution.py:428
  108.8 1.1 %copy-start.10 = (bf16[2,16,64,384]{3,2,1,0:T(8,128)(2,1)}, bf16[2,16,64,384]{3,2,1,0:T(8,128)(2,1)S(1)}, u32[]{:S(2)}) copy-start(bf16[2,16,64,384]{3,2,1,0:T(8,128)(2,1)S(1)} %constant_dynamic-update-slice_fusion) | copy-start | bytes 4718596

commit v6 on v5

--- a/solution.py
+++ b/solution.py
@@ -188,23 +188,21 @@
 
 def run_pack(place, before, grouped, begin, count):
     slots, _, cells, features = grouped.shape
-    shape = (slots, 1, cells, features)
+    shape = (slots, count, cells, features)
 
     def source(delta):
-        return pl.BlockSpec(
-            shape, lambda i, at: (0, begin + (at[4] ^ delta) * count + i, 0, 0)
-        )
+        return pl.BlockSpec(shape, lambda i, at: (0, begin // count + (at[4] ^ delta), 0, 0))
 
     return pl.pallas_call(
         pack_kernel,
         grid_spec=pltpu.PrefetchScalarGridSpec(
             num_scalar_prefetch=1,
-            grid=(count,),
+            grid=(1,),
             in_specs=[ANYWHERE] + [source(delta) for delta in (1, 2, 3)],
-            out_specs=[pl.BlockSpec(shape, lambda i, at: (0, i, 0, 0))] * 3,
+            out_specs=[pl.BlockSpec(shape, lambda i, at: (0, 0, 0, 0))] * 3,
         ),
         out_shape=[jax.ShapeDtypeStruct((slots, count, cells, features), grouped.dtype)] * 3,
-        compiler_params=params(4),
+        compiler_params=params(6),
         cost_estimate=moved(3 * slots * count * cells * features),
         name="pack",
     )(place, before, grouped, grouped, grouped)
@@ -267,7 +265,8 @@
             mixed = jnp.dot(
                 jnp.concatenate(terms, axis=1), split_values, preferred_element_type=jnp.float32
             )
-            columns.append((mixed[:, :pair_width] / mixed[:, pair_width:]).astype(jnp.bfloat16))
+            inverse = pl.reciprocal(mixed[:, pair_width:], approx=True)
+            columns.append((mixed[:, :pair_width] * inverse).astype(jnp.bfloat16))
         rows.append(jnp.concatenate(columns, axis=1))
     attended = jnp.concatenate(rows, axis=0)
 
@@ -277,14 +276,15 @@
     mid_float = mid_state.astype(jnp.float32)
     normed_two = normalize(mid_float).astype(jnp.bfloat16)
     total = mid_float
-    width = features
+    width = math.gcd(w_up.shape[1], 512)
     for at in range(0, w_up.shape[1], width):
         lifted = jnp.dot(normed_two, w_up[:, at : at + width], preferred_element_type=jnp.float32)
+        lifted = lifted.astype(jnp.bfloat16)
         inner = lifted * (
             math.sqrt(2 / math.pi) + (math.sqrt(2 / math.pi) * 0.044715) * (lifted * lifted)
         )
         halved = 0.5 * lifted
-        hidden = (halved + halved * jnp.tanh(inner)).astype(jnp.bfloat16)
+        hidden = halved + halved * jnp.tanh(inner)
         total = total + jnp.dot(hidden, w_down[at : at + width], preferred_element_type=jnp.float32)
     sectioned = total.astype(jnp.bfloat16)
     for block in range(2):
@@ -294,10 +294,9 @@
 
 def gate(center, preact):
     features = center.shape[-1]
-    gated = jnp.tanh(preact[:, :features]) * (
-        0.5 + 0.5 * jnp.tanh(0.5 * preact[:, features:])
-    )
-    return (center.astype(jnp.float32) + gated).astype(jnp.bfloat16)
+    preact = preact.astype(jnp.bfloat16)
+    opened = 0.5 + 0.5 * jnp.tanh(0.5 * preact[:, features:])
+    return center + jnp.tanh(preact[:, :features]) * opened
 
 
 def temporal_kernel(
@@ -385,7 +384,7 @@
     blocks, count, cells, features = even.shape
     block_in = pl.BlockSpec((blocks, 1, cells, features), lambda i, at: (0, i, 0, 0))
     block_out = pl.BlockSpec((2, 1, cells // 2, features), lambda i, at: (0, i, 0, 0))
-    shape = jax.ShapeDtypeStruct((2, count, cells // 2, features), jnp.bfloat16)
+    shape = pltpu.HBM((2, count, cells // 2, features), jnp.bfloat16)
     tokens = 2 * blocks * count * cells
     return pl.pallas_call(
         temporal_kernel,

time: 110 us -> 105 us (0.955)
  Pallas kernels: 41.7 us -> 39.3 us
  local copies, waits for them, and re-layouts: 5.64 us -> 3.73 us
    pallas_call x2, Pallas kernels: 22.3 us -> 19.3 us  [run_section(): pl.pallas_call(section_kernel, grid_spec=pltpu.PrefetchScalarGridSpec(num...]
    unnamed x22 -> x20, local copies, waits for them, and re-layouts: 4.13 us -> 2.22 us
  transfers between devices with their start and end apart: 18 -> 18, of which waited for: 7 -> 6; matrix products, arithmetic and copies ran while one was open for 1% -> 1% of each run, Pallas kernels for 36% -> 35%
where the time goes in v6:
time: 105 us
  Pallas kernels  39.3 us (37%)
  waiting for transfers between devices  37.1 us (35%)
  starting transfers between devices  24.7 us (24%)
  local copies, waits for them, and re-layouts  3.73 us (4%)
    ppermute x12, waiting for transfers between devices, exchange(): return lax.ppermute(piece, GROUP, [(i, i ^ delta) for i in range(4)])  37.1 us
    pallas_call x2, Pallas kernels, run_section(): pl.pallas_call(section_kernel, grid_spec=pltpu.PrefetchScalarGridSpec(num...  19.3 us
    ppermute x12, starting transfers between devices, exchange(): return lax.ppermute(piece, GROUP, [(i, i ^ delta) for i in range(4)])  18.8 us
    pallas_call x2, Pallas kernels, run_temporal(): pl.pallas_call(temporal_kernel, grid_spec=pltpu.PrefetchScalarGridSpec(nu...  14.8 us
    ppermute x2, starting transfers between devices, paired(): right_even = lax.ppermute(even, RING, leftward)  5.27 us
    pallas_call x2, Pallas kernels, run_pack(): pl.pallas_call(pack_kernel, grid_spec=pltpu.PrefetchScalarGridSpec(num_sc...  3.72 us
    unnamed x20, local copies, waits for them, and re-layouts  2.22 us
  transfers between devices with their start and end apart: 18, of which 6 were waited for; matrix products, arithmetic and copies ran while one was open for 1% of the time, Pallas kernels for 35%

profile of v6, /device:TPU:0, one launch (start us, length us, event | category | flops | bytes accessed | tf_op | source)
XLA Modules:
  0.0 105.1 jit_solution(4638176753048751416)
XLA Ops:
  0.1 2.0 %pack.2 = (bf16[2,2,64,384]{3,2,1,0:T(8,128)(2,1)S(1)}, bf16[2,2,64,384]{3,2,1,0:T(8,128)(2,1)S(1)}, bf16[2,2,64,384]{3,2,1,0:T(8,128)(2,1)S(1)}) custom-call(s32[5]{0:T(128)S(1)} %stack.31.place.before, s32[5]{0:T(128)S(1)} %stack.31.place.before, bf16[2,16,64,384]{3,2,1,0:T(8,128)(2,1)} %bitcast.7, bf16[2,16,64,384]{3,2,1,0:T(8,128)(2,1)} %bitcast.8, ...), custom_call_target="tpu_custom_call" | custom-call | bytes 294912 | tf_op jit(solution)/shard_map/pack/pallas_call | solution.py:196
  2.2 0.1 copy-done.5
  2.3 0.3 pack_weights.1
  2.6 0.5 collective-permute-start
  3.2 2.9 %collective-permute-start.2 = (bf16[2,2,64,384]{3,2,1,0:T(8,128)(2,1)S(1)}, bf16[2,2,64,384]{3,2,1,0:T(8,128)(2,1)S(1)}, u32[]{:S(2)}, u32[]{:S(2)}) collective-permute-start(bf16[2,2,64,384]{3,2,1,0:T(8,128)(2,1)S(1)} %get-tuple-element.31.before), channel_id=1, source_target_pairs={{0,2},{2,0},{16,18},{18,16},{1,3},{3,1},{17,19},{19,17},{4,6},{6,4... | collective-permute-start | bytes 589832 | tf_op jit(solution)/shard_map/ppermute | solution.py:427
  6.1 2.6 %collective-permute-start.3 = (bf16[2,2,64,384]{3,2,1,0:T(8,128)(2,1)S(1)}, bf16[2,2,64,384]{3,2,1,0:T(8,128)(2,1)S(1)}, u32[]{:S(2)}, u32[]{:S(2)}) collective-permute-start(bf16[2,2,64,384]{3,2,1,0:T(8,128)(2,1)S(1)} %get-tuple-element.36), channel_id=1, source_target_pairs={{0,16},{2,18},{16,0},{18,2},{1,17},{3,19},{17,1},{19,3},{4,20},{6,... | collective-permute-start | bytes 589832 | tf_op jit(solution)/shard_map/ppermute | solution.py:427
  8.7 1.7 %pack.3 = (bf16[2,2,64,384]{3,2,1,0:T(8,128)(2,1)S(1)}, bf16[2,2,64,384]{3,2,1,0:T(8,128)(2,1)S(1)}, bf16[2,2,64,384]{3,2,1,0:T(8,128)(2,1)S(1)}) custom-call(s32[5]{0:T(128)S(1)} %stack.31.place.before, bf16[2304,384]{1,0:T(8,128)(2,1)S(1)} %get-tuple-element.32.before.refs_0_, bf16[2,16,64,384]{3,2,1,0:T(8,128)(2,1)} %bitcast.10, ...), custom_call_target="tpu_custom_call" | custom-call | bytes 294912 | tf_op jit(solution)/shard_map/pack/pallas_call | solution.py:196
  10.4 0.8 collective-permute-done.2.near_cells
  11.3 1.7 %collective-permute-start.5 = (bf16[2,2,64,384]{3,2,1,0:T(8,128)(2,1)S(1)}, bf16[2,2,64,384]{3,2,1,0:T(8,128)(2,1)S(1)}, u32[]{:S(2)}, u32[]{:S(2)}) collective-permute-start(bf16[2,2,64,384]{3,2,1,0:T(8,128)(2,1)S(1)} %get-tuple-element.33.before), channel_id=1, source_target_pairs={{0,2},{2,0},{16,18},{18,16},{1,3},{3,1},{17,19},{19,17},{4,6},{6,4... | collective-permute-start | bytes 589832 | tf_op jit(solution)/shard_map/ppermute | solution.py:427
  13.0 2.6 %collective-permute-start.6 = (bf16[2,2,64,384]{3,2,1,0:T(8,128)(2,1)S(1)}, bf16[2,2,64,384]{3,2,1,0:T(8,128)(2,1)S(1)}, u32[]{:S(2)}, u32[]{:S(2)}) collective-permute-start(bf16[2,2,64,384]{3,2,1,0:T(8,128)(2,1)S(1)} %get-tuple-element.42), channel_id=1, source_target_pairs={{0,16},{2,18},{16,0},{18,2},{1,17},{3,19},{17,1},{19,3},{4,20},{6,... | collective-permute-start | bytes 589832 | tf_op jit(solution)/shard_map/ppermute | solution.py:427
  15.7 1.2 %join_weights.1 = (bf16[384,1152]{1,0:T(8,128)(2,1)S(1)}, bf16[384,384]{1,0:T(8,128)(2,1)S(1)}, bf16[384,1536]{1,0:T(8,128)(2,1)S(1)}, bf16[1536,384]{1,0:T(8,12...) custom-call(s32[5]{0:T(128)S(1)} %stack.31.place.before, ...), custom_call_target="tpu_custom_call" | custom-call | bytes 1769472 | tf_op jit(solution)/shard_map/join_weights/pallas_call | solution.py:172
  16.8 14.8 %collective-permute-done.3.far_own = bf16[2,2,64,384]{3,2,1,0:T(8,128)(2,1)S(1)} collective-permute-done((bf16[2,2,64,384]{3,2,1,0:T(8,128)(2,1)S(1)}, bf16[2,2,64,384]{3,2,1,0:T(8,128)(2,1)S(1)}, u32[]{:S(2)}, u32[]{:S(2)}) %collective-permute-start.3) | collective-permute-done | bytes 196640 | tf_op jit(solution)/shard_map/ppermute | solution.py:427
  31.6 3.9 %collective-permute-done.4.far_cells = bf16[2,2,64,384]{3,2,1,0:T(8,128)(2,1)S(1)} collective-permute-done((bf16[2,2,64,384]{3,2,1,0:T(8,128)(2,1)S(1)}, bf16[2,2,64,384]{3,2,1,0:T(8,128)(2,1)S(1)}, u32[]{:S(2)}, u32[]{:S(2)}) %collective-permute-start.4) | collective-permute-done | bytes 196640 | tf_op jit(solution)/shard_map/ppermute | solution.py:427
  35.5 9.3 %section.2 = (bf16[2,2,128,384]{3,2,1,0:T(8,128)(2,1)S(1)}, bf16[2,2,128,384]{3,2,1,0:T(8,128)(2,1)S(1)}) custom-call(s32[5]{0:T(128)S(1)} %stack.31.place.before, bf16[384,1152]{1,0:T(8,128)(2,1)S(1)} %get-tuple-element.35.before.w_qkv, bf16[2,16,64,384]{3,2,1,0:T(8,128)(2,1)} %bitcast.13, bf16[2,2,64,384]{3,2,1,0:T(8,128)(2,1)S(1)} %collective-permute-done.2.near_cells, ...), custom_call_target="tpu_custom_call" | custom-call | flops 239075328 | bytes 393216 | tf_op jit(solution)/shard_map/section/pallas_call | solution.py:366
  44.9 2.6 %collective-permute-start.9 = (bf16[2,2,128,384]{3,2,1,0:T(8,128)(2,1)S(1)}, bf16[2,2,128,384]{3,2,1,0:T(8,128)(2,1)S(1)}, u32[]{:S(2)}, u32[]{:S(2)}) collective-permute-start(bf16[2,2,128,384]{3,2,1,0:T(8,128)(2,1)S(1)} %get-tuple-element.41.before.even), channel_id=1, source_target_pairs={{1,0},{4,1},{5,4},{8,5},{9,8},{12,9},{13,12},{0,13},{3,2},{6,3},{7... | collective-permute-start | bytes 1179656 | tf_op jit(solution)/shard_map/ppermute | solution.py:458
  47.5 10.0 %section.3 = (bf16[2,2,128,384]{3,2,1,0:T(8,128)(2,1)}, bf16[2,2,128,384]{3,2,1,0:T(8,128)(2,1)}) custom-call(s32[5]{0:T(128)S(1)} %stack.31.place.before, bf16[2,2,128,384]{3,2,1,0:T(8,128)(2,1)S(1)} %get-tuple-element.41.before.even, bf16[2,16,64,384]{3,2,1,0:T(8,128)(2,1)} %bitcast.14, bf16[2,2,64,384]{3,2,1,0:T(8,128)(2,1)S(1)} %collective-permute-done.5.near_cells, ...), custom_call_target="tpu_custom_call" | custom-call | flops 239075328 | bytes 393216 | tf_op jit(solution)/shard_map/section/pallas_call | solution.py:366
  57.5 2.6 %collective-permute-start.14 = (bf16[2,2,128,384]{3,2,1,0:T(8,128)(2,1)}, bf16[2,2,128,384]{3,2,1,0:T(8,128)(2,1)}, u32[]{:S(2)}, u32[]{:S(2)}) collective-permute-start(bf16[2,2,128,384]{3,2,1,0:T(8,128)(2,1)} %get-tuple-element.44.before.even), channel_id=1, source_target_pairs={{1,0},{4,1},{5,4},{8,5},{9,8},{12,9},{13,12},{0,13},{3,2},{6,3},{7... | collective-permute-start | bytes 1179656 | tf_op jit(solution)/shard_map/ppermute | solution.py:458
  60.2 6.9 %temporal.2 = (bf16[2,2,64,384]{3,2,1,0:T(8,128)(2,1)}, bf16[2,2,64,384]{3,2,1,0:T(8,128)(2,1)}, bf16[2,2,64,384]{3,2,1,0:T(8,128)(2,1)}, bf16[2,2,64,384]{3,2,1,0:T(8,128)(2,1)}) custom-call(s32[5]{0:T(128)S(1)} %stack.31.place.before, bf16[2,2,128,384]{3,2,1,0:T(8,128)(2,1)} %get-tuple-element.44.before.even, ...), custom_call_target="tpu_custom_call" | custom-call | flops 37748736 | bytes 393216 | tf_op jit(solution)/shard_map/temporal/pallas_call | solution.py:389
  67.1 1.8 %collective-permute-start.10 = (bf16[2,2,64,384]{3,2,1,0:T(8,128)(2,1)}, bf16[2,2,64,384]{3,2,1,0:T(8,128)(2,1)}, u32[]{:S(2)}, u32[]{:S(2)}) collective-permute-start(bf16[2,2,64,384]{3,2,1,0:T(8,128)(2,1)} %get-tuple-element.49), channel_id=1, source_target_pairs={{0,2},{2,0},{16,18},{18,16},{1,3},{3,1},{17,19},{19,17},{4,6},{6,4... | collective-permute-start | bytes 589832 | tf_op jit(solution)/shard_map/ppermute | solution.py:427
  68.9 0.9 collective-permute-start.11
  69.8 1.7 %collective-permute-start.12 = (bf16[2,2,64,384]{3,2,1,0:T(8,128)(2,1)}, bf16[2,2,64,384]{3,2,1,0:T(8,128)(2,1)S(1)}, u32[]{:S(2)}, u32[]{:S(2)}) collective-permute-start(bf16[2,2,64,384]{3,2,1,0:T(8,128)(2,1)} %get-tuple-element.51), channel_id=1, source_target_pairs={{0,18},{2,16},{16,2},{18,0},{1,19},{3,17},{17,3},{19,1},{4,22},{6,... | collective-permute-start | bytes 589832 | tf_op jit(solution)/shard_map/ppermute | solution.py:427
  71.5 0.9 copy-done.2
  72.4 7.9 %temporal.3 = (bf16[2,2,64,384]{3,2,1,0:T(8,128)(2,1)}, bf16[2,2,64,384]{3,2,1,0:T(8,128)(2,1)}, bf16[2,2,64,384]{3,2,1,0:T(8,128)(2,1)}, bf16[2,2,64,384]{3,2,1,0:T(8,128)(2,1)}) custom-call(s32[5]{0:T(128)S(1)} %stack.31.place.before, bf16[2,2,64,384]{3,2,1,0:T(8,128)(2,1)S(1)} %copy-done.2, bf16[2,2,128,384]{3,2,1,0:T(8,128)(2,1)} %get-tuple-element.44.before.even, ...), custom_call_target="tpu_custom_call" | custom-call | flops 37748736 | bytes 393216 | tf_op jit(solution)/shard_map/temporal/pallas_call | solution.py:389
  80.3 1.9 %collective-permute-start.15 = (bf16[2,2,64,384]{3,2,1,0:T(8,128)(2,1)}, bf16[2,2,64,384]{3,2,1,0:T(8,128)(2,1)S(1)}, u32[]{:S(2)}, u32[]{:S(2)}) collective-permute-start(bf16[2,2,64,384]{3,2,1,0:T(8,128)(2,1)} %get-tuple-element.54), channel_id=1, source_target_pairs={{0,2},{2,0},{16,18},{18,16},{1,3},{3,1},{17,19},{19,17},{4,6},{6,4... | collective-permute-start | bytes 589832 | tf_op jit(solution)/shard_map/ppermute | solution.py:427
  82.2 0.9 collective-permute-start.16
  83.1 0.2 broadcast_in_dim.3
  83.4 1.7 %collective-permute-start.17 = (bf16[2,2,64,384]{3,2,1,0:T(8,128)(2,1)S(1)}, bf16[2,2,64,384]{3,2,1,0:T(8,128)(2,1)S(1)}, u32[]{:S(2)}, u32[]{:S(2)}) collective-permute-start(bf16[2,2,64,384]{3,2,1,0:T(8,128)(2,1)S(1)} %copy-done.9), channel_id=1, source_target_pairs={{0,18},{2,16},{16,2},{18,0},{1,19},{3,17},{17,3},{19,1},{4,22},{6,... | collective-permute-start | bytes 589832 | tf_op jit(solution)/shard_map/ppermute | solution.py:427
  85.1 1.0 constant_dynamic-update-slice_fusion.6
  86.2 10.2 %collective-permute-done.12 = bf16[2,2,64,384]{3,2,1,0:T(8,128)(2,1)S(1)} collective-permute-done((bf16[2,2,64,384]{3,2,1,0:T(8,128)(2,1)}, bf16[2,2,64,384]{3,2,1,0:T(8,128)(2,1)S(1)}, u32[]{:S(2)}, u32[]{:S(2)}) %collective-permute-start.12) | collective-permute-done | bytes 196640 | tf_op jit(solution)/shard_map/ppermute | solution.py:427
  96.5 3.4 %collective-permute-done.16 = bf16[2,2,64,384]{3,2,1,0:T(8,128)(2,1)S(1)} collective-permute-done((bf16[2,2,64,384]{3,2,1,0:T(8,128)(2,1)}, bf16[2,2,64,384]{3,2,1,0:T(8,128)(2,1)S(1)}, u32[]{:S(2)}, u32[]{:S(2)}) %collective-permute-start.16) | collective-permute-done | bytes 196640 | tf_op jit(solution)/shard_map/ppermute | solution.py:427
  100.0 3.9 %collective-permute-done.17 = bf16[2,2,64,384]{3,2,1,0:T(8,128)(2,1)S(1)} collective-permute-done((bf16[2,2,64,384]{3,2,1,0:T(8,128)(2,1)S(1)}, bf16[2,2,64,384]{3,2,1,0:T(8,128)(2,1)S(1)}, u32[]{:S(2)}, u32[]{:S(2)}) %collective-permute-start.17) | collective-permute-done | bytes 196640 | tf_op jit(solution)/shard_map/ppermute | solution.py:427
  103.9 1.1 %copy-done.7 = bf16[2,16,64,384]{3,2,1,0:T(8,128)(2,1)} copy-done((bf16[2,16,64,384]{3,2,1,0:T(8,128)(2,1)}, bf16[2,16,64,384]{3,2,1,0:T(8,128)(2,1)S(1)}, u32[]{:S(2)}) %copy-start.7) | copy-done | bytes 1572888
  (42 shorter events, 0.6 us)
Async XLA Ops:
  0.1 2.1 %copy-start = (bf16[576,768]{1,0:T(8,128)(2,1)S(1)}, bf16[576,768]{1,0:T(8,128)(2,1)}, u32[]{:S(2)}) copy-start(bf16[576,768]{1,0:T(8,128)(2,1)} %refs_4_.1) | copy-start | bytes 2654212
  0.1 2.1 %copy-start.1 = (bf16[576,768]{1,0:T(8,128)(2,1)S(1)}, bf16[576,768]{1,0:T(8,128)(2,1)}, u32[]{:S(2)}) copy-start(bf16[576,768]{1,0:T(8,128)(2,1)} %refs_5_.1) | copy-start | bytes 2654212
  0.1 2.1 %copy-start.3 = (bf16[192,1536]{1,0:T(8,128)(2,1)S(1)}, bf16[192,1536]{1,0:T(8,128)(2,1)}, u32[]{:S(2)}) copy-start(bf16[192,1536]{1,0:T(8,128)(2,1)} %refs_2_.1) | copy-start | bytes 1769476
  0.1 2.1 %copy-start.4 = (bf16[768,384]{1,0:T(8,128)(2,1)S(1)}, bf16[768,384]{1,0:T(8,128)(2,1)}, u32[]{:S(2)}) copy-start(bf16[768,384]{1,0:T(8,128)(2,1)} %refs_3_.1) | copy-start | bytes 1769476
  0.1 2.2 %copy-start.5 = (bf16[192,1152]{1,0:T(8,128)(2,1)S(1)}, bf16[192,1152]{1,0:T(8,128)(2,1)}, u32[]{:S(2)}) copy-start(bf16[192,1152]{1,0:T(8,128)(2,1)} %refs_0_.1) | copy-start | bytes 1327108
  0.1 2.2 %copy-start.6 = (bf16[192,384]{1,0:T(8,128)(2,1)S(1)}, bf16[192,384]{1,0:T(8,128)(2,1)}, u32[]{:S(2)}) copy-start(bf16[192,384]{1,0:T(8,128)(2,1)} %refs_1_.1) | copy-start | bytes 442372
  2.6 10.4 %collective-permute-start = (bf16[2304,384]{1,0:T(8,128)(2,1)S(1)}, bf16[2304,384]{1,0:T(8,128)(2,1)S(1)}, u32[]{:S(2)}, u32[]{:S(2)}) collective-permute-start(bf16[2304,384]{1,0:T(8,128)(2,1)S(1)} %get-tuple-element.32.before.refs_0_), channel_id=1, source_target_pairs={{0,1},{1,0},{2,3},{3,2},{4,5},{5,4},{6,7},{7,6},{8,9},{9,8},{10,11... | collective-permute-start | bytes 5308424 | tf_op jit(solution)/shard_map/ppermute | solution.py:436
  3.1 12.5 %collective-permute-start.1 = (bf16[2304,384]{1,0:T(8,128)(2,1)S(1)}, bf16[2304,384]{1,0:T(8,128)(2,1)S(1)}, u32[]{:S(2)}, u32[]{:S(2)}) collective-permute-start(bf16[2304,384]{1,0:T(8,128)(2,1)S(1)} %get-tuple-element.34.refs_2_), channel_id=1, source_target_pairs={{0,1},{1,0},{2,3},{3,2},{4,5},{5,4},{6,7},{7,6},{8,9},{9,8},{10,11... | collective-permute-start | bytes 5308424 | tf_op jit(solution)/shard_map/ppermute | solution.py:436
  3.2 8.1 %collective-permute-start.2 = (bf16[2,2,64,384]{3,2,1,0:T(8,128)(2,1)S(1)}, bf16[2,2,64,384]{3,2,1,0:T(8,128)(2,1)S(1)}, u32[]{:S(2)}, u32[]{:S(2)}) collective-permute-start(bf16[2,2,64,384]{3,2,1,0:T(8,128)(2,1)S(1)} %get-tuple-element.31.before), channel_id=1, source_target_pairs={{0,2},{2,0},{16,18},{18,16},{1,3},{3,1},{17,19},{19,17},{4,6},{6,4... | collective-permute-start | bytes 589832 | tf_op jit(solution)/shard_map/ppermute | solution.py:427
  6.1 25.5 %collective-permute-start.3 = (bf16[2,2,64,384]{3,2,1,0:T(8,128)(2,1)S(1)}, bf16[2,2,64,384]{3,2,1,0:T(8,128)(2,1)S(1)}, u32[]{:S(2)}, u32[]{:S(2)}) collective-permute-start(bf16[2,2,64,384]{3,2,1,0:T(8,128)(2,1)S(1)} %get-tuple-element.36), channel_id=1, source_target_pairs={{0,16},{2,18},{16,0},{18,2},{1,17},{3,19},{17,1},{19,3},{4,20},{6,... | collective-permute-start | bytes 589832 | tf_op jit(solution)/shard_map/ppermute | solution.py:427
  8.7 26.8 %collective-permute-start.4 = (bf16[2,2,64,384]{3,2,1,0:T(8,128)(2,1)S(1)}, bf16[2,2,64,384]{3,2,1,0:T(8,128)(2,1)S(1)}, u32[]{:S(2)}, u32[]{:S(2)}) collective-permute-start(bf16[2,2,64,384]{3,2,1,0:T(8,128)(2,1)S(1)} %get-tuple-element.37), channel_id=1, source_target_pairs={{0,18},{2,16},{16,2},{18,0},{1,19},{3,17},{17,3},{19,1},{4,22},{6,... | collective-permute-start | bytes 589832 | tf_op jit(solution)/shard_map/ppermute | solution.py:427
  11.3 36.3 %collective-permute-start.5 = (bf16[2,2,64,384]{3,2,1,0:T(8,128)(2,1)S(1)}, bf16[2,2,64,384]{3,2,1,0:T(8,128)(2,1)S(1)}, u32[]{:S(2)}, u32[]{:S(2)}) collective-permute-start(bf16[2,2,64,384]{3,2,1,0:T(8,128)(2,1)S(1)} %get-tuple-element.33.before), channel_id=1, source_target_pairs={{0,2},{2,0},{16,18},{18,16},{1,3},{3,1},{17,19},{19,17},{4,6},{6,4... | collective-permute-start | bytes 589832 | tf_op jit(solution)/shard_map/ppermute | solution.py:427
  13.0 34.5 %collective-permute-start.6 = (bf16[2,2,64,384]{3,2,1,0:T(8,128)(2,1)S(1)}, bf16[2,2,64,384]{3,2,1,0:T(8,128)(2,1)S(1)}, u32[]{:S(2)}, u32[]{:S(2)}) collective-permute-start(bf16[2,2,64,384]{3,2,1,0:T(8,128)(2,1)S(1)} %get-tuple-element.42), channel_id=1, source_target_pairs={{0,16},{2,18},{16,0},{18,2},{1,17},{3,19},{17,1},{19,3},{4,20},{6,... | collective-permute-start | bytes 589832 | tf_op jit(solution)/shard_map/ppermute | solution.py:427
  15.6 31.9 %collective-permute-start.7 = (bf16[2,2,64,384]{3,2,1,0:T(8,128)(2,1)S(1)}, bf16[2,2,64,384]{3,2,1,0:T(8,128)(2,1)S(1)}, u32[]{:S(2)}, u32[]{:S(2)}) collective-permute-start(bf16[2,2,64,384]{3,2,1,0:T(8,128)(2,1)S(1)} %get-tuple-element.43), channel_id=1, source_target_pairs={{0,18},{2,16},{16,2},{18,0},{1,19},{3,17},{17,3},{19,1},{4,22},{6,... | collective-permute-start | bytes 589832 | tf_op jit(solution)/shard_map/ppermute | solution.py:427
  44.8 15.4 %collective-permute-start.8 = (bf16[2,2,128,384]{3,2,1,0:T(8,128)(2,1)S(1)}, bf16[2,2,128,384]{3,2,1,0:T(8,128)(2,1)S(1)}, u32[]{:S(2)}, u32[]{:S(2)}) collective-permute-start(bf16[2,2,128,384]{3,2,1,0:T(8,128)(2,1)S(1)} %get-tuple-element.45.odd), channel_id=1, source_target_pairs={{0,1},{1,4},{4,5},{5,8},{8,9},{9,12},{12,13},{13,0},{2,3},{3,6},{6... | collective-permute-start | bytes 1179656 | tf_op jit(solution)/shard_map/ppermute | solution.py:457
  44.9 15.3 %collective-permute-start.9 = (bf16[2,2,128,384]{3,2,1,0:T(8,128)(2,1)S(1)}, bf16[2,2,128,384]{3,2,1,0:T(8,128)(2,1)S(1)}, u32[]{:S(2)}, u32[]{:S(2)}) collective-permute-start(bf16[2,2,128,384]{3,2,1,0:T(8,128)(2,1)S(1)} %get-tuple-element.41.before.even), channel_id=1, source_target_pairs={{1,0},{4,1},{5,4},{8,5},{9,8},{12,9},{13,12},{0,13},{3,2},{6,3},{7... | collective-permute-start | bytes 1179656 | tf_op jit(solution)/shard_map/ppermute | solution.py:458
  57.5 13.9 %collective-permute-start.13 = (bf16[2,2,128,384]{3,2,1,0:T(8,128)(2,1)}, bf16[2,2,128,384]{3,2,1,0:T(8,128)(2,1)}, u32[]{:S(2)}, u32[]{:S(2)}) collective-permute-start(bf16[2,2,128,384]{3,2,1,0:T(8,128)(2,1)} %get-tuple-element.52.odd), channel_id=1, source_target_pairs={{0,1},{1,4},{4,5},{5,8},{8,9},{9,12},{12,13},{13,0},{2,3},{3,6},{6... | collective-permute-start | bytes 1179656 | tf_op jit(solution)/shard_map/ppermute | solution.py:457
  57.5 13.9 %collective-permute-start.14 = (bf16[2,2,128,384]{3,2,1,0:T(8,128)(2,1)}, bf16[2,2,128,384]{3,2,1,0:T(8,128)(2,1)}, u32[]{:S(2)}, u32[]{:S(2)}) collective-permute-start(bf16[2,2,128,384]{3,2,1,0:T(8,128)(2,1)} %get-tuple-element.44.before.even), channel_id=1, source_target_pairs={{1,0},{4,1},{5,4},{8,5},{9,8},{12,9},{13,12},{0,13},{3,2},{6,3},{7... | collective-permute-start | bytes 1179656 | tf_op jit(solution)/shard_map/ppermute | solution.py:458
  67.1 16.3 %collective-permute-start.10 = (bf16[2,2,64,384]{3,2,1,0:T(8,128)(2,1)}, bf16[2,2,64,384]{3,2,1,0:T(8,128)(2,1)}, u32[]{:S(2)}, u32[]{:S(2)}) collective-permute-start(bf16[2,2,64,384]{3,2,1,0:T(8,128)(2,1)} %get-tuple-element.49), channel_id=1, source_target_pairs={{0,2},{2,0},{16,18},{18,16},{1,3},{3,1},{17,19},{19,17},{4,6},{6,4... | collective-permute-start | bytes 589832 | tf_op jit(solution)/shard_map/ppermute | solution.py:427
  68.9 17.2 %collective-permute-start.11 = (bf16[2,2,64,384]{3,2,1,0:T(8,128)(2,1)}, bf16[2,2,64,384]{3,2,1,0:T(8,128)(2,1)S(1)}, u32[]{:S(2)}, u32[]{:S(2)}) collective-permute-start(bf16[2,2,64,384]{3,2,1,0:T(8,128)(2,1)} %get-tuple-element.50), channel_id=1, source_target_pairs={{0,16},{2,18},{16,0},{18,2},{1,17},{3,19},{17,1},{19,3},{4,20},{6,... | collective-permute-start | bytes 589832 | tf_op jit(solution)/shard_map/ppermute | solution.py:427
  69.8 26.6 %collective-permute-start.12 = (bf16[2,2,64,384]{3,2,1,0:T(8,128)(2,1)}, bf16[2,2,64,384]{3,2,1,0:T(8,128)(2,1)S(1)}, u32[]{:S(2)}, u32[]{:S(2)}) collective-permute-start(bf16[2,2,64,384]{3,2,1,0:T(8,128)(2,1)} %get-tuple-element.51), channel_id=1, source_target_pairs={{0,18},{2,16},{16,2},{18,0},{1,19},{3,17},{17,3},{19,1},{4,22},{6,... | collective-permute-start | bytes 589832 | tf_op jit(solution)/shard_map/ppermute | solution.py:427
  71.5 0.9 copy-start.2
  80.3 3.1 %copy-start.9 = (bf16[2,2,64,384]{3,2,1,0:T(8,128)(2,1)S(1)}, bf16[2,2,64,384]{3,2,1,0:T(8,128)(2,1)}, u32[]{:S(2)}) copy-start(bf16[2,2,64,384]{3,2,1,0:T(8,128)(2,1)} %get-tuple-element.56) | copy-start | bytes 589828
  80.3 16.2 %collective-permute-start.15 = (bf16[2,2,64,384]{3,2,1,0:T(8,128)(2,1)}, bf16[2,2,64,384]{3,2,1,0:T(8,128)(2,1)S(1)}, u32[]{:S(2)}, u32[]{:S(2)}) collective-permute-start(bf16[2,2,64,384]{3,2,1,0:T(8,128)(2,1)} %get-tuple-element.54), channel_id=1, source_target_pairs={{0,2},{2,0},{16,18},{18,16},{1,3},{3,1},{17,19},{19,17},{4,6},{6,4... | collective-permute-start | bytes 589832 | tf_op jit(solution)/shard_map/ppermute | solution.py:427
  82.2 14.2 %copy-start.8 = (bf16[2,2,64,384]{3,2,1,0:T(8,128)(2,1)S(1)}, bf16[2,2,64,384]{3,2,1,0:T(8,128)(2,1)}, u32[]{:S(2)}) copy-start(bf16[2,2,64,384]{3,2,1,0:T(8,128)(2,1)} %get-tuple-element.53) | copy-start | bytes 589828
  82.2 17.8 %collective-permute-start.16 = (bf16[2,2,64,384]{3,2,1,0:T(8,128)(2,1)}, bf16[2,2,64,384]{3,2,1,0:T(8,128)(2,1)S(1)}, u32[]{:S(2)}, u32[]{:S(2)}) collective-permute-start(bf16[2,2,64,384]{3,2,1,0:T(8,128)(2,1)} %get-tuple-element.55), channel_id=1, source_target_pairs={{0,16},{2,18},{16,0},{18,2},{1,17},{3,19},{17,1},{19,3},{4,20},{6,... | collective-permute-start | bytes 589832 | tf_op jit(solution)/shard_map/ppermute | solution.py:427
  83.4 20.5 %collective-permute-start.17 = (bf16[2,2,64,384]{3,2,1,0:T(8,128)(2,1)S(1)}, bf16[2,2,64,384]{3,2,1,0:T(8,128)(2,1)S(1)}, u32[]{:S(2)}, u32[]{:S(2)}) collective-permute-start(bf16[2,2,64,384]{3,2,1,0:T(8,128)(2,1)S(1)} %copy-done.9), channel_id=1, source_target_pairs={{0,18},{2,16},{16,2},{18,0},{1,19},{3,17},{17,3},{19,1},{4,22},{6,... | collective-permute-start | bytes 589832 | tf_op jit(solution)/shard_map/ppermute | solution.py:427
  103.9 1.1 %copy-start.7 = (bf16[2,16,64,384]{3,2,1,0:T(8,128)(2,1)}, bf16[2,16,64,384]{3,2,1,0:T(8,128)(2,1)S(1)}, u32[]{:S(2)}) copy-start(bf16[2,16,64,384]{3,2,1,0:T(8,128)(2,1)S(1)} %constant_dynamic-update-slice_fusion) | copy-start | bytes 4718596

commit v7 on v3

--- a/solution.py
+++ b/solution.py
@@ -10,9 +10,8 @@
 HEAD_DIM = 64
 DILATION_FIRST = 16
 DILATION_SECOND = 256
-CHUNKS = (1, 1, 1, 1)
-ORDER = (("s", 0), ("s", 1), ("t", 0), ("s", 2), ("t", 1), ("s", 3), ("t", 2), ("t", 3))
-VMEM_LIMIT = 24 * 1024 * 1024
+CHUNKS = 2
+MIB = 1024 * 1024
 
 
 def with_halo(block, sides, width):
@@ -115,12 +114,12 @@
 SCALARS = pl.BlockSpec(memory_space=pltpu.SMEM)
 
 
-def params():
-    return pltpu.CompilerParams(vmem_limit_bytes=VMEM_LIMIT)
+def params(mib):
+    return pltpu.CompilerParams(vmem_limit_bytes=mib * MIB)
 
 
 def moved(count):
-    return pl.CostEstimate(flops=0, bytes_accessed=4 * count, transcendentals=0)
+    return pl.CostEstimate(flops=0, bytes_accessed=count, transcendentals=0)
 
 
 def pack_weights_kernel(before, *refs):
@@ -141,7 +140,7 @@
         out_shape=jax.ShapeDtypeStruct((rows, width), weights[0].dtype),
         in_specs=[ANYWHERE] + [RESIDENT] * len(weights),
         out_specs=RESIDENT,
-        compiler_params=params(),
+        compiler_params=params(8),
         cost_estimate=moved(rows * width),
         name="pack_weights",
     )(before, *weights)
@@ -149,11 +148,11 @@
 
 def join_weights_kernel(place, before, mine, other, *wholes):
     width = mine.shape[1]
-    for source, index in ((mine, place[0]), (other, 1 - place[0])):
+    for source, core in ((mine, place[0]), (other, 1 - place[0])):
         at = 0
         for whole in wholes:
             rows = whole.shape[0] // 2
-            spot = pl.ds(pl.multiple_of(index * rows, 16), rows)
+            spot = pl.ds(pl.multiple_of(core * rows, 16), rows)
             for column in range(0, whole.shape[1], width):
                 whole[spot, column : column + width] = source[at : at + rows]
                 at += rows
@@ -165,8 +164,8 @@
         out_shape=[jax.ShapeDtypeStruct((2 * w.shape[0], w.shape[1]), w.dtype) for w in halves],
         in_specs=[SCALARS, ANYWHERE, RESIDENT, RESIDENT],
         out_specs=[RESIDENT] * len(halves),
-        compiler_params=params(),
-        cost_estimate=moved(2 * mine.size),
+        compiler_params=params(8),
+        cost_estimate=moved(mine.size),
         name="join_weights",
     )(place, before, mine, other)
 
@@ -177,37 +176,34 @@
         packed[...] = source[...]
 
 
-def run_pack(place, before, grouped, begin, count):
+def run_pack(place, before, grouped, units, first, chunks, deltas):
     slots, _, cells, features = grouped.shape
-    shape = (slots, 1, cells, features)
+    shape = (slots, units, cells, features)
 
     def source(delta):
-        return pl.BlockSpec(
-            shape, lambda i, at: (0, begin + (at[4] ^ delta) * count + i, 0, 0)
-        )
-
+        return pl.BlockSpec(shape, lambda i, at: (0, 4 * (first + i) + (at[4] ^ delta), 0, 0))
+
+    out = jax.ShapeDtypeStruct((slots, chunks * units, cells, features), grouped.dtype)
     return pl.pallas_call(
         pack_kernel,
         grid_spec=pltpu.PrefetchScalarGridSpec(
             num_scalar_prefetch=1,
-            grid=(count,),
-            in_specs=[ANYWHERE] + [source(delta) for delta in (1, 2, 3)],
-            out_specs=[pl.BlockSpec(shape, lambda i, at: (0, i, 0, 0))] * 3,
+            grid=(chunks,),
+            in_specs=[ANYWHERE] + [source(delta) for delta in deltas],
+            out_specs=[pl.BlockSpec(shape, lambda i, at: (0, i, 0, 0))] * len(deltas),
         ),
-        out_shape=[jax.ShapeDtypeStruct((slots, count, cells, features), grouped.dtype)] * 3,
-        compiler_params=params(),
-        cost_estimate=moved(3 * slots * count * cells * features),
+        out_shape=[out] * len(deltas),
+        compiler_params=params(6),
+        cost_estimate=moved(len(deltas) * slots * units * cells * features),
         name="pack",
-    )(place, before, grouped, grouped, grouped)
+    )(place, before, *[grouped] * len(deltas))
 
 
 def section_kernel(
     place,
     before,
-    own,
-    near_cells,
-    far_own,
-    far_cells,
+    mine,
+    other,
     w_qkv,
     w_out,
     w_up,
@@ -215,14 +211,14 @@
     even_ref,
     odd_ref,
 ):
-    features = own.shape[-1]
-    cells = 2 * own.shape[2]
+    slots, units, half, features = mine.shape
+    cells = 2 * half
     parts = []
-    for mine, other in ((own, near_cells), (far_own, far_cells)):
-        for slot in range(2):
-            parts += [mine[slot, 0], other[slot, 0]]
+    for slot in range(slots):
+        for unit in range(units):
+            parts += [mine[slot, unit], other[slot, unit]]
     residual = jnp.concatenate(parts, axis=0).astype(jnp.float32)
-    frame_count = 4
+    frame_count = slots * units
     normed = normalize(residual).astype(jnp.bfloat16)
     projected = jnp.dot(normed, w_qkv[...], preferred_element_type=jnp.float32).astype(jnp.bfloat16)
     pair_width = 2 * HEAD_DIM
@@ -258,7 +254,8 @@
             mixed = jnp.dot(
                 jnp.concatenate(terms, axis=1), split_values, preferred_element_type=jnp.float32
             )
-            columns.append((mixed[:, :pair_width] / mixed[:, pair_width:]).astype(jnp.bfloat16))
+            inverse = pl.reciprocal(mixed[:, pair_width:], approx=True)
+            columns.append((mixed[:, :pair_width] * inverse).astype(jnp.bfloat16))
         rows.append(jnp.concatenate(columns, axis=1))
     attended = jnp.concatenate(rows, axis=0)
 
@@ -268,53 +265,41 @@
     mid_float = mid_state.astype(jnp.float32)
     normed_two = normalize(mid_float).astype(jnp.bfloat16)
     total = mid_float
-    width = features
+    width = math.gcd(w_up.shape[1], 512)
     for at in range(0, w_up.shape[1], width):
         lifted = jnp.dot(normed_two, w_up[:, at : at + width], preferred_element_type=jnp.float32)
+        lifted = lifted.astype(jnp.bfloat16)
         inner = lifted * (
             math.sqrt(2 / math.pi) + (math.sqrt(2 / math.pi) * 0.044715) * (lifted * lifted)
         )
         halved = 0.5 * lifted
-        hidden = (halved + halved * jnp.tanh(inner)).astype(jnp.bfloat16)
+        hidden = halved + halved * jnp.tanh(inner)
         total = total + jnp.dot(hidden, w_down[at : at + width], preferred_element_type=jnp.float32)
     sectioned = total.astype(jnp.bfloat16)
-    for block in range(2):
-        even_ref[block, 0] = sectioned[(2 * block) * cells : (2 * block + 1) * cells]
-        odd_ref[block, 0] = sectioned[(2 * block + 1) * cells : (2 * block + 2) * cells]
+    for unit in range(units):
+        even_ref[unit] = sectioned[unit * cells : (unit + 1) * cells]
+        odd_ref[unit] = sectioned[(units + unit) * cells : (units + unit + 1) * cells]
 
 
 def gate(center, preact):
     features = center.shape[-1]
-    gated = jnp.tanh(preact[:, :features]) * (
-        0.5 + 0.5 * jnp.tanh(0.5 * preact[:, features:])
-    )
-    return (center.astype(jnp.float32) + gated).astype(jnp.bfloat16)
-
-
-def temporal_kernel(
-    place,
-    before,
-    even,
-    odd,
-    left_odd,
-    right_even,
-    w_first,
-    w_second,
-    out0,
-    out1,
-    out2,
-    out3,
-):
+    preact = preact.astype(jnp.bfloat16)
+    opened = 0.5 + 0.5 * jnp.tanh(0.5 * preact[:, features:])
+    return center + jnp.tanh(preact[:, :features]) * opened
+
+
+def temporal_kernel(place, before, *refs):
+    *fields, w_first, w_second, out0, out1, out2, out3 = refs
     near, is_first, is_last = place[1], place[2], place[3]
-    far = 1 - near
-    features = even.shape[-1]
-    cells = even.shape[2]
-    zero = jnp.zeros((cells, features), even.dtype)
-    even_n, odd_n, even_f, odd_f = even[near, 0], odd[near, 0], even[far, 0], odd[far, 0]
-    left_n = jnp.where(is_first == 1, zero, left_odd[near, 0])
-    left_f = left_odd[jnp.where(is_first == 1, near, far), 0]
-    right_n = right_even[jnp.where(is_last == 1, far, near), 0]
-    right_f = jnp.where(is_last == 1, zero, right_even[far, 0])
+    cells, features = fields[0].shape[1:]
+    zero = jnp.zeros((cells, features), fields[0].dtype)
+    pairs = [(fields[i][0], fields[i + 4][0]) for i in range(4)]
+    even_n, odd_n, left_a, right_a = [jnp.where(near == 0, a, b) for a, b in pairs]
+    even_f, odd_f, left_b, right_b = [jnp.where(near == 0, b, a) for a, b in pairs]
+    left_n = jnp.where(is_first == 1, zero, left_a)
+    left_f = jnp.where(is_first == 1, left_a, left_b)
+    right_n = jnp.where(is_last == 1, right_b, right_a)
+    right_f = jnp.where(is_last == 1, zero, right_b)
     center = jnp.concatenate([even_n, odd_n, even_f, odd_f], axis=0)
     stacked = jnp.concatenate(
         [
@@ -345,56 +330,48 @@
         out3[slot, 0] = other[at + half : at + cells]
 
 
-def run_section(place, before, grouped, begin, pieces, weights):
-    slots, count, cells, features = pieces[0].shape
-    ff = weights[2].shape[1]
-    shape_in = (slots, 1, cells, features)
-    own = pl.BlockSpec(shape_in, lambda i, at: (0, begin + at[4] * count + i, 0, 0))
-    block_in = pl.BlockSpec(shape_in, lambda i, at: (0, i, 0, 0))
-    block_out = pl.BlockSpec((2, 1, 2 * cells, features), lambda i, at: (0, i, 0, 0))
-    shape = jax.ShapeDtypeStruct((2, count, 2 * cells, features), jnp.bfloat16)
-    tokens = 2 * slots * count * 2 * cells
-    macs = tokens * (features * (4 * features + 2 * ff) + 4 * cells * features)
+def run_section(place, before, mine, other, weights, units, chunks, from_frames):
+    slots, _, half, features = mine.shape
+    shape_in = (slots, units, half, features)
+    piece = pl.BlockSpec(shape_in, lambda i, at: (0, i, 0, 0))
+    own = pl.BlockSpec(shape_in, lambda i, at: (0, 4 * i + at[4], 0, 0))
+    block_out = pl.BlockSpec((units, 2 * half, features), lambda i, at: (i, 0, 0))
+    place_out = pltpu.HBM if from_frames else jax.ShapeDtypeStruct
+    shape = place_out((chunks * units, 2 * half, features), jnp.bfloat16)
     return pl.pallas_call(
         section_kernel,
         grid_spec=pltpu.PrefetchScalarGridSpec(
             num_scalar_prefetch=1,
-            grid=(count,),
-            in_specs=[ANYWHERE, own] + [block_in] * 3 + [RESIDENT] * 4,
+            grid=(chunks,),
+            in_specs=[ANYWHERE, own if from_frames else piece, piece] + [RESIDENT] * 4,
             out_specs=[block_out, block_out],
         ),
         out_shape=[shape, shape],
-        compiler_params=params(),
-        cost_estimate=pl.CostEstimate(
-            flops=6 * macs, bytes_accessed=8 * tokens * features, transcendentals=tokens * ff
-        ),
+        compiler_params=params(16),
+        cost_estimate=moved(chunks * units * half * features),
         name="section",
-    )(place, before, grouped, *pieces, *weights)
-
-
-def run_temporal(place, before, even, odd, left_odd, right_even, weights):
-    blocks, count, cells, features = even.shape
-    block_in = pl.BlockSpec((blocks, 1, cells, features), lambda i, at: (0, i, 0, 0))
+    )(place, before, mine, other, *weights)
+
+
+def run_temporal(place, before, own, far, weights, begin, count):
+    _, cells, features = own[0].shape
+    block_own = pl.BlockSpec((1, cells, features), lambda i, at: (begin + i, 0, 0))
+    block_far = pl.BlockSpec((1, cells, features), lambda i, at: (i, 0, 0))
     block_out = pl.BlockSpec((2, 1, cells // 2, features), lambda i, at: (0, i, 0, 0))
-    shape = jax.ShapeDtypeStruct((2, count, cells // 2, features), jnp.bfloat16)
-    tokens = 2 * blocks * count * cells
+    shape = pltpu.HBM((2, count, cells // 2, features), jnp.bfloat16)
     return pl.pallas_call(
         temporal_kernel,
         grid_spec=pltpu.PrefetchScalarGridSpec(
             num_scalar_prefetch=1,
             grid=(count,),
-            in_specs=[ANYWHERE] + [block_in] * 4 + [RESIDENT] * 2,
+            in_specs=[ANYWHERE] + [block_own] * 4 + [block_far] * 4 + [RESIDENT] * 2,
             out_specs=[block_out] * 4,
         ),
         out_shape=[shape] * 4,
-        compiler_params=params(),
-        cost_estimate=pl.CostEstimate(
-            flops=60 * tokens * features * features,
-            bytes_accessed=8 * tokens * features,
-            transcendentals=4 * tokens * features,
-        ),
+        compiler_params=params(16),
+        cost_estimate=moved(count * cells * features),
         name="temporal",
-    )(place, before, even, odd, left_odd, right_even, *weights)
+    )(place, before, *own, *far, *weights)
 
 
 GROUP = ("far", "cell")
@@ -413,56 +390,49 @@
     leftward = [(target, source) for source, target in rightward]
     slots = frames_local // DILATION_FIRST
     grouped = frames.reshape(slots, DILATION_FIRST, cells, features)
-    begins = [4 * sum(CHUNKS[:index]) for index in range(len(CHUNKS))]
+    pinned = pltpu.with_memory_space_constraint(grouped, pltpu.HBM)
+    units = DILATION_FIRST // 4 // CHUNKS
 
     def exchange(piece, delta):
         return lax.ppermute(piece, GROUP, [(i, i ^ delta) for i in range(4)])
 
-    def send(before, index):
-        cut = run_pack(place, before, grouped, begins[index], CHUNKS[index])
-        return cut[0], [exchange(piece, delta) for delta, piece in zip((1, 2, 3), cut)]
-
-    def swap_core(packed):
-        return lax.ppermute(packed, "sub", [(0, 1), (1, 0)])
-
-    section_halves = (w_qkv, w_out, w_up, w_down)
-    temporal_halves = (temporal_weight_first, temporal_weight_second)
-    arrived = {}
-    before, arrived[0] = send(place, 0)
-    section_mine = pack_weights(before, section_halves, features)
-    section_weights = join_weights(
-        place, before, section_mine, swap_core(section_mine), section_halves
-    )
-    before, arrived[1] = send(section_weights[0], 1)
-    temporal_mine = pack_weights(before, temporal_halves, features)
-    temporal_weights = join_weights(
-        place, before, temporal_mine, swap_core(temporal_mine), temporal_halves
-    )
-    before = temporal_weights[0]
-    for index in range(2, len(CHUNKS)):
-        before, arrived[index] = send(before, index)
-
-    waiting, outs = {}, {}
-    before = place
-    for kind, index in ORDER:
-        if kind == "s":
-            even, odd = run_section(
-                place, before, grouped, begins[index], arrived[index], section_weights
-            )
-            left_odd = lax.ppermute(odd, RING, rightward)
-            right_even = lax.ppermute(even, RING, leftward)
-            waiting[index] = (even, odd, left_odd, right_even)
-            before = even
-        else:
-            sent = run_temporal(place, before, *waiting[index], temporal_weights)
-            outs[index] = [sent[0]] + [exchange(sent[delta], delta) for delta in (1, 2, 3)]
-            before = sent[0]
+    def halo(even, odd):
+        return [even, odd, lax.ppermute(odd, RING, rightward), lax.ppermute(even, RING, leftward)]
+
+    halves = (w_qkv, w_out, w_up, w_down, temporal_weight_first, temporal_weight_second)
+    (beside,) = run_pack(place, place, pinned, units, 0, CHUNKS, (1,))
+    cuts = [run_pack(place, beside, pinned, units, 0, 1, (2, 3))]
+    mine = pack_weights(cuts[0][0], halves, features)
+    for index in range(1, CHUNKS):
+        cuts.append(run_pack(place, mine, pinned, units, index, 1, (2, 3)))
+    beside = exchange(beside, 1)
+    crossed = [[exchange(piece, delta) for delta, piece in zip((2, 3), cut)] for cut in cuts]
+    other = lax.ppermute(mine, "sub", [(0, 1), (1, 0)])
+    weights = join_weights(place, mine, mine, other, halves)
+    section_weights, temporal_weights = weights[:4], weights[4:]
+
+    even, odd = run_section(
+        place, weights[0], pinned, beside, section_weights, units, CHUNKS, True
+    )
+    own = [pltpu.with_memory_space_constraint(field, pltpu.HBM) for field in halo(even, odd)]
+    before = even
+    far = []
+    for pieces in crossed:
+        even, odd = run_section(place, before, *pieces, section_weights, units, 1, False)
+        far.append(halo(even, odd))
+        before = even
+    outs = []
+    for index in range(CHUNKS):
+        sent = run_temporal(
+            place, before, own, far[index], temporal_weights, index * units, units
+        )
+        outs.append([sent[0]] + [exchange(sent[delta], delta) for delta in (1, 2, 3)])
+        before = sent[0]
     result = jnp.zeros_like(grouped)
-    for index, count in enumerate(CHUNKS):
+    for index, received in enumerate(outs):
         for delta in range(4):
-            result = lax.dynamic_update_slice_in_dim(
-                result, outs[index][delta], begins[index] + (quarter ^ delta) * count, axis=1
-            )
+            at = (4 * index + (quarter ^ delta)) * units
+            result = lax.dynamic_update_slice_in_dim(result, received[delta], at, axis=1)
     return result.reshape(frames.shape)
 
 
@@ -480,7 +450,7 @@
             and cell == 2
             and sub == 2
             and (cells // cell) % 16 == 0
-            and DILATION_FIRST == 4 * sum(CHUNKS)
+            and DILATION_FIRST % (4 * CHUNKS) == 0
         )
         if fits:
             devices = mesh.devices.reshape(groups, 2, tm // 2, cell, sub)

time: 133 us -> 101 us (0.76); the launches traced: 131 us -> 101 us
  starting transfers between devices: 49.7 us -> 33.5 us
  waiting for transfers between devices: 30 us -> 19.5 us
  local copies, waits for them, and re-layouts: 10.4 us -> 5.63 us
    ppermute x24 -> x11, starting transfers between devices: 39.8 us -> 21.4 us  [exchange(): return lax.ppermute(piece, GROUP, [(i, i ^ delta) for i in range(4)])]
    ppermute x24 -> x11, waiting for transfers between devices: 26.6 us -> 19.5 us  [exchange(): return lax.ppermute(piece, GROUP, [(i, i ^ delta) for i in range(4)])]
    unnamed x46 -> x26, local copies, waits for them, and re-layouts: 9.78 us -> 4.11 us
    ppermute x10 -> x7, waiting for transfers between devices: 3.34 us -> 0.02 us  [the longest x3 0.01 us: halo(): lax.ppermute(odd, RING, rightward)]
    pallas_call x4 -> x2, Pallas kernels: 12.8 us -> 15.6 us  [run_temporal(): pl.pallas_call(temporal_kernel, grid_spec=pltpu.PrefetchScalarGridSpec(nu...]
    ppermute x10 -> x7, starting transfers between devices: 9.86 us -> 12.1 us  [the longest x3 11.5 us: halo(): lax.ppermute(even, RING, leftward)]
    pallas_call x4 -> x3, Pallas kernels: 3.04 us -> 5.16 us  [run_pack(): pl.pallas_call(pack_kernel, grid_spec=pltpu.PrefetchScalarGridSpec(num_sc...]
    pallas_call x4 -> x3, Pallas kernels: 21.6 us -> 19.5 us  [run_section(): pl.pallas_call(section_kernel, grid_spec=pltpu.PrefetchScalarGridSpec(num...]
  transfers between devices with their start and end apart: 34 -> 18, of which waited for: 11 -> 4; matrix products, arithmetic and copies ran while one was open for 0% -> 1% of each run, Pallas kernels for 29% -> 38%
where the time goes in v7:
time: 101 us
  Pallas kernels  41.7 us (41%)
  starting transfers between devices  33.5 us (33%)
  waiting for transfers between devices  19.5 us (19%)
  local copies, waits for them, and re-layouts  5.63 us (6%)
    ppermute x11, starting transfers between devices, exchange(): return lax.ppermute(piece, GROUP, [(i, i ^ delta) for i in range(4)])  21.4 us
    pallas_call x3, Pallas kernels, run_section(): pl.pallas_call(section_kernel, grid_spec=pltpu.PrefetchScalarGridSpec(num...  19.5 us
    ppermute x11, waiting for transfers between devices, exchange(): return lax.ppermute(piece, GROUP, [(i, i ^ delta) for i in range(4)])  19.5 us
    pallas_call x2, Pallas kernels, run_temporal(): pl.pallas_call(temporal_kernel, grid_spec=pltpu.PrefetchScalarGridSpec(nu...  15.6 us
    ppermute x3, starting transfers between devices, halo(): lax.ppermute(even, RING, leftward)  11.5 us
    pallas_call x3, Pallas kernels, run_pack(): pl.pallas_call(pack_kernel, grid_spec=pltpu.PrefetchScalarGridSpec(num_sc...  5.16 us
    unnamed x26, local copies, waits for them, and re-layouts  4.11 us
  transfers between devices with their start and end apart: 18, of which 4 were waited for; matrix products, arithmetic and copies ran while one was open for 1% of the time, Pallas kernels for 38%

profile of v7, /device:TPU:0, one launch (start us, length us, event | category | flops | bytes accessed | tf_op | source)
XLA Modules:
  0.0 100.7 jit_solution(6262113227953984909)
XLA Ops:
  0.1 1.6 %pack.3.before = bf16[2,4,64,384]{3,2,1,0:T(8,128)(2,1)S(1)} custom-call(s32[5]{0:T(128)S(1)} %stack.31.place.before, s32[5]{0:T(128)S(1)} %stack.31.place.before, bf16[2,16,64,384]{3,2,1,0:T(8,128)(2,1)} %bitcast.7), custom_call_target="tpu_custom_call" | custom-call | bytes 98304 | tf_op jit(solution)/shard_map/pack/pallas_call | solution.py:187
  1.8 1.9 %pack.4 = (bf16[2,2,64,384]{3,2,1,0:T(8,128)(2,1)S(1)}, bf16[2,2,64,384]{3,2,1,0:T(8,128)(2,1)S(1)}) custom-call(s32[5]{0:T(128)S(1)} %stack.31.place.before, bf16[2,4,64,384]{3,2,1,0:T(8,128)(2,1)S(1)} %pack.3.before, bf16[2,16,64,384]{3,2,1,0:T(8,128)(2,1)} %bitcast.8, bf16[2,16,64,384]{3,2,1,0:T(8,128)(2,1)} %bitcast.9), custom_call_target="tpu_custom_call" | custom-call | bytes 196608 | tf_op jit(solution)/shard_map/pack/pallas_call | solution.py:187
  4.2 0.5 collective-permute-start
  4.7 2.6 %collective-permute-start.1 = (bf16[2,4,64,384]{3,2,1,0:T(8,128)(2,1)S(1)}, bf16[2,4,64,384]{3,2,1,0:T(8,128)(2,1)S(1)}, u32[]{:S(2)}, u32[]{:S(2)}) collective-permute-start(bf16[2,4,64,384]{3,2,1,0:T(8,128)(2,1)S(1)} %pack.3.before), channel_id=1, source_target_pairs={{0,2},{2,0},{16,18},{18,16},{1,3},{3,1},{17,19},{19,17},{4,6},{6,4... | collective-permute-start | bytes 1179656 | tf_op jit(solution)/shard_map/ppermute | solution.py:397
  7.3 2.6 %collective-permute-start.2 = (bf16[2,2,64,384]{3,2,1,0:T(8,128)(2,1)S(1)}, bf16[2,2,64,384]{3,2,1,0:T(8,128)(2,1)S(1)}, u32[]{:S(2)}, u32[]{:S(2)}) collective-permute-start(bf16[2,2,64,384]{3,2,1,0:T(8,128)(2,1)S(1)} %get-tuple-element.29.before), channel_id=1, source_target_pairs={{0,16},{2,18},{16,0},{18,2},{1,17},{3,19},{17,1},{19,3},{4,20},{6,... | collective-permute-start | bytes 589832 | tf_op jit(solution)/shard_map/ppermute | solution.py:397
  9.8 1.6 %pack.5 = (bf16[2,2,64,384]{3,2,1,0:T(8,128)(2,1)S(1)}, bf16[2,2,64,384]{3,2,1,0:T(8,128)(2,1)S(1)}) custom-call(s32[5]{0:T(128)S(1)} %stack.31.place.before, bf16[4608,384]{1,0:T(8,128)(2,1)S(1)} %pack_weights.1.before.mine, bf16[2,16,64,384]{3,2,1,0:T(8,128)(2,1)} %bitcast.10, bf16[2,16,64,384]{3,2,1,0:T(8,128)(2,1)} %bitcast.11), custom_call_target="tpu_custom_call" | custom-call | bytes 196608 | tf_op jit(solution)/shard_map/pack/pallas_call | solution.py:187
  11.5 3.0 %collective-permute-start.4 = (bf16[2,2,64,384]{3,2,1,0:T(8,128)(2,1)S(1)}, bf16[2,2,64,384]{3,2,1,0:T(8,128)(2,1)S(1)}, u32[]{:S(2)}, u32[]{:S(2)}) collective-permute-start(bf16[2,2,64,384]{3,2,1,0:T(8,128)(2,1)S(1)} %get-tuple-element.37), channel_id=1, source_target_pairs={{0,16},{2,18},{16,0},{18,2},{1,17},{3,19},{17,1},{19,3},{4,20},{6,... | collective-permute-start | bytes 589832 | tf_op jit(solution)/shard_map/ppermute | solution.py:397
  14.4 1.2 %join_weights.1 = (bf16[384,1152]{1,0:T(8,128)(2,1)S(1)}, bf16[384,384]{1,0:T(8,128)(2,1)S(1)}, bf16[384,1536]{1,0:T(8,128)(2,1)S(1)}, bf16[1536,384]{1,0:T(8,12...) custom-call(s32[5]{0:T(128)S(1)} %stack.31.place.before, ...), custom_call_target="tpu_custom_call" | custom-call | bytes 1769472 | tf_op jit(solution)/shard_map/join_weights/pallas_call | solution.py:162
  15.6 1.4 %collective-permute-done.1.other = bf16[2,4,64,384]{3,2,1,0:T(8,128)(2,1)S(1)} collective-permute-done((bf16[2,4,64,384]{3,2,1,0:T(8,128)(2,1)S(1)}, bf16[2,4,64,384]{3,2,1,0:T(8,128)(2,1)S(1)}, u32[]{:S(2)}, u32[]{:S(2)}) %collective-permute-start.1) | collective-permute-done | bytes 393248 | tf_op jit(solution)/shard_map/ppermute | solution.py:397
  17.0 10.0 %section.3 = (bf16[4,128,384]{2,1,0:T(8,128)(2,1)}, bf16[4,128,384]{2,1,0:T(8,128)(2,1)}) custom-call(s32[5]{0:T(128)S(1)} %stack.31.place.before, bf16[384,1152]{1,0:T(8,128)(2,1)S(1)} %get-tuple-element.30.before.w_qkv, bf16[2,16,64,384]{3,2,1,0:T(8,128)(2,1)} %bitcast.12, bf16[2,4,64,384]{3,2,1,0:T(8,128)(2,1)S(1)} %collective-permute-done.1.other, ...), custom_call_target="tpu_custom_call" | custom-call | bytes 98304 | tf_op jit(solution)/shard_map/section/pallas_call | solution.py:341
  26.9 6.3 %collective-permute-start.7 = (bf16[4,128,384]{2,1,0:T(8,128)(2,1)}, bf16[4,128,384]{2,1,0:T(8,128)(2,1)S(1)}, u32[]{:S(2)}, u32[]{:S(2)}) collective-permute-start(bf16[4,128,384]{2,1,0:T(8,128)(2,1)} %get-tuple-element.34.before.refs_0_), channel_id=1, source_target_pairs={{1,0},{4,1},{5,4},{8,5},{9,8},{12,9},{13,12},{0,13},{3,2},{6,3},{7... | collective-permute-start | bytes 1179656 | tf_op jit(solution)/shard_map/ppermute | solution.py:400
  33.2 4.4 %collective-permute-start.5 = (bf16[2,2,64,384]{3,2,1,0:T(8,128)(2,1)S(1)}, bf16[2,2,64,384]{3,2,1,0:T(8,128)(2,1)S(1)}, u32[]{:S(2)}, u32[]{:S(2)}) collective-permute-start(bf16[2,2,64,384]{3,2,1,0:T(8,128)(2,1)S(1)} %get-tuple-element.38), channel_id=1, source_target_pairs={{0,18},{2,16},{16,2},{18,0},{1,19},{3,17},{17,3},{19,1},{4,22},{6,... | collective-permute-start | bytes 589832 | tf_op jit(solution)/shard_map/ppermute | solution.py:397
  37.6 1.0 copy-done
  38.6 4.4 %section.4 = (bf16[2,128,384]{2,1,0:T(8,128)(2,1)S(1)}, bf16[2,128,384]{2,1,0:T(8,128)(2,1)S(1)}) custom-call(s32[5]{0:T(128)S(1)} %stack.31.place.before, bf16[4,128,384]{2,1,0:T(8,128)(2,1)S(1)} %copy-done, bf16[2,2,64,384]{3,2,1,0:T(8,128)(2,1)S(1)} %collective-permute-done.2.mine, bf16[2,2,64,384]{3,2,1,0:T(8,128)(2,1)S(1)} %collective-permute-done.3.other, ...), custom_call_target="tpu_custom_call" | custom-call | bytes 49152 | tf_op jit(solution)/shard_map/section/pallas_call | solution.py:341
  43.1 2.6 %collective-permute-start.9 = (bf16[2,128,384]{2,1,0:T(8,128)(2,1)S(1)}, bf16[2,128,384]{2,1,0:T(8,128)(2,1)S(1)}, u32[]{:S(2)}, u32[]{:S(2)}) collective-permute-start(bf16[2,128,384]{2,1,0:T(8,128)(2,1)S(1)} %get-tuple-element.36.before.refs_4_), channel_id=1, source_target_pairs={{1,0},{4,1},{5,4},{8,5},{9,8},{12,9},{13,12},{0,13},{3,2},{6,3},{7... | collective-permute-start | bytes 589832 | tf_op jit(solution)/shard_map/ppermute | solution.py:400
  45.7 5.1 %section.5 = (bf16[2,128,384]{2,1,0:T(8,128)(2,1)}, bf16[2,128,384]{2,1,0:T(8,128)(2,1)}) custom-call(s32[5]{0:T(128)S(1)} %stack.31.place.before, bf16[2,128,384]{2,1,0:T(8,128)(2,1)S(1)} %get-tuple-element.36.before.refs_4_, bf16[2,2,64,384]{3,2,1,0:T(8,128)(2,1)S(1)} %collective-permute-done.4.mine, ...), custom_call_target="tpu_custom_call" | custom-call | bytes 49152 | tf_op jit(solution)/shard_map/section/pallas_call | solution.py:341
  50.8 2.6 %collective-permute-start.14 = (bf16[2,128,384]{2,1,0:T(8,128)(2,1)}, bf16[2,128,384]{2,1,0:T(8,128)(2,1)}, u32[]{:S(2)}, u32[]{:S(2)}) collective-permute-start(bf16[2,128,384]{2,1,0:T(8,128)(2,1)} %get-tuple-element.39.before.refs_4_), channel_id=1, source_target_pairs={{1,0},{4,1},{5,4},{8,5},{9,8},{12,9},{13,12},{0,13},{3,2},{6,3},{7... | collective-permute-start | bytes 589832 | tf_op jit(solution)/shard_map/ppermute | solution.py:400
  53.5 0.7 copy-done.8
  54.4 7.7 %temporal.2 = (bf16[2,2,64,384]{3,2,1,0:T(8,128)(2,1)}, bf16[2,2,64,384]{3,2,1,0:T(8,128)(2,1)}, bf16[2,2,64,384]{3,2,1,0:T(8,128)(2,1)}, bf16[2,2,64,384]{3,2,1,0:T(8,128)(2,1)}) custom-call(s32[5]{0:T(128)S(1)} %stack.31.place.before, bf16[2,128,384]{2,1,0:T(8,128)(2,1)} %get-tuple-element.39.before.refs_4_, ...), custom_call_target="tpu_custom_call" | custom-call | bytes 98304 | tf_op jit(solution)/shard_map/temporal/pallas_call | solution.py:362
  62.1 0.6 collective-permute-start.10
  62.7 1.9 %collective-permute-start.11 = (bf16[2,2,64,384]{3,2,1,0:T(8,128)(2,1)}, bf16[2,2,64,384]{3,2,1,0:T(8,128)(2,1)S(1)}, u32[]{:S(2)}, u32[]{:S(2)}) collective-permute-start(bf16[2,2,64,384]{3,2,1,0:T(8,128)(2,1)} %get-tuple-element.46), channel_id=1, source_target_pairs={{0,16},{2,18},{16,0},{18,2},{1,17},{3,19},{17,1},{19,3},{4,20},{6,... | collective-permute-start | bytes 589832 | tf_op jit(solution)/shard_map/ppermute | solution.py:397
  64.6 1.9 %collective-permute-start.12 = (bf16[2,2,64,384]{3,2,1,0:T(8,128)(2,1)}, bf16[2,2,64,384]{3,2,1,0:T(8,128)(2,1)S(1)}, u32[]{:S(2)}, u32[]{:S(2)}) collective-permute-start(bf16[2,2,64,384]{3,2,1,0:T(8,128)(2,1)} %get-tuple-element.47), channel_id=1, source_target_pairs={{0,18},{2,16},{16,2},{18,0},{1,19},{3,17},{17,3},{19,1},{4,22},{6,... | collective-permute-start | bytes 589832 | tf_op jit(solution)/shard_map/ppermute | solution.py:397
  66.6 0.9 copy-done.3
  67.5 7.9 %temporal.3 = (bf16[2,2,64,384]{3,2,1,0:T(8,128)(2,1)}, bf16[2,2,64,384]{3,2,1,0:T(8,128)(2,1)}, bf16[2,2,64,384]{3,2,1,0:T(8,128)(2,1)}, bf16[2,2,64,384]{3,2,1,0:T(8,128)(2,1)}) custom-call(s32[5]{0:T(128)S(1)} %stack.31.place.before, bf16[2,2,64,384]{3,2,1,0:T(8,128)(2,1)S(1)} %copy-done.3, bf16[4,128,384]{2,1,0:T(8,128)(2,1)} %get-tuple-element.34.before.refs_0_, ...), custom_call_target="tpu_custom_call" | custom-call | bytes 98304 | tf_op jit(solution)/shard_map/temporal/pallas_call | solution.py:362
  75.4 0.6 collective-permute-start.15
  76.0 1.9 %collective-permute-start.16 = (bf16[2,2,64,384]{3,2,1,0:T(8,128)(2,1)}, bf16[2,2,64,384]{3,2,1,0:T(8,128)(2,1)S(1)}, u32[]{:S(2)}, u32[]{:S(2)}) collective-permute-start(bf16[2,2,64,384]{3,2,1,0:T(8,128)(2,1)} %get-tuple-element.51), channel_id=1, source_target_pairs={{0,16},{2,18},{16,0},{18,2},{1,17},{3,19},{17,1},{19,3},{4,20},{6,... | collective-permute-start | bytes 589832 | tf_op jit(solution)/shard_map/ppermute | solution.py:397
  78.2 2.0 %collective-permute-start.17 = (bf16[2,2,64,384]{3,2,1,0:T(8,128)(2,1)S(1)}, bf16[2,2,64,384]{3,2,1,0:T(8,128)(2,1)S(1)}, u32[]{:S(2)}, u32[]{:S(2)}) collective-permute-start(bf16[2,2,64,384]{3,2,1,0:T(8,128)(2,1)S(1)} %copy-done.12), channel_id=1, source_target_pairs={{0,18},{2,16},{16,2},{18,0},{1,19},{3,17},{17,3},{19,1},{4,22},{6,... | collective-permute-start | bytes 589832 | tf_op jit(solution)/shard_map/ppermute | solution.py:397
  80.2 1.0 constant_dynamic-update-slice_fusion.6
  81.2 10.4 %collective-permute-done.12 = bf16[2,2,64,384]{3,2,1,0:T(8,128)(2,1)S(1)} collective-permute-done((bf16[2,2,64,384]{3,2,1,0:T(8,128)(2,1)}, bf16[2,2,64,384]{3,2,1,0:T(8,128)(2,1)S(1)}, u32[]{:S(2)}, u32[]{:S(2)}) %collective-permute-start.12) | collective-permute-done | bytes 196640 | tf_op jit(solution)/shard_map/ppermute | solution.py:397
  91.8 3.4 %collective-permute-done.16 = bf16[2,2,64,384]{3,2,1,0:T(8,128)(2,1)S(1)} collective-permute-done((bf16[2,2,64,384]{3,2,1,0:T(8,128)(2,1)}, bf16[2,2,64,384]{3,2,1,0:T(8,128)(2,1)S(1)}, u32[]{:S(2)}, u32[]{:S(2)}) %collective-permute-start.16) | collective-permute-done | bytes 196640 | tf_op jit(solution)/shard_map/ppermute | solution.py:397
  95.2 4.3 %collective-permute-done.17 = bf16[2,2,64,384]{3,2,1,0:T(8,128)(2,1)S(1)} collective-permute-done((bf16[2,2,64,384]{3,2,1,0:T(8,128)(2,1)S(1)}, bf16[2,2,64,384]{3,2,1,0:T(8,128)(2,1)S(1)}, u32[]{:S(2)}, u32[]{:S(2)}) %collective-permute-start.17) | collective-permute-done | bytes 196640 | tf_op jit(solution)/shard_map/ppermute | solution.py:397
  99.5 1.1 %copy-done.10 = bf16[2,16,64,384]{3,2,1,0:T(8,128)(2,1)} copy-done((bf16[2,16,64,384]{3,2,1,0:T(8,128)(2,1)}, bf16[2,16,64,384]{3,2,1,0:T(8,128)(2,1)S(1)}, u32[]{:S(2)}) %copy-start.10) | copy-done | bytes 1572888
  (50 shorter events, 1.3 us)
Async XLA Ops:
  1.7 2.0 %copy-start.1 = (bf16[576,768]{1,0:T(8,128)(2,1)S(1)}, bf16[576,768]{1,0:T(8,128)(2,1)}, u32[]{:S(2)}) copy-start(bf16[576,768]{1,0:T(8,128)(2,1)} %refs_4_.1) | copy-start | bytes 2654212
  1.8 2.0 %copy-start.2 = (bf16[576,768]{1,0:T(8,128)(2,1)S(1)}, bf16[576,768]{1,0:T(8,128)(2,1)}, u32[]{:S(2)}) copy-start(bf16[576,768]{1,0:T(8,128)(2,1)} %refs_5_.1) | copy-start | bytes 2654212
  1.8 2.0 %copy-start.4 = (bf16[192,1536]{1,0:T(8,128)(2,1)S(1)}, bf16[192,1536]{1,0:T(8,128)(2,1)}, u32[]{:S(2)}) copy-start(bf16[192,1536]{1,0:T(8,128)(2,1)} %refs_2_.1) | copy-start | bytes 1769476
  1.8 2.0 %copy-start.5 = (bf16[768,384]{1,0:T(8,128)(2,1)S(1)}, bf16[768,384]{1,0:T(8,128)(2,1)}, u32[]{:S(2)}) copy-start(bf16[768,384]{1,0:T(8,128)(2,1)} %refs_3_.1) | copy-start | bytes 1769476
  1.8 2.0 %copy-start.6 = (bf16[192,1152]{1,0:T(8,128)(2,1)S(1)}, bf16[192,1152]{1,0:T(8,128)(2,1)}, u32[]{:S(2)}) copy-start(bf16[192,1152]{1,0:T(8,128)(2,1)} %refs_0_.1) | copy-start | bytes 1327108
  1.8 2.1 %copy-start.7 = (bf16[192,384]{1,0:T(8,128)(2,1)S(1)}, bf16[192,384]{1,0:T(8,128)(2,1)}, u32[]{:S(2)}) copy-start(bf16[192,384]{1,0:T(8,128)(2,1)} %refs_1_.1) | copy-start | bytes 442372
  4.2 10.2 %collective-permute-start = (bf16[4608,384]{1,0:T(8,128)(2,1)S(1)}, bf16[4608,384]{1,0:T(8,128)(2,1)S(1)}, u32[]{:S(2)}, u32[]{:S(2)}) collective-permute-start(bf16[4608,384]{1,0:T(8,128)(2,1)S(1)} %pack_weights.1.before.mine), channel_id=1, source_target_pairs={{0,1},{1,0},{2,3},{3,2},{4,5},{5,4},{6,7},{7,6},{8,9},{9,8},{10,11... | collective-permute-start | bytes 10616840 | tf_op jit(solution)/shard_map/ppermute | solution.py:410
  4.7 12.3 %collective-permute-start.1 = (bf16[2,4,64,384]{3,2,1,0:T(8,128)(2,1)S(1)}, bf16[2,4,64,384]{3,2,1,0:T(8,128)(2,1)S(1)}, u32[]{:S(2)}, u32[]{:S(2)}) collective-permute-start(bf16[2,4,64,384]{3,2,1,0:T(8,128)(2,1)S(1)} %pack.3.before), channel_id=1, source_target_pairs={{0,2},{2,0},{16,18},{18,16},{1,3},{3,1},{17,19},{19,17},{4,6},{6,4... | collective-permute-start | bytes 1179656 | tf_op jit(solution)/shard_map/ppermute | solution.py:397
  7.3 26.0 %collective-permute-start.2 = (bf16[2,2,64,384]{3,2,1,0:T(8,128)(2,1)S(1)}, bf16[2,2,64,384]{3,2,1,0:T(8,128)(2,1)S(1)}, u32[]{:S(2)}, u32[]{:S(2)}) collective-permute-start(bf16[2,2,64,384]{3,2,1,0:T(8,128)(2,1)S(1)} %get-tuple-element.29.before), channel_id=1, source_target_pairs={{0,16},{2,18},{16,0},{18,2},{1,17},{3,19},{17,1},{19,3},{4,20},{6,... | collective-permute-start | bytes 589832 | tf_op jit(solution)/shard_map/ppermute | solution.py:397
  9.8 27.7 %collective-permute-start.3 = (bf16[2,2,64,384]{3,2,1,0:T(8,128)(2,1)S(1)}, bf16[2,2,64,384]{3,2,1,0:T(8,128)(2,1)S(1)}, u32[]{:S(2)}, u32[]{:S(2)}) collective-permute-start(bf16[2,2,64,384]{3,2,1,0:T(8,128)(2,1)S(1)} %get-tuple-element.35), channel_id=1, source_target_pairs={{0,18},{2,16},{16,2},{18,0},{1,19},{3,17},{17,3},{19,1},{4,22},{6,... | collective-permute-start | bytes 589832 | tf_op jit(solution)/shard_map/ppermute | solution.py:397
  11.5 31.6 %collective-permute-start.4 = (bf16[2,2,64,384]{3,2,1,0:T(8,128)(2,1)S(1)}, bf16[2,2,64,384]{3,2,1,0:T(8,128)(2,1)S(1)}, u32[]{:S(2)}, u32[]{:S(2)}) collective-permute-start(bf16[2,2,64,384]{3,2,1,0:T(8,128)(2,1)S(1)} %get-tuple-element.37), channel_id=1, source_target_pairs={{0,16},{2,18},{16,0},{18,2},{1,17},{3,19},{17,1},{19,3},{4,20},{6,... | collective-permute-start | bytes 589832 | tf_op jit(solution)/shard_map/ppermute | solution.py:397
  26.9 26.5 %collective-permute-start.6 = (bf16[4,128,384]{2,1,0:T(8,128)(2,1)}, bf16[4,128,384]{2,1,0:T(8,128)(2,1)S(1)}, u32[]{:S(2)}, u32[]{:S(2)}) collective-permute-start(bf16[4,128,384]{2,1,0:T(8,128)(2,1)} %get-tuple-element.40.refs_1_), channel_id=1, source_target_pairs={{0,1},{1,4},{4,5},{5,8},{8,9},{9,12},{12,13},{13,0},{2,3},{3,6},{6... | collective-permute-start | bytes 1179656 | tf_op jit(solution)/shard_map/ppermute | solution.py:400
  26.9 26.5 %collective-permute-start.7 = (bf16[4,128,384]{2,1,0:T(8,128)(2,1)}, bf16[4,128,384]{2,1,0:T(8,128)(2,1)S(1)}, u32[]{:S(2)}, u32[]{:S(2)}) collective-permute-start(bf16[4,128,384]{2,1,0:T(8,128)(2,1)} %get-tuple-element.34.before.refs_0_), channel_id=1, source_target_pairs={{1,0},{4,1},{5,4},{8,5},{9,8},{12,9},{13,12},{0,13},{3,2},{6,3},{7... | collective-permute-start | bytes 1179656 | tf_op jit(solution)/shard_map/ppermute | solution.py:400
  33.2 12.5 %collective-permute-start.5 = (bf16[2,2,64,384]{3,2,1,0:T(8,128)(2,1)S(1)}, bf16[2,2,64,384]{3,2,1,0:T(8,128)(2,1)S(1)}, u32[]{:S(2)}, u32[]{:S(2)}) collective-permute-start(bf16[2,2,64,384]{3,2,1,0:T(8,128)(2,1)S(1)} %get-tuple-element.38), channel_id=1, source_target_pairs={{0,18},{2,16},{16,2},{18,0},{1,19},{3,17},{17,3},{19,1},{4,22},{6,... | collective-permute-start | bytes 589832 | tf_op jit(solution)/shard_map/ppermute | solution.py:397
  37.6 1.0 copy-start
  43.0 7.8 %collective-permute-start.8 = (bf16[2,128,384]{2,1,0:T(8,128)(2,1)S(1)}, bf16[2,128,384]{2,1,0:T(8,128)(2,1)S(1)}, u32[]{:S(2)}, u32[]{:S(2)}) collective-permute-start(bf16[2,128,384]{2,1,0:T(8,128)(2,1)S(1)} %get-tuple-element.41.refs_5_), channel_id=1, source_target_pairs={{0,1},{1,4},{4,5},{5,8},{8,9},{9,12},{12,13},{13,0},{2,3},{3,6},{6... | collective-permute-start | bytes 589832 | tf_op jit(solution)/shard_map/ppermute | solution.py:400
  43.1 10.4 %collective-permute-start.9 = (bf16[2,128,384]{2,1,0:T(8,128)(2,1)S(1)}, bf16[2,128,384]{2,1,0:T(8,128)(2,1)S(1)}, u32[]{:S(2)}, u32[]{:S(2)}) collective-permute-start(bf16[2,128,384]{2,1,0:T(8,128)(2,1)S(1)} %get-tuple-element.36.before.refs_4_), channel_id=1, source_target_pairs={{1,0},{4,1},{5,4},{8,5},{9,8},{12,9},{13,12},{0,13},{3,2},{6,3},{7... | collective-permute-start | bytes 589832 | tf_op jit(solution)/shard_map/ppermute | solution.py:400
  50.8 15.7 %collective-permute-start.13 = (bf16[2,128,384]{2,1,0:T(8,128)(2,1)}, bf16[2,128,384]{2,1,0:T(8,128)(2,1)}, u32[]{:S(2)}, u32[]{:S(2)}) collective-permute-start(bf16[2,128,384]{2,1,0:T(8,128)(2,1)} %get-tuple-element.48.refs_5_), channel_id=1, source_target_pairs={{0,1},{1,4},{4,5},{5,8},{8,9},{9,12},{12,13},{13,0},{2,3},{3,6},{6... | collective-permute-start | bytes 589832 | tf_op jit(solution)/shard_map/ppermute | solution.py:400
  50.8 15.7 %collective-permute-start.14 = (bf16[2,128,384]{2,1,0:T(8,128)(2,1)}, bf16[2,128,384]{2,1,0:T(8,128)(2,1)}, u32[]{:S(2)}, u32[]{:S(2)}) collective-permute-start(bf16[2,128,384]{2,1,0:T(8,128)(2,1)} %get-tuple-element.39.before.refs_4_), channel_id=1, source_target_pairs={{1,0},{4,1},{5,4},{8,5},{9,8},{12,9},{13,12},{0,13},{3,2},{6,3},{7... | collective-permute-start | bytes 589832 | tf_op jit(solution)/shard_map/ppermute | solution.py:400
  53.5 0.8 copy-start.8
  53.5 0.9 copy-start.9
  62.1 16.1 %collective-permute-start.10 = (bf16[2,2,64,384]{3,2,1,0:T(8,128)(2,1)}, bf16[2,2,64,384]{3,2,1,0:T(8,128)(2,1)}, u32[]{:S(2)}, u32[]{:S(2)}) collective-permute-start(bf16[2,2,64,384]{3,2,1,0:T(8,128)(2,1)} %get-tuple-element.45), channel_id=1, source_target_pairs={{0,2},{2,0},{16,18},{18,16},{1,3},{3,1},{17,19},{19,17},{4,6},{6,4... | collective-permute-start | bytes 589832 | tf_op jit(solution)/shard_map/ppermute | solution.py:397
  62.7 18.5 %collective-permute-start.11 = (bf16[2,2,64,384]{3,2,1,0:T(8,128)(2,1)}, bf16[2,2,64,384]{3,2,1,0:T(8,128)(2,1)S(1)}, u32[]{:S(2)}, u32[]{:S(2)}) collective-permute-start(bf16[2,2,64,384]{3,2,1,0:T(8,128)(2,1)} %get-tuple-element.46), channel_id=1, source_target_pairs={{0,16},{2,18},{16,0},{18,2},{1,17},{3,19},{17,1},{19,3},{4,20},{6,... | collective-permute-start | bytes 589832 | tf_op jit(solution)/shard_map/ppermute | solution.py:397
  64.6 27.0 %collective-permute-start.12 = (bf16[2,2,64,384]{3,2,1,0:T(8,128)(2,1)}, bf16[2,2,64,384]{3,2,1,0:T(8,128)(2,1)S(1)}, u32[]{:S(2)}, u32[]{:S(2)}) collective-permute-start(bf16[2,2,64,384]{3,2,1,0:T(8,128)(2,1)} %get-tuple-element.47), channel_id=1, source_target_pairs={{0,18},{2,16},{16,2},{18,0},{1,19},{3,17},{17,3},{19,1},{4,22},{6,... | collective-permute-start | bytes 589832 | tf_op jit(solution)/shard_map/ppermute | solution.py:397
  66.6 0.9 copy-start.3
  75.4 2.8 %copy-start.12 = (bf16[2,2,64,384]{3,2,1,0:T(8,128)(2,1)S(1)}, bf16[2,2,64,384]{3,2,1,0:T(8,128)(2,1)}, u32[]{:S(2)}) copy-start(bf16[2,2,64,384]{3,2,1,0:T(8,128)(2,1)} %get-tuple-element.52) | copy-start | bytes 589828
  75.4 16.3 %collective-permute-start.15 = (bf16[2,2,64,384]{3,2,1,0:T(8,128)(2,1)}, bf16[2,2,64,384]{3,2,1,0:T(8,128)(2,1)S(1)}, u32[]{:S(2)}, u32[]{:S(2)}) collective-permute-start(bf16[2,2,64,384]{3,2,1,0:T(8,128)(2,1)} %get-tuple-element.50), channel_id=1, source_target_pairs={{0,2},{2,0},{16,18},{18,16},{1,3},{3,1},{17,19},{19,17},{4,6},{6,4... | collective-permute-start | bytes 589832 | tf_op jit(solution)/shard_map/ppermute | solution.py:397
  76.0 15.6 %copy-start.11 = (bf16[2,2,64,384]{3,2,1,0:T(8,128)(2,1)S(1)}, bf16[2,2,64,384]{3,2,1,0:T(8,128)(2,1)}, u32[]{:S(2)}) copy-start(bf16[2,2,64,384]{3,2,1,0:T(8,128)(2,1)} %get-tuple-element.49) | copy-start | bytes 589828
  76.0 19.1 %collective-permute-start.16 = (bf16[2,2,64,384]{3,2,1,0:T(8,128)(2,1)}, bf16[2,2,64,384]{3,2,1,0:T(8,128)(2,1)S(1)}, u32[]{:S(2)}, u32[]{:S(2)}) collective-permute-start(bf16[2,2,64,384]{3,2,1,0:T(8,128)(2,1)} %get-tuple-element.51), channel_id=1, source_target_pairs={{0,16},{2,18},{16,0},{18,2},{1,17},{3,19},{17,1},{19,3},{4,20},{6,... | collective-permute-start | bytes 589832 | tf_op jit(solution)/shard_map/ppermute | solution.py:397
  78.2 21.3 %collective-permute-start.17 = (bf16[2,2,64,384]{3,2,1,0:T(8,128)(2,1)S(1)}, bf16[2,2,64,384]{3,2,1,0:T(8,128)(2,1)S(1)}, u32[]{:S(2)}, u32[]{:S(2)}) collective-permute-start(bf16[2,2,64,384]{3,2,1,0:T(8,128)(2,1)S(1)} %copy-done.12), channel_id=1, source_target_pairs={{0,18},{2,16},{16,2},{18,0},{1,19},{3,17},{17,3},{19,1},{4,22},{6,... | collective-permute-start | bytes 589832 | tf_op jit(solution)/shard_map/ppermute | solution.py:397
  99.5 1.1 %copy-start.10 = (bf16[2,16,64,384]{3,2,1,0:T(8,128)(2,1)}, bf16[2,16,64,384]{3,2,1,0:T(8,128)(2,1)S(1)}, u32[]{:S(2)}) copy-start(bf16[2,16,64,384]{3,2,1,0:T(8,128)(2,1)S(1)} %constant_dynamic-update-slice_fusion) | copy-start | bytes 4718596

commit v8 on v7

--- a/solution.py
+++ b/solution.py
@@ -1,3 +1,4 @@
+import functools
 import math
 
 import jax
@@ -11,6 +12,7 @@
 DILATION_FIRST = 16
 DILATION_SECOND = 256
 CHUNKS = 2
+ORDER = (("s", 0), ("s", 1), ("t", 0), ("t", 1))
 MIB = 1024 * 1024
 
 
@@ -114,6 +116,10 @@
 SCALARS = pl.BlockSpec(memory_space=pltpu.SMEM)
 
 
+TOKEN = jax.ShapeDtypeStruct((8, 128), jnp.float32)
+TOKEN_SPEC = pl.BlockSpec((8, 128), lambda *at: (0, 0))
+
+
 def params(mib):
     return pltpu.CompilerParams(vmem_limit_bytes=mib * MIB)
 
@@ -170,33 +176,41 @@
     )(place, before, mine, other)
 
 
-def pack_kernel(place, before, *refs):
-    half = len(refs) // 2
-    for source, packed in zip(refs[:half], refs[half:]):
+def pack_kernel(chunks, place, *refs):
+    sources, (both, *cuts) = refs[: 3 * chunks], refs[3 * chunks :]
+    units = sources[0].shape[1]
+    for chunk in range(chunks):
+        both[:, chunk * units : (chunk + 1) * units] = sources[chunk][...]
+    for source, packed in zip(sources[chunks:], cuts):
         packed[...] = source[...]
 
 
-def run_pack(place, before, grouped, units, first, chunks, deltas):
+def run_pack(place, grouped, units, chunks):
     slots, _, cells, features = grouped.shape
     shape = (slots, units, cells, features)
-
-    def source(delta):
-        return pl.BlockSpec(shape, lambda i, at: (0, 4 * (first + i) + (at[4] ^ delta), 0, 0))
-
-    out = jax.ShapeDtypeStruct((slots, chunks * units, cells, features), grouped.dtype)
-    return pl.pallas_call(
-        pack_kernel,
+    wanted = [(delta, chunk) for chunk in range(chunks) for delta in (2, 3)]
+    beside = [(1, chunk) for chunk in range(chunks)]
+
+    def source(delta, chunk):
+        return pl.BlockSpec(shape, lambda i, at: (0, 4 * chunk + (at[4] ^ delta), 0, 0))
+
+    whole = (slots, chunks * units, cells, features)
+    both, *cuts = pl.pallas_call(
+        functools.partial(pack_kernel, chunks),
         grid_spec=pltpu.PrefetchScalarGridSpec(
             num_scalar_prefetch=1,
-            grid=(chunks,),
-            in_specs=[ANYWHERE] + [source(delta) for delta in deltas],
-            out_specs=[pl.BlockSpec(shape, lambda i, at: (0, i, 0, 0))] * len(deltas),
+            grid=(1,),
+            in_specs=[source(*piece) for piece in beside + wanted],
+            out_specs=[pl.BlockSpec(whole, lambda i, at: (0, 0, 0, 0))]
+            + [pl.BlockSpec(shape, lambda i, at: (0, 0, 0, 0))] * len(wanted),
         ),
-        out_shape=[out] * len(deltas),
-        compiler_params=params(6),
-        cost_estimate=moved(len(deltas) * slots * units * cells * features),
+        out_shape=[jax.ShapeDtypeStruct(whole, grouped.dtype)]
+        + [jax.ShapeDtypeStruct(shape, grouped.dtype)] * len(wanted),
+        compiler_params=params(8),
+        cost_estimate=moved(grouped.size),
         name="pack",
-    )(place, before, *[grouped] * len(deltas))
+    )(place, *[grouped] * len(beside + wanted))
+    return both, [cuts[2 * chunk : 2 * chunk + 2] for chunk in range(chunks)]
 
 
 def section_kernel(
@@ -210,7 +224,9 @@
     w_down,
     even_ref,
     odd_ref,
+    token,
 ):
+    token[...] = jnp.zeros_like(token)
     slots, units, half, features = mine.shape
     cells = 2 * half
     parts = []
@@ -289,11 +305,13 @@
 
 
 def temporal_kernel(place, before, *refs):
-    *fields, w_first, w_second, out0, out1, out2, out3 = refs
+    *fields, w_first, w_second, out0, out1, out2, out3, token = refs
+    token[...] = jnp.zeros_like(token)
     near, is_first, is_last = place[1], place[2], place[3]
-    cells, features = fields[0].shape[1:]
-    zero = jnp.zeros((cells, features), fields[0].dtype)
-    pairs = [(fields[i][0], fields[i + 4][0]) for i in range(4)]
+    units, cells, features = fields[0].shape
+    flat = [field[...].reshape(units * cells, features) for field in fields]
+    zero = jnp.zeros_like(flat[0])
+    pairs = [(flat[i], flat[i + 4]) for i in range(4)]
     even_n, odd_n, left_a, right_a = [jnp.where(near == 0, a, b) for a, b in pairs]
     even_f, odd_f, left_b, right_b = [jnp.where(near == 0, b, a) for a, b in pairs]
     left_n = jnp.where(is_first == 1, zero, left_a)
@@ -310,7 +328,7 @@
         axis=1,
     )
     opening = gate(center, jnp.dot(stacked, w_first[...], preferred_element_type=jnp.float32))
-    rows = 2 * cells
+    rows = 2 * units * cells
     near_part, far_part = opening[:rows], opening[rows:]
     both = jnp.concatenate([near_part, far_part], axis=1)
     result_n = gate(
@@ -323,11 +341,12 @@
     other = jnp.where(near == 0, result_f, result_n)
     half = cells // 2
     for slot in range(2):
-        at = slot * cells
-        out0[slot, 0] = same[at : at + half]
-        out1[slot, 0] = same[at + half : at + cells]
-        out2[slot, 0] = other[at : at + half]
-        out3[slot, 0] = other[at + half : at + cells]
+        for unit in range(units):
+            at = (slot * units + unit) * cells
+            out0[slot, unit] = same[at : at + half]
+            out1[slot, unit] = same[at + half : at + cells]
+            out2[slot, unit] = other[at : at + half]
+            out3[slot, unit] = other[at + half : at + cells]
 
 
 def run_section(place, before, mine, other, weights, units, chunks, from_frames):
@@ -344,31 +363,31 @@
             num_scalar_prefetch=1,
             grid=(chunks,),
             in_specs=[ANYWHERE, own if from_frames else piece, piece] + [RESIDENT] * 4,
-            out_specs=[block_out, block_out],
+            out_specs=[block_out, block_out, TOKEN_SPEC],
         ),
-        out_shape=[shape, shape],
+        out_shape=[shape, shape, TOKEN],
         compiler_params=params(16),
         cost_estimate=moved(chunks * units * half * features),
         name="section",
     )(place, before, mine, other, *weights)
 
 
-def run_temporal(place, before, own, far, weights, begin, count):
+def run_temporal(place, before, own, far, weights, chunk, count):
     _, cells, features = own[0].shape
-    block_own = pl.BlockSpec((1, cells, features), lambda i, at: (begin + i, 0, 0))
-    block_far = pl.BlockSpec((1, cells, features), lambda i, at: (i, 0, 0))
-    block_out = pl.BlockSpec((2, 1, cells // 2, features), lambda i, at: (0, i, 0, 0))
+    block_own = pl.BlockSpec((count, cells, features), lambda i, at: (chunk, 0, 0))
+    block_far = pl.BlockSpec((count, cells, features), lambda i, at: (0, 0, 0))
+    block_out = pl.BlockSpec((2, count, cells // 2, features), lambda i, at: (0, 0, 0, 0))
     shape = pltpu.HBM((2, count, cells // 2, features), jnp.bfloat16)
     return pl.pallas_call(
         temporal_kernel,
         grid_spec=pltpu.PrefetchScalarGridSpec(
             num_scalar_prefetch=1,
-            grid=(count,),
+            grid=(1,),
             in_specs=[ANYWHERE] + [block_own] * 4 + [block_far] * 4 + [RESIDENT] * 2,
-            out_specs=[block_out] * 4,
+            out_specs=[block_out] * 4 + [TOKEN_SPEC],
         ),
-        out_shape=[shape] * 4,
-        compiler_params=params(16),
+        out_shape=[shape] * 4 + [TOKEN],
+        compiler_params=params(28),
         cost_estimate=moved(count * cells * features),
         name="temporal",
     )(place, before, *own, *far, *weights)
@@ -400,34 +419,30 @@
         return [even, odd, lax.ppermute(odd, RING, rightward), lax.ppermute(even, RING, leftward)]
 
     halves = (w_qkv, w_out, w_up, w_down, temporal_weight_first, temporal_weight_second)
-    (beside,) = run_pack(place, place, pinned, units, 0, CHUNKS, (1,))
-    cuts = [run_pack(place, beside, pinned, units, 0, 1, (2, 3))]
+    beside, cuts = run_pack(place, pinned, units, CHUNKS)
     mine = pack_weights(cuts[0][0], halves, features)
-    for index in range(1, CHUNKS):
-        cuts.append(run_pack(place, mine, pinned, units, index, 1, (2, 3)))
     beside = exchange(beside, 1)
     crossed = [[exchange(piece, delta) for delta, piece in zip((2, 3), cut)] for cut in cuts]
     other = lax.ppermute(mine, "sub", [(0, 1), (1, 0)])
     weights = join_weights(place, mine, mine, other, halves)
     section_weights, temporal_weights = weights[:4], weights[4:]
 
-    even, odd = run_section(
-        place, weights[0], pinned, beside, section_weights, units, CHUNKS, True
+    even, odd, before = run_section(
+        place, place, pinned, beside, section_weights, units, CHUNKS, True
     )
     own = [pltpu.with_memory_space_constraint(field, pltpu.HBM) for field in halo(even, odd)]
-    before = even
-    far = []
-    for pieces in crossed:
-        even, odd = run_section(place, before, *pieces, section_weights, units, 1, False)
-        far.append(halo(even, odd))
-        before = even
-    outs = []
-    for index in range(CHUNKS):
-        sent = run_temporal(
-            place, before, own, far[index], temporal_weights, index * units, units
-        )
-        outs.append([sent[0]] + [exchange(sent[delta], delta) for delta in (1, 2, 3)])
-        before = sent[0]
+    far, outs = [], []
+    for kind, index in ORDER:
+        if kind == "s":
+            even, odd, before = run_section(
+                place, before, *crossed[index], section_weights, units, 1, False
+            )
+            far.append(halo(even, odd))
+        else:
+            *sent, before = run_temporal(
+                place, before, own, far[index], temporal_weights, index, units
+            )
+            outs.append([sent[0]] + [exchange(sent[delta], delta) for delta in (1, 2, 3)])
     result = jnp.zeros_like(grouped)
     for index, received in enumerate(outs):
         for delta in range(4):

time: 101 us -> 99.3 us (0.983)
  waiting for transfers between devices: 19.5 us -> 23.1 us
  Pallas kernels: 41.7 us -> 38.7 us
  local copies, waits for them, and re-layouts: 5.63 us -> 3.59 us
    ppermute x11, waiting for transfers between devices: 19.5 us -> 23.1 us  [exchange(): return lax.ppermute(piece, GROUP, [(i, i ^ delta) for i in range(4)])]
    pallas_call x3 -> x1, Pallas kernels: 5.16 us -> 2.27 us  [run_pack(): pl.pallas_call(functools.partial(pack_kernel, chunks), grid_spec=pltpu.Pr...]
    unnamed x26 -> x24, local copies, waits for them, and re-layouts: 4.11 us -> 2.08 us
  transfers between devices with their start and end apart: 18 -> 18, of which waited for: 4 -> 5; matrix products, arithmetic and copies ran while one was open for 1% -> 1% of each run, Pallas kernels for 38% -> 36%
where the time goes in v8:
time: 99.3 us; the launch traced here: 99.1 us
  Pallas kernels  38.7 us (39%)
  starting transfers between devices  33.4 us (34%)
  waiting for transfers between devices  23.1 us (23%)
  local copies, waits for them, and re-layouts  3.59 us (4%)
    ppermute x11, waiting for transfers between devices, exchange(): return lax.ppermute(piece, GROUP, [(i, i ^ delta) for i in range(4)])  23.1 us
    ppermute x11, starting transfers between devices, exchange(): return lax.ppermute(piece, GROUP, [(i, i ^ delta) for i in range(4)])  21.3 us
    pallas_call x3, Pallas kernels, run_section(): pl.pallas_call(section_kernel, grid_spec=pltpu.PrefetchScalarGridSpec(num...  19.5 us
    pallas_call x2, Pallas kernels, run_temporal(): pl.pallas_call(temporal_kernel, grid_spec=pltpu.PrefetchScalarGridSpec(nu...  15.5 us
    ppermute x3, starting transfers between devices, halo(): lax.ppermute(even, RING, leftward)  11.5 us
    pallas_call x1, Pallas kernels, run_pack(): pl.pallas_call(functools.partial(pack_kernel, chunks), grid_spec=pltpu.Pr...  2.27 us
    unnamed x24, local copies, waits for them, and re-layouts  2.08 us
  transfers between devices with their start and end apart: 18, of which 5 were waited for; matrix products, arithmetic and copies ran while one was open for 1% of the time, Pallas kernels for 36%

profile of v8, /device:TPU:0, one launch (start us, length us, event | category | flops | bytes accessed | tf_op | source)
XLA Modules:
  0.0 99.1 jit_solution(2497562272665465229)
XLA Ops:
  0.1 2.3 %pack.1 = (bf16[2,4,64,384]{3,2,1,0:T(8,128)(2,1)S(1)}, bf16[2,2,64,384]{3,2,1,0:T(8,128)(2,1)S(1)}, bf16[2,2,64,384]{3,2,1,0:T(8,128)(2,1)S(1)}, bf16[2,2,64,38...) custom-call(s32[5]{0:T(128)S(1)} %stack.31.place.before, bf16[2,16,64,384]{3,2,1,0:T(8,128)(2,1)} %bitcast.7, ...), custom_call_target="tpu_custom_call" | custom-call | bytes 786432 | tf_op jit(solution)/shard_map/pack/pallas_call | solution.py:198
  2.5 0.3 pack_weights.1.before.mine
  2.8 0.5 collective-permute-start.1
  3.3 2.6 %collective-permute-start = (bf16[2,4,64,384]{3,2,1,0:T(8,128)(2,1)S(1)}, bf16[2,4,64,384]{3,2,1,0:T(8,128)(2,1)S(1)}, u32[]{:S(2)}, u32[]{:S(2)}) collective-permute-start(bf16[2,4,64,384]{3,2,1,0:T(8,128)(2,1)S(1)} %get-tuple-element.34), channel_id=1, source_target_pairs={{0,2},{2,0},{16,18},{18,16},{1,3},{3,1},{17,19},{19,17},{4,6},{6,4... | collective-permute-start | bytes 1179656 | tf_op jit(solution)/shard_map/ppermute | solution.py:416
  5.9 2.6 %collective-permute-start.2 = (bf16[2,2,64,384]{3,2,1,0:T(8,128)(2,1)S(1)}, bf16[2,2,64,384]{3,2,1,0:T(8,128)(2,1)S(1)}, u32[]{:S(2)}, u32[]{:S(2)}) collective-permute-start(bf16[2,2,64,384]{3,2,1,0:T(8,128)(2,1)S(1)} %get-tuple-element.35.before), channel_id=1, source_target_pairs={{0,16},{2,18},{16,0},{18,2},{1,17},{3,19},{17,1},{19,3},{4,20},{6,... | collective-permute-start | bytes 589832 | tf_op jit(solution)/shard_map/ppermute | solution.py:416
  8.5 2.9 %collective-permute-start.4 = (bf16[2,2,64,384]{3,2,1,0:T(8,128)(2,1)S(1)}, bf16[2,2,64,384]{3,2,1,0:T(8,128)(2,1)S(1)}, u32[]{:S(2)}, u32[]{:S(2)}) collective-permute-start(bf16[2,2,64,384]{3,2,1,0:T(8,128)(2,1)S(1)} %get-tuple-element.43), channel_id=1, source_target_pairs={{0,16},{2,18},{16,0},{18,2},{1,17},{3,19},{17,1},{19,3},{4,20},{6,... | collective-permute-start | bytes 589832 | tf_op jit(solution)/shard_map/ppermute | solution.py:416
  11.4 1.2 %join_weights.1 = (bf16[384,1152]{1,0:T(8,128)(2,1)S(1)}, bf16[384,384]{1,0:T(8,128)(2,1)S(1)}, bf16[384,1536]{1,0:T(8,128)(2,1)S(1)}, bf16[1536,384]{1,0:T(8,12...) custom-call(s32[5]{0:T(128)S(1)} %stack.31.place.before, ...), custom_call_target="tpu_custom_call" | custom-call | bytes 1769472 | tf_op jit(solution)/shard_map/join_weights/pallas_call | solution.py:168
  12.5 3.1 %collective-permute-done.other = bf16[2,4,64,384]{3,2,1,0:T(8,128)(2,1)S(1)} collective-permute-done((bf16[2,4,64,384]{3,2,1,0:T(8,128)(2,1)S(1)}, bf16[2,4,64,384]{3,2,1,0:T(8,128)(2,1)S(1)}, u32[]{:S(2)}, u32[]{:S(2)}) %collective-permute-start) | collective-permute-done | bytes 393248 | tf_op jit(solution)/shard_map/ppermute | solution.py:416
  15.6 9.9 %section.3 = (bf16[4,128,384]{2,1,0:T(8,128)(2,1)}, bf16[4,128,384]{2,1,0:T(8,128)(2,1)}, f32[8,128]{1,0:T(8,128)S(1)}) custom-call(s32[5]{0:T(128)S(1)} %stack.31.place.before, s32[5]{0:T(128)S(1)} %stack.31.place.before, bf16[2,16,64,384]{3,2,1,0:T(8,128)(2,1)} %bitcast.13, bf16[2,4,64,384]{3,2,1,0:T(8,128)(2,1)S(1)} %collective-permute-done.other, ...), custom_call_target="tpu_custom_call" | custom-call | bytes 98304 | tf_op jit(solution)/shard_map/section/pallas_call | solution.py:360
  25.5 6.3 %collective-permute-start.7 = (bf16[4,128,384]{2,1,0:T(8,128)(2,1)}, bf16[4,128,384]{2,1,0:T(8,128)(2,1)S(1)}, u32[]{:S(2)}, u32[]{:S(2)}) collective-permute-start(bf16[4,128,384]{2,1,0:T(8,128)(2,1)} %get-tuple-element.46.refs_0_), channel_id=1, source_target_pairs={{1,0},{4,1},{5,4},{8,5},{9,8},{12,9},{13,12},{0,13},{3,2},{6,3},{7... | collective-permute-start | bytes 1179656 | tf_op jit(solution)/shard_map/ppermute | solution.py:419
  31.8 4.4 %collective-permute-start.5 = (bf16[2,2,64,384]{3,2,1,0:T(8,128)(2,1)S(1)}, bf16[2,2,64,384]{3,2,1,0:T(8,128)(2,1)S(1)}, u32[]{:S(2)}, u32[]{:S(2)}) collective-permute-start(bf16[2,2,64,384]{3,2,1,0:T(8,128)(2,1)S(1)} %get-tuple-element.44), channel_id=1, source_target_pairs={{0,18},{2,16},{16,2},{18,0},{1,19},{3,17},{17,3},{19,1},{4,22},{6,... | collective-permute-start | bytes 589832 | tf_op jit(solution)/shard_map/ppermute | solution.py:416
  36.2 4.4 %section.4 = (bf16[2,128,384]{2,1,0:T(8,128)(2,1)S(1)}, bf16[2,128,384]{2,1,0:T(8,128)(2,1)S(1)}, f32[8,128]{1,0:T(8,128)S(1)}) custom-call(s32[5]{0:T(128)S(1)} %stack.31.place.before, f32[8,128]{1,0:T(8,128)S(1)} %get-tuple-element.40.before, bf16[2,2,64,384]{3,2,1,0:T(8,128)(2,1)S(1)} %collective-permute-done.2.mine, ...), custom_call_target="tpu_custom_call" | custom-call | bytes 49152 | tf_op jit(solution)/shard_map/section/pallas_call | solution.py:360
  40.7 2.6 %collective-permute-start.9 = (bf16[2,128,384]{2,1,0:T(8,128)(2,1)S(1)}, bf16[2,128,384]{2,1,0:T(8,128)(2,1)S(1)}, u32[]{:S(2)}, u32[]{:S(2)}) collective-permute-start(bf16[2,128,384]{2,1,0:T(8,128)(2,1)S(1)} %get-tuple-element.48.refs_4_), channel_id=1, source_target_pairs={{1,0},{4,1},{5,4},{8,5},{9,8},{12,9},{13,12},{0,13},{3,2},{6,3},{7... | collective-permute-start | bytes 589832 | tf_op jit(solution)/shard_map/ppermute | solution.py:419
  43.3 5.1 %section.5 = (bf16[2,128,384]{2,1,0:T(8,128)(2,1)}, bf16[2,128,384]{2,1,0:T(8,128)(2,1)}, f32[8,128]{1,0:T(8,128)S(1)}) custom-call(s32[5]{0:T(128)S(1)} %stack.31.place.before, f32[8,128]{1,0:T(8,128)S(1)} %get-tuple-element.42.before, bf16[2,2,64,384]{3,2,1,0:T(8,128)(2,1)S(1)} %collective-permute-done.4.mine, ...), custom_call_target="tpu_custom_call" | custom-call | bytes 49152 | tf_op jit(solution)/shard_map/section/pallas_call | solution.py:360
  48.4 2.6 %collective-permute-start.14 = (bf16[2,128,384]{2,1,0:T(8,128)(2,1)}, bf16[2,128,384]{2,1,0:T(8,128)(2,1)}, u32[]{:S(2)}, u32[]{:S(2)}) collective-permute-start(bf16[2,128,384]{2,1,0:T(8,128)(2,1)} %get-tuple-element.57.refs_4_), channel_id=1, source_target_pairs={{1,0},{4,1},{5,4},{8,5},{9,8},{12,9},{13,12},{0,13},{3,2},{6,3},{7... | collective-permute-start | bytes 589832 | tf_op jit(solution)/shard_map/ppermute | solution.py:419
  51.1 0.7 copy-done.7
  51.8 0.2 copy-done.8
  52.0 7.6 %temporal.2 = (bf16[2,2,64,384]{3,2,1,0:T(8,128)(2,1)}, bf16[2,2,64,384]{3,2,1,0:T(8,128)(2,1)}, bf16[2,2,64,384]{3,2,1,0:T(8,128)(2,1)}, bf16[2,2,64,384]{3,2,1,0:T(8,128)(2,1)}, f32[8,128]{1,0:T(8,128)S(1)}) custom-call(s32[5]{0:T(128)S(1)} %stack.31.place.before, f32[8,128]{1,0:T(8,128)S(1)} %get-tuple-element.45.before, ...), custom_call_target="tpu_custom_call" | custom-call | bytes 98304 | tf_op jit(solution)/shard_map/temporal/pallas_call | solution.py:381
  59.6 0.6 collective-permute-start.10
  60.1 3.0 %collective-permute-start.11 = (bf16[2,2,64,384]{3,2,1,0:T(8,128)(2,1)}, bf16[2,2,64,384]{3,2,1,0:T(8,128)(2,1)S(1)}, u32[]{:S(2)}, u32[]{:S(2)}) collective-permute-start(bf16[2,2,64,384]{3,2,1,0:T(8,128)(2,1)} %get-tuple-element.54), channel_id=1, source_target_pairs={{0,16},{2,18},{16,0},{18,2},{1,17},{3,19},{17,1},{19,3},{4,20},{6,... | collective-permute-start | bytes 589832 | tf_op jit(solution)/shard_map/ppermute | solution.py:416
  63.1 0.9 collective-permute-start.12
  64.0 7.9 %temporal.3 = (bf16[2,2,64,384]{3,2,1,0:T(8,128)(2,1)}, bf16[2,2,64,384]{3,2,1,0:T(8,128)(2,1)}, bf16[2,2,64,384]{3,2,1,0:T(8,128)(2,1)}, bf16[2,2,64,384]{3,2,1,0:T(8,128)(2,1)}, f32[8,128]{1,0:T(8,128)}) custom-call(s32[5]{0:T(128)S(1)} %stack.31.place.before, f32[8,128]{1,0:T(8,128)S(1)} %get-tuple-element.56.before, ...), custom_call_target="tpu_custom_call" | custom-call | bytes 98304 | tf_op jit(solution)/shard_map/temporal/pallas_call | solution.py:381
  71.8 0.7 collective-permute-start.15
  72.5 2.9 %collective-permute-start.16 = (bf16[2,2,64,384]{3,2,1,0:T(8,128)(2,1)}, bf16[2,2,64,384]{3,2,1,0:T(8,128)(2,1)S(1)}, u32[]{:S(2)}, u32[]{:S(2)}) collective-permute-start(bf16[2,2,64,384]{3,2,1,0:T(8,128)(2,1)} %get-tuple-element.61), channel_id=1, source_target_pairs={{0,16},{2,18},{16,0},{18,2},{1,17},{3,19},{17,1},{19,3},{4,20},{6,... | collective-permute-start | bytes 589832 | tf_op jit(solution)/shard_map/ppermute | solution.py:416
  75.4 0.2 broadcast_in_dim.3
  75.7 0.9 collective-permute-start.17
  76.7 1.0 constant_dynamic-update-slice_fusion.6
  77.6 7.6 %collective-permute-done.11 = bf16[2,2,64,384]{3,2,1,0:T(8,128)(2,1)S(1)} collective-permute-done((bf16[2,2,64,384]{3,2,1,0:T(8,128)(2,1)}, bf16[2,2,64,384]{3,2,1,0:T(8,128)(2,1)S(1)}, u32[]{:S(2)}, u32[]{:S(2)}) %collective-permute-start.11) | collective-permute-done | bytes 196640 | tf_op jit(solution)/shard_map/ppermute | solution.py:416
  85.2 4.8 %collective-permute-done.12 = bf16[2,2,64,384]{3,2,1,0:T(8,128)(2,1)S(1)} collective-permute-done((bf16[2,2,64,384]{3,2,1,0:T(8,128)(2,1)}, bf16[2,2,64,384]{3,2,1,0:T(8,128)(2,1)S(1)}, u32[]{:S(2)}, u32[]{:S(2)}) %collective-permute-start.12) | collective-permute-done | bytes 196640 | tf_op jit(solution)/shard_map/ppermute | solution.py:416
  90.2 3.4 %collective-permute-done.16 = bf16[2,2,64,384]{3,2,1,0:T(8,128)(2,1)S(1)} collective-permute-done((bf16[2,2,64,384]{3,2,1,0:T(8,128)(2,1)}, bf16[2,2,64,384]{3,2,1,0:T(8,128)(2,1)S(1)}, u32[]{:S(2)}, u32[]{:S(2)}) %collective-permute-start.16) | collective-permute-done | bytes 196640 | tf_op jit(solution)/shard_map/ppermute | solution.py:416
  93.7 4.2 %collective-permute-done.17 = bf16[2,2,64,384]{3,2,1,0:T(8,128)(2,1)S(1)} collective-permute-done((bf16[2,2,64,384]{3,2,1,0:T(8,128)(2,1)S(1)}, bf16[2,2,64,384]{3,2,1,0:T(8,128)(2,1)S(1)}, u32[]{:S(2)}, u32[]{:S(2)}) %collective-permute-start.17) | collective-permute-done | bytes 196640 | tf_op jit(solution)/shard_map/ppermute | solution.py:416
  97.9 1.1 %copy-done.6 = bf16[2,16,64,384]{3,2,1,0:T(8,128)(2,1)} copy-done((bf16[2,16,64,384]{3,2,1,0:T(8,128)(2,1)}, bf16[2,16,64,384]{3,2,1,0:T(8,128)(2,1)S(1)}, u32[]{:S(2)}) %copy-start.6) | copy-done | bytes 1572888
  (46 shorter events, 0.5 us)
Async XLA Ops:
  0.1 2.3 %copy-start = (bf16[576,768]{1,0:T(8,128)(2,1)S(1)}, bf16[576,768]{1,0:T(8,128)(2,1)}, u32[]{:S(2)}) copy-start(bf16[576,768]{1,0:T(8,128)(2,1)} %refs_4_.1) | copy-start | bytes 2654212
  0.1 2.3 %copy-start.1 = (bf16[576,768]{1,0:T(8,128)(2,1)S(1)}, bf16[576,768]{1,0:T(8,128)(2,1)}, u32[]{:S(2)}) copy-start(bf16[576,768]{1,0:T(8,128)(2,1)} %refs_5_.1) | copy-start | bytes 2654212
  0.1 2.3 %copy-start.2 = (bf16[192,1536]{1,0:T(8,128)(2,1)S(1)}, bf16[192,1536]{1,0:T(8,128)(2,1)}, u32[]{:S(2)}) copy-start(bf16[192,1536]{1,0:T(8,128)(2,1)} %refs_2_.1) | copy-start | bytes 1769476
  0.1 2.3 %copy-start.3 = (bf16[768,384]{1,0:T(8,128)(2,1)S(1)}, bf16[768,384]{1,0:T(8,128)(2,1)}, u32[]{:S(2)}) copy-start(bf16[768,384]{1,0:T(8,128)(2,1)} %refs_3_.1) | copy-start | bytes 1769476
  0.1 2.3 %copy-start.4 = (bf16[192,1152]{1,0:T(8,128)(2,1)S(1)}, bf16[192,1152]{1,0:T(8,128)(2,1)}, u32[]{:S(2)}) copy-start(bf16[192,1152]{1,0:T(8,128)(2,1)} %refs_0_.1) | copy-start | bytes 1327108
  0.1 2.4 %copy-start.5 = (bf16[192,384]{1,0:T(8,128)(2,1)S(1)}, bf16[192,384]{1,0:T(8,128)(2,1)}, u32[]{:S(2)}) copy-start(bf16[192,384]{1,0:T(8,128)(2,1)} %refs_1_.1) | copy-start | bytes 442372
  2.8 8.6 %collective-permute-start.1 = (bf16[4608,384]{1,0:T(8,128)(2,1)S(1)}, bf16[4608,384]{1,0:T(8,128)(2,1)S(1)}, u32[]{:S(2)}, u32[]{:S(2)}) collective-permute-start(bf16[4608,384]{1,0:T(8,128)(2,1)S(1)} %pack_weights.1.before.mine), channel_id=1, source_target_pairs={{0,1},{1,0},{2,3},{3,2},{4,5},{5,4},{6,7},{7,6},{8,9},{9,8},{10,11... | collective-permute-start | bytes 10616840 | tf_op jit(solution)/shard_map/ppermute | solution.py:426
  3.3 12.3 %collective-permute-start = (bf16[2,4,64,384]{3,2,1,0:T(8,128)(2,1)S(1)}, bf16[2,4,64,384]{3,2,1,0:T(8,128)(2,1)S(1)}, u32[]{:S(2)}, u32[]{:S(2)}) collective-permute-start(bf16[2,4,64,384]{3,2,1,0:T(8,128)(2,1)S(1)} %get-tuple-element.34), channel_id=1, source_target_pairs={{0,2},{2,0},{16,18},{18,16},{1,3},{3,1},{17,19},{19,17},{4,6},{6,4... | collective-permute-start | bytes 1179656 | tf_op jit(solution)/shard_map/ppermute | solution.py:416
  5.9 25.9 %collective-permute-start.2 = (bf16[2,2,64,384]{3,2,1,0:T(8,128)(2,1)S(1)}, bf16[2,2,64,384]{3,2,1,0:T(8,128)(2,1)S(1)}, u32[]{:S(2)}, u32[]{:S(2)}) collective-permute-start(bf16[2,2,64,384]{3,2,1,0:T(8,128)(2,1)S(1)} %get-tuple-element.35.before), channel_id=1, source_target_pairs={{0,16},{2,18},{16,0},{18,2},{1,17},{3,19},{17,1},{19,3},{4,20},{6,... | collective-permute-start | bytes 589832 | tf_op jit(solution)/shard_map/ppermute | solution.py:416
  8.5 27.7 %collective-permute-start.3 = (bf16[2,2,64,384]{3,2,1,0:T(8,128)(2,1)S(1)}, bf16[2,2,64,384]{3,2,1,0:T(8,128)(2,1)S(1)}, u32[]{:S(2)}, u32[]{:S(2)}) collective-permute-start(bf16[2,2,64,384]{3,2,1,0:T(8,128)(2,1)S(1)} %get-tuple-element.41), channel_id=1, source_target_pairs={{0,18},{2,16},{16,2},{18,0},{1,19},{3,17},{17,3},{19,1},{4,22},{6,... | collective-permute-start | bytes 589832 | tf_op jit(solution)/shard_map/ppermute | solution.py:416
  8.5 32.2 %collective-permute-start.4 = (bf16[2,2,64,384]{3,2,1,0:T(8,128)(2,1)S(1)}, bf16[2,2,64,384]{3,2,1,0:T(8,128)(2,1)S(1)}, u32[]{:S(2)}, u32[]{:S(2)}) collective-permute-start(bf16[2,2,64,384]{3,2,1,0:T(8,128)(2,1)S(1)} %get-tuple-element.43), channel_id=1, source_target_pairs={{0,16},{2,18},{16,0},{18,2},{1,17},{3,19},{17,1},{19,3},{4,20},{6,... | collective-permute-start | bytes 589832 | tf_op jit(solution)/shard_map/ppermute | solution.py:416
  25.5 25.5 %collective-permute-start.6 = (bf16[4,128,384]{2,1,0:T(8,128)(2,1)}, bf16[4,128,384]{2,1,0:T(8,128)(2,1)S(1)}, u32[]{:S(2)}, u32[]{:S(2)}) collective-permute-start(bf16[4,128,384]{2,1,0:T(8,128)(2,1)} %get-tuple-element.47.refs_1_), channel_id=1, source_target_pairs={{0,1},{1,4},{4,5},{5,8},{8,9},{9,12},{12,13},{13,0},{2,3},{3,6},{6... | collective-permute-start | bytes 1179656 | tf_op jit(solution)/shard_map/ppermute | solution.py:419
  25.5 25.5 %collective-permute-start.7 = (bf16[4,128,384]{2,1,0:T(8,128)(2,1)}, bf16[4,128,384]{2,1,0:T(8,128)(2,1)S(1)}, u32[]{:S(2)}, u32[]{:S(2)}) collective-permute-start(bf16[4,128,384]{2,1,0:T(8,128)(2,1)} %get-tuple-element.46.refs_0_), channel_id=1, source_target_pairs={{1,0},{4,1},{5,4},{8,5},{9,8},{12,9},{13,12},{0,13},{3,2},{6,3},{7... | collective-permute-start | bytes 1179656 | tf_op jit(solution)/shard_map/ppermute | solution.py:419
  31.8 11.5 %collective-permute-start.5 = (bf16[2,2,64,384]{3,2,1,0:T(8,128)(2,1)S(1)}, bf16[2,2,64,384]{3,2,1,0:T(8,128)(2,1)S(1)}, u32[]{:S(2)}, u32[]{:S(2)}) collective-permute-start(bf16[2,2,64,384]{3,2,1,0:T(8,128)(2,1)S(1)} %get-tuple-element.44), channel_id=1, source_target_pairs={{0,18},{2,16},{16,2},{18,0},{1,19},{3,17},{17,3},{19,1},{4,22},{6,... | collective-permute-start | bytes 589832 | tf_op jit(solution)/shard_map/ppermute | solution.py:416
  40.6 7.8 %collective-permute-start.8 = (bf16[2,128,384]{2,1,0:T(8,128)(2,1)S(1)}, bf16[2,128,384]{2,1,0:T(8,128)(2,1)S(1)}, u32[]{:S(2)}, u32[]{:S(2)}) collective-permute-start(bf16[2,128,384]{2,1,0:T(8,128)(2,1)S(1)} %get-tuple-element.49.refs_5_), channel_id=1, source_target_pairs={{0,1},{1,4},{4,5},{5,8},{8,9},{9,12},{12,13},{13,0},{2,3},{3,6},{6... | collective-permute-start | bytes 589832 | tf_op jit(solution)/shard_map/ppermute | solution.py:419
  40.7 10.4 %collective-permute-start.9 = (bf16[2,128,384]{2,1,0:T(8,128)(2,1)S(1)}, bf16[2,128,384]{2,1,0:T(8,128)(2,1)S(1)}, u32[]{:S(2)}, u32[]{:S(2)}) collective-permute-start(bf16[2,128,384]{2,1,0:T(8,128)(2,1)S(1)} %get-tuple-element.48.refs_4_), channel_id=1, source_target_pairs={{1,0},{4,1},{5,4},{8,5},{9,8},{12,9},{13,12},{0,13},{3,2},{6,3},{7... | collective-permute-start | bytes 589832 | tf_op jit(solution)/shard_map/ppermute | solution.py:419
  48.4 15.6 %collective-permute-start.13 = (bf16[2,128,384]{2,1,0:T(8,128)(2,1)}, bf16[2,128,384]{2,1,0:T(8,128)(2,1)}, u32[]{:S(2)}, u32[]{:S(2)}) collective-permute-start(bf16[2,128,384]{2,1,0:T(8,128)(2,1)} %get-tuple-element.58.refs_5_), channel_id=1, source_target_pairs={{0,1},{1,4},{4,5},{5,8},{8,9},{9,12},{12,13},{13,0},{2,3},{3,6},{6... | collective-permute-start | bytes 589832 | tf_op jit(solution)/shard_map/ppermute | solution.py:419
  48.4 15.6 %collective-permute-start.14 = (bf16[2,128,384]{2,1,0:T(8,128)(2,1)}, bf16[2,128,384]{2,1,0:T(8,128)(2,1)}, u32[]{:S(2)}, u32[]{:S(2)}) collective-permute-start(bf16[2,128,384]{2,1,0:T(8,128)(2,1)} %get-tuple-element.57.refs_4_), channel_id=1, source_target_pairs={{1,0},{4,1},{5,4},{8,5},{9,8},{12,9},{13,12},{0,13},{3,2},{6,3},{7... | collective-permute-start | bytes 589832 | tf_op jit(solution)/shard_map/ppermute | solution.py:419
  51.0 0.8 copy-start.7
  51.1 0.9 copy-start.8
  59.6 16.1 %collective-permute-start.10 = (bf16[2,2,64,384]{3,2,1,0:T(8,128)(2,1)}, bf16[2,2,64,384]{3,2,1,0:T(8,128)(2,1)}, u32[]{:S(2)}, u32[]{:S(2)}) collective-permute-start(bf16[2,2,64,384]{3,2,1,0:T(8,128)(2,1)} %get-tuple-element.53), channel_id=1, source_target_pairs={{0,2},{2,0},{16,18},{18,16},{1,3},{3,1},{17,19},{19,17},{4,6},{6,4... | collective-permute-start | bytes 589832 | tf_op jit(solution)/shard_map/ppermute | solution.py:416
  60.1 25.1 %collective-permute-start.11 = (bf16[2,2,64,384]{3,2,1,0:T(8,128)(2,1)}, bf16[2,2,64,384]{3,2,1,0:T(8,128)(2,1)S(1)}, u32[]{:S(2)}, u32[]{:S(2)}) collective-permute-start(bf16[2,2,64,384]{3,2,1,0:T(8,128)(2,1)} %get-tuple-element.54), channel_id=1, source_target_pairs={{0,16},{2,18},{16,0},{18,2},{1,17},{3,19},{17,1},{19,3},{4,20},{6,... | collective-permute-start | bytes 589832 | tf_op jit(solution)/shard_map/ppermute | solution.py:416
  63.1 27.0 %collective-permute-start.12 = (bf16[2,2,64,384]{3,2,1,0:T(8,128)(2,1)}, bf16[2,2,64,384]{3,2,1,0:T(8,128)(2,1)S(1)}, u32[]{:S(2)}, u32[]{:S(2)}) collective-permute-start(bf16[2,2,64,384]{3,2,1,0:T(8,128)(2,1)} %get-tuple-element.55), channel_id=1, source_target_pairs={{0,18},{2,16},{16,2},{18,0},{1,19},{3,17},{17,3},{19,1},{4,22},{6,... | collective-permute-start | bytes 589832 | tf_op jit(solution)/shard_map/ppermute | solution.py:416
  71.8 3.8 %copy-start.9 = (bf16[2,2,64,384]{3,2,1,0:T(8,128)(2,1)S(1)}, bf16[2,2,64,384]{3,2,1,0:T(8,128)(2,1)}, u32[]{:S(2)}) copy-start(bf16[2,2,64,384]{3,2,1,0:T(8,128)(2,1)} %get-tuple-element.52) | copy-start | bytes 589828
  71.8 3.9 %copy-start.11 = (bf16[2,2,64,384]{3,2,1,0:T(8,128)(2,1)S(1)}, bf16[2,2,64,384]{3,2,1,0:T(8,128)(2,1)}, u32[]{:S(2)}) copy-start(bf16[2,2,64,384]{3,2,1,0:T(8,128)(2,1)} %get-tuple-element.62) | copy-start | bytes 589828
  71.8 18.3 %collective-permute-start.15 = (bf16[2,2,64,384]{3,2,1,0:T(8,128)(2,1)}, bf16[2,2,64,384]{3,2,1,0:T(8,128)(2,1)S(1)}, u32[]{:S(2)}, u32[]{:S(2)}) collective-permute-start(bf16[2,2,64,384]{3,2,1,0:T(8,128)(2,1)} %get-tuple-element.60), channel_id=1, source_target_pairs={{0,2},{2,0},{16,18},{18,16},{1,3},{3,1},{17,19},{19,17},{4,6},{6,4... | collective-permute-start | bytes 589832 | tf_op jit(solution)/shard_map/ppermute | solution.py:416
  72.5 21.2 %collective-permute-start.16 = (bf16[2,2,64,384]{3,2,1,0:T(8,128)(2,1)}, bf16[2,2,64,384]{3,2,1,0:T(8,128)(2,1)S(1)}, u32[]{:S(2)}, u32[]{:S(2)}) collective-permute-start(bf16[2,2,64,384]{3,2,1,0:T(8,128)(2,1)} %get-tuple-element.61), channel_id=1, source_target_pairs={{0,16},{2,18},{16,0},{18,2},{1,17},{3,19},{17,1},{19,3},{4,20},{6,... | collective-permute-start | bytes 589832 | tf_op jit(solution)/shard_map/ppermute | solution.py:416
  75.4 14.7 %copy-start.10 = (bf16[2,2,64,384]{3,2,1,0:T(8,128)(2,1)S(1)}, bf16[2,2,64,384]{3,2,1,0:T(8,128)(2,1)}, u32[]{:S(2)}) copy-start(bf16[2,2,64,384]{3,2,1,0:T(8,128)(2,1)} %get-tuple-element.59) | copy-start | bytes 589828
  75.7 22.2 %collective-permute-start.17 = (bf16[2,2,64,384]{3,2,1,0:T(8,128)(2,1)S(1)}, bf16[2,2,64,384]{3,2,1,0:T(8,128)(2,1)S(1)}, u32[]{:S(2)}, u32[]{:S(2)}) collective-permute-start(bf16[2,2,64,384]{3,2,1,0:T(8,128)(2,1)S(1)} %copy-done.11), channel_id=1, source_target_pairs={{0,18},{2,16},{16,2},{18,0},{1,19},{3,17},{17,3},{19,1},{4,22},{6,... | collective-permute-start | bytes 589832 | tf_op jit(solution)/shard_map/ppermute | solution.py:416
  97.9 1.1 %copy-start.6 = (bf16[2,16,64,384]{3,2,1,0:T(8,128)(2,1)}, bf16[2,16,64,384]{3,2,1,0:T(8,128)(2,1)S(1)}, u32[]{:S(2)}) copy-start(bf16[2,16,64,384]{3,2,1,0:T(8,128)(2,1)S(1)} %constant_dynamic-update-slice_fusion) | copy-start | bytes 4718596

commit v9 on v8

--- a/solution.py
+++ b/solution.py
@@ -201,8 +201,7 @@
             num_scalar_prefetch=1,
             grid=(1,),
             in_specs=[source(*piece) for piece in beside + wanted],
-            out_specs=[pl.BlockSpec(whole, lambda i, at: (0, 0, 0, 0))]
-            + [pl.BlockSpec(shape, lambda i, at: (0, 0, 0, 0))] * len(wanted),
+            out_specs=[RESIDENT] * (1 + len(wanted)),
         ),
         out_shape=[jax.ShapeDtypeStruct(whole, grouped.dtype)]
         + [jax.ShapeDtypeStruct(shape, grouped.dtype)] * len(wanted),
@@ -305,48 +304,58 @@
 
 
 def temporal_kernel(place, before, *refs):
-    *fields, w_first, w_second, out0, out1, out2, out3, token = refs
+    *fields, w_first, w_second, out0, out1, out2, out3, token, stacked, results = refs
     token[...] = jnp.zeros_like(token)
-    near, is_first, is_last = place[1], place[2], place[3]
+    side, is_first, is_last = place[1], place[2], place[3]
     units, cells, features = fields[0].shape
-    flat = [field[...].reshape(units * cells, features) for field in fields]
-    zero = jnp.zeros_like(flat[0])
-    pairs = [(flat[i], flat[i + 4]) for i in range(4)]
-    even_n, odd_n, left_a, right_a = [jnp.where(near == 0, a, b) for a, b in pairs]
-    even_f, odd_f, left_b, right_b = [jnp.where(near == 0, b, a) for a, b in pairs]
-    left_n = jnp.where(is_first == 1, zero, left_a)
-    left_f = jnp.where(is_first == 1, left_a, left_b)
-    right_n = jnp.where(is_last == 1, right_b, right_a)
-    right_f = jnp.where(is_last == 1, zero, right_b)
-    center = jnp.concatenate([even_n, odd_n, even_f, odd_f], axis=0)
-    stacked = jnp.concatenate(
-        [
-            jnp.concatenate([left_n, even_n, left_f, even_f], axis=0),
-            center,
-            jnp.concatenate([odd_n, right_n, odd_f, right_f], axis=0),
-        ],
-        axis=1,
-    )
-    opening = gate(center, jnp.dot(stacked, w_first[...], preferred_element_type=jnp.float32))
-    rows = 2 * units * cells
+    slab = units * cells
+    rows = 2 * slab
+    for index in range(2):
+        even, odd, left, right = fields[4 * index : 4 * index + 4]
+        base = pl.multiple_of(jnp.where(side == index, 0, rows), slab)
+        left_base = pl.multiple_of(jnp.where(is_first == 1, rows - base, base), slab)
+        right_base = pl.multiple_of(jnp.where(is_last == 1, rows - base, base), slab)
+        for unit in range(units):
+            low, high = unit * cells, slab + unit * cells
+            even_rows = pl.ds(pl.multiple_of(base + low, cells), cells)
+            odd_rows = pl.ds(pl.multiple_of(base + high, cells), cells)
+            stacked[even_rows, features : 2 * features] = even[unit]
+            stacked[odd_rows, features : 2 * features] = odd[unit]
+            stacked[odd_rows, :features] = even[unit]
+            stacked[even_rows, 2 * features :] = odd[unit]
+            left_rows = pl.ds(pl.multiple_of(left_base + low, cells), cells)
+            right_rows = pl.ds(pl.multiple_of(right_base + high, cells), cells)
+            stacked[left_rows, :features] = left[unit]
+            stacked[right_rows, 2 * features :] = right[unit]
+
+    @pl.when(is_first == 1)
+    def _():
+        stacked[:slab, :features] = jnp.zeros((slab, features), stacked.dtype)
+
+    @pl.when(is_last == 1)
+    def _():
+        stacked[rows + slab :, 2 * features :] = jnp.zeros((slab, features), stacked.dtype)
+
+    opening = gate(
+        stacked[:, features : 2 * features],
+        jnp.dot(stacked[...], w_first[...], preferred_element_type=jnp.float32),
+    )
     near_part, far_part = opening[:rows], opening[rows:]
     both = jnp.concatenate([near_part, far_part], axis=1)
-    result_n = gate(
+    results[:rows] = gate(
         near_part, jnp.dot(both, w_second[features:], preferred_element_type=jnp.float32)
     )
-    result_f = gate(
+    results[rows:] = gate(
         far_part, jnp.dot(both, w_second[: 2 * features], preferred_element_type=jnp.float32)
     )
-    same = jnp.where(near == 0, result_n, result_f)
-    other = jnp.where(near == 0, result_f, result_n)
     half = cells // 2
-    for slot in range(2):
-        for unit in range(units):
-            at = (slot * units + unit) * cells
-            out0[slot, unit] = same[at : at + half]
-            out1[slot, unit] = same[at + half : at + cells]
-            out2[slot, unit] = other[at : at + half]
-            out3[slot, unit] = other[at + half : at + cells]
+    for index, (near_out, far_out) in enumerate(((out0, out1), (out2, out3))):
+        base = jnp.where(side == index, 0, rows)
+        for slot in range(2):
+            for unit in range(units):
+                at = base + (slot * units + unit) * cells
+                near_out[slot, unit] = results[pl.ds(pl.multiple_of(at, half), half)]
+                far_out[slot, unit] = results[pl.ds(pl.multiple_of(at + half, half), half)]
 
 
 def run_section(place, before, mine, other, weights, units, chunks, from_frames):
@@ -362,8 +371,9 @@
         grid_spec=pltpu.PrefetchScalarGridSpec(
             num_scalar_prefetch=1,
             grid=(chunks,),
-            in_specs=[ANYWHERE, own if from_frames else piece, piece] + [RESIDENT] * 4,
-            out_specs=[block_out, block_out, TOKEN_SPEC],
+            in_specs=([ANYWHERE, own, piece] if from_frames else [ANYWHERE, RESIDENT, RESIDENT])
+            + [RESIDENT] * 4,
+            out_specs=([block_out] * 2 if from_frames else [RESIDENT] * 2) + [TOKEN_SPEC],
         ),
         out_shape=[shape, shape, TOKEN],
         compiler_params=params(16),
@@ -385,12 +395,43 @@
             grid=(1,),
             in_specs=[ANYWHERE] + [block_own] * 4 + [block_far] * 4 + [RESIDENT] * 2,
             out_specs=[block_out] * 4 + [TOKEN_SPEC],
+            scratch_shapes=[
+                pltpu.VMEM((4 * count * cells, 3 * features), jnp.bfloat16),
+                pltpu.VMEM((4 * count * cells, features), jnp.bfloat16),
+            ],
         ),
         out_shape=[shape] * 4 + [TOKEN],
         compiler_params=params(28),
         cost_estimate=moved(count * cells * features),
         name="temporal",
     )(place, before, *own, *far, *weights)
+
+
+def unpack_kernel(place, before, buffer, *refs):
+    *pieces, result = refs
+    for delta, piece in enumerate(pieces):
+
+        @pl.when(pl.program_id(0) == delta)
+        def _():
+            result[...] = piece[...]
+
+
+def run_unpack(place, before, buffer, pieces, chunk, shape):
+    piece = pieces[0].shape
+    return pl.pallas_call(
+        unpack_kernel,
+        grid_spec=pltpu.PrefetchScalarGridSpec(
+            num_scalar_prefetch=1,
+            grid=(4,),
+            in_specs=[ANYWHERE, ANYWHERE] + [RESIDENT] * 4,
+            out_specs=pl.BlockSpec(piece, lambda i, at: (0, 4 * chunk + (at[4] ^ i), 0, 0)),
+        ),
+        out_shape=pltpu.HBM(shape, pieces[0].dtype),
+        input_output_aliases={} if chunk == 0 else {2: 0},
+        compiler_params=params(8),
+        cost_estimate=moved(4 * pieces[0].size),
+        name="unpack",
+    )(place, before, buffer, *pieces)
 
 
 GROUP = ("far", "cell")
@@ -443,11 +484,9 @@
                 place, before, own, far[index], temporal_weights, index, units
             )
             outs.append([sent[0]] + [exchange(sent[delta], delta) for delta in (1, 2, 3)])
-    result = jnp.zeros_like(grouped)
+    result = before
     for index, received in enumerate(outs):
-        for delta in range(4):
-            at = (4 * index + (quarter ^ delta)) * units
-            result = lax.dynamic_update_slice_in_dim(result, received[delta], at, axis=1)
+        result = run_unpack(place, before, result, received, index, grouped.shape)
     return result.reshape(frames.shape)
 
 

time: 99.3 us -> 100 us (level)
  Pallas kernels: 38.7 us -> 42.6 us
  local copies, waits for them, and re-layouts: 3.59 us -> 1 us
  starting transfers between devices: 33.4 us -> 31 us
  waiting for transfers between devices: 23.1 us -> 25.5 us
    pallas_call x0 -> x2, Pallas kernels: none -> 4.09 us  [run_unpack(): pl.pallas_call(unpack_kernel, grid_spec=pltpu.PrefetchScalarGridSpec(num_...]
    ppermute x11, waiting for transfers between devices: 23.1 us -> 25.5 us  [exchange(): return lax.ppermute(piece, GROUP, [(i, i ^ delta) for i in range(4)])]
    ppermute x11, starting transfers between devices: 21.3 us -> 19.1 us  [exchange(): return lax.ppermute(piece, GROUP, [(i, i ^ delta) for i in range(4)])]
    dynamic_update_slice x8 -> x0, local copies, waits for them, and re-layouts: 1.2 us -> none  [paired(): lax.dynamic_update_slice_in_dim(result, received[delta], at, axis=1)]
    unnamed x24 -> x20, local copies, waits for them, and re-layouts: 2.08 us -> 0.92 us
  transfers between devices with their start and end apart: 18 -> 18, of which waited for: 5 -> 6; matrix products, arithmetic and copies ran while one was open for 1% -> 0% of each run, Pallas kernels for 36% -> 38%
where the time goes in v9:
time: 100 us
  Pallas kernels  42.6 us (43%)
  starting transfers between devices  31 us (31%)
  waiting for transfers between devices  25.5 us (26%)
  local copies, waits for them, and re-layouts  1 us (1%)
    ppermute x11, waiting for transfers between devices, exchange(): return lax.ppermute(piece, GROUP, [(i, i ^ delta) for i in range(4)])  25.5 us
    ppermute x11, starting transfers between devices, exchange(): return lax.ppermute(piece, GROUP, [(i, i ^ delta) for i in range(4)])  19.1 us
    pallas_call x3, Pallas kernels, run_section(): pl.pallas_call(section_kernel, grid_spec=pltpu.PrefetchScalarGridSpec(num...  18.8 us
    pallas_call x2, Pallas kernels, run_temporal(): pl.pallas_call(temporal_kernel, grid_spec=pltpu.PrefetchScalarGridSpec(nu...  15.9 us
    ppermute x3, starting transfers between devices, halo(): lax.ppermute(even, RING, leftward)  11.4 us
    pallas_call x2, Pallas kernels, run_unpack(): pl.pallas_call(unpack_kernel, grid_spec=pltpu.PrefetchScalarGridSpec(num_...  4.09 us
    pallas_call x1, Pallas kernels, run_pack(): pl.pallas_call(functools.partial(pack_kernel, chunks), grid_spec=pltpu.Pr...  2.27 us
  transfers between devices with their start and end apart: 18, of which 6 were waited for; matrix products, arithmetic and copies ran while one was open for 0% of the time, Pallas kernels for 38%

profile of v9, /device:TPU:0, one launch (start us, length us, event | category | flops | bytes accessed | tf_op | source)
XLA Modules:
  0.0 100.3 jit_solution(8001671579087547386)
XLA Ops:
  0.1 2.3 %pack.1 = (bf16[2,4,64,384]{3,2,1,0:T(8,128)(2,1)S(1)}, bf16[2,2,64,384]{3,2,1,0:T(8,128)(2,1)S(1)}, bf16[2,2,64,384]{3,2,1,0:T(8,128)(2,1)S(1)}, bf16[2,2,64,38...) custom-call(s32[5]{0:T(128)S(1)} %stack.31.place.before, bf16[2,16,64,384]{3,2,1,0:T(8,128)(2,1)} %bitcast.7, ...), custom_call_target="tpu_custom_call" | custom-call | bytes 786432 | tf_op jit(solution)/shard_map/pack/pallas_call | solution.py:198
  2.5 0.3 pack_weights.1.before.mine
  2.8 0.5 collective-permute-start.1
  3.3 2.6 %collective-permute-start = (bf16[2,4,64,384]{3,2,1,0:T(8,128)(2,1)S(1)}, bf16[2,4,64,384]{3,2,1,0:T(8,128)(2,1)S(1)}, u32[]{:S(2)}, u32[]{:S(2)}) collective-permute-start(bf16[2,4,64,384]{3,2,1,0:T(8,128)(2,1)S(1)} %get-tuple-element.35), channel_id=1, source_target_pairs={{0,2},{2,0},{16,18},{18,16},{1,3},{3,1},{17,19},{19,17},{4,6},{6,4... | collective-permute-start | bytes 1179656 | tf_op jit(solution)/shard_map/ppermute | solution.py:457
  5.9 2.6 %collective-permute-start.2 = (bf16[2,2,64,384]{3,2,1,0:T(8,128)(2,1)S(1)}, bf16[2,2,64,384]{3,2,1,0:T(8,128)(2,1)S(1)}, u32[]{:S(2)}, u32[]{:S(2)}) collective-permute-start(bf16[2,2,64,384]{3,2,1,0:T(8,128)(2,1)S(1)} %get-tuple-element.36.before), channel_id=1, source_target_pairs={{0,16},{2,18},{16,0},{18,2},{1,17},{3,19},{17,1},{19,3},{4,20},{6,... | collective-permute-start | bytes 589832 | tf_op jit(solution)/shard_map/ppermute | solution.py:457
  8.5 2.9 %collective-permute-start.4 = (bf16[2,2,64,384]{3,2,1,0:T(8,128)(2,1)S(1)}, bf16[2,2,64,384]{3,2,1,0:T(8,128)(2,1)S(1)}, u32[]{:S(2)}, u32[]{:S(2)}) collective-permute-start(bf16[2,2,64,384]{3,2,1,0:T(8,128)(2,1)S(1)} %get-tuple-element.44), channel_id=1, source_target_pairs={{0,16},{2,18},{16,0},{18,2},{1,17},{3,19},{17,1},{19,3},{4,20},{6,... | collective-permute-start | bytes 589832 | tf_op jit(solution)/shard_map/ppermute | solution.py:457
  11.4 1.2 %join_weights.1 = (bf16[384,1152]{1,0:T(8,128)(2,1)S(1)}, bf16[384,384]{1,0:T(8,128)(2,1)S(1)}, bf16[384,1536]{1,0:T(8,128)(2,1)S(1)}, bf16[1536,384]{1,0:T(8,12...) custom-call(s32[5]{0:T(128)S(1)} %stack.31.place.before, ...), custom_call_target="tpu_custom_call" | custom-call | bytes 1769472 | tf_op jit(solution)/shard_map/join_weights/pallas_call | solution.py:168
  12.5 3.1 %collective-permute-done.other = bf16[2,4,64,384]{3,2,1,0:T(8,128)(2,1)S(1)} collective-permute-done((bf16[2,4,64,384]{3,2,1,0:T(8,128)(2,1)S(1)}, bf16[2,4,64,384]{3,2,1,0:T(8,128)(2,1)S(1)}, u32[]{:S(2)}, u32[]{:S(2)}) %collective-permute-start) | collective-permute-done | bytes 393248 | tf_op jit(solution)/shard_map/ppermute | solution.py:457
  15.6 10.0 %section.3 = (bf16[4,128,384]{2,1,0:T(8,128)(2,1)}, bf16[4,128,384]{2,1,0:T(8,128)(2,1)}, f32[8,128]{1,0:T(8,128)S(1)}) custom-call(s32[5]{0:T(128)S(1)} %stack.31.place.before, s32[5]{0:T(128)S(1)} %stack.31.place.before, bf16[2,16,64,384]{3,2,1,0:T(8,128)(2,1)} %bitcast.13, bf16[2,4,64,384]{3,2,1,0:T(8,128)(2,1)S(1)} %collective-permute-done.other, ...), custom_call_target="tpu_custom_call" | custom-call | bytes 98304 | tf_op jit(solution)/shard_map/section/pallas_call | solution.py:369
  25.5 6.3 %collective-permute-start.7 = (bf16[4,128,384]{2,1,0:T(8,128)(2,1)}, bf16[4,128,384]{2,1,0:T(8,128)(2,1)S(1)}, u32[]{:S(2)}, u32[]{:S(2)}) collective-permute-start(bf16[4,128,384]{2,1,0:T(8,128)(2,1)} %get-tuple-element.47.refs_0_), channel_id=1, source_target_pairs={{1,0},{4,1},{5,4},{8,5},{9,8},{12,9},{13,12},{0,13},{3,2},{6,3},{7... | collective-permute-start | bytes 1179656 | tf_op jit(solution)/shard_map/ppermute | solution.py:460
  31.8 2.2 %collective-permute-start.5 = (bf16[2,2,64,384]{3,2,1,0:T(8,128)(2,1)S(1)}, bf16[2,2,64,384]{3,2,1,0:T(8,128)(2,1)S(1)}, u32[]{:S(2)}, u32[]{:S(2)}) collective-permute-start(bf16[2,2,64,384]{3,2,1,0:T(8,128)(2,1)S(1)} %get-tuple-element.45), channel_id=1, source_target_pairs={{0,18},{2,16},{16,2},{18,0},{1,19},{3,17},{17,3},{19,1},{4,22},{6,... | collective-permute-start | bytes 589832 | tf_op jit(solution)/shard_map/ppermute | solution.py:457
  34.1 4.4 %section.4 = (bf16[2,128,384]{2,1,0:T(8,128)(2,1)S(1)}, bf16[2,128,384]{2,1,0:T(8,128)(2,1)S(1)}, f32[8,128]{1,0:T(8,128)S(1)}) custom-call(s32[5]{0:T(128)S(1)} %stack.31.place.before, f32[8,128]{1,0:T(8,128)S(1)} %get-tuple-element.41.before, bf16[2,2,64,384]{3,2,1,0:T(8,128)(2,1)S(1)} %collective-permute-done.2.mine, ...), custom_call_target="tpu_custom_call" | custom-call | bytes 49152 | tf_op jit(solution)/shard_map/section/pallas_call | solution.py:369
  38.5 1.9 %collective-permute-start.9 = (bf16[2,128,384]{2,1,0:T(8,128)(2,1)S(1)}, bf16[2,128,384]{2,1,0:T(8,128)(2,1)S(1)}, u32[]{:S(2)}, u32[]{:S(2)}) collective-permute-start(bf16[2,128,384]{2,1,0:T(8,128)(2,1)S(1)} %get-tuple-element.49.refs_4_), channel_id=1, source_target_pairs={{1,0},{4,1},{5,4},{8,5},{9,8},{12,9},{13,12},{0,13},{3,2},{6,3},{7... | collective-permute-start | bytes 589832 | tf_op jit(solution)/shard_map/ppermute | solution.py:460
  40.4 2.0 %collective-permute-done.5.other = bf16[2,2,64,384]{3,2,1,0:T(8,128)(2,1)S(1)} collective-permute-done((bf16[2,2,64,384]{3,2,1,0:T(8,128)(2,1)S(1)}, bf16[2,2,64,384]{3,2,1,0:T(8,128)(2,1)S(1)}, u32[]{:S(2)}, u32[]{:S(2)}) %collective-permute-start.5) | collective-permute-done | bytes 196640 | tf_op jit(solution)/shard_map/ppermute | solution.py:457
  42.4 4.4 %section.5 = (bf16[2,128,384]{2,1,0:T(8,128)(2,1)S(1)}, bf16[2,128,384]{2,1,0:T(8,128)(2,1)S(1)}, f32[8,128]{1,0:T(8,128)S(1)}) custom-call(s32[5]{0:T(128)S(1)} %stack.31.place.before, f32[8,128]{1,0:T(8,128)S(1)} %get-tuple-element.43.before, bf16[2,2,64,384]{3,2,1,0:T(8,128)(2,1)S(1)} %collective-permute-done.4.mine, ...), custom_call_target="tpu_custom_call" | custom-call | bytes 49152 | tf_op jit(solution)/shard_map/section/pallas_call | solution.py:369
  46.8 3.2 %collective-permute-start.11 = (bf16[2,128,384]{2,1,0:T(8,128)(2,1)S(1)}, bf16[2,128,384]{2,1,0:T(8,128)(2,1)S(1)}, u32[]{:S(2)}, u32[]{:S(2)}) collective-permute-start(bf16[2,128,384]{2,1,0:T(8,128)(2,1)S(1)} %get-tuple-element.54.refs_4_), channel_id=1, source_target_pairs={{1,0},{4,1},{5,4},{8,5},{9,8},{12,9},{13,12},{0,13},{3,2},{6,3},{7... | collective-permute-start | bytes 589832 | tf_op jit(solution)/shard_map/ppermute | solution.py:460
  50.1 0.7 copy-done.8
  50.9 0.1 copy-done.9
  51.0 8.0 %temporal.2 = (bf16[2,2,64,384]{3,2,1,0:T(8,128)(2,1)}, bf16[2,2,64,384]{3,2,1,0:T(8,128)(2,1)}, bf16[2,2,64,384]{3,2,1,0:T(8,128)(2,1)}, bf16[2,2,64,384]{3,2,1,0:T(8,128)(2,1)}, f32[8,128]{1,0:T(8,128)S(1)}) custom-call(s32[5]{0:T(128)S(1)} %stack.31.place.before, f32[8,128]{1,0:T(8,128)S(1)} %get-tuple-element.46.before, ...), custom_call_target="tpu_custom_call" | custom-call | bytes 98304 | tf_op jit(solution)/shard_map/temporal/pallas_call | solution.py:391
  58.9 0.6 collective-permute-start.12
  59.5 2.6 %collective-permute-start.13 = (bf16[2,2,64,384]{3,2,1,0:T(8,128)(2,1)}, bf16[2,2,64,384]{3,2,1,0:T(8,128)(2,1)S(1)}, u32[]{:S(2)}, u32[]{:S(2)}) collective-permute-start(bf16[2,2,64,384]{3,2,1,0:T(8,128)(2,1)} %get-tuple-element.59), channel_id=1, source_target_pairs={{0,16},{2,18},{16,0},{18,2},{1,17},{3,19},{17,1},{19,3},{4,20},{6,... | collective-permute-start | bytes 589832 | tf_op jit(solution)/shard_map/ppermute | solution.py:457
  62.1 1.2 %collective-permute-start.14 = (bf16[2,2,64,384]{3,2,1,0:T(8,128)(2,1)}, bf16[2,2,64,384]{3,2,1,0:T(8,128)(2,1)S(1)}, u32[]{:S(2)}, u32[]{:S(2)}) collective-permute-start(bf16[2,2,64,384]{3,2,1,0:T(8,128)(2,1)} %get-tuple-element.60), channel_id=1, source_target_pairs={{0,18},{2,16},{16,2},{18,0},{1,19},{3,17},{17,3},{19,1},{4,22},{6,... | collective-permute-start | bytes 589832 | tf_op jit(solution)/shard_map/ppermute | solution.py:457
  63.3 8.0 %temporal.3 = (bf16[2,2,64,384]{3,2,1,0:T(8,128)(2,1)}, bf16[2,2,64,384]{3,2,1,0:T(8,128)(2,1)}, bf16[2,2,64,384]{3,2,1,0:T(8,128)(2,1)}, bf16[2,2,64,384]{3,2,1,0:T(8,128)(2,1)}, f32[8,128]{1,0:T(8,128)S(1)}) custom-call(s32[5]{0:T(128)S(1)} %stack.31.place.before, f32[8,128]{1,0:T(8,128)S(1)} %get-tuple-element.53.before, ...), custom_call_target="tpu_custom_call" | custom-call | bytes 98304 | tf_op jit(solution)/shard_map/temporal/pallas_call | solution.py:391
  71.3 0.6 collective-permute-start.15
  71.9 2.6 %collective-permute-start.16 = (bf16[2,2,64,384]{3,2,1,0:T(8,128)(2,1)}, bf16[2,2,64,384]{3,2,1,0:T(8,128)(2,1)S(1)}, u32[]{:S(2)}, u32[]{:S(2)}) collective-permute-start(bf16[2,2,64,384]{3,2,1,0:T(8,128)(2,1)} %get-tuple-element.63), channel_id=1, source_target_pairs={{0,16},{2,18},{16,0},{18,2},{1,17},{3,19},{17,1},{19,3},{4,20},{6,... | collective-permute-start | bytes 589832 | tf_op jit(solution)/shard_map/ppermute | solution.py:457
  74.5 1.2 %collective-permute-start.17 = (bf16[2,2,64,384]{3,2,1,0:T(8,128)(2,1)}, bf16[2,2,64,384]{3,2,1,0:T(8,128)(2,1)S(1)}, u32[]{:S(2)}, u32[]{:S(2)}) collective-permute-start(bf16[2,2,64,384]{3,2,1,0:T(8,128)(2,1)} %get-tuple-element.64), channel_id=1, source_target_pairs={{0,18},{2,16},{16,2},{18,0},{1,19},{3,17},{17,3},{19,1},{4,22},{6,... | collective-permute-start | bytes 589832 | tf_op jit(solution)/shard_map/ppermute | solution.py:457
  75.7 9.2 %collective-permute-done.13.refs_2_ = bf16[2,2,64,384]{3,2,1,0:T(8,128)(2,1)S(1)} collective-permute-done((bf16[2,2,64,384]{3,2,1,0:T(8,128)(2,1)}, bf16[2,2,64,384]{3,2,1,0:T(8,128)(2,1)S(1)}, u32[]{:S(2)}, u32[]{:S(2)}) %collective-permute-start.13) | collective-permute-done | bytes 196640 | tf_op jit(solution)/shard_map/ppermute | solution.py:457
  84.9 4.9 %collective-permute-done.14.refs_3_ = bf16[2,2,64,384]{3,2,1,0:T(8,128)(2,1)S(1)} collective-permute-done((bf16[2,2,64,384]{3,2,1,0:T(8,128)(2,1)}, bf16[2,2,64,384]{3,2,1,0:T(8,128)(2,1)S(1)}, u32[]{:S(2)}, u32[]{:S(2)}) %collective-permute-start.14) | collective-permute-done | bytes 196640 | tf_op jit(solution)/shard_map/ppermute | solution.py:457
  89.8 2.0 %unpack.2.buffer = bf16[2,16,64,384]{3,2,1,0:T(8,128)(2,1)} custom-call(s32[5]{0:T(128)S(1)} %stack.31.place.before, f32[8,128]{1,0:T(8,128)S(1)} %get-tuple-element.56.before.buffer, f32[8,128]{1,0:T(8,128)S(1)} %get-tuple-element.56.before.buffer, bf16[2,2,64,384]{3,2,1,0:T(8,128)(2,1)S(1)} %copy-done.6, ...), custom_call_target="tpu_custom_call" | custom-call | bytes 393216 | tf_op jit(solution)/shard_map/unpack/pallas_call | solution.py:421
  91.8 1.5 %collective-permute-done.16.refs_2_ = bf16[2,2,64,384]{3,2,1,0:T(8,128)(2,1)S(1)} collective-permute-done((bf16[2,2,64,384]{3,2,1,0:T(8,128)(2,1)}, bf16[2,2,64,384]{3,2,1,0:T(8,128)(2,1)S(1)}, u32[]{:S(2)}, u32[]{:S(2)}) %collective-permute-start.16) | collective-permute-done | bytes 196640 | tf_op jit(solution)/shard_map/ppermute | solution.py:457
  93.3 4.9 %collective-permute-done.17.refs_3_ = bf16[2,2,64,384]{3,2,1,0:T(8,128)(2,1)S(1)} collective-permute-done((bf16[2,2,64,384]{3,2,1,0:T(8,128)(2,1)}, bf16[2,2,64,384]{3,2,1,0:T(8,128)(2,1)S(1)}, u32[]{:S(2)}, u32[]{:S(2)}) %collective-permute-start.17) | collective-permute-done | bytes 196640 | tf_op jit(solution)/shard_map/ppermute | solution.py:457
  98.2 2.0 %unpack.3 = bf16[2,16,64,384]{3,2,1,0:T(8,128)(2,1)} custom-call(s32[5]{0:T(128)S(1)} %stack.31.place.before, f32[8,128]{1,0:T(8,128)S(1)} %get-tuple-element.56.before.buffer, bf16[2,16,64,384]{3,2,1,0:T(8,128)(2,1)} %unpack.2.buffer, bf16[2,2,64,384]{3,2,1,0:T(8,128)(2,1)S(1)} %copy-done.5, ...), custom_call_target="tpu_custom_call", output_to_operand_aliasing={{}: (2, {})} | custom-call | bytes 393216 | tf_op jit(solution)/shard_map/unpack/pallas_call | solution.py:421
  (35 shorter events, 0.2 us)
Async XLA Ops:
  0.1 2.3 %copy-start = (bf16[576,768]{1,0:T(8,128)(2,1)S(1)}, bf16[576,768]{1,0:T(8,128)(2,1)}, u32[]{:S(2)}) copy-start(bf16[576,768]{1,0:T(8,128)(2,1)} %refs_4_.1) | copy-start | bytes 2654212
  0.1 2.3 %copy-start.1 = (bf16[576,768]{1,0:T(8,128)(2,1)S(1)}, bf16[576,768]{1,0:T(8,128)(2,1)}, u32[]{:S(2)}) copy-start(bf16[576,768]{1,0:T(8,128)(2,1)} %refs_5_.1) | copy-start | bytes 2654212
  0.1 2.3 %copy-start.2 = (bf16[192,1536]{1,0:T(8,128)(2,1)S(1)}, bf16[192,1536]{1,0:T(8,128)(2,1)}, u32[]{:S(2)}) copy-start(bf16[192,1536]{1,0:T(8,128)(2,1)} %refs_2_.1) | copy-start | bytes 1769476
  0.1 2.3 %copy-start.3 = (bf16[768,384]{1,0:T(8,128)(2,1)S(1)}, bf16[768,384]{1,0:T(8,128)(2,1)}, u32[]{:S(2)}) copy-start(bf16[768,384]{1,0:T(8,128)(2,1)} %refs_3_.1) | copy-start | bytes 1769476
  0.1 2.3 %copy-start.4 = (bf16[192,1152]{1,0:T(8,128)(2,1)S(1)}, bf16[192,1152]{1,0:T(8,128)(2,1)}, u32[]{:S(2)}) copy-start(bf16[192,1152]{1,0:T(8,128)(2,1)} %refs_0_.1) | copy-start | bytes 1327108
  0.1 2.4 %copy-start.7 = (bf16[192,384]{1,0:T(8,128)(2,1)S(1)}, bf16[192,384]{1,0:T(8,128)(2,1)}, u32[]{:S(2)}) copy-start(bf16[192,384]{1,0:T(8,128)(2,1)} %refs_1_.1) | copy-start | bytes 442372
  2.8 8.6 %collective-permute-start.1 = (bf16[4608,384]{1,0:T(8,128)(2,1)S(1)}, bf16[4608,384]{1,0:T(8,128)(2,1)S(1)}, u32[]{:S(2)}, u32[]{:S(2)}) collective-permute-start(bf16[4608,384]{1,0:T(8,128)(2,1)S(1)} %pack_weights.1.before.mine), channel_id=1, source_target_pairs={{0,1},{1,0},{2,3},{3,2},{4,5},{5,4},{6,7},{7,6},{8,9},{9,8},{10,11... | collective-permute-start | bytes 10616840 | tf_op jit(solution)/shard_map/ppermute | solution.py:467
  3.3 12.3 %collective-permute-start = (bf16[2,4,64,384]{3,2,1,0:T(8,128)(2,1)S(1)}, bf16[2,4,64,384]{3,2,1,0:T(8,128)(2,1)S(1)}, u32[]{:S(2)}, u32[]{:S(2)}) collective-permute-start(bf16[2,4,64,384]{3,2,1,0:T(8,128)(2,1)S(1)} %get-tuple-element.35), channel_id=1, source_target_pairs={{0,2},{2,0},{16,18},{18,16},{1,3},{3,1},{17,19},{19,17},{4,6},{6,4... | collective-permute-start | bytes 1179656 | tf_op jit(solution)/shard_map/ppermute | solution.py:457
  5.9 28.2 %collective-permute-start.2 = (bf16[2,2,64,384]{3,2,1,0:T(8,128)(2,1)S(1)}, bf16[2,2,64,384]{3,2,1,0:T(8,128)(2,1)S(1)}, u32[]{:S(2)}, u32[]{:S(2)}) collective-permute-start(bf16[2,2,64,384]{3,2,1,0:T(8,128)(2,1)S(1)} %get-tuple-element.36.before), channel_id=1, source_target_pairs={{0,16},{2,18},{16,0},{18,2},{1,17},{3,19},{17,1},{19,3},{4,20},{6,... | collective-permute-start | bytes 589832 | tf_op jit(solution)/shard_map/ppermute | solution.py:457
  8.5 23.4 %collective-permute-start.3 = (bf16[2,2,64,384]{3,2,1,0:T(8,128)(2,1)S(1)}, bf16[2,2,64,384]{3,2,1,0:T(8,128)(2,1)S(1)}, u32[]{:S(2)}, u32[]{:S(2)}) collective-permute-start(bf16[2,2,64,384]{3,2,1,0:T(8,128)(2,1)S(1)} %get-tuple-element.42), channel_id=1, source_target_pairs={{0,18},{2,16},{16,2},{18,0},{1,19},{3,17},{17,3},{19,1},{4,22},{6,... | collective-permute-start | bytes 589832 | tf_op jit(solution)/shard_map/ppermute | solution.py:457
  8.5 31.9 %collective-permute-start.4 = (bf16[2,2,64,384]{3,2,1,0:T(8,128)(2,1)S(1)}, bf16[2,2,64,384]{3,2,1,0:T(8,128)(2,1)S(1)}, u32[]{:S(2)}, u32[]{:S(2)}) collective-permute-start(bf16[2,2,64,384]{3,2,1,0:T(8,128)(2,1)S(1)} %get-tuple-element.44), channel_id=1, source_target_pairs={{0,16},{2,18},{16,0},{18,2},{1,17},{3,19},{17,1},{19,3},{4,20},{6,... | collective-permute-start | bytes 589832 | tf_op jit(solution)/shard_map/ppermute | solution.py:457
  25.5 24.5 %collective-permute-start.7 = (bf16[4,128,384]{2,1,0:T(8,128)(2,1)}, bf16[4,128,384]{2,1,0:T(8,128)(2,1)S(1)}, u32[]{:S(2)}, u32[]{:S(2)}) collective-permute-start(bf16[4,128,384]{2,1,0:T(8,128)(2,1)} %get-tuple-element.47.refs_0_), channel_id=1, source_target_pairs={{1,0},{4,1},{5,4},{8,5},{9,8},{12,9},{13,12},{0,13},{3,2},{6,3},{7... | collective-permute-start | bytes 1179656 | tf_op jit(solution)/shard_map/ppermute | solution.py:460
  31.8 18.3 %collective-permute-start.6 = (bf16[4,128,384]{2,1,0:T(8,128)(2,1)}, bf16[4,128,384]{2,1,0:T(8,128)(2,1)S(1)}, u32[]{:S(2)}, u32[]{:S(2)}) collective-permute-start(bf16[4,128,384]{2,1,0:T(8,128)(2,1)} %get-tuple-element.48.refs_1_), channel_id=1, source_target_pairs={{0,1},{1,4},{4,5},{5,8},{8,9},{9,12},{12,13},{13,0},{2,3},{3,6},{6... | collective-permute-start | bytes 1179656 | tf_op jit(solution)/shard_map/ppermute | solution.py:460
  31.8 10.6 %collective-permute-start.5 = (bf16[2,2,64,384]{3,2,1,0:T(8,128)(2,1)S(1)}, bf16[2,2,64,384]{3,2,1,0:T(8,128)(2,1)S(1)}, u32[]{:S(2)}, u32[]{:S(2)}) collective-permute-start(bf16[2,2,64,384]{3,2,1,0:T(8,128)(2,1)S(1)} %get-tuple-element.45), channel_id=1, source_target_pairs={{0,18},{2,16},{16,2},{18,0},{1,19},{3,17},{17,3},{19,1},{4,22},{6,... | collective-permute-start | bytes 589832 | tf_op jit(solution)/shard_map/ppermute | solution.py:457
  38.5 11.6 %collective-permute-start.9 = (bf16[2,128,384]{2,1,0:T(8,128)(2,1)S(1)}, bf16[2,128,384]{2,1,0:T(8,128)(2,1)S(1)}, u32[]{:S(2)}, u32[]{:S(2)}) collective-permute-start(bf16[2,128,384]{2,1,0:T(8,128)(2,1)S(1)} %get-tuple-element.49.refs_4_), channel_id=1, source_target_pairs={{1,0},{4,1},{5,4},{8,5},{9,8},{12,9},{13,12},{0,13},{3,2},{6,3},{7... | collective-permute-start | bytes 589832 | tf_op jit(solution)/shard_map/ppermute | solution.py:460
  40.4 9.7 %collective-permute-start.8 = (bf16[2,128,384]{2,1,0:T(8,128)(2,1)S(1)}, bf16[2,128,384]{2,1,0:T(8,128)(2,1)S(1)}, u32[]{:S(2)}, u32[]{:S(2)}) collective-permute-start(bf16[2,128,384]{2,1,0:T(8,128)(2,1)S(1)} %get-tuple-element.50.refs_5_), channel_id=1, source_target_pairs={{0,1},{1,4},{4,5},{5,8},{8,9},{9,12},{12,13},{13,0},{2,3},{3,6},{6... | collective-permute-start | bytes 589832 | tf_op jit(solution)/shard_map/ppermute | solution.py:460
  46.8 16.5 %collective-permute-start.11 = (bf16[2,128,384]{2,1,0:T(8,128)(2,1)S(1)}, bf16[2,128,384]{2,1,0:T(8,128)(2,1)S(1)}, u32[]{:S(2)}, u32[]{:S(2)}) collective-permute-start(bf16[2,128,384]{2,1,0:T(8,128)(2,1)S(1)} %get-tuple-element.54.refs_4_), channel_id=1, source_target_pairs={{1,0},{4,1},{5,4},{8,5},{9,8},{12,9},{13,12},{0,13},{3,2},{6,3},{7... | collective-permute-start | bytes 589832 | tf_op jit(solution)/shard_map/ppermute | solution.py:460
  50.1 13.3 %collective-permute-start.10 = (bf16[2,128,384]{2,1,0:T(8,128)(2,1)S(1)}, bf16[2,128,384]{2,1,0:T(8,128)(2,1)S(1)}, u32[]{:S(2)}, u32[]{:S(2)}) collective-permute-start(bf16[2,128,384]{2,1,0:T(8,128)(2,1)S(1)} %get-tuple-element.55.refs_5_), channel_id=1, source_target_pairs={{0,1},{1,4},{4,5},{5,8},{8,9},{9,12},{12,13},{13,0},{2,3},{3,6},{6... | collective-permute-start | bytes 589832 | tf_op jit(solution)/shard_map/ppermute | solution.py:460
  50.1 0.8 copy-start.8
  50.1 0.9 copy-start.9
  58.9 15.6 %collective-permute-start.12 = (bf16[2,2,64,384]{3,2,1,0:T(8,128)(2,1)}, bf16[2,2,64,384]{3,2,1,0:T(8,128)(2,1)S(1)}, u32[]{:S(2)}, u32[]{:S(2)}) collective-permute-start(bf16[2,2,64,384]{3,2,1,0:T(8,128)(2,1)} %get-tuple-element.58), channel_id=1, source_target_pairs={{0,2},{2,0},{16,18},{18,16},{1,3},{3,1},{17,19},{19,17},{4,6},{6,4... | collective-permute-start | bytes 589832 | tf_op jit(solution)/shard_map/ppermute | solution.py:457
  59.5 25.4 %collective-permute-start.13 = (bf16[2,2,64,384]{3,2,1,0:T(8,128)(2,1)}, bf16[2,2,64,384]{3,2,1,0:T(8,128)(2,1)S(1)}, u32[]{:S(2)}, u32[]{:S(2)}) collective-permute-start(bf16[2,2,64,384]{3,2,1,0:T(8,128)(2,1)} %get-tuple-element.59), channel_id=1, source_target_pairs={{0,16},{2,18},{16,0},{18,2},{1,17},{3,19},{17,1},{19,3},{4,20},{6,... | collective-permute-start | bytes 589832 | tf_op jit(solution)/shard_map/ppermute | solution.py:457
  62.1 27.7 %collective-permute-start.14 = (bf16[2,2,64,384]{3,2,1,0:T(8,128)(2,1)}, bf16[2,2,64,384]{3,2,1,0:T(8,128)(2,1)S(1)}, u32[]{:S(2)}, u32[]{:S(2)}) collective-permute-start(bf16[2,2,64,384]{3,2,1,0:T(8,128)(2,1)} %get-tuple-element.60), channel_id=1, source_target_pairs={{0,18},{2,16},{16,2},{18,0},{1,19},{3,17},{17,3},{19,1},{4,22},{6,... | collective-permute-start | bytes 589832 | tf_op jit(solution)/shard_map/ppermute | solution.py:457
  63.3 26.5 %copy-start.6 = (bf16[2,2,64,384]{3,2,1,0:T(8,128)(2,1)S(1)}, bf16[2,2,64,384]{3,2,1,0:T(8,128)(2,1)}, u32[]{:S(2)}) copy-start(bf16[2,2,64,384]{3,2,1,0:T(8,128)(2,1)} %get-tuple-element.57.refs_0_) | copy-start | bytes 589828
  71.3 26.9 %copy-start.5 = (bf16[2,2,64,384]{3,2,1,0:T(8,128)(2,1)S(1)}, bf16[2,2,64,384]{3,2,1,0:T(8,128)(2,1)}, u32[]{:S(2)}) copy-start(bf16[2,2,64,384]{3,2,1,0:T(8,128)(2,1)} %get-tuple-element.61.refs_0_) | copy-start | bytes 589828
  71.3 20.5 %collective-permute-start.15 = (bf16[2,2,64,384]{3,2,1,0:T(8,128)(2,1)}, bf16[2,2,64,384]{3,2,1,0:T(8,128)(2,1)S(1)}, u32[]{:S(2)}, u32[]{:S(2)}) collective-permute-start(bf16[2,2,64,384]{3,2,1,0:T(8,128)(2,1)} %get-tuple-element.62), channel_id=1, source_target_pairs={{0,2},{2,0},{16,18},{18,16},{1,3},{3,1},{17,19},{19,17},{4,6},{6,4... | collective-permute-start | bytes 589832 | tf_op jit(solution)/shard_map/ppermute | solution.py:457
  71.9 21.4 %collective-permute-start.16 = (bf16[2,2,64,384]{3,2,1,0:T(8,128)(2,1)}, bf16[2,2,64,384]{3,2,1,0:T(8,128)(2,1)S(1)}, u32[]{:S(2)}, u32[]{:S(2)}) collective-permute-start(bf16[2,2,64,384]{3,2,1,0:T(8,128)(2,1)} %get-tuple-element.63), channel_id=1, source_target_pairs={{0,16},{2,18},{16,0},{18,2},{1,17},{3,19},{17,1},{19,3},{4,20},{6,... | collective-permute-start | bytes 589832 | tf_op jit(solution)/shard_map/ppermute | solution.py:457
  74.5 23.7 %collective-permute-start.17 = (bf16[2,2,64,384]{3,2,1,0:T(8,128)(2,1)}, bf16[2,2,64,384]{3,2,1,0:T(8,128)(2,1)S(1)}, u32[]{:S(2)}, u32[]{:S(2)}) collective-permute-start(bf16[2,2,64,384]{3,2,1,0:T(8,128)(2,1)} %get-tuple-element.64), channel_id=1, source_target_pairs={{0,18},{2,16},{16,2},{18,0},{1,19},{3,17},{17,3},{19,1},{4,22},{6,... | collective-permute-start | bytes 589832 | tf_op jit(solution)/shard_map/ppermute | solution.py:457

commit v10 on v8

--- a/solution.py
+++ b/solution.py
@@ -201,8 +201,7 @@
             num_scalar_prefetch=1,
             grid=(1,),
             in_specs=[source(*piece) for piece in beside + wanted],
-            out_specs=[pl.BlockSpec(whole, lambda i, at: (0, 0, 0, 0))]
-            + [pl.BlockSpec(shape, lambda i, at: (0, 0, 0, 0))] * len(wanted),
+            out_specs=[RESIDENT] * (1 + len(wanted)),
         ),
         out_shape=[jax.ShapeDtypeStruct(whole, grouped.dtype)]
         + [jax.ShapeDtypeStruct(shape, grouped.dtype)] * len(wanted),
@@ -304,12 +303,13 @@
     return center + jnp.tanh(preact[:, :features]) * opened
 
 
-def temporal_kernel(place, before, *refs):
+def temporal_kernel(chunk, place, before, *refs):
     *fields, w_first, w_second, out0, out1, out2, out3, token = refs
     token[...] = jnp.zeros_like(token)
     near, is_first, is_last = place[1], place[2], place[3]
-    units, cells, features = fields[0].shape
-    flat = [field[...].reshape(units * cells, features) for field in fields]
+    units, cells, features = fields[4].shape
+    spans = [slice(chunk * units, (chunk + 1) * units)] * 4 + [slice(0, units)] * 4
+    flat = [field[at].reshape(units * cells, features) for field, at in zip(fields, spans)]
     zero = jnp.zeros_like(flat[0])
     pairs = [(flat[i], flat[i + 4]) for i in range(4)]
     even_n, odd_n, left_a, right_a = [jnp.where(near == 0, a, b) for a, b in pairs]
@@ -355,15 +355,15 @@
     piece = pl.BlockSpec(shape_in, lambda i, at: (0, i, 0, 0))
     own = pl.BlockSpec(shape_in, lambda i, at: (0, 4 * i + at[4], 0, 0))
     block_out = pl.BlockSpec((units, 2 * half, features), lambda i, at: (i, 0, 0))
-    place_out = pltpu.HBM if from_frames else jax.ShapeDtypeStruct
-    shape = place_out((chunks * units, 2 * half, features), jnp.bfloat16)
+    shape = jax.ShapeDtypeStruct((chunks * units, 2 * half, features), jnp.bfloat16)
     return pl.pallas_call(
         section_kernel,
         grid_spec=pltpu.PrefetchScalarGridSpec(
             num_scalar_prefetch=1,
             grid=(chunks,),
-            in_specs=[ANYWHERE, own if from_frames else piece, piece] + [RESIDENT] * 4,
-            out_specs=[block_out, block_out, TOKEN_SPEC],
+            in_specs=([ANYWHERE, own, piece] if from_frames else [ANYWHERE, RESIDENT, RESIDENT])
+            + [RESIDENT] * 4,
+            out_specs=([block_out] * 2 if from_frames else [RESIDENT] * 2) + [TOKEN_SPEC],
         ),
         out_shape=[shape, shape, TOKEN],
         compiler_params=params(16),
@@ -372,22 +372,22 @@
     )(place, before, mine, other, *weights)
 
 
-def run_temporal(place, before, own, far, weights, chunk, count):
+def run_temporal(place, before, own, far, weights, chunk, count, last):
     _, cells, features = own[0].shape
+    shape = (2, count, cells // 2, features)
+    block_out = pl.BlockSpec(shape, lambda i, at: (0, 0, 0, 0))
     block_own = pl.BlockSpec((count, cells, features), lambda i, at: (chunk, 0, 0))
-    block_far = pl.BlockSpec((count, cells, features), lambda i, at: (0, 0, 0))
-    block_out = pl.BlockSpec((2, count, cells // 2, features), lambda i, at: (0, 0, 0, 0))
-    shape = pltpu.HBM((2, count, cells // 2, features), jnp.bfloat16)
+    kept = (jax.ShapeDtypeStruct if last else pltpu.HBM)(shape, jnp.bfloat16)
     return pl.pallas_call(
-        temporal_kernel,
+        functools.partial(temporal_kernel, 0 if last else chunk),
         grid_spec=pltpu.PrefetchScalarGridSpec(
             num_scalar_prefetch=1,
             grid=(1,),
-            in_specs=[ANYWHERE] + [block_own] * 4 + [block_far] * 4 + [RESIDENT] * 2,
-            out_specs=[block_out] * 4 + [TOKEN_SPEC],
+            in_specs=[ANYWHERE] + [block_own if last else RESIDENT] * 4 + [RESIDENT] * 6,
+            out_specs=[RESIDENT if last else block_out] * 4 + [TOKEN_SPEC],
         ),
-        out_shape=[shape] * 4 + [TOKEN],
-        compiler_params=params(28),
+        out_shape=[kept] * 4 + [TOKEN],
+        compiler_params=params(24),
         cost_estimate=moved(count * cells * features),
         name="temporal",
     )(place, before, *own, *far, *weights)
@@ -430,7 +430,7 @@
     even, odd, before = run_section(
         place, place, pinned, beside, section_weights, units, CHUNKS, True
     )
-    own = [pltpu.with_memory_space_constraint(field, pltpu.HBM) for field in halo(even, odd)]
+    own = halo(even, odd)
     far, outs = [], []
     for kind, index in ORDER:
         if kind == "s":
@@ -440,7 +440,7 @@
             far.append(halo(even, odd))
         else:
             *sent, before = run_temporal(
-                place, before, own, far[index], temporal_weights, index, units
+                place, before, own, far[index], temporal_weights, index, units, index == CHUNKS - 1
             )
             outs.append([sent[0]] + [exchange(sent[delta], delta) for delta in (1, 2, 3)])
     result = jnp.zeros_like(grouped)

time: 99.3 us -> 97.4 us (0.981)
  local copies, waits for them, and re-layouts: 3.59 us -> 6.7 us
  waiting for transfers between devices: 23.1 us -> 20.4 us
  Pallas kernels: 38.7 us -> 36.2 us
    unnamed x24 -> x32, local copies, waits for them, and re-layouts: 2.08 us -> 5.19 us
    ppermute x11, waiting for transfers between devices: 23.1 us -> 20.3 us  [exchange(): return lax.ppermute(piece, GROUP, [(i, i ^ delta) for i in range(4)])]
    pallas_call x2, Pallas kernels: 15.5 us -> 13.7 us  [run_temporal(): pl.pallas_call(functools.partial(temporal_kernel, 0 if last else chunk),...]
  transfers between devices with their start and end apart: 18 -> 18, of which waited for: 5 -> 4; matrix products, arithmetic and copies ran while one was open for 1% -> 1% of each run, Pallas kernels for 36% -> 35%
where the time goes in v10:
time: 97.4 us; the launch traced here: 97 us
  Pallas kernels  36.2 us (37%)
  starting transfers between devices  33.4 us (34%)
  waiting for transfers between devices  20.4 us (21%)
  local copies, waits for them, and re-layouts  6.7 us (7%)
    ppermute x11, starting transfers between devices, exchange(): return lax.ppermute(piece, GROUP, [(i, i ^ delta) for i in range(4)])  21.2 us
    ppermute x11, waiting for transfers between devices, exchange(): return lax.ppermute(piece, GROUP, [(i, i ^ delta) for i in range(4)])  20.3 us
    pallas_call x3, Pallas kernels, run_section(): pl.pallas_call(section_kernel, grid_spec=pltpu.PrefetchScalarGridSpec(num...  18.8 us
    pallas_call x2, Pallas kernels, run_temporal(): pl.pallas_call(functools.partial(temporal_kernel, 0 if last else chunk),...  13.7 us
    ppermute x3, starting transfers between devices, halo(): lax.ppermute(even, RING, leftward)  11.6 us
    unnamed x32, local copies, waits for them, and re-layouts  5.19 us
    pallas_call x1, Pallas kernels, run_pack(): pl.pallas_call(functools.partial(pack_kernel, chunks), grid_spec=pltpu.Pr...  2.27 us
  transfers between devices with their start and end apart: 18, of which 4 were waited for; matrix products, arithmetic and copies ran while one was open for 1% of the time, Pallas kernels for 35%

profile of v10, /device:TPU:0, one launch (start us, length us, event | category | flops | bytes accessed | tf_op | source)
XLA Modules:
  0.0 97.0 jit_solution(7660419197774771675)
XLA Ops:
  0.1 2.3 %pack.1 = (bf16[2,4,64,384]{3,2,1,0:T(8,128)(2,1)S(1)}, bf16[2,2,64,384]{3,2,1,0:T(8,128)(2,1)S(1)}, bf16[2,2,64,384]{3,2,1,0:T(8,128)(2,1)S(1)}, bf16[2,2,64,38...) custom-call(s32[5]{0:T(128)S(1)} %stack.31.place.before, bf16[2,16,64,384]{3,2,1,0:T(8,128)(2,1)} %bitcast.7, ...), custom_call_target="tpu_custom_call" | custom-call | bytes 786432 | tf_op jit(solution)/shard_map/pack/pallas_call | solution.py:198
  2.5 0.3 pack_weights.1.before.mine
  2.8 0.5 collective-permute-start.1
  3.3 2.6 %collective-permute-start = (bf16[2,4,64,384]{3,2,1,0:T(8,128)(2,1)S(1)}, bf16[2,4,64,384]{3,2,1,0:T(8,128)(2,1)S(1)}, u32[]{:S(2)}, u32[]{:S(2)}) collective-permute-start(bf16[2,4,64,384]{3,2,1,0:T(8,128)(2,1)S(1)} %get-tuple-element.34), channel_id=1, source_target_pairs={{0,2},{2,0},{16,18},{18,16},{1,3},{3,1},{17,19},{19,17},{4,6},{6,4... | collective-permute-start | bytes 1179656 | tf_op jit(solution)/shard_map/ppermute | solution.py:416
  5.9 2.6 %collective-permute-start.2 = (bf16[2,2,64,384]{3,2,1,0:T(8,128)(2,1)S(1)}, bf16[2,2,64,384]{3,2,1,0:T(8,128)(2,1)S(1)}, u32[]{:S(2)}, u32[]{:S(2)}) collective-permute-start(bf16[2,2,64,384]{3,2,1,0:T(8,128)(2,1)S(1)} %get-tuple-element.35.before), channel_id=1, source_target_pairs={{0,16},{2,18},{16,0},{18,2},{1,17},{3,19},{17,1},{19,3},{4,20},{6,... | collective-permute-start | bytes 589832 | tf_op jit(solution)/shard_map/ppermute | solution.py:416
  8.5 2.9 %collective-permute-start.4 = (bf16[2,2,64,384]{3,2,1,0:T(8,128)(2,1)S(1)}, bf16[2,2,64,384]{3,2,1,0:T(8,128)(2,1)S(1)}, u32[]{:S(2)}, u32[]{:S(2)}) collective-permute-start(bf16[2,2,64,384]{3,2,1,0:T(8,128)(2,1)S(1)} %get-tuple-element.43), channel_id=1, source_target_pairs={{0,16},{2,18},{16,0},{18,2},{1,17},{3,19},{17,1},{19,3},{4,20},{6,... | collective-permute-start | bytes 589832 | tf_op jit(solution)/shard_map/ppermute | solution.py:416
  11.4 1.2 %join_weights.1 = (bf16[384,1152]{1,0:T(8,128)(2,1)S(1)}, bf16[384,384]{1,0:T(8,128)(2,1)S(1)}, bf16[384,1536]{1,0:T(8,128)(2,1)S(1)}, bf16[1536,384]{1,0:T(8,12...) custom-call(s32[5]{0:T(128)S(1)} %stack.31.place.before, ...), custom_call_target="tpu_custom_call" | custom-call | bytes 1769472 | tf_op jit(solution)/shard_map/join_weights/pallas_call | solution.py:168
  12.5 3.1 %collective-permute-done.other = bf16[2,4,64,384]{3,2,1,0:T(8,128)(2,1)S(1)} collective-permute-done((bf16[2,4,64,384]{3,2,1,0:T(8,128)(2,1)S(1)}, bf16[2,4,64,384]{3,2,1,0:T(8,128)(2,1)S(1)}, u32[]{:S(2)}, u32[]{:S(2)}) %collective-permute-start) | collective-permute-done | bytes 393248 | tf_op jit(solution)/shard_map/ppermute | solution.py:416
  15.6 9.3 %section.3 = (bf16[4,128,384]{2,1,0:T(8,128)(2,1)S(1)}, bf16[4,128,384]{2,1,0:T(8,128)(2,1)S(1)}, f32[8,128]{1,0:T(8,128)S(1)}) custom-call(s32[5]{0:T(128)S(1)} %stack.31.place.before, s32[5]{0:T(128)S(1)} %stack.31.place.before, bf16[2,16,64,384]{3,2,1,0:T(8,128)(2,1)} %bitcast.13, bf16[2,4,64,384]{3,2,1,0:T(8,128)(2,1)S(1)} %collective-permute-done.other, ...), custom_call_target="tpu_custom_call" | custom-call | bytes 98304 | tf_op jit(solution)/shard_map/section/pallas_call | solution.py:359
  25.0 6.3 %collective-permute-start.7 = (bf16[4,128,384]{2,1,0:T(8,128)(2,1)S(1)}, bf16[4,128,384]{2,1,0:T(8,128)(2,1)S(1)}, u32[]{:S(2)}, u32[]{:S(2)}) collective-permute-start(bf16[4,128,384]{2,1,0:T(8,128)(2,1)S(1)} %get-tuple-element.46.refs_0_), channel_id=1, source_target_pairs={{1,0},{4,1},{5,4},{8,5},{9,8},{12,9},{13,12},{0,13},{3,2},{6,3},{7... | collective-permute-start | bytes 1179656 | tf_op jit(solution)/shard_map/ppermute | solution.py:419
  31.3 4.3 %collective-permute-start.5 = (bf16[2,2,64,384]{3,2,1,0:T(8,128)(2,1)S(1)}, bf16[2,2,64,384]{3,2,1,0:T(8,128)(2,1)S(1)}, u32[]{:S(2)}, u32[]{:S(2)}) collective-permute-start(bf16[2,2,64,384]{3,2,1,0:T(8,128)(2,1)S(1)} %get-tuple-element.44), channel_id=1, source_target_pairs={{0,18},{2,16},{16,2},{18,0},{1,19},{3,17},{17,3},{19,1},{4,22},{6,... | collective-permute-start | bytes 589832 | tf_op jit(solution)/shard_map/ppermute | solution.py:416
  35.6 4.4 %section.4 = (bf16[2,128,384]{2,1,0:T(8,128)(2,1)S(1)}, bf16[2,128,384]{2,1,0:T(8,128)(2,1)S(1)}, f32[8,128]{1,0:T(8,128)S(1)}) custom-call(s32[5]{0:T(128)S(1)} %stack.31.place.before, f32[8,128]{1,0:T(8,128)S(1)} %get-tuple-element.40.before, bf16[2,2,64,384]{3,2,1,0:T(8,128)(2,1)S(1)} %collective-permute-done.2.mine, ...), custom_call_target="tpu_custom_call" | custom-call | bytes 49152 | tf_op jit(solution)/shard_map/section/pallas_call | solution.py:359
  40.1 2.6 %collective-permute-start.9 = (bf16[2,128,384]{2,1,0:T(8,128)(2,1)S(1)}, bf16[2,128,384]{2,1,0:T(8,128)(2,1)S(1)}, u32[]{:S(2)}, u32[]{:S(2)}) collective-permute-start(bf16[2,128,384]{2,1,0:T(8,128)(2,1)S(1)} %get-tuple-element.48.refs_4_), channel_id=1, source_target_pairs={{1,0},{4,1},{5,4},{8,5},{9,8},{12,9},{13,12},{0,13},{3,2},{6,3},{7... | collective-permute-start | bytes 589832 | tf_op jit(solution)/shard_map/ppermute | solution.py:419
  42.7 5.1 %section.5 = (bf16[2,128,384]{2,1,0:T(8,128)(2,1)}, bf16[2,128,384]{2,1,0:T(8,128)(2,1)}, f32[8,128]{1,0:T(8,128)S(1)}) custom-call(s32[5]{0:T(128)S(1)} %stack.31.place.before, f32[8,128]{1,0:T(8,128)S(1)} %get-tuple-element.42.before, bf16[2,2,64,384]{3,2,1,0:T(8,128)(2,1)S(1)} %collective-permute-done.4.mine, ...), custom_call_target="tpu_custom_call" | custom-call | bytes 49152 | tf_op jit(solution)/shard_map/section/pallas_call | solution.py:359
  47.9 2.6 %collective-permute-start.14 = (bf16[2,128,384]{2,1,0:T(8,128)(2,1)}, bf16[2,128,384]{2,1,0:T(8,128)(2,1)}, u32[]{:S(2)}, u32[]{:S(2)}) collective-permute-start(bf16[2,128,384]{2,1,0:T(8,128)(2,1)} %get-tuple-element.57.refs_4_), channel_id=1, source_target_pairs={{1,0},{4,1},{5,4},{8,5},{9,8},{12,9},{13,12},{0,13},{3,2},{6,3},{7... | collective-permute-start | bytes 589832 | tf_op jit(solution)/shard_map/ppermute | solution.py:419
  50.5 6.4 %temporal.2 = (bf16[2,2,64,384]{3,2,1,0:T(8,128)(2,1)}, bf16[2,2,64,384]{3,2,1,0:T(8,128)(2,1)}, bf16[2,2,64,384]{3,2,1,0:T(8,128)(2,1)}, bf16[2,2,64,384]{3,2,1,0:T(8,128)(2,1)}, f32[8,128]{1,0:T(8,128)S(1)}) custom-call(s32[5]{0:T(128)S(1)} %stack.31.place.before, f32[8,128]{1,0:T(8,128)S(1)} %get-tuple-element.45.before, ...), custom_call_target="tpu_custom_call" | custom-call | bytes 98304 | tf_op jit(solution)/shard_map/temporal/pallas_call | solution.py:381
  57.0 0.5 collective-permute-start.10
  57.5 3.7 %collective-permute-start.11 = (bf16[2,2,64,384]{3,2,1,0:T(8,128)(2,1)}, bf16[2,2,64,384]{3,2,1,0:T(8,128)(2,1)S(1)}, u32[]{:S(2)}, u32[]{:S(2)}) collective-permute-start(bf16[2,2,64,384]{3,2,1,0:T(8,128)(2,1)} %get-tuple-element.54), channel_id=1, source_target_pairs={{0,16},{2,18},{16,0},{18,2},{1,17},{3,19},{17,1},{19,3},{4,20},{6,... | collective-permute-start | bytes 589832 | tf_op jit(solution)/shard_map/ppermute | solution.py:416
  61.4 1.0 %copy-done.1 = bf16[4,128,384]{2,1,0:T(8,128)(2,1)S(1)} copy-done((bf16[4,128,384]{2,1,0:T(8,128)(2,1)S(1)}, bf16[4,128,384]{2,1,0:T(8,128)(2,1)}, u32[]{:S(2)}) %copy-start.1) | copy-done | bytes 393240
  62.4 1.0 %copy-done.3 = bf16[4,128,384]{2,1,0:T(8,128)(2,1)S(1)} copy-done((bf16[4,128,384]{2,1,0:T(8,128)(2,1)S(1)}, bf16[4,128,384]{2,1,0:T(8,128)(2,1)}, u32[]{:S(2)}) %copy-start.3) | copy-done | bytes 393240
  63.3 1.0 %copy-done.5 = bf16[4,128,384]{2,1,0:T(8,128)(2,1)S(1)} copy-done((bf16[4,128,384]{2,1,0:T(8,128)(2,1)S(1)}, bf16[4,128,384]{2,1,0:T(8,128)(2,1)}, u32[]{:S(2)}) %copy-start.5) | copy-done | bytes 393240
  64.3 1.0 %copy-done.7 = bf16[4,128,384]{2,1,0:T(8,128)(2,1)S(1)} copy-done((bf16[4,128,384]{2,1,0:T(8,128)(2,1)S(1)}, bf16[4,128,384]{2,1,0:T(8,128)(2,1)}, u32[]{:S(2)}) %copy-start.7) | copy-done | bytes 393240
  65.3 7.3 %temporal.3 = (bf16[2,2,64,384]{3,2,1,0:T(8,128)(2,1)S(1)}, bf16[2,2,64,384]{3,2,1,0:T(8,128)(2,1)S(1)}, bf16[2,2,64,384]{3,2,1,0:T(8,128)(2,1)S(1)}, bf16[2,2,64,384]{3,2,1,0:T(8,128)(2,1)S(1)}, f32[8,128]{1,0:T(8,128)}) custom-call(s32[5]{0:T(128)S(1)} %stack.31.place.before, f32[8,128]{1,0:T(8,128)S(1)} %get-tuple-element.56.before, ...), custom_call_target="tpu_custom_call" | custom-call | bytes 98304 | tf_op jit(solution)/shard_map/temporal/pallas_call | solution.py:381
  72.6 1.3 %collective-permute-start.15 = (bf16[2,2,64,384]{3,2,1,0:T(8,128)(2,1)S(1)}, bf16[2,2,64,384]{3,2,1,0:T(8,128)(2,1)S(1)}, u32[]{:S(2)}, u32[]{:S(2)}) collective-permute-start(bf16[2,2,64,384]{3,2,1,0:T(8,128)(2,1)S(1)} %get-tuple-element.60), channel_id=1, source_target_pairs={{0,2},{2,0},{16,18},{18,16},{1,3},{3,1},{17,19},{19,17},{4,6},{6,4... | collective-permute-start | bytes 589832 | tf_op jit(solution)/shard_map/ppermute | solution.py:416
  73.9 2.9 %collective-permute-start.16 = (bf16[2,2,64,384]{3,2,1,0:T(8,128)(2,1)S(1)}, bf16[2,2,64,384]{3,2,1,0:T(8,128)(2,1)S(1)}, u32[]{:S(2)}, u32[]{:S(2)}) collective-permute-start(bf16[2,2,64,384]{3,2,1,0:T(8,128)(2,1)S(1)} %get-tuple-element.61), channel_id=1, source_target_pairs={{0,16},{2,18},{16,0},{18,2},{1,17},{3,19},{17,1},{19,3},{4,20},{6,... | collective-permute-start | bytes 589832 | tf_op jit(solution)/shard_map/ppermute | solution.py:416
  76.9 0.2 broadcast_in_dim.3
  77.2 0.2 collective-permute-start.17
  77.4 1.0 constant_dynamic-update-slice_fusion.6
  78.4 9.3 %collective-permute-done.12 = bf16[2,2,64,384]{3,2,1,0:T(8,128)(2,1)S(1)} collective-permute-done((bf16[2,2,64,384]{3,2,1,0:T(8,128)(2,1)}, bf16[2,2,64,384]{3,2,1,0:T(8,128)(2,1)S(1)}, u32[]{:S(2)}, u32[]{:S(2)}) %collective-permute-start.12) | collective-permute-done | bytes 196640 | tf_op jit(solution)/shard_map/ppermute | solution.py:416
  87.8 4.1 %collective-permute-done.16 = bf16[2,2,64,384]{3,2,1,0:T(8,128)(2,1)S(1)} collective-permute-done((bf16[2,2,64,384]{3,2,1,0:T(8,128)(2,1)S(1)}, bf16[2,2,64,384]{3,2,1,0:T(8,128)(2,1)S(1)}, u32[]{:S(2)}, u32[]{:S(2)}) %collective-permute-start.16) | collective-permute-done | bytes 196640 | tf_op jit(solution)/shard_map/ppermute | solution.py:416
  92.0 3.9 %collective-permute-done.17 = bf16[2,2,64,384]{3,2,1,0:T(8,128)(2,1)S(1)} collective-permute-done((bf16[2,2,64,384]{3,2,1,0:T(8,128)(2,1)S(1)}, bf16[2,2,64,384]{3,2,1,0:T(8,128)(2,1)S(1)}, u32[]{:S(2)}, u32[]{:S(2)}) %collective-permute-start.17) | collective-permute-done | bytes 196640 | tf_op jit(solution)/shard_map/ppermute | solution.py:416
  95.9 1.1 %copy-done.14 = bf16[2,16,64,384]{3,2,1,0:T(8,128)(2,1)} copy-done((bf16[2,16,64,384]{3,2,1,0:T(8,128)(2,1)}, bf16[2,16,64,384]{3,2,1,0:T(8,128)(2,1)S(1)}, u32[]{:S(2)}) %copy-start.14) | copy-done | bytes 1572888
  (54 shorter events, 0.7 us)
Async XLA Ops:
  0.1 2.3 %copy-start.8 = (bf16[576,768]{1,0:T(8,128)(2,1)S(1)}, bf16[576,768]{1,0:T(8,128)(2,1)}, u32[]{:S(2)}) copy-start(bf16[576,768]{1,0:T(8,128)(2,1)} %refs_4_.1) | copy-start | bytes 2654212
  0.1 2.3 %copy-start.9 = (bf16[576,768]{1,0:T(8,128)(2,1)S(1)}, bf16[576,768]{1,0:T(8,128)(2,1)}, u32[]{:S(2)}) copy-start(bf16[576,768]{1,0:T(8,128)(2,1)} %refs_5_.1) | copy-start | bytes 2654212
  0.1 2.3 %copy-start.10 = (bf16[192,1536]{1,0:T(8,128)(2,1)S(1)}, bf16[192,1536]{1,0:T(8,128)(2,1)}, u32[]{:S(2)}) copy-start(bf16[192,1536]{1,0:T(8,128)(2,1)} %refs_2_.1) | copy-start | bytes 1769476
  0.1 2.3 %copy-start.11 = (bf16[768,384]{1,0:T(8,128)(2,1)S(1)}, bf16[768,384]{1,0:T(8,128)(2,1)}, u32[]{:S(2)}) copy-start(bf16[768,384]{1,0:T(8,128)(2,1)} %refs_3_.1) | copy-start | bytes 1769476
  0.1 2.3 %copy-start.12 = (bf16[192,1152]{1,0:T(8,128)(2,1)S(1)}, bf16[192,1152]{1,0:T(8,128)(2,1)}, u32[]{:S(2)}) copy-start(bf16[192,1152]{1,0:T(8,128)(2,1)} %refs_0_.1) | copy-start | bytes 1327108
  0.1 2.4 %copy-start.13 = (bf16[192,384]{1,0:T(8,128)(2,1)S(1)}, bf16[192,384]{1,0:T(8,128)(2,1)}, u32[]{:S(2)}) copy-start(bf16[192,384]{1,0:T(8,128)(2,1)} %refs_1_.1) | copy-start | bytes 442372
  2.8 8.6 %collective-permute-start.1 = (bf16[4608,384]{1,0:T(8,128)(2,1)S(1)}, bf16[4608,384]{1,0:T(8,128)(2,1)S(1)}, u32[]{:S(2)}, u32[]{:S(2)}) collective-permute-start(bf16[4608,384]{1,0:T(8,128)(2,1)S(1)} %pack_weights.1.before.mine), channel_id=1, source_target_pairs={{0,1},{1,0},{2,3},{3,2},{4,5},{5,4},{6,7},{7,6},{8,9},{9,8},{10,11... | collective-permute-start | bytes 10616840 | tf_op jit(solution)/shard_map/ppermute | solution.py:426
  3.3 12.3 %collective-permute-start = (bf16[2,4,64,384]{3,2,1,0:T(8,128)(2,1)S(1)}, bf16[2,4,64,384]{3,2,1,0:T(8,128)(2,1)S(1)}, u32[]{:S(2)}, u32[]{:S(2)}) collective-permute-start(bf16[2,4,64,384]{3,2,1,0:T(8,128)(2,1)S(1)} %get-tuple-element.34), channel_id=1, source_target_pairs={{0,2},{2,0},{16,18},{18,16},{1,3},{3,1},{17,19},{19,17},{4,6},{6,4... | collective-permute-start | bytes 1179656 | tf_op jit(solution)/shard_map/ppermute | solution.py:416
  5.9 25.4 %collective-permute-start.2 = (bf16[2,2,64,384]{3,2,1,0:T(8,128)(2,1)S(1)}, bf16[2,2,64,384]{3,2,1,0:T(8,128)(2,1)S(1)}, u32[]{:S(2)}, u32[]{:S(2)}) collective-permute-start(bf16[2,2,64,384]{3,2,1,0:T(8,128)(2,1)S(1)} %get-tuple-element.35.before), channel_id=1, source_target_pairs={{0,16},{2,18},{16,0},{18,2},{1,17},{3,19},{17,1},{19,3},{4,20},{6,... | collective-permute-start | bytes 589832 | tf_op jit(solution)/shard_map/ppermute | solution.py:416
  8.5 27.2 %collective-permute-start.3 = (bf16[2,2,64,384]{3,2,1,0:T(8,128)(2,1)S(1)}, bf16[2,2,64,384]{3,2,1,0:T(8,128)(2,1)S(1)}, u32[]{:S(2)}, u32[]{:S(2)}) collective-permute-start(bf16[2,2,64,384]{3,2,1,0:T(8,128)(2,1)S(1)} %get-tuple-element.41), channel_id=1, source_target_pairs={{0,18},{2,16},{16,2},{18,0},{1,19},{3,17},{17,3},{19,1},{4,22},{6,... | collective-permute-start | bytes 589832 | tf_op jit(solution)/shard_map/ppermute | solution.py:416
  8.5 31.6 %collective-permute-start.4 = (bf16[2,2,64,384]{3,2,1,0:T(8,128)(2,1)S(1)}, bf16[2,2,64,384]{3,2,1,0:T(8,128)(2,1)S(1)}, u32[]{:S(2)}, u32[]{:S(2)}) collective-permute-start(bf16[2,2,64,384]{3,2,1,0:T(8,128)(2,1)S(1)} %get-tuple-element.43), channel_id=1, source_target_pairs={{0,16},{2,18},{16,0},{18,2},{1,17},{3,19},{17,1},{19,3},{4,20},{6,... | collective-permute-start | bytes 589832 | tf_op jit(solution)/shard_map/ppermute | solution.py:416
  24.9 25.7 %copy-start = (bf16[4,128,384]{2,1,0:T(8,128)(2,1)}, bf16[4,128,384]{2,1,0:T(8,128)(2,1)S(1)}, u32[]{:S(2)}) copy-start(bf16[4,128,384]{2,1,0:T(8,128)(2,1)S(1)} %get-tuple-element.46.refs_0_) | copy-start | bytes 1179652
  24.9 25.7 %copy-start.2 = (bf16[4,128,384]{2,1,0:T(8,128)(2,1)}, bf16[4,128,384]{2,1,0:T(8,128)(2,1)S(1)}, u32[]{:S(2)}) copy-start(bf16[4,128,384]{2,1,0:T(8,128)(2,1)S(1)} %get-tuple-element.47.refs_1_) | copy-start | bytes 1179652
  24.9 25.6 %collective-permute-start.6 = (bf16[4,128,384]{2,1,0:T(8,128)(2,1)S(1)}, bf16[4,128,384]{2,1,0:T(8,128)(2,1)S(1)}, u32[]{:S(2)}, u32[]{:S(2)}) collective-permute-start(bf16[4,128,384]{2,1,0:T(8,128)(2,1)S(1)} %get-tuple-element.47.refs_1_), channel_id=1, source_target_pairs={{0,1},{1,4},{4,5},{5,8},{8,9},{9,12},{12,13},{13,0},{2,3},{3,6},{6... | collective-permute-start | bytes 1179656 | tf_op jit(solution)/shard_map/ppermute | solution.py:419
  25.0 25.6 %collective-permute-start.7 = (bf16[4,128,384]{2,1,0:T(8,128)(2,1)S(1)}, bf16[4,128,384]{2,1,0:T(8,128)(2,1)S(1)}, u32[]{:S(2)}, u32[]{:S(2)}) collective-permute-start(bf16[4,128,384]{2,1,0:T(8,128)(2,1)S(1)} %get-tuple-element.46.refs_0_), channel_id=1, source_target_pairs={{1,0},{4,1},{5,4},{8,5},{9,8},{12,9},{13,12},{0,13},{3,2},{6,3},{7... | collective-permute-start | bytes 1179656 | tf_op jit(solution)/shard_map/ppermute | solution.py:419
  31.3 11.5 %collective-permute-start.5 = (bf16[2,2,64,384]{3,2,1,0:T(8,128)(2,1)S(1)}, bf16[2,2,64,384]{3,2,1,0:T(8,128)(2,1)S(1)}, u32[]{:S(2)}, u32[]{:S(2)}) collective-permute-start(bf16[2,2,64,384]{3,2,1,0:T(8,128)(2,1)S(1)} %get-tuple-element.44), channel_id=1, source_target_pairs={{0,18},{2,16},{16,2},{18,0},{1,19},{3,17},{17,3},{19,1},{4,22},{6,... | collective-permute-start | bytes 589832 | tf_op jit(solution)/shard_map/ppermute | solution.py:416
  40.0 7.8 %collective-permute-start.8 = (bf16[2,128,384]{2,1,0:T(8,128)(2,1)S(1)}, bf16[2,128,384]{2,1,0:T(8,128)(2,1)S(1)}, u32[]{:S(2)}, u32[]{:S(2)}) collective-permute-start(bf16[2,128,384]{2,1,0:T(8,128)(2,1)S(1)} %get-tuple-element.49.refs_5_), channel_id=1, source_target_pairs={{0,1},{1,4},{4,5},{5,8},{8,9},{9,12},{12,13},{13,0},{2,3},{3,6},{6... | collective-permute-start | bytes 589832 | tf_op jit(solution)/shard_map/ppermute | solution.py:419
  40.1 10.4 %collective-permute-start.9 = (bf16[2,128,384]{2,1,0:T(8,128)(2,1)S(1)}, bf16[2,128,384]{2,1,0:T(8,128)(2,1)S(1)}, u32[]{:S(2)}, u32[]{:S(2)}) collective-permute-start(bf16[2,128,384]{2,1,0:T(8,128)(2,1)S(1)} %get-tuple-element.48.refs_4_), channel_id=1, source_target_pairs={{1,0},{4,1},{5,4},{8,5},{9,8},{12,9},{13,12},{0,13},{3,2},{6,3},{7... | collective-permute-start | bytes 589832 | tf_op jit(solution)/shard_map/ppermute | solution.py:419
  47.8 13.5 %collective-permute-start.13 = (bf16[2,128,384]{2,1,0:T(8,128)(2,1)}, bf16[2,128,384]{2,1,0:T(8,128)(2,1)}, u32[]{:S(2)}, u32[]{:S(2)}) collective-permute-start(bf16[2,128,384]{2,1,0:T(8,128)(2,1)} %get-tuple-element.58.refs_5_), channel_id=1, source_target_pairs={{0,1},{1,4},{4,5},{5,8},{8,9},{9,12},{12,13},{13,0},{2,3},{3,6},{6... | collective-permute-start | bytes 589832 | tf_op jit(solution)/shard_map/ppermute | solution.py:419
  47.9 13.5 %collective-permute-start.14 = (bf16[2,128,384]{2,1,0:T(8,128)(2,1)}, bf16[2,128,384]{2,1,0:T(8,128)(2,1)}, u32[]{:S(2)}, u32[]{:S(2)}) collective-permute-start(bf16[2,128,384]{2,1,0:T(8,128)(2,1)} %get-tuple-element.57.refs_4_), channel_id=1, source_target_pairs={{1,0},{4,1},{5,4},{8,5},{9,8},{12,9},{13,12},{0,13},{3,2},{6,3},{7... | collective-permute-start | bytes 589832 | tf_op jit(solution)/shard_map/ppermute | solution.py:419
  50.5 6.4 %copy-start.4 = (bf16[4,128,384]{2,1,0:T(8,128)(2,1)}, bf16[4,128,384]{2,1,0:T(8,128)(2,1)S(1)}, u32[]{:S(2)}) copy-start(bf16[4,128,384]{2,1,0:T(8,128)(2,1)S(1)} %collective-permute-done.6.refs_2_) | copy-start | bytes 1179652
  50.5 6.4 %copy-start.6 = (bf16[4,128,384]{2,1,0:T(8,128)(2,1)}, bf16[4,128,384]{2,1,0:T(8,128)(2,1)S(1)}, u32[]{:S(2)}) copy-start(bf16[4,128,384]{2,1,0:T(8,128)(2,1)S(1)} %collective-permute-done.7.refs_3_) | copy-start | bytes 1179652
  57.0 20.2 %collective-permute-start.10 = (bf16[2,2,64,384]{3,2,1,0:T(8,128)(2,1)}, bf16[2,2,64,384]{3,2,1,0:T(8,128)(2,1)}, u32[]{:S(2)}, u32[]{:S(2)}) collective-permute-start(bf16[2,2,64,384]{3,2,1,0:T(8,128)(2,1)} %get-tuple-element.53), channel_id=1, source_target_pairs={{0,2},{2,0},{16,18},{18,16},{1,3},{3,1},{17,19},{19,17},{4,6},{6,4... | collective-permute-start | bytes 589832 | tf_op jit(solution)/shard_map/ppermute | solution.py:416
  57.5 20.9 %collective-permute-start.11 = (bf16[2,2,64,384]{3,2,1,0:T(8,128)(2,1)}, bf16[2,2,64,384]{3,2,1,0:T(8,128)(2,1)S(1)}, u32[]{:S(2)}, u32[]{:S(2)}) collective-permute-start(bf16[2,2,64,384]{3,2,1,0:T(8,128)(2,1)} %get-tuple-element.54), channel_id=1, source_target_pairs={{0,16},{2,18},{16,0},{18,2},{1,17},{3,19},{17,1},{19,3},{4,20},{6,... | collective-permute-start | bytes 589832 | tf_op jit(solution)/shard_map/ppermute | solution.py:416
  61.2 26.5 %collective-permute-start.12 = (bf16[2,2,64,384]{3,2,1,0:T(8,128)(2,1)}, bf16[2,2,64,384]{3,2,1,0:T(8,128)(2,1)S(1)}, u32[]{:S(2)}, u32[]{:S(2)}) collective-permute-start(bf16[2,2,64,384]{3,2,1,0:T(8,128)(2,1)} %get-tuple-element.55), channel_id=1, source_target_pairs={{0,18},{2,16},{16,2},{18,0},{1,19},{3,17},{17,3},{19,1},{4,22},{6,... | collective-permute-start | bytes 589832 | tf_op jit(solution)/shard_map/ppermute | solution.py:416
  61.4 1.0 %copy-start.1 = (bf16[4,128,384]{2,1,0:T(8,128)(2,1)S(1)}, bf16[4,128,384]{2,1,0:T(8,128)(2,1)}, u32[]{:S(2)}) copy-start(bf16[4,128,384]{2,1,0:T(8,128)(2,1)} %copy-done) | copy-start | bytes 1179652
  62.3 1.0 %copy-start.3 = (bf16[4,128,384]{2,1,0:T(8,128)(2,1)S(1)}, bf16[4,128,384]{2,1,0:T(8,128)(2,1)}, u32[]{:S(2)}) copy-start(bf16[4,128,384]{2,1,0:T(8,128)(2,1)} %copy-done.2) | copy-start | bytes 1179652
  72.6 4.5 %copy-start.15 = (bf16[2,2,64,384]{3,2,1,0:T(8,128)(2,1)S(1)}, bf16[2,2,64,384]{3,2,1,0:T(8,128)(2,1)}, u32[]{:S(2)}) copy-start(bf16[2,2,64,384]{3,2,1,0:T(8,128)(2,1)} %get-tuple-element.52) | copy-start | bytes 589828
  72.6 15.1 %collective-permute-start.15 = (bf16[2,2,64,384]{3,2,1,0:T(8,128)(2,1)S(1)}, bf16[2,2,64,384]{3,2,1,0:T(8,128)(2,1)S(1)}, u32[]{:S(2)}, u32[]{:S(2)}) collective-permute-start(bf16[2,2,64,384]{3,2,1,0:T(8,128)(2,1)S(1)} %get-tuple-element.60), channel_id=1, source_target_pairs={{0,2},{2,0},{16,18},{18,16},{1,3},{3,1},{17,19},{19,17},{4,6},{6,4... | collective-permute-start | bytes 589832 | tf_op jit(solution)/shard_map/ppermute | solution.py:416
  73.9 18.0 %collective-permute-start.16 = (bf16[2,2,64,384]{3,2,1,0:T(8,128)(2,1)S(1)}, bf16[2,2,64,384]{3,2,1,0:T(8,128)(2,1)S(1)}, u32[]{:S(2)}, u32[]{:S(2)}) collective-permute-start(bf16[2,2,64,384]{3,2,1,0:T(8,128)(2,1)S(1)} %get-tuple-element.61), channel_id=1, source_target_pairs={{0,16},{2,18},{16,0},{18,2},{1,17},{3,19},{17,1},{19,3},{4,20},{6,... | collective-permute-start | bytes 589832 | tf_op jit(solution)/shard_map/ppermute | solution.py:416
  77.2 18.7 %collective-permute-start.17 = (bf16[2,2,64,384]{3,2,1,0:T(8,128)(2,1)S(1)}, bf16[2,2,64,384]{3,2,1,0:T(8,128)(2,1)S(1)}, u32[]{:S(2)}, u32[]{:S(2)}) collective-permute-start(bf16[2,2,64,384]{3,2,1,0:T(8,128)(2,1)S(1)} %get-tuple-element.62), channel_id=1, source_target_pairs={{0,18},{2,16},{16,2},{18,0},{1,19},{3,17},{17,3},{19,1},{4,22},{6,... | collective-permute-start | bytes 589832 | tf_op jit(solution)/shard_map/ppermute | solution.py:416
  95.9 1.1 %copy-start.14 = (bf16[2,16,64,384]{3,2,1,0:T(8,128)(2,1)}, bf16[2,16,64,384]{3,2,1,0:T(8,128)(2,1)S(1)}, u32[]{:S(2)}) copy-start(bf16[2,16,64,384]{3,2,1,0:T(8,128)(2,1)S(1)} %constant_dynamic-update-slice_fusion) | copy-start | bytes 4718596
  (2 other events, 2.0 us)

commit v11 on v10

--- a/solution.py
+++ b/solution.py
@@ -355,7 +355,8 @@
     piece = pl.BlockSpec(shape_in, lambda i, at: (0, i, 0, 0))
     own = pl.BlockSpec(shape_in, lambda i, at: (0, 4 * i + at[4], 0, 0))
     block_out = pl.BlockSpec((units, 2 * half, features), lambda i, at: (i, 0, 0))
-    shape = jax.ShapeDtypeStruct((chunks * units, 2 * half, features), jnp.bfloat16)
+    held = jax.ShapeDtypeStruct if from_frames else pltpu.VMEM
+    shape = held((chunks * units, 2 * half, features), jnp.bfloat16)
     return pl.pallas_call(
         section_kernel,
         grid_spec=pltpu.PrefetchScalarGridSpec(
@@ -439,8 +440,11 @@
             )
             far.append(halo(even, odd))
         else:
+            last = index == CHUNKS - 1
+            if last:
+                own = [pltpu.with_memory_space_constraint(field, pltpu.HBM) for field in own]
             *sent, before = run_temporal(
-                place, before, own, far[index], temporal_weights, index, units, index == CHUNKS - 1
+                place, before, own, far[index], temporal_weights, index, units, last
             )
             outs.append([sent[0]] + [exchange(sent[delta], delta) for delta in (1, 2, 3)])
     result = jnp.zeros_like(grouped)

time: 97.4 us -> 97.2 us (level)
  local copies, waits for them, and re-layouts: 6.7 us -> 2.72 us
  waiting for transfers between devices: 20.4 us -> 24.2 us
    unnamed x32 -> x24, local copies, waits for them, and re-layouts: 5.19 us -> 1.21 us
    ppermute x11, waiting for transfers between devices: 20.3 us -> 24.1 us  [exchange(): return lax.ppermute(piece, GROUP, [(i, i ^ delta) for i in range(4)])]
  transfers between devices with their start and end apart: 18 -> 18, of which waited for: 4 -> 5; matrix products, arithmetic and copies ran while one was open for 1% -> 1% of each run, Pallas kernels for 35% -> 35%
where the time goes in v11:
time: 97.2 us; the launch traced here: 97 us
  Pallas kernels  36.4 us (37%)
  starting transfers between devices  33.4 us (34%)
  waiting for transfers between devices  24.2 us (25%)
  local copies, waits for them, and re-layouts  2.72 us (3%)
    ppermute x11, waiting for transfers between devices, exchange(): return lax.ppermute(piece, GROUP, [(i, i ^ delta) for i in range(4)])  24.1 us
    ppermute x11, starting transfers between devices, exchange(): return lax.ppermute(piece, GROUP, [(i, i ^ delta) for i in range(4)])  21.2 us
    pallas_call x3, Pallas kernels, run_section(): pl.pallas_call(section_kernel, grid_spec=pltpu.PrefetchScalarGridSpec(num...  18.8 us
    pallas_call x2, Pallas kernels, run_temporal(): pl.pallas_call(functools.partial(temporal_kernel, 0 if last else chunk),...  13.9 us
    ppermute x3, starting transfers between devices, halo(): lax.ppermute(even, RING, leftward)  11.6 us
    pallas_call x1, Pallas kernels, run_pack(): pl.pallas_call(functools.partial(pack_kernel, chunks), grid_spec=pltpu.Pr...  2.27 us
  transfers between devices with their start and end apart: 18, of which 5 were waited for; matrix products, arithmetic and copies ran while one was open for 1% of the time, Pallas kernels for 35%

profile of v11, /device:TPU:0, one launch (start us, length us, event | category | flops | bytes accessed | tf_op | source)
XLA Modules:
  0.0 97.0 jit_solution(17517683730610830348)
XLA Ops:
  0.0 0.1 stack.31.place.before
  0.1 2.3 %pack.1 = (bf16[2,4,64,384]{3,2,1,0:T(8,128)(2,1)S(1)}, bf16[2,2,64,384]{3,2,1,0:T(8,128)(2,1)S(1)}, bf16[2,2,64,384]{3,2,1,0:T(8,128)(2,1)S(1)}, bf16[2,2,64,38...) custom-call(s32[5]{0:T(128)S(1)} %stack.31.place.before, bf16[2,16,64,384]{3,2,1,0:T(8,128)(2,1)} %bitcast.7, ...), custom_call_target="tpu_custom_call" | custom-call | bytes 786432 | tf_op jit(solution)/shard_map/pack/pallas_call | solution.py:198
  2.5 0.3 pack_weights.1.before.mine
  2.8 0.5 collective-permute-start.1
  3.3 2.6 %collective-permute-start = (bf16[2,4,64,384]{3,2,1,0:T(8,128)(2,1)S(1)}, bf16[2,4,64,384]{3,2,1,0:T(8,128)(2,1)S(1)}, u32[]{:S(2)}, u32[]{:S(2)}) collective-permute-start(bf16[2,4,64,384]{3,2,1,0:T(8,128)(2,1)S(1)} %get-tuple-element.34), channel_id=1, source_target_pairs={{0,2},{2,0},{16,18},{18,16},{1,3},{3,1},{17,19},{19,17},{4,6},{6,4... | collective-permute-start | bytes 1179656 | tf_op jit(solution)/shard_map/ppermute | solution.py:417
  5.9 2.6 %collective-permute-start.2 = (bf16[2,2,64,384]{3,2,1,0:T(8,128)(2,1)S(1)}, bf16[2,2,64,384]{3,2,1,0:T(8,128)(2,1)S(1)}, u32[]{:S(2)}, u32[]{:S(2)}) collective-permute-start(bf16[2,2,64,384]{3,2,1,0:T(8,128)(2,1)S(1)} %get-tuple-element.35.before), channel_id=1, source_target_pairs={{0,16},{2,18},{16,0},{18,2},{1,17},{3,19},{17,1},{19,3},{4,20},{6,... | collective-permute-start | bytes 589832 | tf_op jit(solution)/shard_map/ppermute | solution.py:417
  8.5 2.9 %collective-permute-start.4 = (bf16[2,2,64,384]{3,2,1,0:T(8,128)(2,1)S(1)}, bf16[2,2,64,384]{3,2,1,0:T(8,128)(2,1)S(1)}, u32[]{:S(2)}, u32[]{:S(2)}) collective-permute-start(bf16[2,2,64,384]{3,2,1,0:T(8,128)(2,1)S(1)} %get-tuple-element.43), channel_id=1, source_target_pairs={{0,16},{2,18},{16,0},{18,2},{1,17},{3,19},{17,1},{19,3},{4,20},{6,... | collective-permute-start | bytes 589832 | tf_op jit(solution)/shard_map/ppermute | solution.py:417
  11.4 1.2 %join_weights.1 = (bf16[384,1152]{1,0:T(8,128)(2,1)S(1)}, bf16[384,384]{1,0:T(8,128)(2,1)S(1)}, bf16[384,1536]{1,0:T(8,128)(2,1)S(1)}, bf16[1536,384]{1,0:T(8,12...) custom-call(s32[5]{0:T(128)S(1)} %stack.31.place.before, ...), custom_call_target="tpu_custom_call" | custom-call | bytes 1769472 | tf_op jit(solution)/shard_map/join_weights/pallas_call | solution.py:168
  12.5 3.1 %collective-permute-done.other = bf16[2,4,64,384]{3,2,1,0:T(8,128)(2,1)S(1)} collective-permute-done((bf16[2,4,64,384]{3,2,1,0:T(8,128)(2,1)S(1)}, bf16[2,4,64,384]{3,2,1,0:T(8,128)(2,1)S(1)}, u32[]{:S(2)}, u32[]{:S(2)}) %collective-permute-start) | collective-permute-done | bytes 393248 | tf_op jit(solution)/shard_map/ppermute | solution.py:417
  15.6 9.3 %section.3 = (bf16[4,128,384]{2,1,0:T(8,128)(2,1)S(1)}, bf16[4,128,384]{2,1,0:T(8,128)(2,1)S(1)}, f32[8,128]{1,0:T(8,128)S(1)}) custom-call(s32[5]{0:T(128)S(1)} %stack.31.place.before, s32[5]{0:T(128)S(1)} %stack.31.place.before, bf16[2,16,64,384]{3,2,1,0:T(8,128)(2,1)} %bitcast.13, bf16[2,4,64,384]{3,2,1,0:T(8,128)(2,1)S(1)} %collective-permute-done.other, ...), custom_call_target="tpu_custom_call" | custom-call | bytes 98304 | tf_op jit(solution)/shard_map/section/pallas_call | solution.py:360
  25.0 6.3 %collective-permute-start.7 = (bf16[4,128,384]{2,1,0:T(8,128)(2,1)S(1)}, bf16[4,128,384]{2,1,0:T(8,128)(2,1)S(1)}, u32[]{:S(2)}, u32[]{:S(2)}) collective-permute-start(bf16[4,128,384]{2,1,0:T(8,128)(2,1)S(1)} %get-tuple-element.46.refs_0_), channel_id=1, source_target_pairs={{1,0},{4,1},{5,4},{8,5},{9,8},{12,9},{13,12},{0,13},{3,2},{6,3},{7... | collective-permute-start | bytes 1179656 | tf_op jit(solution)/shard_map/ppermute | solution.py:420
  31.3 4.3 %collective-permute-start.5 = (bf16[2,2,64,384]{3,2,1,0:T(8,128)(2,1)S(1)}, bf16[2,2,64,384]{3,2,1,0:T(8,128)(2,1)S(1)}, u32[]{:S(2)}, u32[]{:S(2)}) collective-permute-start(bf16[2,2,64,384]{3,2,1,0:T(8,128)(2,1)S(1)} %get-tuple-element.44), channel_id=1, source_target_pairs={{0,18},{2,16},{16,2},{18,0},{1,19},{3,17},{17,3},{19,1},{4,22},{6,... | collective-permute-start | bytes 589832 | tf_op jit(solution)/shard_map/ppermute | solution.py:417
  35.6 4.4 %section.4 = (bf16[2,128,384]{2,1,0:T(8,128)(2,1)S(1)}, bf16[2,128,384]{2,1,0:T(8,128)(2,1)S(1)}, f32[8,128]{1,0:T(8,128)S(1)}) custom-call(s32[5]{0:T(128)S(1)} %stack.31.place.before, f32[8,128]{1,0:T(8,128)S(1)} %get-tuple-element.40.before, bf16[2,2,64,384]{3,2,1,0:T(8,128)(2,1)S(1)} %collective-permute-done.2.mine, ...), custom_call_target="tpu_custom_call" | custom-call | bytes 49152 | tf_op jit(solution)/shard_map/section/pallas_call | solution.py:360
  40.0 0.1 collective-permute-start.8
  40.1 2.6 %collective-permute-start.9 = (bf16[2,128,384]{2,1,0:T(8,128)(2,1)S(1)}, bf16[2,128,384]{2,1,0:T(8,128)(2,1)S(1)}, u32[]{:S(2)}, u32[]{:S(2)}) collective-permute-start(bf16[2,128,384]{2,1,0:T(8,128)(2,1)S(1)} %get-tuple-element.48.refs_4_), channel_id=1, source_target_pairs={{1,0},{4,1},{5,4},{8,5},{9,8},{12,9},{13,12},{0,13},{3,2},{6,3},{7... | collective-permute-start | bytes 589832 | tf_op jit(solution)/shard_map/ppermute | solution.py:420
  42.7 5.1 %section.5 = (bf16[2,128,384]{2,1,0:T(8,128)(2,1)}, bf16[2,128,384]{2,1,0:T(8,128)(2,1)}, f32[8,128]{1,0:T(8,128)S(1)}) custom-call(s32[5]{0:T(128)S(1)} %stack.31.place.before, f32[8,128]{1,0:T(8,128)S(1)} %get-tuple-element.42.before, bf16[2,2,64,384]{3,2,1,0:T(8,128)(2,1)S(1)} %collective-permute-done.4.mine, ...), custom_call_target="tpu_custom_call" | custom-call | bytes 49152 | tf_op jit(solution)/shard_map/section/pallas_call | solution.py:360
  47.8 2.6 %collective-permute-start.14 = (bf16[2,128,384]{2,1,0:T(8,128)(2,1)}, bf16[2,128,384]{2,1,0:T(8,128)(2,1)}, u32[]{:S(2)}, u32[]{:S(2)}) collective-permute-start(bf16[2,128,384]{2,1,0:T(8,128)(2,1)} %get-tuple-element.57.refs_4_), channel_id=1, source_target_pairs={{1,0},{4,1},{5,4},{8,5},{9,8},{12,9},{13,12},{0,13},{3,2},{6,3},{7... | collective-permute-start | bytes 589832 | tf_op jit(solution)/shard_map/ppermute | solution.py:420
  50.5 6.4 %temporal.2 = (bf16[2,2,64,384]{3,2,1,0:T(8,128)(2,1)}, bf16[2,2,64,384]{3,2,1,0:T(8,128)(2,1)}, bf16[2,2,64,384]{3,2,1,0:T(8,128)(2,1)}, bf16[2,2,64,384]{3,2,1,0:T(8,128)(2,1)}, f32[8,128]{1,0:T(8,128)S(1)}) custom-call(s32[5]{0:T(128)S(1)} %stack.31.place.before, f32[8,128]{1,0:T(8,128)S(1)} %get-tuple-element.45.before, ...), custom_call_target="tpu_custom_call" | custom-call | bytes 98304 | tf_op jit(solution)/shard_map/temporal/pallas_call | solution.py:382
  56.9 0.5 collective-permute-start.10
  57.5 3.7 %collective-permute-start.11 = (bf16[2,2,64,384]{3,2,1,0:T(8,128)(2,1)}, bf16[2,2,64,384]{3,2,1,0:T(8,128)(2,1)S(1)}, u32[]{:S(2)}, u32[]{:S(2)}) collective-permute-start(bf16[2,2,64,384]{3,2,1,0:T(8,128)(2,1)} %get-tuple-element.54), channel_id=1, source_target_pairs={{0,16},{2,18},{16,0},{18,2},{1,17},{3,19},{17,1},{19,3},{4,20},{6,... | collective-permute-start | bytes 589832 | tf_op jit(solution)/shard_map/ppermute | solution.py:417
  61.2 0.1 collective-permute-start.12
  61.3 7.5 %temporal.3 = (bf16[2,2,64,384]{3,2,1,0:T(8,128)(2,1)S(1)}, bf16[2,2,64,384]{3,2,1,0:T(8,128)(2,1)S(1)}, bf16[2,2,64,384]{3,2,1,0:T(8,128)(2,1)S(1)}, bf16[2,2,64,384]{3,2,1,0:T(8,128)(2,1)S(1)}, f32[8,128]{1,0:T(8,128)}) custom-call(s32[5]{0:T(128)S(1)} %stack.31.place.before, f32[8,128]{1,0:T(8,128)S(1)} %get-tuple-element.56.before, ...), custom_call_target="tpu_custom_call" | custom-call | bytes 98304 | tf_op jit(solution)/shard_map/temporal/pallas_call | solution.py:382
  68.8 1.3 %collective-permute-start.15 = (bf16[2,2,64,384]{3,2,1,0:T(8,128)(2,1)S(1)}, bf16[2,2,64,384]{3,2,1,0:T(8,128)(2,1)S(1)}, u32[]{:S(2)}, u32[]{:S(2)}) collective-permute-start(bf16[2,2,64,384]{3,2,1,0:T(8,128)(2,1)S(1)} %get-tuple-element.60), channel_id=1, source_target_pairs={{0,2},{2,0},{16,18},{18,16},{1,3},{3,1},{17,19},{19,17},{4,6},{6,4... | collective-permute-start | bytes 589832 | tf_op jit(solution)/shard_map/ppermute | solution.py:417
  70.1 2.9 %collective-permute-start.16 = (bf16[2,2,64,384]{3,2,1,0:T(8,128)(2,1)S(1)}, bf16[2,2,64,384]{3,2,1,0:T(8,128)(2,1)S(1)}, u32[]{:S(2)}, u32[]{:S(2)}) collective-permute-start(bf16[2,2,64,384]{3,2,1,0:T(8,128)(2,1)S(1)} %get-tuple-element.61), channel_id=1, source_target_pairs={{0,16},{2,18},{16,0},{18,2},{1,17},{3,19},{17,1},{19,3},{4,20},{6,... | collective-permute-start | bytes 589832 | tf_op jit(solution)/shard_map/ppermute | solution.py:417
  73.1 0.2 broadcast_in_dim.3
  73.4 0.2 collective-permute-start.17
  73.6 1.0 constant_dynamic-update-slice_fusion.6
  74.5 9.0 %collective-permute-done.11 = bf16[2,2,64,384]{3,2,1,0:T(8,128)(2,1)S(1)} collective-permute-done((bf16[2,2,64,384]{3,2,1,0:T(8,128)(2,1)}, bf16[2,2,64,384]{3,2,1,0:T(8,128)(2,1)S(1)}, u32[]{:S(2)}, u32[]{:S(2)}) %collective-permute-start.11) | collective-permute-done | bytes 196640 | tf_op jit(solution)/shard_map/ppermute | solution.py:417
  83.5 4.1 %collective-permute-done.12 = bf16[2,2,64,384]{3,2,1,0:T(8,128)(2,1)S(1)} collective-permute-done((bf16[2,2,64,384]{3,2,1,0:T(8,128)(2,1)}, bf16[2,2,64,384]{3,2,1,0:T(8,128)(2,1)S(1)}, u32[]{:S(2)}, u32[]{:S(2)}) %collective-permute-start.12) | collective-permute-done | bytes 196640 | tf_op jit(solution)/shard_map/ppermute | solution.py:417
  87.8 4.1 %collective-permute-done.16 = bf16[2,2,64,384]{3,2,1,0:T(8,128)(2,1)S(1)} collective-permute-done((bf16[2,2,64,384]{3,2,1,0:T(8,128)(2,1)S(1)}, bf16[2,2,64,384]{3,2,1,0:T(8,128)(2,1)S(1)}, u32[]{:S(2)}, u32[]{:S(2)}) %collective-permute-start.16) | collective-permute-done | bytes 196640 | tf_op jit(solution)/shard_map/ppermute | solution.py:417
  91.9 3.9 %collective-permute-done.17 = bf16[2,2,64,384]{3,2,1,0:T(8,128)(2,1)S(1)} collective-permute-done((bf16[2,2,64,384]{3,2,1,0:T(8,128)(2,1)S(1)}, bf16[2,2,64,384]{3,2,1,0:T(8,128)(2,1)S(1)}, u32[]{:S(2)}, u32[]{:S(2)}) %collective-permute-start.17) | collective-permute-done | bytes 196640 | tf_op jit(solution)/shard_map/ppermute | solution.py:417
  95.9 1.1 %copy-done.10 = bf16[2,16,64,384]{3,2,1,0:T(8,128)(2,1)} copy-done((bf16[2,16,64,384]{3,2,1,0:T(8,128)(2,1)}, bf16[2,16,64,384]{3,2,1,0:T(8,128)(2,1)S(1)}, u32[]{:S(2)}) %copy-start.10) | copy-done | bytes 1572888
  (46 shorter events, 0.4 us)
Async XLA Ops:
  0.1 2.3 %copy-start.4 = (bf16[576,768]{1,0:T(8,128)(2,1)S(1)}, bf16[576,768]{1,0:T(8,128)(2,1)}, u32[]{:S(2)}) copy-start(bf16[576,768]{1,0:T(8,128)(2,1)} %refs_4_.1) | copy-start | bytes 2654212
  0.1 2.3 %copy-start.5 = (bf16[576,768]{1,0:T(8,128)(2,1)S(1)}, bf16[576,768]{1,0:T(8,128)(2,1)}, u32[]{:S(2)}) copy-start(bf16[576,768]{1,0:T(8,128)(2,1)} %refs_5_.1) | copy-start | bytes 2654212
  0.1 2.3 %copy-start.6 = (bf16[192,1536]{1,0:T(8,128)(2,1)S(1)}, bf16[192,1536]{1,0:T(8,128)(2,1)}, u32[]{:S(2)}) copy-start(bf16[192,1536]{1,0:T(8,128)(2,1)} %refs_2_.1) | copy-start | bytes 1769476
  0.1 2.3 %copy-start.7 = (bf16[768,384]{1,0:T(8,128)(2,1)S(1)}, bf16[768,384]{1,0:T(8,128)(2,1)}, u32[]{:S(2)}) copy-start(bf16[768,384]{1,0:T(8,128)(2,1)} %refs_3_.1) | copy-start | bytes 1769476
  0.1 2.3 %copy-start.8 = (bf16[192,1152]{1,0:T(8,128)(2,1)S(1)}, bf16[192,1152]{1,0:T(8,128)(2,1)}, u32[]{:S(2)}) copy-start(bf16[192,1152]{1,0:T(8,128)(2,1)} %refs_0_.1) | copy-start | bytes 1327108
  0.1 2.4 %copy-start.9 = (bf16[192,384]{1,0:T(8,128)(2,1)S(1)}, bf16[192,384]{1,0:T(8,128)(2,1)}, u32[]{:S(2)}) copy-start(bf16[192,384]{1,0:T(8,128)(2,1)} %refs_1_.1) | copy-start | bytes 442372
  2.8 8.6 %collective-permute-start.1 = (bf16[4608,384]{1,0:T(8,128)(2,1)S(1)}, bf16[4608,384]{1,0:T(8,128)(2,1)S(1)}, u32[]{:S(2)}, u32[]{:S(2)}) collective-permute-start(bf16[4608,384]{1,0:T(8,128)(2,1)S(1)} %pack_weights.1.before.mine), channel_id=1, source_target_pairs={{0,1},{1,0},{2,3},{3,2},{4,5},{5,4},{6,7},{7,6},{8,9},{9,8},{10,11... | collective-permute-start | bytes 10616840 | tf_op jit(solution)/shard_map/ppermute | solution.py:427
  3.3 12.3 %collective-permute-start = (bf16[2,4,64,384]{3,2,1,0:T(8,128)(2,1)S(1)}, bf16[2,4,64,384]{3,2,1,0:T(8,128)(2,1)S(1)}, u32[]{:S(2)}, u32[]{:S(2)}) collective-permute-start(bf16[2,4,64,384]{3,2,1,0:T(8,128)(2,1)S(1)} %get-tuple-element.34), channel_id=1, source_target_pairs={{0,2},{2,0},{16,18},{18,16},{1,3},{3,1},{17,19},{19,17},{4,6},{6,4... | collective-permute-start | bytes 1179656 | tf_op jit(solution)/shard_map/ppermute | solution.py:417
  5.9 25.4 %collective-permute-start.2 = (bf16[2,2,64,384]{3,2,1,0:T(8,128)(2,1)S(1)}, bf16[2,2,64,384]{3,2,1,0:T(8,128)(2,1)S(1)}, u32[]{:S(2)}, u32[]{:S(2)}) collective-permute-start(bf16[2,2,64,384]{3,2,1,0:T(8,128)(2,1)S(1)} %get-tuple-element.35.before), channel_id=1, source_target_pairs={{0,16},{2,18},{16,0},{18,2},{1,17},{3,19},{17,1},{19,3},{4,20},{6,... | collective-permute-start | bytes 589832 | tf_op jit(solution)/shard_map/ppermute | solution.py:417
  8.5 27.2 %collective-permute-start.3 = (bf16[2,2,64,384]{3,2,1,0:T(8,128)(2,1)S(1)}, bf16[2,2,64,384]{3,2,1,0:T(8,128)(2,1)S(1)}, u32[]{:S(2)}, u32[]{:S(2)}) collective-permute-start(bf16[2,2,64,384]{3,2,1,0:T(8,128)(2,1)S(1)} %get-tuple-element.41), channel_id=1, source_target_pairs={{0,18},{2,16},{16,2},{18,0},{1,19},{3,17},{17,3},{19,1},{4,22},{6,... | collective-permute-start | bytes 589832 | tf_op jit(solution)/shard_map/ppermute | solution.py:417
  8.5 31.6 %collective-permute-start.4 = (bf16[2,2,64,384]{3,2,1,0:T(8,128)(2,1)S(1)}, bf16[2,2,64,384]{3,2,1,0:T(8,128)(2,1)S(1)}, u32[]{:S(2)}, u32[]{:S(2)}) collective-permute-start(bf16[2,2,64,384]{3,2,1,0:T(8,128)(2,1)S(1)} %get-tuple-element.43), channel_id=1, source_target_pairs={{0,16},{2,18},{16,0},{18,2},{1,17},{3,19},{17,1},{19,3},{4,20},{6,... | collective-permute-start | bytes 589832 | tf_op jit(solution)/shard_map/ppermute | solution.py:417
  24.9 25.6 %copy-start = (bf16[4,128,384]{2,1,0:T(8,128)(2,1)}, bf16[4,128,384]{2,1,0:T(8,128)(2,1)S(1)}, u32[]{:S(2)}) copy-start(bf16[4,128,384]{2,1,0:T(8,128)(2,1)S(1)} %get-tuple-element.46.refs_0_) | copy-start | bytes 1179652
  24.9 25.6 %copy-start.1 = (bf16[4,128,384]{2,1,0:T(8,128)(2,1)}, bf16[4,128,384]{2,1,0:T(8,128)(2,1)S(1)}, u32[]{:S(2)}) copy-start(bf16[4,128,384]{2,1,0:T(8,128)(2,1)S(1)} %get-tuple-element.47.refs_1_) | copy-start | bytes 1179652
  24.9 25.6 %collective-permute-start.6 = (bf16[4,128,384]{2,1,0:T(8,128)(2,1)S(1)}, bf16[4,128,384]{2,1,0:T(8,128)(2,1)S(1)}, u32[]{:S(2)}, u32[]{:S(2)}) collective-permute-start(bf16[4,128,384]{2,1,0:T(8,128)(2,1)S(1)} %get-tuple-element.47.refs_1_), channel_id=1, source_target_pairs={{0,1},{1,4},{4,5},{5,8},{8,9},{9,12},{12,13},{13,0},{2,3},{3,6},{6... | collective-permute-start | bytes 1179656 | tf_op jit(solution)/shard_map/ppermute | solution.py:420
  25.0 25.5 %collective-permute-start.7 = (bf16[4,128,384]{2,1,0:T(8,128)(2,1)S(1)}, bf16[4,128,384]{2,1,0:T(8,128)(2,1)S(1)}, u32[]{:S(2)}, u32[]{:S(2)}) collective-permute-start(bf16[4,128,384]{2,1,0:T(8,128)(2,1)S(1)} %get-tuple-element.46.refs_0_), channel_id=1, source_target_pairs={{1,0},{4,1},{5,4},{8,5},{9,8},{12,9},{13,12},{0,13},{3,2},{6,3},{7... | collective-permute-start | bytes 1179656 | tf_op jit(solution)/shard_map/ppermute | solution.py:420
  31.3 11.5 %collective-permute-start.5 = (bf16[2,2,64,384]{3,2,1,0:T(8,128)(2,1)S(1)}, bf16[2,2,64,384]{3,2,1,0:T(8,128)(2,1)S(1)}, u32[]{:S(2)}, u32[]{:S(2)}) collective-permute-start(bf16[2,2,64,384]{3,2,1,0:T(8,128)(2,1)S(1)} %get-tuple-element.44), channel_id=1, source_target_pairs={{0,18},{2,16},{16,2},{18,0},{1,19},{3,17},{17,3},{19,1},{4,22},{6,... | collective-permute-start | bytes 589832 | tf_op jit(solution)/shard_map/ppermute | solution.py:417
  40.0 7.8 %collective-permute-start.8 = (bf16[2,128,384]{2,1,0:T(8,128)(2,1)S(1)}, bf16[2,128,384]{2,1,0:T(8,128)(2,1)S(1)}, u32[]{:S(2)}, u32[]{:S(2)}) collective-permute-start(bf16[2,128,384]{2,1,0:T(8,128)(2,1)S(1)} %get-tuple-element.49.refs_5_), channel_id=1, source_target_pairs={{0,1},{1,4},{4,5},{5,8},{8,9},{9,12},{12,13},{13,0},{2,3},{3,6},{6... | collective-permute-start | bytes 589832 | tf_op jit(solution)/shard_map/ppermute | solution.py:420
  40.1 10.4 %collective-permute-start.9 = (bf16[2,128,384]{2,1,0:T(8,128)(2,1)S(1)}, bf16[2,128,384]{2,1,0:T(8,128)(2,1)S(1)}, u32[]{:S(2)}, u32[]{:S(2)}) collective-permute-start(bf16[2,128,384]{2,1,0:T(8,128)(2,1)S(1)} %get-tuple-element.48.refs_4_), channel_id=1, source_target_pairs={{1,0},{4,1},{5,4},{8,5},{9,8},{12,9},{13,12},{0,13},{3,2},{6,3},{7... | collective-permute-start | bytes 589832 | tf_op jit(solution)/shard_map/ppermute | solution.py:420
  47.8 13.5 %collective-permute-start.13 = (bf16[2,128,384]{2,1,0:T(8,128)(2,1)}, bf16[2,128,384]{2,1,0:T(8,128)(2,1)}, u32[]{:S(2)}, u32[]{:S(2)}) collective-permute-start(bf16[2,128,384]{2,1,0:T(8,128)(2,1)} %get-tuple-element.58.refs_5_), channel_id=1, source_target_pairs={{0,1},{1,4},{4,5},{5,8},{8,9},{9,12},{12,13},{13,0},{2,3},{3,6},{6... | collective-permute-start | bytes 589832 | tf_op jit(solution)/shard_map/ppermute | solution.py:420
  47.8 13.5 %collective-permute-start.14 = (bf16[2,128,384]{2,1,0:T(8,128)(2,1)}, bf16[2,128,384]{2,1,0:T(8,128)(2,1)}, u32[]{:S(2)}, u32[]{:S(2)}) collective-permute-start(bf16[2,128,384]{2,1,0:T(8,128)(2,1)} %get-tuple-element.57.refs_4_), channel_id=1, source_target_pairs={{1,0},{4,1},{5,4},{8,5},{9,8},{12,9},{13,12},{0,13},{3,2},{6,3},{7... | collective-permute-start | bytes 589832 | tf_op jit(solution)/shard_map/ppermute | solution.py:420
  50.5 6.4 %copy-start.2 = (bf16[4,128,384]{2,1,0:T(8,128)(2,1)}, bf16[4,128,384]{2,1,0:T(8,128)(2,1)S(1)}, u32[]{:S(2)}) copy-start(bf16[4,128,384]{2,1,0:T(8,128)(2,1)S(1)} %collective-permute-done.6.refs_2_) | copy-start | bytes 1179652
  50.5 6.4 %copy-start.3 = (bf16[4,128,384]{2,1,0:T(8,128)(2,1)}, bf16[4,128,384]{2,1,0:T(8,128)(2,1)S(1)}, u32[]{:S(2)}) copy-start(bf16[4,128,384]{2,1,0:T(8,128)(2,1)S(1)} %collective-permute-done.7.refs_3_) | copy-start | bytes 1179652
  56.9 16.4 %collective-permute-start.10 = (bf16[2,2,64,384]{3,2,1,0:T(8,128)(2,1)}, bf16[2,2,64,384]{3,2,1,0:T(8,128)(2,1)}, u32[]{:S(2)}, u32[]{:S(2)}) collective-permute-start(bf16[2,2,64,384]{3,2,1,0:T(8,128)(2,1)} %get-tuple-element.53), channel_id=1, source_target_pairs={{0,2},{2,0},{16,18},{18,16},{1,3},{3,1},{17,19},{19,17},{4,6},{6,4... | collective-permute-start | bytes 589832 | tf_op jit(solution)/shard_map/ppermute | solution.py:417
  57.5 26.0 %collective-permute-start.11 = (bf16[2,2,64,384]{3,2,1,0:T(8,128)(2,1)}, bf16[2,2,64,384]{3,2,1,0:T(8,128)(2,1)S(1)}, u32[]{:S(2)}, u32[]{:S(2)}) collective-permute-start(bf16[2,2,64,384]{3,2,1,0:T(8,128)(2,1)} %get-tuple-element.54), channel_id=1, source_target_pairs={{0,16},{2,18},{16,0},{18,2},{1,17},{3,19},{17,1},{19,3},{4,20},{6,... | collective-permute-start | bytes 589832 | tf_op jit(solution)/shard_map/ppermute | solution.py:417
  61.2 26.5 %collective-permute-start.12 = (bf16[2,2,64,384]{3,2,1,0:T(8,128)(2,1)}, bf16[2,2,64,384]{3,2,1,0:T(8,128)(2,1)S(1)}, u32[]{:S(2)}, u32[]{:S(2)}) collective-permute-start(bf16[2,2,64,384]{3,2,1,0:T(8,128)(2,1)} %get-tuple-element.55), channel_id=1, source_target_pairs={{0,18},{2,16},{16,2},{18,0},{1,19},{3,17},{17,3},{19,1},{4,22},{6,... | collective-permute-start | bytes 589832 | tf_op jit(solution)/shard_map/ppermute | solution.py:417
  68.8 4.5 %copy-start.11 = (bf16[2,2,64,384]{3,2,1,0:T(8,128)(2,1)S(1)}, bf16[2,2,64,384]{3,2,1,0:T(8,128)(2,1)}, u32[]{:S(2)}) copy-start(bf16[2,2,64,384]{3,2,1,0:T(8,128)(2,1)} %get-tuple-element.52) | copy-start | bytes 589828
  68.8 18.9 %collective-permute-start.15 = (bf16[2,2,64,384]{3,2,1,0:T(8,128)(2,1)S(1)}, bf16[2,2,64,384]{3,2,1,0:T(8,128)(2,1)S(1)}, u32[]{:S(2)}, u32[]{:S(2)}) collective-permute-start(bf16[2,2,64,384]{3,2,1,0:T(8,128)(2,1)S(1)} %get-tuple-element.60), channel_id=1, source_target_pairs={{0,2},{2,0},{16,18},{18,16},{1,3},{3,1},{17,19},{19,17},{4,6},{6,4... | collective-permute-start | bytes 589832 | tf_op jit(solution)/shard_map/ppermute | solution.py:417
  70.1 21.8 %collective-permute-start.16 = (bf16[2,2,64,384]{3,2,1,0:T(8,128)(2,1)S(1)}, bf16[2,2,64,384]{3,2,1,0:T(8,128)(2,1)S(1)}, u32[]{:S(2)}, u32[]{:S(2)}) collective-permute-start(bf16[2,2,64,384]{3,2,1,0:T(8,128)(2,1)S(1)} %get-tuple-element.61), channel_id=1, source_target_pairs={{0,16},{2,18},{16,0},{18,2},{1,17},{3,19},{17,1},{19,3},{4,20},{6,... | collective-permute-start | bytes 589832 | tf_op jit(solution)/shard_map/ppermute | solution.py:417
  73.4 22.4 %collective-permute-start.17 = (bf16[2,2,64,384]{3,2,1,0:T(8,128)(2,1)S(1)}, bf16[2,2,64,384]{3,2,1,0:T(8,128)(2,1)S(1)}, u32[]{:S(2)}, u32[]{:S(2)}) collective-permute-start(bf16[2,2,64,384]{3,2,1,0:T(8,128)(2,1)S(1)} %get-tuple-element.62), channel_id=1, source_target_pairs={{0,18},{2,16},{16,2},{18,0},{1,19},{3,17},{17,3},{19,1},{4,22},{6,... | collective-permute-start | bytes 589832 | tf_op jit(solution)/shard_map/ppermute | solution.py:417
  95.8 1.1 %copy-start.10 = (bf16[2,16,64,384]{3,2,1,0:T(8,128)(2,1)}, bf16[2,16,64,384]{3,2,1,0:T(8,128)(2,1)S(1)}, u32[]{:S(2)}) copy-start(bf16[2,16,64,384]{3,2,1,0:T(8,128)(2,1)S(1)} %constant_dynamic-update-slice_fusion) | copy-start | bytes 4718596

commit v12 on v11

--- a/solution.py
+++ b/solution.py
@@ -212,28 +212,10 @@
     return both, [cuts[2 * chunk : 2 * chunk + 2] for chunk in range(chunks)]
 
 
-def section_kernel(
-    place,
-    before,
-    mine,
-    other,
-    w_qkv,
-    w_out,
-    w_up,
-    w_down,
-    even_ref,
-    odd_ref,
-    token,
-):
-    token[...] = jnp.zeros_like(token)
-    slots, units, half, features = mine.shape
-    cells = 2 * half
-    parts = []
-    for slot in range(slots):
-        for unit in range(units):
-            parts += [mine[slot, unit], other[slot, unit]]
+def section_rows(parts, cells, w_qkv, w_out, w_up, w_down):
+    features = parts[0].shape[-1]
     residual = jnp.concatenate(parts, axis=0).astype(jnp.float32)
-    frame_count = slots * units
+    frame_count = residual.shape[0] // cells
     normed = normalize(residual).astype(jnp.bfloat16)
     projected = jnp.dot(normed, w_qkv[...], preferred_element_type=jnp.float32).astype(jnp.bfloat16)
     pair_width = 2 * HEAD_DIM
@@ -290,7 +272,35 @@
         halved = 0.5 * lifted
         hidden = halved + halved * jnp.tanh(inner)
         total = total + jnp.dot(hidden, w_down[at : at + width], preferred_element_type=jnp.float32)
-    sectioned = total.astype(jnp.bfloat16)
+    return total.astype(jnp.bfloat16)
+
+
+def section_kernel(
+    place,
+    before,
+    mine,
+    other,
+    w_qkv,
+    w_out,
+    w_up,
+    w_down,
+    even_ref,
+    odd_ref,
+    token,
+):
+    token[...] = jnp.zeros_like(token)
+    slots, units, half, features = mine.shape
+    cells = 2 * half
+    parts = []
+    for slot in range(slots):
+        for unit in range(units):
+            parts += [mine[slot, unit], other[slot, unit]]
+    frames = slots * units
+    per = max(frames // 2, 1)
+    done = []
+    for at in range(0, frames, per):
+        done.append(section_rows(parts[2 * at : 2 * (at + per)], cells, w_qkv, w_out, w_up, w_down))
+    sectioned = jnp.concatenate(done, axis=0)
     for unit in range(units):
         even_ref[unit] = sectioned[unit * cells : (unit + 1) * cells]
         odd_ref[unit] = sectioned[(units + unit) * cells : (units + unit + 1) * cells]
@@ -303,12 +313,11 @@
     return center + jnp.tanh(preact[:, :features]) * opened
 
 
-def temporal_kernel(chunk, place, before, *refs):
-    *fields, w_first, w_second, out0, out1, out2, out3, token = refs
-    token[...] = jnp.zeros_like(token)
+def temporal_unit(place, fields, w_first, w_second, outs, own_unit, far_unit):
     near, is_first, is_last = place[1], place[2], place[3]
-    units, cells, features = fields[4].shape
-    spans = [slice(chunk * units, (chunk + 1) * units)] * 4 + [slice(0, units)] * 4
+    cells, features = fields[0].shape[1:]
+    spans = [slice(own_unit, own_unit + 1)] * 4 + [slice(far_unit, far_unit + 1)] * 4
+    units = 1
     flat = [field[at].reshape(units * cells, features) for field, at in zip(fields, spans)]
     zero = jnp.zeros_like(flat[0])
     pairs = [(flat[i], flat[i + 4]) for i in range(4)]
@@ -341,12 +350,19 @@
     other = jnp.where(near == 0, result_f, result_n)
     half = cells // 2
     for slot in range(2):
-        for unit in range(units):
-            at = (slot * units + unit) * cells
-            out0[slot, unit] = same[at : at + half]
-            out1[slot, unit] = same[at + half : at + cells]
-            out2[slot, unit] = other[at : at + half]
-            out3[slot, unit] = other[at + half : at + cells]
+        at = slot * cells
+        outs[0][slot, far_unit] = same[at : at + half]
+        outs[1][slot, far_unit] = same[at + half : at + cells]
+        outs[2][slot, far_unit] = other[at : at + half]
+        outs[3][slot, far_unit] = other[at + half : at + cells]
+
+
+def temporal_kernel(chunk, place, before, *refs):
+    fields, (w_first, w_second, *outs, token) = refs[:8], refs[8:]
+    token[...] = jnp.zeros_like(token)
+    count = fields[4].shape[0]
+    for unit in range(count):
+        temporal_unit(place, fields, w_first, w_second, outs, chunk * count + unit, unit)
 
 
 def run_section(place, before, mine, other, weights, units, chunks, from_frames):

time: 97.2 us -> 99.2 us (1.021)
  Pallas kernels: 36.4 us -> 39.2 us
    pallas_call x3, Pallas kernels: 18.8 us -> 23.4 us  [run_section(): pl.pallas_call(section_kernel, grid_spec=pltpu.PrefetchScalarGridSpec(num...]
    pallas_call x2, Pallas kernels: 13.9 us -> 12.1 us  [run_temporal(): pl.pallas_call(functools.partial(temporal_kernel, 0 if last else chunk),...]
  transfers between devices with their start and end apart: 18 -> 18, of which waited for: 5 -> 5; matrix products, arithmetic and copies ran while one was open for 1% -> 1% of each run, Pallas kernels for 35% -> 37%
where the time goes in v12:
time: 99.2 us; the launch traced here: 99 us
  Pallas kernels  39.2 us (40%)
  starting transfers between devices  33.4 us (34%)
  waiting for transfers between devices  23.4 us (24%)
  local copies, waits for them, and re-layouts  2.72 us (3%)
    ppermute x11, waiting for transfers between devices, exchange(): return lax.ppermute(piece, GROUP, [(i, i ^ delta) for i in range(4)])  23.4 us
    pallas_call x3, Pallas kernels, run_section(): pl.pallas_call(section_kernel, grid_spec=pltpu.PrefetchScalarGridSpec(num...  23.4 us
    ppermute x11, starting transfers between devices, exchange(): return lax.ppermute(piece, GROUP, [(i, i ^ delta) for i in range(4)])  21.2 us
    pallas_call x2, Pallas kernels, run_temporal(): pl.pallas_call(functools.partial(temporal_kernel, 0 if last else chunk),...  12.1 us
    ppermute x3, starting transfers between devices, halo(): lax.ppermute(even, RING, leftward)  11.6 us
    pallas_call x1, Pallas kernels, run_pack(): pl.pallas_call(functools.partial(pack_kernel, chunks), grid_spec=pltpu.Pr...  2.27 us
  transfers between devices with their start and end apart: 18, of which 5 were waited for; matrix products, arithmetic and copies ran while one was open for 1% of the time, Pallas kernels for 37%

profile of v12, /device:TPU:0, one launch (start us, length us, event | category | flops | bytes accessed | tf_op | source)
XLA Modules:
  0.0 99.0 jit_solution(484299302611669307)
XLA Ops:
  0.0 0.1 stack.31.place.before
  0.1 2.3 %pack.1 = (bf16[2,4,64,384]{3,2,1,0:T(8,128)(2,1)S(1)}, bf16[2,2,64,384]{3,2,1,0:T(8,128)(2,1)S(1)}, bf16[2,2,64,384]{3,2,1,0:T(8,128)(2,1)S(1)}, bf16[2,2,64,38...) custom-call(s32[5]{0:T(128)S(1)} %stack.31.place.before, bf16[2,16,64,384]{3,2,1,0:T(8,128)(2,1)} %bitcast.7, ...), custom_call_target="tpu_custom_call" | custom-call | bytes 786432 | tf_op jit(solution)/shard_map/pack/pallas_call | solution.py:198
  2.5 0.3 pack_weights.1.before.mine
  2.8 0.5 collective-permute-start.1
  3.3 2.6 %collective-permute-start = (bf16[2,4,64,384]{3,2,1,0:T(8,128)(2,1)S(1)}, bf16[2,4,64,384]{3,2,1,0:T(8,128)(2,1)S(1)}, u32[]{:S(2)}, u32[]{:S(2)}) collective-permute-start(bf16[2,4,64,384]{3,2,1,0:T(8,128)(2,1)S(1)} %get-tuple-element.34), channel_id=1, source_target_pairs={{0,2},{2,0},{16,18},{18,16},{1,3},{3,1},{17,19},{19,17},{4,6},{6,4... | collective-permute-start | bytes 1179656 | tf_op jit(solution)/shard_map/ppermute | solution.py:433
  5.9 2.6 %collective-permute-start.2 = (bf16[2,2,64,384]{3,2,1,0:T(8,128)(2,1)S(1)}, bf16[2,2,64,384]{3,2,1,0:T(8,128)(2,1)S(1)}, u32[]{:S(2)}, u32[]{:S(2)}) collective-permute-start(bf16[2,2,64,384]{3,2,1,0:T(8,128)(2,1)S(1)} %get-tuple-element.35.before), channel_id=1, source_target_pairs={{0,16},{2,18},{16,0},{18,2},{1,17},{3,19},{17,1},{19,3},{4,20},{6,... | collective-permute-start | bytes 589832 | tf_op jit(solution)/shard_map/ppermute | solution.py:433
  8.5 2.9 %collective-permute-start.4 = (bf16[2,2,64,384]{3,2,1,0:T(8,128)(2,1)S(1)}, bf16[2,2,64,384]{3,2,1,0:T(8,128)(2,1)S(1)}, u32[]{:S(2)}, u32[]{:S(2)}) collective-permute-start(bf16[2,2,64,384]{3,2,1,0:T(8,128)(2,1)S(1)} %get-tuple-element.43), channel_id=1, source_target_pairs={{0,16},{2,18},{16,0},{18,2},{1,17},{3,19},{17,1},{19,3},{4,20},{6,... | collective-permute-start | bytes 589832 | tf_op jit(solution)/shard_map/ppermute | solution.py:433
  11.4 1.2 %join_weights.1 = (bf16[384,1152]{1,0:T(8,128)(2,1)S(1)}, bf16[384,384]{1,0:T(8,128)(2,1)S(1)}, bf16[384,1536]{1,0:T(8,128)(2,1)S(1)}, bf16[1536,384]{1,0:T(8,12...) custom-call(s32[5]{0:T(128)S(1)} %stack.31.place.before, ...), custom_call_target="tpu_custom_call" | custom-call | bytes 1769472 | tf_op jit(solution)/shard_map/join_weights/pallas_call | solution.py:168
  12.5 3.1 %collective-permute-done.other = bf16[2,4,64,384]{3,2,1,0:T(8,128)(2,1)S(1)} collective-permute-done((bf16[2,4,64,384]{3,2,1,0:T(8,128)(2,1)S(1)}, bf16[2,4,64,384]{3,2,1,0:T(8,128)(2,1)S(1)}, u32[]{:S(2)}, u32[]{:S(2)}) %collective-permute-start) | collective-permute-done | bytes 393248 | tf_op jit(solution)/shard_map/ppermute | solution.py:433
  15.6 11.6 %section.3 = (bf16[4,128,384]{2,1,0:T(8,128)(2,1)S(1)}, bf16[4,128,384]{2,1,0:T(8,128)(2,1)S(1)}, f32[8,128]{1,0:T(8,128)S(1)}) custom-call(s32[5]{0:T(128)S(1)} %stack.31.place.before, s32[5]{0:T(128)S(1)} %stack.31.place.before, bf16[2,16,64,384]{3,2,1,0:T(8,128)(2,1)} %bitcast.13, bf16[2,4,64,384]{3,2,1,0:T(8,128)(2,1)S(1)} %collective-permute-done.other, ...), custom_call_target="tpu_custom_call" | custom-call | bytes 98304 | tf_op jit(solution)/shard_map/section/pallas_call | solution.py:376
  27.2 0.1 collective-permute-start.6
  27.3 6.3 %collective-permute-start.7 = (bf16[4,128,384]{2,1,0:T(8,128)(2,1)S(1)}, bf16[4,128,384]{2,1,0:T(8,128)(2,1)S(1)}, u32[]{:S(2)}, u32[]{:S(2)}) collective-permute-start(bf16[4,128,384]{2,1,0:T(8,128)(2,1)S(1)} %get-tuple-element.46.refs_0_), channel_id=1, source_target_pairs={{1,0},{4,1},{5,4},{8,5},{9,8},{12,9},{13,12},{0,13},{3,2},{6,3},{7... | collective-permute-start | bytes 1179656 | tf_op jit(solution)/shard_map/ppermute | solution.py:436
  33.6 4.3 %collective-permute-start.5 = (bf16[2,2,64,384]{3,2,1,0:T(8,128)(2,1)S(1)}, bf16[2,2,64,384]{3,2,1,0:T(8,128)(2,1)S(1)}, u32[]{:S(2)}, u32[]{:S(2)}) collective-permute-start(bf16[2,2,64,384]{3,2,1,0:T(8,128)(2,1)S(1)} %get-tuple-element.44), channel_id=1, source_target_pairs={{0,18},{2,16},{16,2},{18,0},{1,19},{3,17},{17,3},{19,1},{4,22},{6,... | collective-permute-start | bytes 589832 | tf_op jit(solution)/shard_map/ppermute | solution.py:433
  37.9 5.6 %section.4 = (bf16[2,128,384]{2,1,0:T(8,128)(2,1)S(1)}, bf16[2,128,384]{2,1,0:T(8,128)(2,1)S(1)}, f32[8,128]{1,0:T(8,128)S(1)}) custom-call(s32[5]{0:T(128)S(1)} %stack.31.place.before, f32[8,128]{1,0:T(8,128)S(1)} %get-tuple-element.40.before, bf16[2,2,64,384]{3,2,1,0:T(8,128)(2,1)S(1)} %collective-permute-done.2.mine, ...), custom_call_target="tpu_custom_call" | custom-call | bytes 49152 | tf_op jit(solution)/shard_map/section/pallas_call | solution.py:376
  43.6 2.6 %collective-permute-start.9 = (bf16[2,128,384]{2,1,0:T(8,128)(2,1)S(1)}, bf16[2,128,384]{2,1,0:T(8,128)(2,1)S(1)}, u32[]{:S(2)}, u32[]{:S(2)}) collective-permute-start(bf16[2,128,384]{2,1,0:T(8,128)(2,1)S(1)} %get-tuple-element.48.refs_4_), channel_id=1, source_target_pairs={{1,0},{4,1},{5,4},{8,5},{9,8},{12,9},{13,12},{0,13},{3,2},{6,3},{7... | collective-permute-start | bytes 589832 | tf_op jit(solution)/shard_map/ppermute | solution.py:436
  46.2 6.2 %section.5 = (bf16[2,128,384]{2,1,0:T(8,128)(2,1)}, bf16[2,128,384]{2,1,0:T(8,128)(2,1)}, f32[8,128]{1,0:T(8,128)S(1)}) custom-call(s32[5]{0:T(128)S(1)} %stack.31.place.before, f32[8,128]{1,0:T(8,128)S(1)} %get-tuple-element.42.before, bf16[2,2,64,384]{3,2,1,0:T(8,128)(2,1)S(1)} %collective-permute-done.4.mine, ...), custom_call_target="tpu_custom_call" | custom-call | bytes 49152 | tf_op jit(solution)/shard_map/section/pallas_call | solution.py:376
  52.4 2.6 %collective-permute-start.14 = (bf16[2,128,384]{2,1,0:T(8,128)(2,1)}, bf16[2,128,384]{2,1,0:T(8,128)(2,1)}, u32[]{:S(2)}, u32[]{:S(2)}) collective-permute-start(bf16[2,128,384]{2,1,0:T(8,128)(2,1)} %get-tuple-element.57.refs_4_), channel_id=1, source_target_pairs={{1,0},{4,1},{5,4},{8,5},{9,8},{12,9},{13,12},{0,13},{3,2},{6,3},{7... | collective-permute-start | bytes 589832 | tf_op jit(solution)/shard_map/ppermute | solution.py:436
  55.1 5.5 %temporal.2 = (bf16[2,2,64,384]{3,2,1,0:T(8,128)(2,1)}, bf16[2,2,64,384]{3,2,1,0:T(8,128)(2,1)}, bf16[2,2,64,384]{3,2,1,0:T(8,128)(2,1)}, bf16[2,2,64,384]{3,2,1,0:T(8,128)(2,1)}, f32[8,128]{1,0:T(8,128)S(1)}) custom-call(s32[5]{0:T(128)S(1)} %stack.31.place.before, f32[8,128]{1,0:T(8,128)S(1)} %get-tuple-element.45.before, ...), custom_call_target="tpu_custom_call" | custom-call | bytes 98304 | tf_op jit(solution)/shard_map/temporal/pallas_call | solution.py:398
  60.6 0.5 collective-permute-start.10
  61.1 1.4 %collective-permute-start.11 = (bf16[2,2,64,384]{3,2,1,0:T(8,128)(2,1)}, bf16[2,2,64,384]{3,2,1,0:T(8,128)(2,1)S(1)}, u32[]{:S(2)}, u32[]{:S(2)}) collective-permute-start(bf16[2,2,64,384]{3,2,1,0:T(8,128)(2,1)} %get-tuple-element.54), channel_id=1, source_target_pairs={{0,16},{2,18},{16,0},{18,2},{1,17},{3,19},{17,1},{19,3},{4,20},{6,... | collective-permute-start | bytes 589832 | tf_op jit(solution)/shard_map/ppermute | solution.py:433
  62.5 2.5 %collective-permute-start.12 = (bf16[2,2,64,384]{3,2,1,0:T(8,128)(2,1)}, bf16[2,2,64,384]{3,2,1,0:T(8,128)(2,1)S(1)}, u32[]{:S(2)}, u32[]{:S(2)}) collective-permute-start(bf16[2,2,64,384]{3,2,1,0:T(8,128)(2,1)} %get-tuple-element.55), channel_id=1, source_target_pairs={{0,18},{2,16},{16,2},{18,0},{1,19},{3,17},{17,3},{19,1},{4,22},{6,... | collective-permute-start | bytes 589832 | tf_op jit(solution)/shard_map/ppermute | solution.py:433
  65.0 6.6 %temporal.3 = (bf16[2,2,64,384]{3,2,1,0:T(8,128)(2,1)S(1)}, bf16[2,2,64,384]{3,2,1,0:T(8,128)(2,1)S(1)}, bf16[2,2,64,384]{3,2,1,0:T(8,128)(2,1)S(1)}, bf16[2,2,64,384]{3,2,1,0:T(8,128)(2,1)S(1)}, f32[8,128]{1,0:T(8,128)}) custom-call(s32[5]{0:T(128)S(1)} %stack.31.place.before, f32[8,128]{1,0:T(8,128)S(1)} %get-tuple-element.56.before, ...), custom_call_target="tpu_custom_call" | custom-call | bytes 98304 | tf_op jit(solution)/shard_map/temporal/pallas_call | solution.py:398
  71.6 0.5 collective-permute-start.15
  72.1 1.4 %collective-permute-start.16 = (bf16[2,2,64,384]{3,2,1,0:T(8,128)(2,1)S(1)}, bf16[2,2,64,384]{3,2,1,0:T(8,128)(2,1)S(1)}, u32[]{:S(2)}, u32[]{:S(2)}) collective-permute-start(bf16[2,2,64,384]{3,2,1,0:T(8,128)(2,1)S(1)} %get-tuple-element.61), channel_id=1, source_target_pairs={{0,16},{2,18},{16,0},{18,2},{1,17},{3,19},{17,1},{19,3},{4,20},{6,... | collective-permute-start | bytes 589832 | tf_op jit(solution)/shard_map/ppermute | solution.py:433
  73.5 0.2 broadcast_in_dim.3
  73.8 2.6 %collective-permute-start.17 = (bf16[2,2,64,384]{3,2,1,0:T(8,128)(2,1)S(1)}, bf16[2,2,64,384]{3,2,1,0:T(8,128)(2,1)S(1)}, u32[]{:S(2)}, u32[]{:S(2)}) collective-permute-start(bf16[2,2,64,384]{3,2,1,0:T(8,128)(2,1)S(1)} %get-tuple-element.62), channel_id=1, source_target_pairs={{0,18},{2,16},{16,2},{18,0},{1,19},{3,17},{17,3},{19,1},{4,22},{6,... | collective-permute-start | bytes 589832 | tf_op jit(solution)/shard_map/ppermute | solution.py:433
  76.4 1.0 constant_dynamic-update-slice_fusion.6
  77.3 7.5 %collective-permute-done.11 = bf16[2,2,64,384]{3,2,1,0:T(8,128)(2,1)S(1)} collective-permute-done((bf16[2,2,64,384]{3,2,1,0:T(8,128)(2,1)}, bf16[2,2,64,384]{3,2,1,0:T(8,128)(2,1)S(1)}, u32[]{:S(2)}, u32[]{:S(2)}) %collective-permute-start.11) | collective-permute-done | bytes 196640 | tf_op jit(solution)/shard_map/ppermute | solution.py:433
  84.9 4.7 %collective-permute-done.12 = bf16[2,2,64,384]{3,2,1,0:T(8,128)(2,1)S(1)} collective-permute-done((bf16[2,2,64,384]{3,2,1,0:T(8,128)(2,1)}, bf16[2,2,64,384]{3,2,1,0:T(8,128)(2,1)S(1)}, u32[]{:S(2)}, u32[]{:S(2)}) %collective-permute-start.12) | collective-permute-done | bytes 196640 | tf_op jit(solution)/shard_map/ppermute | solution.py:433
  89.6 3.6 %collective-permute-done.16 = bf16[2,2,64,384]{3,2,1,0:T(8,128)(2,1)S(1)} collective-permute-done((bf16[2,2,64,384]{3,2,1,0:T(8,128)(2,1)S(1)}, bf16[2,2,64,384]{3,2,1,0:T(8,128)(2,1)S(1)}, u32[]{:S(2)}, u32[]{:S(2)}) %collective-permute-start.16) | collective-permute-done | bytes 196640 | tf_op jit(solution)/shard_map/ppermute | solution.py:433
  93.3 4.6 %collective-permute-done.17 = bf16[2,2,64,384]{3,2,1,0:T(8,128)(2,1)S(1)} collective-permute-done((bf16[2,2,64,384]{3,2,1,0:T(8,128)(2,1)S(1)}, bf16[2,2,64,384]{3,2,1,0:T(8,128)(2,1)S(1)}, u32[]{:S(2)}, u32[]{:S(2)}) %collective-permute-start.17) | collective-permute-done | bytes 196640 | tf_op jit(solution)/shard_map/ppermute | solution.py:433
  97.9 1.1 %copy-done.10 = bf16[2,16,64,384]{3,2,1,0:T(8,128)(2,1)} copy-done((bf16[2,16,64,384]{3,2,1,0:T(8,128)(2,1)}, bf16[2,16,64,384]{3,2,1,0:T(8,128)(2,1)S(1)}, u32[]{:S(2)}) %copy-start.10) | copy-done | bytes 1572888
  (46 shorter events, 0.4 us)
Async XLA Ops:
  0.1 2.3 %copy-start.4 = (bf16[576,768]{1,0:T(8,128)(2,1)S(1)}, bf16[576,768]{1,0:T(8,128)(2,1)}, u32[]{:S(2)}) copy-start(bf16[576,768]{1,0:T(8,128)(2,1)} %refs_4_.1) | copy-start | bytes 2654212
  0.1 2.3 %copy-start.5 = (bf16[576,768]{1,0:T(8,128)(2,1)S(1)}, bf16[576,768]{1,0:T(8,128)(2,1)}, u32[]{:S(2)}) copy-start(bf16[576,768]{1,0:T(8,128)(2,1)} %refs_5_.1) | copy-start | bytes 2654212
  0.1 2.3 %copy-start.6 = (bf16[192,1536]{1,0:T(8,128)(2,1)S(1)}, bf16[192,1536]{1,0:T(8,128)(2,1)}, u32[]{:S(2)}) copy-start(bf16[192,1536]{1,0:T(8,128)(2,1)} %refs_2_.1) | copy-start | bytes 1769476
  0.1 2.3 %copy-start.7 = (bf16[768,384]{1,0:T(8,128)(2,1)S(1)}, bf16[768,384]{1,0:T(8,128)(2,1)}, u32[]{:S(2)}) copy-start(bf16[768,384]{1,0:T(8,128)(2,1)} %refs_3_.1) | copy-start | bytes 1769476
  0.1 2.3 %copy-start.8 = (bf16[192,1152]{1,0:T(8,128)(2,1)S(1)}, bf16[192,1152]{1,0:T(8,128)(2,1)}, u32[]{:S(2)}) copy-start(bf16[192,1152]{1,0:T(8,128)(2,1)} %refs_0_.1) | copy-start | bytes 1327108
  0.1 2.4 %copy-start.9 = (bf16[192,384]{1,0:T(8,128)(2,1)S(1)}, bf16[192,384]{1,0:T(8,128)(2,1)}, u32[]{:S(2)}) copy-start(bf16[192,384]{1,0:T(8,128)(2,1)} %refs_1_.1) | copy-start | bytes 442372
  2.8 8.6 %collective-permute-start.1 = (bf16[4608,384]{1,0:T(8,128)(2,1)S(1)}, bf16[4608,384]{1,0:T(8,128)(2,1)S(1)}, u32[]{:S(2)}, u32[]{:S(2)}) collective-permute-start(bf16[4608,384]{1,0:T(8,128)(2,1)S(1)} %pack_weights.1.before.mine), channel_id=1, source_target_pairs={{0,1},{1,0},{2,3},{3,2},{4,5},{5,4},{6,7},{7,6},{8,9},{9,8},{10,11... | collective-permute-start | bytes 10616840 | tf_op jit(solution)/shard_map/ppermute | solution.py:443
  3.3 12.3 %collective-permute-start = (bf16[2,4,64,384]{3,2,1,0:T(8,128)(2,1)S(1)}, bf16[2,4,64,384]{3,2,1,0:T(8,128)(2,1)S(1)}, u32[]{:S(2)}, u32[]{:S(2)}) collective-permute-start(bf16[2,4,64,384]{3,2,1,0:T(8,128)(2,1)S(1)} %get-tuple-element.34), channel_id=1, source_target_pairs={{0,2},{2,0},{16,18},{18,16},{1,3},{3,1},{17,19},{19,17},{4,6},{6,4... | collective-permute-start | bytes 1179656 | tf_op jit(solution)/shard_map/ppermute | solution.py:433
  5.9 27.7 %collective-permute-start.2 = (bf16[2,2,64,384]{3,2,1,0:T(8,128)(2,1)S(1)}, bf16[2,2,64,384]{3,2,1,0:T(8,128)(2,1)S(1)}, u32[]{:S(2)}, u32[]{:S(2)}) collective-permute-start(bf16[2,2,64,384]{3,2,1,0:T(8,128)(2,1)S(1)} %get-tuple-element.35.before), channel_id=1, source_target_pairs={{0,16},{2,18},{16,0},{18,2},{1,17},{3,19},{17,1},{19,3},{4,20},{6,... | collective-permute-start | bytes 589832 | tf_op jit(solution)/shard_map/ppermute | solution.py:433
  8.5 29.4 %collective-permute-start.3 = (bf16[2,2,64,384]{3,2,1,0:T(8,128)(2,1)S(1)}, bf16[2,2,64,384]{3,2,1,0:T(8,128)(2,1)S(1)}, u32[]{:S(2)}, u32[]{:S(2)}) collective-permute-start(bf16[2,2,64,384]{3,2,1,0:T(8,128)(2,1)S(1)} %get-tuple-element.41), channel_id=1, source_target_pairs={{0,18},{2,16},{16,2},{18,0},{1,19},{3,17},{17,3},{19,1},{4,22},{6,... | collective-permute-start | bytes 589832 | tf_op jit(solution)/shard_map/ppermute | solution.py:433
  8.5 35.1 %collective-permute-start.4 = (bf16[2,2,64,384]{3,2,1,0:T(8,128)(2,1)S(1)}, bf16[2,2,64,384]{3,2,1,0:T(8,128)(2,1)S(1)}, u32[]{:S(2)}, u32[]{:S(2)}) collective-permute-start(bf16[2,2,64,384]{3,2,1,0:T(8,128)(2,1)S(1)} %get-tuple-element.43), channel_id=1, source_target_pairs={{0,16},{2,18},{16,0},{18,2},{1,17},{3,19},{17,1},{19,3},{4,20},{6,... | collective-permute-start | bytes 589832 | tf_op jit(solution)/shard_map/ppermute | solution.py:433
  27.2 27.9 %copy-start = (bf16[4,128,384]{2,1,0:T(8,128)(2,1)}, bf16[4,128,384]{2,1,0:T(8,128)(2,1)S(1)}, u32[]{:S(2)}) copy-start(bf16[4,128,384]{2,1,0:T(8,128)(2,1)S(1)} %get-tuple-element.46.refs_0_) | copy-start | bytes 1179652
  27.2 27.9 %copy-start.1 = (bf16[4,128,384]{2,1,0:T(8,128)(2,1)}, bf16[4,128,384]{2,1,0:T(8,128)(2,1)S(1)}, u32[]{:S(2)}) copy-start(bf16[4,128,384]{2,1,0:T(8,128)(2,1)S(1)} %get-tuple-element.47.refs_1_) | copy-start | bytes 1179652
  27.2 27.9 %collective-permute-start.6 = (bf16[4,128,384]{2,1,0:T(8,128)(2,1)S(1)}, bf16[4,128,384]{2,1,0:T(8,128)(2,1)S(1)}, u32[]{:S(2)}, u32[]{:S(2)}) collective-permute-start(bf16[4,128,384]{2,1,0:T(8,128)(2,1)S(1)} %get-tuple-element.47.refs_1_), channel_id=1, source_target_pairs={{0,1},{1,4},{4,5},{5,8},{8,9},{9,12},{12,13},{13,0},{2,3},{3,6},{6... | collective-permute-start | bytes 1179656 | tf_op jit(solution)/shard_map/ppermute | solution.py:436
  27.3 27.8 %collective-permute-start.7 = (bf16[4,128,384]{2,1,0:T(8,128)(2,1)S(1)}, bf16[4,128,384]{2,1,0:T(8,128)(2,1)S(1)}, u32[]{:S(2)}, u32[]{:S(2)}) collective-permute-start(bf16[4,128,384]{2,1,0:T(8,128)(2,1)S(1)} %get-tuple-element.46.refs_0_), channel_id=1, source_target_pairs={{1,0},{4,1},{5,4},{8,5},{9,8},{12,9},{13,12},{0,13},{3,2},{6,3},{7... | collective-permute-start | bytes 1179656 | tf_op jit(solution)/shard_map/ppermute | solution.py:436
  33.6 12.6 %collective-permute-start.5 = (bf16[2,2,64,384]{3,2,1,0:T(8,128)(2,1)S(1)}, bf16[2,2,64,384]{3,2,1,0:T(8,128)(2,1)S(1)}, u32[]{:S(2)}, u32[]{:S(2)}) collective-permute-start(bf16[2,2,64,384]{3,2,1,0:T(8,128)(2,1)S(1)} %get-tuple-element.44), channel_id=1, source_target_pairs={{0,18},{2,16},{16,2},{18,0},{1,19},{3,17},{17,3},{19,1},{4,22},{6,... | collective-permute-start | bytes 589832 | tf_op jit(solution)/shard_map/ppermute | solution.py:433
  43.5 8.9 %collective-permute-start.8 = (bf16[2,128,384]{2,1,0:T(8,128)(2,1)S(1)}, bf16[2,128,384]{2,1,0:T(8,128)(2,1)S(1)}, u32[]{:S(2)}, u32[]{:S(2)}) collective-permute-start(bf16[2,128,384]{2,1,0:T(8,128)(2,1)S(1)} %get-tuple-element.49.refs_5_), channel_id=1, source_target_pairs={{0,1},{1,4},{4,5},{5,8},{8,9},{9,12},{12,13},{13,0},{2,3},{3,6},{6... | collective-permute-start | bytes 589832 | tf_op jit(solution)/shard_map/ppermute | solution.py:436
  43.6 11.5 %collective-permute-start.9 = (bf16[2,128,384]{2,1,0:T(8,128)(2,1)S(1)}, bf16[2,128,384]{2,1,0:T(8,128)(2,1)S(1)}, u32[]{:S(2)}, u32[]{:S(2)}) collective-permute-start(bf16[2,128,384]{2,1,0:T(8,128)(2,1)S(1)} %get-tuple-element.48.refs_4_), channel_id=1, source_target_pairs={{1,0},{4,1},{5,4},{8,5},{9,8},{12,9},{13,12},{0,13},{3,2},{6,3},{7... | collective-permute-start | bytes 589832 | tf_op jit(solution)/shard_map/ppermute | solution.py:436
  52.4 12.6 %collective-permute-start.13 = (bf16[2,128,384]{2,1,0:T(8,128)(2,1)}, bf16[2,128,384]{2,1,0:T(8,128)(2,1)}, u32[]{:S(2)}, u32[]{:S(2)}) collective-permute-start(bf16[2,128,384]{2,1,0:T(8,128)(2,1)} %get-tuple-element.58.refs_5_), channel_id=1, source_target_pairs={{0,1},{1,4},{4,5},{5,8},{8,9},{9,12},{12,13},{13,0},{2,3},{3,6},{6... | collective-permute-start | bytes 589832 | tf_op jit(solution)/shard_map/ppermute | solution.py:436
  52.4 12.6 %collective-permute-start.14 = (bf16[2,128,384]{2,1,0:T(8,128)(2,1)}, bf16[2,128,384]{2,1,0:T(8,128)(2,1)}, u32[]{:S(2)}, u32[]{:S(2)}) collective-permute-start(bf16[2,128,384]{2,1,0:T(8,128)(2,1)} %get-tuple-element.57.refs_4_), channel_id=1, source_target_pairs={{1,0},{4,1},{5,4},{8,5},{9,8},{12,9},{13,12},{0,13},{3,2},{6,3},{7... | collective-permute-start | bytes 589832 | tf_op jit(solution)/shard_map/ppermute | solution.py:436
  55.1 5.5 %copy-start.2 = (bf16[4,128,384]{2,1,0:T(8,128)(2,1)}, bf16[4,128,384]{2,1,0:T(8,128)(2,1)S(1)}, u32[]{:S(2)}) copy-start(bf16[4,128,384]{2,1,0:T(8,128)(2,1)S(1)} %collective-permute-done.6.refs_2_) | copy-start | bytes 1179652
  55.1 5.5 %copy-start.3 = (bf16[4,128,384]{2,1,0:T(8,128)(2,1)}, bf16[4,128,384]{2,1,0:T(8,128)(2,1)S(1)}, u32[]{:S(2)}) copy-start(bf16[4,128,384]{2,1,0:T(8,128)(2,1)S(1)} %collective-permute-done.7.refs_3_) | copy-start | bytes 1179652
  60.6 13.2 %collective-permute-start.10 = (bf16[2,2,64,384]{3,2,1,0:T(8,128)(2,1)}, bf16[2,2,64,384]{3,2,1,0:T(8,128)(2,1)}, u32[]{:S(2)}, u32[]{:S(2)}) collective-permute-start(bf16[2,2,64,384]{3,2,1,0:T(8,128)(2,1)} %get-tuple-element.53), channel_id=1, source_target_pairs={{0,2},{2,0},{16,18},{18,16},{1,3},{3,1},{17,19},{19,17},{4,6},{6,4... | collective-permute-start | bytes 589832 | tf_op jit(solution)/shard_map/ppermute | solution.py:433
  61.1 23.7 %collective-permute-start.11 = (bf16[2,2,64,384]{3,2,1,0:T(8,128)(2,1)}, bf16[2,2,64,384]{3,2,1,0:T(8,128)(2,1)S(1)}, u32[]{:S(2)}, u32[]{:S(2)}) collective-permute-start(bf16[2,2,64,384]{3,2,1,0:T(8,128)(2,1)} %get-tuple-element.54), channel_id=1, source_target_pairs={{0,16},{2,18},{16,0},{18,2},{1,17},{3,19},{17,1},{19,3},{4,20},{6,... | collective-permute-start | bytes 589832 | tf_op jit(solution)/shard_map/ppermute | solution.py:433
  62.5 27.0 %collective-permute-start.12 = (bf16[2,2,64,384]{3,2,1,0:T(8,128)(2,1)}, bf16[2,2,64,384]{3,2,1,0:T(8,128)(2,1)S(1)}, u32[]{:S(2)}, u32[]{:S(2)}) collective-permute-start(bf16[2,2,64,384]{3,2,1,0:T(8,128)(2,1)} %get-tuple-element.55), channel_id=1, source_target_pairs={{0,18},{2,16},{16,2},{18,0},{1,19},{3,17},{17,3},{19,1},{4,22},{6,... | collective-permute-start | bytes 589832 | tf_op jit(solution)/shard_map/ppermute | solution.py:433
  71.6 2.1 %copy-start.11 = (bf16[2,2,64,384]{3,2,1,0:T(8,128)(2,1)S(1)}, bf16[2,2,64,384]{3,2,1,0:T(8,128)(2,1)}, u32[]{:S(2)}) copy-start(bf16[2,2,64,384]{3,2,1,0:T(8,128)(2,1)} %get-tuple-element.52) | copy-start | bytes 589828
  71.6 18.0 %collective-permute-start.15 = (bf16[2,2,64,384]{3,2,1,0:T(8,128)(2,1)S(1)}, bf16[2,2,64,384]{3,2,1,0:T(8,128)(2,1)S(1)}, u32[]{:S(2)}, u32[]{:S(2)}) collective-permute-start(bf16[2,2,64,384]{3,2,1,0:T(8,128)(2,1)S(1)} %get-tuple-element.60), channel_id=1, source_target_pairs={{0,2},{2,0},{16,18},{18,16},{1,3},{3,1},{17,19},{19,17},{4,6},{6,4... | collective-permute-start | bytes 589832 | tf_op jit(solution)/shard_map/ppermute | solution.py:433
  72.1 21.1 %collective-permute-start.16 = (bf16[2,2,64,384]{3,2,1,0:T(8,128)(2,1)S(1)}, bf16[2,2,64,384]{3,2,1,0:T(8,128)(2,1)S(1)}, u32[]{:S(2)}, u32[]{:S(2)}) collective-permute-start(bf16[2,2,64,384]{3,2,1,0:T(8,128)(2,1)S(1)} %get-tuple-element.61), channel_id=1, source_target_pairs={{0,16},{2,18},{16,0},{18,2},{1,17},{3,19},{17,1},{19,3},{4,20},{6,... | collective-permute-start | bytes 589832 | tf_op jit(solution)/shard_map/ppermute | solution.py:433
  73.8 24.0 %collective-permute-start.17 = (bf16[2,2,64,384]{3,2,1,0:T(8,128)(2,1)S(1)}, bf16[2,2,64,384]{3,2,1,0:T(8,128)(2,1)S(1)}, u32[]{:S(2)}, u32[]{:S(2)}) collective-permute-start(bf16[2,2,64,384]{3,2,1,0:T(8,128)(2,1)S(1)} %get-tuple-element.62), channel_id=1, source_target_pairs={{0,18},{2,16},{16,2},{18,0},{1,19},{3,17},{17,3},{19,1},{4,22},{6,... | collective-permute-start | bytes 589832 | tf_op jit(solution)/shard_map/ppermute | solution.py:433
  97.9 1.1 %copy-start.10 = (bf16[2,16,64,384]{3,2,1,0:T(8,128)(2,1)}, bf16[2,16,64,384]{3,2,1,0:T(8,128)(2,1)S(1)}, u32[]{:S(2)}) copy-start(bf16[2,16,64,384]{3,2,1,0:T(8,128)(2,1)S(1)} %constant_dynamic-update-slice_fusion) | copy-start | bytes 4718596

commit v13 on v11

--- a/solution.py
+++ b/solution.py
@@ -303,12 +303,11 @@
     return center + jnp.tanh(preact[:, :features]) * opened
 
 
-def temporal_kernel(chunk, place, before, *refs):
-    *fields, w_first, w_second, out0, out1, out2, out3, token = refs
-    token[...] = jnp.zeros_like(token)
+def temporal_unit(place, fields, w_first, w_second, outs, own_unit, far_unit):
     near, is_first, is_last = place[1], place[2], place[3]
-    units, cells, features = fields[4].shape
-    spans = [slice(chunk * units, (chunk + 1) * units)] * 4 + [slice(0, units)] * 4
+    cells, features = fields[0].shape[1:]
+    spans = [slice(own_unit, own_unit + 1)] * 4 + [slice(far_unit, far_unit + 1)] * 4
+    units = 1
     flat = [field[at].reshape(units * cells, features) for field, at in zip(fields, spans)]
     zero = jnp.zeros_like(flat[0])
     pairs = [(flat[i], flat[i + 4]) for i in range(4)]
@@ -341,12 +340,19 @@
     other = jnp.where(near == 0, result_f, result_n)
     half = cells // 2
     for slot in range(2):
-        for unit in range(units):
-            at = (slot * units + unit) * cells
-            out0[slot, unit] = same[at : at + half]
-            out1[slot, unit] = same[at + half : at + cells]
-            out2[slot, unit] = other[at : at + half]
-            out3[slot, unit] = other[at + half : at + cells]
+        at = slot * cells
+        outs[0][slot, far_unit] = same[at : at + half]
+        outs[1][slot, far_unit] = same[at + half : at + cells]
+        outs[2][slot, far_unit] = other[at : at + half]
+        outs[3][slot, far_unit] = other[at + half : at + cells]
+
+
+def temporal_kernel(chunk, place, before, *refs):
+    fields, (w_first, w_second, *outs, token) = refs[:8], refs[8:]
+    token[...] = jnp.zeros_like(token)
+    count = fields[4].shape[0]
+    for unit in range(count):
+        temporal_unit(place, fields, w_first, w_second, outs, chunk * count + unit, unit)
 
 
 def run_section(place, before, mine, other, weights, units, chunks, from_frames):

time: 97.2 us -> 96.3 us (level)
  Pallas kernels: 36.4 us -> 34.6 us
    pallas_call x2, Pallas kernels: 13.9 us -> 12.1 us  [run_temporal(): pl.pallas_call(functools.partial(temporal_kernel, 0 if last else chunk),...]
  transfers between devices with their start and end apart: 18 -> 18, of which waited for: 5 -> 5; matrix products, arithmetic and copies ran while one was open for 1% -> 1% of each run, Pallas kernels for 35% -> 33%
where the time goes in v13:
time: 96.3 us; the launch traced here: 96.1 us
  Pallas kernels  34.6 us (36%)
  starting transfers between devices  33.4 us (35%)
  waiting for transfers between devices  25.1 us (26%)
  local copies, waits for them, and re-layouts  2.72 us (3%)
    ppermute x11, waiting for transfers between devices, exchange(): return lax.ppermute(piece, GROUP, [(i, i ^ delta) for i in range(4)])  25 us
    ppermute x11, starting transfers between devices, exchange(): return lax.ppermute(piece, GROUP, [(i, i ^ delta) for i in range(4)])  21.2 us
    pallas_call x3, Pallas kernels, run_section(): pl.pallas_call(section_kernel, grid_spec=pltpu.PrefetchScalarGridSpec(num...  18.8 us
    pallas_call x2, Pallas kernels, run_temporal(): pl.pallas_call(functools.partial(temporal_kernel, 0 if last else chunk),...  12.1 us
    ppermute x3, starting transfers between devices, halo(): lax.ppermute(even, RING, leftward)  11.6 us
    pallas_call x1, Pallas kernels, run_pack(): pl.pallas_call(functools.partial(pack_kernel, chunks), grid_spec=pltpu.Pr...  2.27 us
  transfers between devices with their start and end apart: 18, of which 5 were waited for; matrix products, arithmetic and copies ran while one was open for 1% of the time, Pallas kernels for 33%

profile of v13, /device:TPU:0, one launch (start us, length us, event | category | flops | bytes accessed | tf_op | source)
XLA Modules:
  0.0 96.1 jit_solution(9138987214492362507)
XLA Ops:
  0.0 0.1 stack.31.place.before
  0.1 2.3 %pack.1 = (bf16[2,4,64,384]{3,2,1,0:T(8,128)(2,1)S(1)}, bf16[2,2,64,384]{3,2,1,0:T(8,128)(2,1)S(1)}, bf16[2,2,64,384]{3,2,1,0:T(8,128)(2,1)S(1)}, bf16[2,2,64,38...) custom-call(s32[5]{0:T(128)S(1)} %stack.31.place.before, bf16[2,16,64,384]{3,2,1,0:T(8,128)(2,1)} %bitcast.7, ...), custom_call_target="tpu_custom_call" | custom-call | bytes 786432 | tf_op jit(solution)/shard_map/pack/pallas_call | solution.py:198
  2.5 0.3 pack_weights.1.before.mine
  2.8 0.5 collective-permute-start.1
  3.3 2.6 %collective-permute-start = (bf16[2,4,64,384]{3,2,1,0:T(8,128)(2,1)S(1)}, bf16[2,4,64,384]{3,2,1,0:T(8,128)(2,1)S(1)}, u32[]{:S(2)}, u32[]{:S(2)}) collective-permute-start(bf16[2,4,64,384]{3,2,1,0:T(8,128)(2,1)S(1)} %get-tuple-element.34), channel_id=1, source_target_pairs={{0,2},{2,0},{16,18},{18,16},{1,3},{3,1},{17,19},{19,17},{4,6},{6,4... | collective-permute-start | bytes 1179656 | tf_op jit(solution)/shard_map/ppermute | solution.py:423
  5.9 2.6 %collective-permute-start.2 = (bf16[2,2,64,384]{3,2,1,0:T(8,128)(2,1)S(1)}, bf16[2,2,64,384]{3,2,1,0:T(8,128)(2,1)S(1)}, u32[]{:S(2)}, u32[]{:S(2)}) collective-permute-start(bf16[2,2,64,384]{3,2,1,0:T(8,128)(2,1)S(1)} %get-tuple-element.35.before), channel_id=1, source_target_pairs={{0,16},{2,18},{16,0},{18,2},{1,17},{3,19},{17,1},{19,3},{4,20},{6,... | collective-permute-start | bytes 589832 | tf_op jit(solution)/shard_map/ppermute | solution.py:423
  8.5 2.9 %collective-permute-start.4 = (bf16[2,2,64,384]{3,2,1,0:T(8,128)(2,1)S(1)}, bf16[2,2,64,384]{3,2,1,0:T(8,128)(2,1)S(1)}, u32[]{:S(2)}, u32[]{:S(2)}) collective-permute-start(bf16[2,2,64,384]{3,2,1,0:T(8,128)(2,1)S(1)} %get-tuple-element.43), channel_id=1, source_target_pairs={{0,16},{2,18},{16,0},{18,2},{1,17},{3,19},{17,1},{19,3},{4,20},{6,... | collective-permute-start | bytes 589832 | tf_op jit(solution)/shard_map/ppermute | solution.py:423
  11.4 1.2 %join_weights.1 = (bf16[384,1152]{1,0:T(8,128)(2,1)S(1)}, bf16[384,384]{1,0:T(8,128)(2,1)S(1)}, bf16[384,1536]{1,0:T(8,128)(2,1)S(1)}, bf16[1536,384]{1,0:T(8,12...) custom-call(s32[5]{0:T(128)S(1)} %stack.31.place.before, ...), custom_call_target="tpu_custom_call" | custom-call | bytes 1769472 | tf_op jit(solution)/shard_map/join_weights/pallas_call | solution.py:168
  12.5 3.1 %collective-permute-done.other = bf16[2,4,64,384]{3,2,1,0:T(8,128)(2,1)S(1)} collective-permute-done((bf16[2,4,64,384]{3,2,1,0:T(8,128)(2,1)S(1)}, bf16[2,4,64,384]{3,2,1,0:T(8,128)(2,1)S(1)}, u32[]{:S(2)}, u32[]{:S(2)}) %collective-permute-start) | collective-permute-done | bytes 393248 | tf_op jit(solution)/shard_map/ppermute | solution.py:423
  15.6 9.3 %section.3 = (bf16[4,128,384]{2,1,0:T(8,128)(2,1)S(1)}, bf16[4,128,384]{2,1,0:T(8,128)(2,1)S(1)}, f32[8,128]{1,0:T(8,128)S(1)}) custom-call(s32[5]{0:T(128)S(1)} %stack.31.place.before, s32[5]{0:T(128)S(1)} %stack.31.place.before, bf16[2,16,64,384]{3,2,1,0:T(8,128)(2,1)} %bitcast.13, bf16[2,4,64,384]{3,2,1,0:T(8,128)(2,1)S(1)} %collective-permute-done.other, ...), custom_call_target="tpu_custom_call" | custom-call | bytes 98304 | tf_op jit(solution)/shard_map/section/pallas_call | solution.py:366
  24.9 0.1 collective-permute-start.6
  25.0 6.3 %collective-permute-start.7 = (bf16[4,128,384]{2,1,0:T(8,128)(2,1)S(1)}, bf16[4,128,384]{2,1,0:T(8,128)(2,1)S(1)}, u32[]{:S(2)}, u32[]{:S(2)}) collective-permute-start(bf16[4,128,384]{2,1,0:T(8,128)(2,1)S(1)} %get-tuple-element.46.refs_0_), channel_id=1, source_target_pairs={{1,0},{4,1},{5,4},{8,5},{9,8},{12,9},{13,12},{0,13},{3,2},{6,3},{7... | collective-permute-start | bytes 1179656 | tf_op jit(solution)/shard_map/ppermute | solution.py:426
  31.3 4.3 %collective-permute-start.5 = (bf16[2,2,64,384]{3,2,1,0:T(8,128)(2,1)S(1)}, bf16[2,2,64,384]{3,2,1,0:T(8,128)(2,1)S(1)}, u32[]{:S(2)}, u32[]{:S(2)}) collective-permute-start(bf16[2,2,64,384]{3,2,1,0:T(8,128)(2,1)S(1)} %get-tuple-element.44), channel_id=1, source_target_pairs={{0,18},{2,16},{16,2},{18,0},{1,19},{3,17},{17,3},{19,1},{4,22},{6,... | collective-permute-start | bytes 589832 | tf_op jit(solution)/shard_map/ppermute | solution.py:423
  35.6 4.4 %section.4 = (bf16[2,128,384]{2,1,0:T(8,128)(2,1)S(1)}, bf16[2,128,384]{2,1,0:T(8,128)(2,1)S(1)}, f32[8,128]{1,0:T(8,128)S(1)}) custom-call(s32[5]{0:T(128)S(1)} %stack.31.place.before, f32[8,128]{1,0:T(8,128)S(1)} %get-tuple-element.40.before, bf16[2,2,64,384]{3,2,1,0:T(8,128)(2,1)S(1)} %collective-permute-done.2.mine, ...), custom_call_target="tpu_custom_call" | custom-call | bytes 49152 | tf_op jit(solution)/shard_map/section/pallas_call | solution.py:366
  40.1 2.6 %collective-permute-start.9 = (bf16[2,128,384]{2,1,0:T(8,128)(2,1)S(1)}, bf16[2,128,384]{2,1,0:T(8,128)(2,1)S(1)}, u32[]{:S(2)}, u32[]{:S(2)}) collective-permute-start(bf16[2,128,384]{2,1,0:T(8,128)(2,1)S(1)} %get-tuple-element.48.refs_4_), channel_id=1, source_target_pairs={{1,0},{4,1},{5,4},{8,5},{9,8},{12,9},{13,12},{0,13},{3,2},{6,3},{7... | collective-permute-start | bytes 589832 | tf_op jit(solution)/shard_map/ppermute | solution.py:426
  42.7 5.1 %section.5 = (bf16[2,128,384]{2,1,0:T(8,128)(2,1)}, bf16[2,128,384]{2,1,0:T(8,128)(2,1)}, f32[8,128]{1,0:T(8,128)S(1)}) custom-call(s32[5]{0:T(128)S(1)} %stack.31.place.before, f32[8,128]{1,0:T(8,128)S(1)} %get-tuple-element.42.before, bf16[2,2,64,384]{3,2,1,0:T(8,128)(2,1)S(1)} %collective-permute-done.4.mine, ...), custom_call_target="tpu_custom_call" | custom-call | bytes 49152 | tf_op jit(solution)/shard_map/section/pallas_call | solution.py:366
  47.8 2.6 %collective-permute-start.14 = (bf16[2,128,384]{2,1,0:T(8,128)(2,1)}, bf16[2,128,384]{2,1,0:T(8,128)(2,1)}, u32[]{:S(2)}, u32[]{:S(2)}) collective-permute-start(bf16[2,128,384]{2,1,0:T(8,128)(2,1)} %get-tuple-element.57.refs_4_), channel_id=1, source_target_pairs={{1,0},{4,1},{5,4},{8,5},{9,8},{12,9},{13,12},{0,13},{3,2},{6,3},{7... | collective-permute-start | bytes 589832 | tf_op jit(solution)/shard_map/ppermute | solution.py:426
  50.5 5.5 %temporal.2 = (bf16[2,2,64,384]{3,2,1,0:T(8,128)(2,1)}, bf16[2,2,64,384]{3,2,1,0:T(8,128)(2,1)}, bf16[2,2,64,384]{3,2,1,0:T(8,128)(2,1)}, bf16[2,2,64,384]{3,2,1,0:T(8,128)(2,1)}, f32[8,128]{1,0:T(8,128)S(1)}) custom-call(s32[5]{0:T(128)S(1)} %stack.31.place.before, f32[8,128]{1,0:T(8,128)S(1)} %get-tuple-element.45.before, ...), custom_call_target="tpu_custom_call" | custom-call | bytes 98304 | tf_op jit(solution)/shard_map/temporal/pallas_call | solution.py:388
  56.0 0.5 collective-permute-start.10
  56.6 3.7 %collective-permute-start.11 = (bf16[2,2,64,384]{3,2,1,0:T(8,128)(2,1)}, bf16[2,2,64,384]{3,2,1,0:T(8,128)(2,1)S(1)}, u32[]{:S(2)}, u32[]{:S(2)}) collective-permute-start(bf16[2,2,64,384]{3,2,1,0:T(8,128)(2,1)} %get-tuple-element.54), channel_id=1, source_target_pairs={{0,16},{2,18},{16,0},{18,2},{1,17},{3,19},{17,1},{19,3},{4,20},{6,... | collective-permute-start | bytes 589832 | tf_op jit(solution)/shard_map/ppermute | solution.py:423
  60.3 0.1 collective-permute-start.12
  60.4 6.6 %temporal.3 = (bf16[2,2,64,384]{3,2,1,0:T(8,128)(2,1)S(1)}, bf16[2,2,64,384]{3,2,1,0:T(8,128)(2,1)S(1)}, bf16[2,2,64,384]{3,2,1,0:T(8,128)(2,1)S(1)}, bf16[2,2,64,384]{3,2,1,0:T(8,128)(2,1)S(1)}, f32[8,128]{1,0:T(8,128)}) custom-call(s32[5]{0:T(128)S(1)} %stack.31.place.before, f32[8,128]{1,0:T(8,128)S(1)} %get-tuple-element.56.before, ...), custom_call_target="tpu_custom_call" | custom-call | bytes 98304 | tf_op jit(solution)/shard_map/temporal/pallas_call | solution.py:388
  67.0 1.3 %collective-permute-start.15 = (bf16[2,2,64,384]{3,2,1,0:T(8,128)(2,1)S(1)}, bf16[2,2,64,384]{3,2,1,0:T(8,128)(2,1)S(1)}, u32[]{:S(2)}, u32[]{:S(2)}) collective-permute-start(bf16[2,2,64,384]{3,2,1,0:T(8,128)(2,1)S(1)} %get-tuple-element.60), channel_id=1, source_target_pairs={{0,2},{2,0},{16,18},{18,16},{1,3},{3,1},{17,19},{19,17},{4,6},{6,4... | collective-permute-start | bytes 589832 | tf_op jit(solution)/shard_map/ppermute | solution.py:423
  68.3 2.9 %collective-permute-start.16 = (bf16[2,2,64,384]{3,2,1,0:T(8,128)(2,1)S(1)}, bf16[2,2,64,384]{3,2,1,0:T(8,128)(2,1)S(1)}, u32[]{:S(2)}, u32[]{:S(2)}) collective-permute-start(bf16[2,2,64,384]{3,2,1,0:T(8,128)(2,1)S(1)} %get-tuple-element.61), channel_id=1, source_target_pairs={{0,16},{2,18},{16,0},{18,2},{1,17},{3,19},{17,1},{19,3},{4,20},{6,... | collective-permute-start | bytes 589832 | tf_op jit(solution)/shard_map/ppermute | solution.py:423
  71.3 0.2 broadcast_in_dim.3
  71.6 0.2 collective-permute-start.17
  71.8 1.0 constant_dynamic-update-slice_fusion.6
  72.7 9.9 %collective-permute-done.11 = bf16[2,2,64,384]{3,2,1,0:T(8,128)(2,1)S(1)} collective-permute-done((bf16[2,2,64,384]{3,2,1,0:T(8,128)(2,1)}, bf16[2,2,64,384]{3,2,1,0:T(8,128)(2,1)S(1)}, u32[]{:S(2)}, u32[]{:S(2)}) %collective-permute-start.11) | collective-permute-done | bytes 196640 | tf_op jit(solution)/shard_map/ppermute | solution.py:423
  82.6 4.1 %collective-permute-done.12 = bf16[2,2,64,384]{3,2,1,0:T(8,128)(2,1)S(1)} collective-permute-done((bf16[2,2,64,384]{3,2,1,0:T(8,128)(2,1)}, bf16[2,2,64,384]{3,2,1,0:T(8,128)(2,1)S(1)}, u32[]{:S(2)}, u32[]{:S(2)}) %collective-permute-start.12) | collective-permute-done | bytes 196640 | tf_op jit(solution)/shard_map/ppermute | solution.py:423
  86.9 4.1 %collective-permute-done.16 = bf16[2,2,64,384]{3,2,1,0:T(8,128)(2,1)S(1)} collective-permute-done((bf16[2,2,64,384]{3,2,1,0:T(8,128)(2,1)S(1)}, bf16[2,2,64,384]{3,2,1,0:T(8,128)(2,1)S(1)}, u32[]{:S(2)}, u32[]{:S(2)}) %collective-permute-start.16) | collective-permute-done | bytes 196640 | tf_op jit(solution)/shard_map/ppermute | solution.py:423
  91.1 3.9 %collective-permute-done.17 = bf16[2,2,64,384]{3,2,1,0:T(8,128)(2,1)S(1)} collective-permute-done((bf16[2,2,64,384]{3,2,1,0:T(8,128)(2,1)S(1)}, bf16[2,2,64,384]{3,2,1,0:T(8,128)(2,1)S(1)}, u32[]{:S(2)}, u32[]{:S(2)}) %collective-permute-start.17) | collective-permute-done | bytes 196640 | tf_op jit(solution)/shard_map/ppermute | solution.py:423
  95.0 1.1 %copy-done.10 = bf16[2,16,64,384]{3,2,1,0:T(8,128)(2,1)} copy-done((bf16[2,16,64,384]{3,2,1,0:T(8,128)(2,1)}, bf16[2,16,64,384]{3,2,1,0:T(8,128)(2,1)S(1)}, u32[]{:S(2)}) %copy-start.10) | copy-done | bytes 1572888
  (46 shorter events, 0.4 us)
Async XLA Ops:
  0.1 2.3 %copy-start.4 = (bf16[576,768]{1,0:T(8,128)(2,1)S(1)}, bf16[576,768]{1,0:T(8,128)(2,1)}, u32[]{:S(2)}) copy-start(bf16[576,768]{1,0:T(8,128)(2,1)} %refs_4_.1) | copy-start | bytes 2654212
  0.1 2.3 %copy-start.5 = (bf16[576,768]{1,0:T(8,128)(2,1)S(1)}, bf16[576,768]{1,0:T(8,128)(2,1)}, u32[]{:S(2)}) copy-start(bf16[576,768]{1,0:T(8,128)(2,1)} %refs_5_.1) | copy-start | bytes 2654212
  0.1 2.3 %copy-start.6 = (bf16[192,1536]{1,0:T(8,128)(2,1)S(1)}, bf16[192,1536]{1,0:T(8,128)(2,1)}, u32[]{:S(2)}) copy-start(bf16[192,1536]{1,0:T(8,128)(2,1)} %refs_2_.1) | copy-start | bytes 1769476
  0.1 2.3 %copy-start.7 = (bf16[768,384]{1,0:T(8,128)(2,1)S(1)}, bf16[768,384]{1,0:T(8,128)(2,1)}, u32[]{:S(2)}) copy-start(bf16[768,384]{1,0:T(8,128)(2,1)} %refs_3_.1) | copy-start | bytes 1769476
  0.1 2.3 %copy-start.8 = (bf16[192,1152]{1,0:T(8,128)(2,1)S(1)}, bf16[192,1152]{1,0:T(8,128)(2,1)}, u32[]{:S(2)}) copy-start(bf16[192,1152]{1,0:T(8,128)(2,1)} %refs_0_.1) | copy-start | bytes 1327108
  0.1 2.4 %copy-start.9 = (bf16[192,384]{1,0:T(8,128)(2,1)S(1)}, bf16[192,384]{1,0:T(8,128)(2,1)}, u32[]{:S(2)}) copy-start(bf16[192,384]{1,0:T(8,128)(2,1)} %refs_1_.1) | copy-start | bytes 442372
  2.8 8.6 %collective-permute-start.1 = (bf16[4608,384]{1,0:T(8,128)(2,1)S(1)}, bf16[4608,384]{1,0:T(8,128)(2,1)S(1)}, u32[]{:S(2)}, u32[]{:S(2)}) collective-permute-start(bf16[4608,384]{1,0:T(8,128)(2,1)S(1)} %pack_weights.1.before.mine), channel_id=1, source_target_pairs={{0,1},{1,0},{2,3},{3,2},{4,5},{5,4},{6,7},{7,6},{8,9},{9,8},{10,11... | collective-permute-start | bytes 10616840 | tf_op jit(solution)/shard_map/ppermute | solution.py:433
  3.3 12.3 %collective-permute-start = (bf16[2,4,64,384]{3,2,1,0:T(8,128)(2,1)S(1)}, bf16[2,4,64,384]{3,2,1,0:T(8,128)(2,1)S(1)}, u32[]{:S(2)}, u32[]{:S(2)}) collective-permute-start(bf16[2,4,64,384]{3,2,1,0:T(8,128)(2,1)S(1)} %get-tuple-element.34), channel_id=1, source_target_pairs={{0,2},{2,0},{16,18},{18,16},{1,3},{3,1},{17,19},{19,17},{4,6},{6,4... | collective-permute-start | bytes 1179656 | tf_op jit(solution)/shard_map/ppermute | solution.py:423
  5.9 25.4 %collective-permute-start.2 = (bf16[2,2,64,384]{3,2,1,0:T(8,128)(2,1)S(1)}, bf16[2,2,64,384]{3,2,1,0:T(8,128)(2,1)S(1)}, u32[]{:S(2)}, u32[]{:S(2)}) collective-permute-start(bf16[2,2,64,384]{3,2,1,0:T(8,128)(2,1)S(1)} %get-tuple-element.35.before), channel_id=1, source_target_pairs={{0,16},{2,18},{16,0},{18,2},{1,17},{3,19},{17,1},{19,3},{4,20},{6,... | collective-permute-start | bytes 589832 | tf_op jit(solution)/shard_map/ppermute | solution.py:423
  8.5 27.2 %collective-permute-start.3 = (bf16[2,2,64,384]{3,2,1,0:T(8,128)(2,1)S(1)}, bf16[2,2,64,384]{3,2,1,0:T(8,128)(2,1)S(1)}, u32[]{:S(2)}, u32[]{:S(2)}) collective-permute-start(bf16[2,2,64,384]{3,2,1,0:T(8,128)(2,1)S(1)} %get-tuple-element.41), channel_id=1, source_target_pairs={{0,18},{2,16},{16,2},{18,0},{1,19},{3,17},{17,3},{19,1},{4,22},{6,... | collective-permute-start | bytes 589832 | tf_op jit(solution)/shard_map/ppermute | solution.py:423
  8.5 31.6 %collective-permute-start.4 = (bf16[2,2,64,384]{3,2,1,0:T(8,128)(2,1)S(1)}, bf16[2,2,64,384]{3,2,1,0:T(8,128)(2,1)S(1)}, u32[]{:S(2)}, u32[]{:S(2)}) collective-permute-start(bf16[2,2,64,384]{3,2,1,0:T(8,128)(2,1)S(1)} %get-tuple-element.43), channel_id=1, source_target_pairs={{0,16},{2,18},{16,0},{18,2},{1,17},{3,19},{17,1},{19,3},{4,20},{6,... | collective-permute-start | bytes 589832 | tf_op jit(solution)/shard_map/ppermute | solution.py:423
  24.9 25.6 %copy-start = (bf16[4,128,384]{2,1,0:T(8,128)(2,1)}, bf16[4,128,384]{2,1,0:T(8,128)(2,1)S(1)}, u32[]{:S(2)}) copy-start(bf16[4,128,384]{2,1,0:T(8,128)(2,1)S(1)} %get-tuple-element.46.refs_0_) | copy-start | bytes 1179652
  24.9 25.6 %copy-start.1 = (bf16[4,128,384]{2,1,0:T(8,128)(2,1)}, bf16[4,128,384]{2,1,0:T(8,128)(2,1)S(1)}, u32[]{:S(2)}) copy-start(bf16[4,128,384]{2,1,0:T(8,128)(2,1)S(1)} %get-tuple-element.47.refs_1_) | copy-start | bytes 1179652
  24.9 25.6 %collective-permute-start.6 = (bf16[4,128,384]{2,1,0:T(8,128)(2,1)S(1)}, bf16[4,128,384]{2,1,0:T(8,128)(2,1)S(1)}, u32[]{:S(2)}, u32[]{:S(2)}) collective-permute-start(bf16[4,128,384]{2,1,0:T(8,128)(2,1)S(1)} %get-tuple-element.47.refs_1_), channel_id=1, source_target_pairs={{0,1},{1,4},{4,5},{5,8},{8,9},{9,12},{12,13},{13,0},{2,3},{3,6},{6... | collective-permute-start | bytes 1179656 | tf_op jit(solution)/shard_map/ppermute | solution.py:426
  25.0 25.5 %collective-permute-start.7 = (bf16[4,128,384]{2,1,0:T(8,128)(2,1)S(1)}, bf16[4,128,384]{2,1,0:T(8,128)(2,1)S(1)}, u32[]{:S(2)}, u32[]{:S(2)}) collective-permute-start(bf16[4,128,384]{2,1,0:T(8,128)(2,1)S(1)} %get-tuple-element.46.refs_0_), channel_id=1, source_target_pairs={{1,0},{4,1},{5,4},{8,5},{9,8},{12,9},{13,12},{0,13},{3,2},{6,3},{7... | collective-permute-start | bytes 1179656 | tf_op jit(solution)/shard_map/ppermute | solution.py:426
  31.3 11.5 %collective-permute-start.5 = (bf16[2,2,64,384]{3,2,1,0:T(8,128)(2,1)S(1)}, bf16[2,2,64,384]{3,2,1,0:T(8,128)(2,1)S(1)}, u32[]{:S(2)}, u32[]{:S(2)}) collective-permute-start(bf16[2,2,64,384]{3,2,1,0:T(8,128)(2,1)S(1)} %get-tuple-element.44), channel_id=1, source_target_pairs={{0,18},{2,16},{16,2},{18,0},{1,19},{3,17},{17,3},{19,1},{4,22},{6,... | collective-permute-start | bytes 589832 | tf_op jit(solution)/shard_map/ppermute | solution.py:423
  40.0 7.8 %collective-permute-start.8 = (bf16[2,128,384]{2,1,0:T(8,128)(2,1)S(1)}, bf16[2,128,384]{2,1,0:T(8,128)(2,1)S(1)}, u32[]{:S(2)}, u32[]{:S(2)}) collective-permute-start(bf16[2,128,384]{2,1,0:T(8,128)(2,1)S(1)} %get-tuple-element.49.refs_5_), channel_id=1, source_target_pairs={{0,1},{1,4},{4,5},{5,8},{8,9},{9,12},{12,13},{13,0},{2,3},{3,6},{6... | collective-permute-start | bytes 589832 | tf_op jit(solution)/shard_map/ppermute | solution.py:426
  40.1 10.4 %collective-permute-start.9 = (bf16[2,128,384]{2,1,0:T(8,128)(2,1)S(1)}, bf16[2,128,384]{2,1,0:T(8,128)(2,1)S(1)}, u32[]{:S(2)}, u32[]{:S(2)}) collective-permute-start(bf16[2,128,384]{2,1,0:T(8,128)(2,1)S(1)} %get-tuple-element.48.refs_4_), channel_id=1, source_target_pairs={{1,0},{4,1},{5,4},{8,5},{9,8},{12,9},{13,12},{0,13},{3,2},{6,3},{7... | collective-permute-start | bytes 589832 | tf_op jit(solution)/shard_map/ppermute | solution.py:426
  47.8 12.6 %collective-permute-start.13 = (bf16[2,128,384]{2,1,0:T(8,128)(2,1)}, bf16[2,128,384]{2,1,0:T(8,128)(2,1)}, u32[]{:S(2)}, u32[]{:S(2)}) collective-permute-start(bf16[2,128,384]{2,1,0:T(8,128)(2,1)} %get-tuple-element.58.refs_5_), channel_id=1, source_target_pairs={{0,1},{1,4},{4,5},{5,8},{8,9},{9,12},{12,13},{13,0},{2,3},{3,6},{6... | collective-permute-start | bytes 589832 | tf_op jit(solution)/shard_map/ppermute | solution.py:426
  47.8 12.6 %collective-permute-start.14 = (bf16[2,128,384]{2,1,0:T(8,128)(2,1)}, bf16[2,128,384]{2,1,0:T(8,128)(2,1)}, u32[]{:S(2)}, u32[]{:S(2)}) collective-permute-start(bf16[2,128,384]{2,1,0:T(8,128)(2,1)} %get-tuple-element.57.refs_4_), channel_id=1, source_target_pairs={{1,0},{4,1},{5,4},{8,5},{9,8},{12,9},{13,12},{0,13},{3,2},{6,3},{7... | collective-permute-start | bytes 589832 | tf_op jit(solution)/shard_map/ppermute | solution.py:426
  50.5 5.5 %copy-start.2 = (bf16[4,128,384]{2,1,0:T(8,128)(2,1)}, bf16[4,128,384]{2,1,0:T(8,128)(2,1)S(1)}, u32[]{:S(2)}) copy-start(bf16[4,128,384]{2,1,0:T(8,128)(2,1)S(1)} %collective-permute-done.6.refs_2_) | copy-start | bytes 1179652
  50.5 5.5 %copy-start.3 = (bf16[4,128,384]{2,1,0:T(8,128)(2,1)}, bf16[4,128,384]{2,1,0:T(8,128)(2,1)S(1)}, u32[]{:S(2)}) copy-start(bf16[4,128,384]{2,1,0:T(8,128)(2,1)S(1)} %collective-permute-done.7.refs_3_) | copy-start | bytes 1179652
  56.0 15.5 %collective-permute-start.10 = (bf16[2,2,64,384]{3,2,1,0:T(8,128)(2,1)}, bf16[2,2,64,384]{3,2,1,0:T(8,128)(2,1)}, u32[]{:S(2)}, u32[]{:S(2)}) collective-permute-start(bf16[2,2,64,384]{3,2,1,0:T(8,128)(2,1)} %get-tuple-element.53), channel_id=1, source_target_pairs={{0,2},{2,0},{16,18},{18,16},{1,3},{3,1},{17,19},{19,17},{4,6},{6,4... | collective-permute-start | bytes 589832 | tf_op jit(solution)/shard_map/ppermute | solution.py:423
  56.6 26.0 %collective-permute-start.11 = (bf16[2,2,64,384]{3,2,1,0:T(8,128)(2,1)}, bf16[2,2,64,384]{3,2,1,0:T(8,128)(2,1)S(1)}, u32[]{:S(2)}, u32[]{:S(2)}) collective-permute-start(bf16[2,2,64,384]{3,2,1,0:T(8,128)(2,1)} %get-tuple-element.54), channel_id=1, source_target_pairs={{0,16},{2,18},{16,0},{18,2},{1,17},{3,19},{17,1},{19,3},{4,20},{6,... | collective-permute-start | bytes 589832 | tf_op jit(solution)/shard_map/ppermute | solution.py:423
  60.3 26.5 %collective-permute-start.12 = (bf16[2,2,64,384]{3,2,1,0:T(8,128)(2,1)}, bf16[2,2,64,384]{3,2,1,0:T(8,128)(2,1)S(1)}, u32[]{:S(2)}, u32[]{:S(2)}) collective-permute-start(bf16[2,2,64,384]{3,2,1,0:T(8,128)(2,1)} %get-tuple-element.55), channel_id=1, source_target_pairs={{0,18},{2,16},{16,2},{18,0},{1,19},{3,17},{17,3},{19,1},{4,22},{6,... | collective-permute-start | bytes 589832 | tf_op jit(solution)/shard_map/ppermute | solution.py:423
  67.0 4.5 %copy-start.11 = (bf16[2,2,64,384]{3,2,1,0:T(8,128)(2,1)S(1)}, bf16[2,2,64,384]{3,2,1,0:T(8,128)(2,1)}, u32[]{:S(2)}) copy-start(bf16[2,2,64,384]{3,2,1,0:T(8,128)(2,1)} %get-tuple-element.52) | copy-start | bytes 589828
  67.0 19.8 %collective-permute-start.15 = (bf16[2,2,64,384]{3,2,1,0:T(8,128)(2,1)S(1)}, bf16[2,2,64,384]{3,2,1,0:T(8,128)(2,1)S(1)}, u32[]{:S(2)}, u32[]{:S(2)}) collective-permute-start(bf16[2,2,64,384]{3,2,1,0:T(8,128)(2,1)S(1)} %get-tuple-element.60), channel_id=1, source_target_pairs={{0,2},{2,0},{16,18},{18,16},{1,3},{3,1},{17,19},{19,17},{4,6},{6,4... | collective-permute-start | bytes 589832 | tf_op jit(solution)/shard_map/ppermute | solution.py:423
  68.3 22.7 %collective-permute-start.16 = (bf16[2,2,64,384]{3,2,1,0:T(8,128)(2,1)S(1)}, bf16[2,2,64,384]{3,2,1,0:T(8,128)(2,1)S(1)}, u32[]{:S(2)}, u32[]{:S(2)}) collective-permute-start(bf16[2,2,64,384]{3,2,1,0:T(8,128)(2,1)S(1)} %get-tuple-element.61), channel_id=1, source_target_pairs={{0,16},{2,18},{16,0},{18,2},{1,17},{3,19},{17,1},{19,3},{4,20},{6,... | collective-permute-start | bytes 589832 | tf_op jit(solution)/shard_map/ppermute | solution.py:423
  71.6 23.4 %collective-permute-start.17 = (bf16[2,2,64,384]{3,2,1,0:T(8,128)(2,1)S(1)}, bf16[2,2,64,384]{3,2,1,0:T(8,128)(2,1)S(1)}, u32[]{:S(2)}, u32[]{:S(2)}) collective-permute-start(bf16[2,2,64,384]{3,2,1,0:T(8,128)(2,1)S(1)} %get-tuple-element.62), channel_id=1, source_target_pairs={{0,18},{2,16},{16,2},{18,0},{1,19},{3,17},{17,3},{19,1},{4,22},{6,... | collective-permute-start | bytes 589832 | tf_op jit(solution)/shard_map/ppermute | solution.py:423
  95.0 1.1 %copy-start.10 = (bf16[2,16,64,384]{3,2,1,0:T(8,128)(2,1)}, bf16[2,16,64,384]{3,2,1,0:T(8,128)(2,1)S(1)}, u32[]{:S(2)}) copy-start(bf16[2,16,64,384]{3,2,1,0:T(8,128)(2,1)S(1)} %constant_dynamic-update-slice_fusion) | copy-start | bytes 4718596

commit v14 on v13

--- a/solution.py
+++ b/solution.py
@@ -280,7 +280,7 @@
     mid_float = mid_state.astype(jnp.float32)
     normed_two = normalize(mid_float).astype(jnp.bfloat16)
     total = mid_float
-    width = math.gcd(w_up.shape[1], 512)
+    width = math.gcd(w_up.shape[1], 768)
     for at in range(0, w_up.shape[1], width):
         lifted = jnp.dot(normed_two, w_up[:, at : at + width], preferred_element_type=jnp.float32)
         lifted = lifted.astype(jnp.bfloat16)

time: 96.3 us -> 96.4 us (level)
  no operation moved by 1% of the time
where the time goes in v14:
time: 96.4 us; the launch traced here: 96.2 us
  Pallas kernels  34.7 us (36%)
  starting transfers between devices  33.4 us (35%)
  waiting for transfers between devices  25.1 us (26%)
  local copies, waits for them, and re-layouts  2.72 us (3%)
    ppermute x11, waiting for transfers between devices, exchange(): return lax.ppermute(piece, GROUP, [(i, i ^ delta) for i in range(4)])  25 us
    ppermute x11, starting transfers between devices, exchange(): return lax.ppermute(piece, GROUP, [(i, i ^ delta) for i in range(4)])  21.2 us
    pallas_call x3, Pallas kernels, run_section(): pl.pallas_call(section_kernel, grid_spec=pltpu.PrefetchScalarGridSpec(num...  18.9 us
    pallas_call x2, Pallas kernels, run_temporal(): pl.pallas_call(functools.partial(temporal_kernel, 0 if last else chunk),...  12.1 us
    ppermute x3, starting transfers between devices, halo(): lax.ppermute(even, RING, leftward)  11.6 us
    pallas_call x1, Pallas kernels, run_pack(): pl.pallas_call(functools.partial(pack_kernel, chunks), grid_spec=pltpu.Pr...  2.27 us
  transfers between devices with their start and end apart: 18, of which 5 were waited for; matrix products, arithmetic and copies ran while one was open for 1% of the time, Pallas kernels for 33%

profile of v14, /device:TPU:0, one launch (start us, length us, event | category | flops | bytes accessed | tf_op | source)
XLA Modules:
  0.0 96.2 jit_solution(12726400803096992724)
XLA Ops:
  0.0 0.1 stack.31.place.before
  0.1 2.3 %pack.1 = (bf16[2,4,64,384]{3,2,1,0:T(8,128)(2,1)S(1)}, bf16[2,2,64,384]{3,2,1,0:T(8,128)(2,1)S(1)}, bf16[2,2,64,384]{3,2,1,0:T(8,128)(2,1)S(1)}, bf16[2,2,64,38...) custom-call(s32[5]{0:T(128)S(1)} %stack.31.place.before, bf16[2,16,64,384]{3,2,1,0:T(8,128)(2,1)} %bitcast.7, ...), custom_call_target="tpu_custom_call" | custom-call | bytes 786432 | tf_op jit(solution)/shard_map/pack/pallas_call | solution.py:198
  2.5 0.3 pack_weights.1.before.mine
  2.8 0.5 collective-permute-start.1
  3.3 2.6 %collective-permute-start = (bf16[2,4,64,384]{3,2,1,0:T(8,128)(2,1)S(1)}, bf16[2,4,64,384]{3,2,1,0:T(8,128)(2,1)S(1)}, u32[]{:S(2)}, u32[]{:S(2)}) collective-permute-start(bf16[2,4,64,384]{3,2,1,0:T(8,128)(2,1)S(1)} %get-tuple-element.34), channel_id=1, source_target_pairs={{0,2},{2,0},{16,18},{18,16},{1,3},{3,1},{17,19},{19,17},{4,6},{6,4... | collective-permute-start | bytes 1179656 | tf_op jit(solution)/shard_map/ppermute | solution.py:423
  5.9 2.6 %collective-permute-start.2 = (bf16[2,2,64,384]{3,2,1,0:T(8,128)(2,1)S(1)}, bf16[2,2,64,384]{3,2,1,0:T(8,128)(2,1)S(1)}, u32[]{:S(2)}, u32[]{:S(2)}) collective-permute-start(bf16[2,2,64,384]{3,2,1,0:T(8,128)(2,1)S(1)} %get-tuple-element.35.before), channel_id=1, source_target_pairs={{0,16},{2,18},{16,0},{18,2},{1,17},{3,19},{17,1},{19,3},{4,20},{6,... | collective-permute-start | bytes 589832 | tf_op jit(solution)/shard_map/ppermute | solution.py:423
  8.5 2.9 %collective-permute-start.4 = (bf16[2,2,64,384]{3,2,1,0:T(8,128)(2,1)S(1)}, bf16[2,2,64,384]{3,2,1,0:T(8,128)(2,1)S(1)}, u32[]{:S(2)}, u32[]{:S(2)}) collective-permute-start(bf16[2,2,64,384]{3,2,1,0:T(8,128)(2,1)S(1)} %get-tuple-element.43), channel_id=1, source_target_pairs={{0,16},{2,18},{16,0},{18,2},{1,17},{3,19},{17,1},{19,3},{4,20},{6,... | collective-permute-start | bytes 589832 | tf_op jit(solution)/shard_map/ppermute | solution.py:423
  11.4 1.2 %join_weights.1 = (bf16[384,1152]{1,0:T(8,128)(2,1)S(1)}, bf16[384,384]{1,0:T(8,128)(2,1)S(1)}, bf16[384,1536]{1,0:T(8,128)(2,1)S(1)}, bf16[1536,384]{1,0:T(8,12...) custom-call(s32[5]{0:T(128)S(1)} %stack.31.place.before, ...), custom_call_target="tpu_custom_call" | custom-call | bytes 1769472 | tf_op jit(solution)/shard_map/join_weights/pallas_call | solution.py:168
  12.5 3.1 %collective-permute-done.other = bf16[2,4,64,384]{3,2,1,0:T(8,128)(2,1)S(1)} collective-permute-done((bf16[2,4,64,384]{3,2,1,0:T(8,128)(2,1)S(1)}, bf16[2,4,64,384]{3,2,1,0:T(8,128)(2,1)S(1)}, u32[]{:S(2)}, u32[]{:S(2)}) %collective-permute-start) | collective-permute-done | bytes 393248 | tf_op jit(solution)/shard_map/ppermute | solution.py:423
  15.6 9.3 %section.3 = (bf16[4,128,384]{2,1,0:T(8,128)(2,1)S(1)}, bf16[4,128,384]{2,1,0:T(8,128)(2,1)S(1)}, f32[8,128]{1,0:T(8,128)S(1)}) custom-call(s32[5]{0:T(128)S(1)} %stack.31.place.before, s32[5]{0:T(128)S(1)} %stack.31.place.before, bf16[2,16,64,384]{3,2,1,0:T(8,128)(2,1)} %bitcast.13, bf16[2,4,64,384]{3,2,1,0:T(8,128)(2,1)S(1)} %collective-permute-done.other, ...), custom_call_target="tpu_custom_call" | custom-call | bytes 98304 | tf_op jit(solution)/shard_map/section/pallas_call | solution.py:366
  25.0 6.3 %collective-permute-start.7 = (bf16[4,128,384]{2,1,0:T(8,128)(2,1)S(1)}, bf16[4,128,384]{2,1,0:T(8,128)(2,1)S(1)}, u32[]{:S(2)}, u32[]{:S(2)}) collective-permute-start(bf16[4,128,384]{2,1,0:T(8,128)(2,1)S(1)} %get-tuple-element.46.refs_0_), channel_id=1, source_target_pairs={{1,0},{4,1},{5,4},{8,5},{9,8},{12,9},{13,12},{0,13},{3,2},{6,3},{7... | collective-permute-start | bytes 1179656 | tf_op jit(solution)/shard_map/ppermute | solution.py:426
  31.3 4.3 %collective-permute-start.5 = (bf16[2,2,64,384]{3,2,1,0:T(8,128)(2,1)S(1)}, bf16[2,2,64,384]{3,2,1,0:T(8,128)(2,1)S(1)}, u32[]{:S(2)}, u32[]{:S(2)}) collective-permute-start(bf16[2,2,64,384]{3,2,1,0:T(8,128)(2,1)S(1)} %get-tuple-element.44), channel_id=1, source_target_pairs={{0,18},{2,16},{16,2},{18,0},{1,19},{3,17},{17,3},{19,1},{4,22},{6,... | collective-permute-start | bytes 589832 | tf_op jit(solution)/shard_map/ppermute | solution.py:423
  35.6 4.4 %section.4 = (bf16[2,128,384]{2,1,0:T(8,128)(2,1)S(1)}, bf16[2,128,384]{2,1,0:T(8,128)(2,1)S(1)}, f32[8,128]{1,0:T(8,128)S(1)}) custom-call(s32[5]{0:T(128)S(1)} %stack.31.place.before, f32[8,128]{1,0:T(8,128)S(1)} %get-tuple-element.40.before, bf16[2,2,64,384]{3,2,1,0:T(8,128)(2,1)S(1)} %collective-permute-done.2.mine, ...), custom_call_target="tpu_custom_call" | custom-call | bytes 49152 | tf_op jit(solution)/shard_map/section/pallas_call | solution.py:366
  40.1 0.1 collective-permute-start.8
  40.2 2.6 %collective-permute-start.9 = (bf16[2,128,384]{2,1,0:T(8,128)(2,1)S(1)}, bf16[2,128,384]{2,1,0:T(8,128)(2,1)S(1)}, u32[]{:S(2)}, u32[]{:S(2)}) collective-permute-start(bf16[2,128,384]{2,1,0:T(8,128)(2,1)S(1)} %get-tuple-element.48.refs_4_), channel_id=1, source_target_pairs={{1,0},{4,1},{5,4},{8,5},{9,8},{12,9},{13,12},{0,13},{3,2},{6,3},{7... | collective-permute-start | bytes 589832 | tf_op jit(solution)/shard_map/ppermute | solution.py:426
  42.8 5.1 %section.5 = (bf16[2,128,384]{2,1,0:T(8,128)(2,1)}, bf16[2,128,384]{2,1,0:T(8,128)(2,1)}, f32[8,128]{1,0:T(8,128)S(1)}) custom-call(s32[5]{0:T(128)S(1)} %stack.31.place.before, f32[8,128]{1,0:T(8,128)S(1)} %get-tuple-element.42.before, bf16[2,2,64,384]{3,2,1,0:T(8,128)(2,1)S(1)} %collective-permute-done.4.mine, ...), custom_call_target="tpu_custom_call" | custom-call | bytes 49152 | tf_op jit(solution)/shard_map/section/pallas_call | solution.py:366
  47.9 2.6 %collective-permute-start.14 = (bf16[2,128,384]{2,1,0:T(8,128)(2,1)}, bf16[2,128,384]{2,1,0:T(8,128)(2,1)}, u32[]{:S(2)}, u32[]{:S(2)}) collective-permute-start(bf16[2,128,384]{2,1,0:T(8,128)(2,1)} %get-tuple-element.57.refs_4_), channel_id=1, source_target_pairs={{1,0},{4,1},{5,4},{8,5},{9,8},{12,9},{13,12},{0,13},{3,2},{6,3},{7... | collective-permute-start | bytes 589832 | tf_op jit(solution)/shard_map/ppermute | solution.py:426
  50.6 5.5 %temporal.2 = (bf16[2,2,64,384]{3,2,1,0:T(8,128)(2,1)}, bf16[2,2,64,384]{3,2,1,0:T(8,128)(2,1)}, bf16[2,2,64,384]{3,2,1,0:T(8,128)(2,1)}, bf16[2,2,64,384]{3,2,1,0:T(8,128)(2,1)}, f32[8,128]{1,0:T(8,128)S(1)}) custom-call(s32[5]{0:T(128)S(1)} %stack.31.place.before, f32[8,128]{1,0:T(8,128)S(1)} %get-tuple-element.45.before, ...), custom_call_target="tpu_custom_call" | custom-call | bytes 98304 | tf_op jit(solution)/shard_map/temporal/pallas_call | solution.py:388
  56.1 0.5 collective-permute-start.10
  56.6 3.5 %collective-permute-start.11 = (bf16[2,2,64,384]{3,2,1,0:T(8,128)(2,1)}, bf16[2,2,64,384]{3,2,1,0:T(8,128)(2,1)S(1)}, u32[]{:S(2)}, u32[]{:S(2)}) collective-permute-start(bf16[2,2,64,384]{3,2,1,0:T(8,128)(2,1)} %get-tuple-element.54), channel_id=1, source_target_pairs={{0,16},{2,18},{16,0},{18,2},{1,17},{3,19},{17,1},{19,3},{4,20},{6,... | collective-permute-start | bytes 589832 | tf_op jit(solution)/shard_map/ppermute | solution.py:423
  60.1 0.4 collective-permute-start.12
  60.5 6.6 %temporal.3 = (bf16[2,2,64,384]{3,2,1,0:T(8,128)(2,1)S(1)}, bf16[2,2,64,384]{3,2,1,0:T(8,128)(2,1)S(1)}, bf16[2,2,64,384]{3,2,1,0:T(8,128)(2,1)S(1)}, bf16[2,2,64,384]{3,2,1,0:T(8,128)(2,1)S(1)}, f32[8,128]{1,0:T(8,128)}) custom-call(s32[5]{0:T(128)S(1)} %stack.31.place.before, f32[8,128]{1,0:T(8,128)S(1)} %get-tuple-element.56.before, ...), custom_call_target="tpu_custom_call" | custom-call | bytes 98304 | tf_op jit(solution)/shard_map/temporal/pallas_call | solution.py:388
  67.1 1.1 %collective-permute-start.15 = (bf16[2,2,64,384]{3,2,1,0:T(8,128)(2,1)S(1)}, bf16[2,2,64,384]{3,2,1,0:T(8,128)(2,1)S(1)}, u32[]{:S(2)}, u32[]{:S(2)}) collective-permute-start(bf16[2,2,64,384]{3,2,1,0:T(8,128)(2,1)S(1)} %get-tuple-element.60), channel_id=1, source_target_pairs={{0,2},{2,0},{16,18},{18,16},{1,3},{3,1},{17,19},{19,17},{4,6},{6,4... | collective-permute-start | bytes 589832 | tf_op jit(solution)/shard_map/ppermute | solution.py:423
  68.2 2.9 %collective-permute-start.16 = (bf16[2,2,64,384]{3,2,1,0:T(8,128)(2,1)S(1)}, bf16[2,2,64,384]{3,2,1,0:T(8,128)(2,1)S(1)}, u32[]{:S(2)}, u32[]{:S(2)}) collective-permute-start(bf16[2,2,64,384]{3,2,1,0:T(8,128)(2,1)S(1)} %get-tuple-element.61), channel_id=1, source_target_pairs={{0,16},{2,18},{16,0},{18,2},{1,17},{3,19},{17,1},{19,3},{4,20},{6,... | collective-permute-start | bytes 589832 | tf_op jit(solution)/shard_map/ppermute | solution.py:423
  71.1 0.2 broadcast_in_dim.3
  71.4 0.4 collective-permute-start.17
  71.9 1.0 constant_dynamic-update-slice_fusion.6
  72.8 9.8 %collective-permute-done.11 = bf16[2,2,64,384]{3,2,1,0:T(8,128)(2,1)S(1)} collective-permute-done((bf16[2,2,64,384]{3,2,1,0:T(8,128)(2,1)}, bf16[2,2,64,384]{3,2,1,0:T(8,128)(2,1)S(1)}, u32[]{:S(2)}, u32[]{:S(2)}) %collective-permute-start.11) | collective-permute-done | bytes 196640 | tf_op jit(solution)/shard_map/ppermute | solution.py:423
  82.6 4.2 %collective-permute-done.12 = bf16[2,2,64,384]{3,2,1,0:T(8,128)(2,1)S(1)} collective-permute-done((bf16[2,2,64,384]{3,2,1,0:T(8,128)(2,1)}, bf16[2,2,64,384]{3,2,1,0:T(8,128)(2,1)S(1)}, u32[]{:S(2)}, u32[]{:S(2)}) %collective-permute-start.12) | collective-permute-done | bytes 196640 | tf_op jit(solution)/shard_map/ppermute | solution.py:423
  86.9 4.1 %collective-permute-done.16 = bf16[2,2,64,384]{3,2,1,0:T(8,128)(2,1)S(1)} collective-permute-done((bf16[2,2,64,384]{3,2,1,0:T(8,128)(2,1)S(1)}, bf16[2,2,64,384]{3,2,1,0:T(8,128)(2,1)S(1)}, u32[]{:S(2)}, u32[]{:S(2)}) %collective-permute-start.16) | collective-permute-done | bytes 196640 | tf_op jit(solution)/shard_map/ppermute | solution.py:423
  91.0 4.0 %collective-permute-done.17 = bf16[2,2,64,384]{3,2,1,0:T(8,128)(2,1)S(1)} collective-permute-done((bf16[2,2,64,384]{3,2,1,0:T(8,128)(2,1)S(1)}, bf16[2,2,64,384]{3,2,1,0:T(8,128)(2,1)S(1)}, u32[]{:S(2)}, u32[]{:S(2)}) %collective-permute-start.17) | collective-permute-done | bytes 196640 | tf_op jit(solution)/shard_map/ppermute | solution.py:423
  95.0 1.1 %copy-done.10 = bf16[2,16,64,384]{3,2,1,0:T(8,128)(2,1)} copy-done((bf16[2,16,64,384]{3,2,1,0:T(8,128)(2,1)}, bf16[2,16,64,384]{3,2,1,0:T(8,128)(2,1)S(1)}, u32[]{:S(2)}) %copy-start.10) | copy-done | bytes 1572888
  (46 shorter events, 0.4 us)
Async XLA Ops:
  0.1 2.3 %copy-start.4 = (bf16[576,768]{1,0:T(8,128)(2,1)S(1)}, bf16[576,768]{1,0:T(8,128)(2,1)}, u32[]{:S(2)}) copy-start(bf16[576,768]{1,0:T(8,128)(2,1)} %refs_4_.1) | copy-start | bytes 2654212
  0.1 2.3 %copy-start.5 = (bf16[576,768]{1,0:T(8,128)(2,1)S(1)}, bf16[576,768]{1,0:T(8,128)(2,1)}, u32[]{:S(2)}) copy-start(bf16[576,768]{1,0:T(8,128)(2,1)} %refs_5_.1) | copy-start | bytes 2654212
  0.1 2.3 %copy-start.6 = (bf16[192,1536]{1,0:T(8,128)(2,1)S(1)}, bf16[192,1536]{1,0:T(8,128)(2,1)}, u32[]{:S(2)}) copy-start(bf16[192,1536]{1,0:T(8,128)(2,1)} %refs_2_.1) | copy-start | bytes 1769476
  0.1 2.3 %copy-start.7 = (bf16[768,384]{1,0:T(8,128)(2,1)S(1)}, bf16[768,384]{1,0:T(8,128)(2,1)}, u32[]{:S(2)}) copy-start(bf16[768,384]{1,0:T(8,128)(2,1)} %refs_3_.1) | copy-start | bytes 1769476
  0.1 2.3 %copy-start.8 = (bf16[192,1152]{1,0:T(8,128)(2,1)S(1)}, bf16[192,1152]{1,0:T(8,128)(2,1)}, u32[]{:S(2)}) copy-start(bf16[192,1152]{1,0:T(8,128)(2,1)} %refs_0_.1) | copy-start | bytes 1327108
  0.1 2.4 %copy-start.9 = (bf16[192,384]{1,0:T(8,128)(2,1)S(1)}, bf16[192,384]{1,0:T(8,128)(2,1)}, u32[]{:S(2)}) copy-start(bf16[192,384]{1,0:T(8,128)(2,1)} %refs_1_.1) | copy-start | bytes 442372
  2.8 8.6 %collective-permute-start.1 = (bf16[4608,384]{1,0:T(8,128)(2,1)S(1)}, bf16[4608,384]{1,0:T(8,128)(2,1)S(1)}, u32[]{:S(2)}, u32[]{:S(2)}) collective-permute-start(bf16[4608,384]{1,0:T(8,128)(2,1)S(1)} %pack_weights.1.before.mine), channel_id=1, source_target_pairs={{0,1},{1,0},{2,3},{3,2},{4,5},{5,4},{6,7},{7,6},{8,9},{9,8},{10,11... | collective-permute-start | bytes 10616840 | tf_op jit(solution)/shard_map/ppermute | solution.py:433
  3.3 12.3 %collective-permute-start = (bf16[2,4,64,384]{3,2,1,0:T(8,128)(2,1)S(1)}, bf16[2,4,64,384]{3,2,1,0:T(8,128)(2,1)S(1)}, u32[]{:S(2)}, u32[]{:S(2)}) collective-permute-start(bf16[2,4,64,384]{3,2,1,0:T(8,128)(2,1)S(1)} %get-tuple-element.34), channel_id=1, source_target_pairs={{0,2},{2,0},{16,18},{18,16},{1,3},{3,1},{17,19},{19,17},{4,6},{6,4... | collective-permute-start | bytes 1179656 | tf_op jit(solution)/shard_map/ppermute | solution.py:423
  5.9 25.5 %collective-permute-start.2 = (bf16[2,2,64,384]{3,2,1,0:T(8,128)(2,1)S(1)}, bf16[2,2,64,384]{3,2,1,0:T(8,128)(2,1)S(1)}, u32[]{:S(2)}, u32[]{:S(2)}) collective-permute-start(bf16[2,2,64,384]{3,2,1,0:T(8,128)(2,1)S(1)} %get-tuple-element.35.before), channel_id=1, source_target_pairs={{0,16},{2,18},{16,0},{18,2},{1,17},{3,19},{17,1},{19,3},{4,20},{6,... | collective-permute-start | bytes 589832 | tf_op jit(solution)/shard_map/ppermute | solution.py:423
  8.5 27.2 %collective-permute-start.3 = (bf16[2,2,64,384]{3,2,1,0:T(8,128)(2,1)S(1)}, bf16[2,2,64,384]{3,2,1,0:T(8,128)(2,1)S(1)}, u32[]{:S(2)}, u32[]{:S(2)}) collective-permute-start(bf16[2,2,64,384]{3,2,1,0:T(8,128)(2,1)S(1)} %get-tuple-element.41), channel_id=1, source_target_pairs={{0,18},{2,16},{16,2},{18,0},{1,19},{3,17},{17,3},{19,1},{4,22},{6,... | collective-permute-start | bytes 589832 | tf_op jit(solution)/shard_map/ppermute | solution.py:423
  8.5 31.7 %collective-permute-start.4 = (bf16[2,2,64,384]{3,2,1,0:T(8,128)(2,1)S(1)}, bf16[2,2,64,384]{3,2,1,0:T(8,128)(2,1)S(1)}, u32[]{:S(2)}, u32[]{:S(2)}) collective-permute-start(bf16[2,2,64,384]{3,2,1,0:T(8,128)(2,1)S(1)} %get-tuple-element.43), channel_id=1, source_target_pairs={{0,16},{2,18},{16,0},{18,2},{1,17},{3,19},{17,1},{19,3},{4,20},{6,... | collective-permute-start | bytes 589832 | tf_op jit(solution)/shard_map/ppermute | solution.py:423
  24.9 25.7 %copy-start = (bf16[4,128,384]{2,1,0:T(8,128)(2,1)}, bf16[4,128,384]{2,1,0:T(8,128)(2,1)S(1)}, u32[]{:S(2)}) copy-start(bf16[4,128,384]{2,1,0:T(8,128)(2,1)S(1)} %get-tuple-element.46.refs_0_) | copy-start | bytes 1179652
  24.9 25.7 %copy-start.1 = (bf16[4,128,384]{2,1,0:T(8,128)(2,1)}, bf16[4,128,384]{2,1,0:T(8,128)(2,1)S(1)}, u32[]{:S(2)}) copy-start(bf16[4,128,384]{2,1,0:T(8,128)(2,1)S(1)} %get-tuple-element.47.refs_1_) | copy-start | bytes 1179652
  24.9 25.6 %collective-permute-start.6 = (bf16[4,128,384]{2,1,0:T(8,128)(2,1)S(1)}, bf16[4,128,384]{2,1,0:T(8,128)(2,1)S(1)}, u32[]{:S(2)}, u32[]{:S(2)}) collective-permute-start(bf16[4,128,384]{2,1,0:T(8,128)(2,1)S(1)} %get-tuple-element.47.refs_1_), channel_id=1, source_target_pairs={{0,1},{1,4},{4,5},{5,8},{8,9},{9,12},{12,13},{13,0},{2,3},{3,6},{6... | collective-permute-start | bytes 1179656 | tf_op jit(solution)/shard_map/ppermute | solution.py:426
  25.0 25.6 %collective-permute-start.7 = (bf16[4,128,384]{2,1,0:T(8,128)(2,1)S(1)}, bf16[4,128,384]{2,1,0:T(8,128)(2,1)S(1)}, u32[]{:S(2)}, u32[]{:S(2)}) collective-permute-start(bf16[4,128,384]{2,1,0:T(8,128)(2,1)S(1)} %get-tuple-element.46.refs_0_), channel_id=1, source_target_pairs={{1,0},{4,1},{5,4},{8,5},{9,8},{12,9},{13,12},{0,13},{3,2},{6,3},{7... | collective-permute-start | bytes 1179656 | tf_op jit(solution)/shard_map/ppermute | solution.py:426
  31.3 11.4 %collective-permute-start.5 = (bf16[2,2,64,384]{3,2,1,0:T(8,128)(2,1)S(1)}, bf16[2,2,64,384]{3,2,1,0:T(8,128)(2,1)S(1)}, u32[]{:S(2)}, u32[]{:S(2)}) collective-permute-start(bf16[2,2,64,384]{3,2,1,0:T(8,128)(2,1)S(1)} %get-tuple-element.44), channel_id=1, source_target_pairs={{0,18},{2,16},{16,2},{18,0},{1,19},{3,17},{17,3},{19,1},{4,22},{6,... | collective-permute-start | bytes 589832 | tf_op jit(solution)/shard_map/ppermute | solution.py:423
  40.1 7.8 %collective-permute-start.8 = (bf16[2,128,384]{2,1,0:T(8,128)(2,1)S(1)}, bf16[2,128,384]{2,1,0:T(8,128)(2,1)S(1)}, u32[]{:S(2)}, u32[]{:S(2)}) collective-permute-start(bf16[2,128,384]{2,1,0:T(8,128)(2,1)S(1)} %get-tuple-element.49.refs_5_), channel_id=1, source_target_pairs={{0,1},{1,4},{4,5},{5,8},{8,9},{9,12},{12,13},{13,0},{2,3},{3,6},{6... | collective-permute-start | bytes 589832 | tf_op jit(solution)/shard_map/ppermute | solution.py:426
  40.2 10.4 %collective-permute-start.9 = (bf16[2,128,384]{2,1,0:T(8,128)(2,1)S(1)}, bf16[2,128,384]{2,1,0:T(8,128)(2,1)S(1)}, u32[]{:S(2)}, u32[]{:S(2)}) collective-permute-start(bf16[2,128,384]{2,1,0:T(8,128)(2,1)S(1)} %get-tuple-element.48.refs_4_), channel_id=1, source_target_pairs={{1,0},{4,1},{5,4},{8,5},{9,8},{12,9},{13,12},{0,13},{3,2},{6,3},{7... | collective-permute-start | bytes 589832 | tf_op jit(solution)/shard_map/ppermute | solution.py:426
  47.9 12.6 %collective-permute-start.13 = (bf16[2,128,384]{2,1,0:T(8,128)(2,1)}, bf16[2,128,384]{2,1,0:T(8,128)(2,1)}, u32[]{:S(2)}, u32[]{:S(2)}) collective-permute-start(bf16[2,128,384]{2,1,0:T(8,128)(2,1)} %get-tuple-element.58.refs_5_), channel_id=1, source_target_pairs={{0,1},{1,4},{4,5},{5,8},{8,9},{9,12},{12,13},{13,0},{2,3},{3,6},{6... | collective-permute-start | bytes 589832 | tf_op jit(solution)/shard_map/ppermute | solution.py:426
  47.9 12.6 %collective-permute-start.14 = (bf16[2,128,384]{2,1,0:T(8,128)(2,1)}, bf16[2,128,384]{2,1,0:T(8,128)(2,1)}, u32[]{:S(2)}, u32[]{:S(2)}) collective-permute-start(bf16[2,128,384]{2,1,0:T(8,128)(2,1)} %get-tuple-element.57.refs_4_), channel_id=1, source_target_pairs={{1,0},{4,1},{5,4},{8,5},{9,8},{12,9},{13,12},{0,13},{3,2},{6,3},{7... | collective-permute-start | bytes 589832 | tf_op jit(solution)/shard_map/ppermute | solution.py:426
  50.6 5.5 %copy-start.2 = (bf16[4,128,384]{2,1,0:T(8,128)(2,1)}, bf16[4,128,384]{2,1,0:T(8,128)(2,1)S(1)}, u32[]{:S(2)}) copy-start(bf16[4,128,384]{2,1,0:T(8,128)(2,1)S(1)} %collective-permute-done.6.refs_2_) | copy-start | bytes 1179652
  50.6 5.5 %copy-start.3 = (bf16[4,128,384]{2,1,0:T(8,128)(2,1)}, bf16[4,128,384]{2,1,0:T(8,128)(2,1)S(1)}, u32[]{:S(2)}) copy-start(bf16[4,128,384]{2,1,0:T(8,128)(2,1)S(1)} %collective-permute-done.7.refs_3_) | copy-start | bytes 1179652
  56.1 15.3 %collective-permute-start.10 = (bf16[2,2,64,384]{3,2,1,0:T(8,128)(2,1)}, bf16[2,2,64,384]{3,2,1,0:T(8,128)(2,1)}, u32[]{:S(2)}, u32[]{:S(2)}) collective-permute-start(bf16[2,2,64,384]{3,2,1,0:T(8,128)(2,1)} %get-tuple-element.53), channel_id=1, source_target_pairs={{0,2},{2,0},{16,18},{18,16},{1,3},{3,1},{17,19},{19,17},{4,6},{6,4... | collective-permute-start | bytes 589832 | tf_op jit(solution)/shard_map/ppermute | solution.py:423
  56.6 25.9 %collective-permute-start.11 = (bf16[2,2,64,384]{3,2,1,0:T(8,128)(2,1)}, bf16[2,2,64,384]{3,2,1,0:T(8,128)(2,1)S(1)}, u32[]{:S(2)}, u32[]{:S(2)}) collective-permute-start(bf16[2,2,64,384]{3,2,1,0:T(8,128)(2,1)} %get-tuple-element.54), channel_id=1, source_target_pairs={{0,16},{2,18},{16,0},{18,2},{1,17},{3,19},{17,1},{19,3},{4,20},{6,... | collective-permute-start | bytes 589832 | tf_op jit(solution)/shard_map/ppermute | solution.py:423
  60.1 26.7 %collective-permute-start.12 = (bf16[2,2,64,384]{3,2,1,0:T(8,128)(2,1)}, bf16[2,2,64,384]{3,2,1,0:T(8,128)(2,1)S(1)}, u32[]{:S(2)}, u32[]{:S(2)}) collective-permute-start(bf16[2,2,64,384]{3,2,1,0:T(8,128)(2,1)} %get-tuple-element.55), channel_id=1, source_target_pairs={{0,18},{2,16},{16,2},{18,0},{1,19},{3,17},{17,3},{19,1},{4,22},{6,... | collective-permute-start | bytes 589832 | tf_op jit(solution)/shard_map/ppermute | solution.py:423
  67.1 4.2 %copy-start.11 = (bf16[2,2,64,384]{3,2,1,0:T(8,128)(2,1)S(1)}, bf16[2,2,64,384]{3,2,1,0:T(8,128)(2,1)}, u32[]{:S(2)}) copy-start(bf16[2,2,64,384]{3,2,1,0:T(8,128)(2,1)} %get-tuple-element.52) | copy-start | bytes 589828
  67.1 19.8 %collective-permute-start.15 = (bf16[2,2,64,384]{3,2,1,0:T(8,128)(2,1)S(1)}, bf16[2,2,64,384]{3,2,1,0:T(8,128)(2,1)S(1)}, u32[]{:S(2)}, u32[]{:S(2)}) collective-permute-start(bf16[2,2,64,384]{3,2,1,0:T(8,128)(2,1)S(1)} %get-tuple-element.60), channel_id=1, source_target_pairs={{0,2},{2,0},{16,18},{18,16},{1,3},{3,1},{17,19},{19,17},{4,6},{6,4... | collective-permute-start | bytes 589832 | tf_op jit(solution)/shard_map/ppermute | solution.py:423
  68.2 22.8 %collective-permute-start.16 = (bf16[2,2,64,384]{3,2,1,0:T(8,128)(2,1)S(1)}, bf16[2,2,64,384]{3,2,1,0:T(8,128)(2,1)S(1)}, u32[]{:S(2)}, u32[]{:S(2)}) collective-permute-start(bf16[2,2,64,384]{3,2,1,0:T(8,128)(2,1)S(1)} %get-tuple-element.61), channel_id=1, source_target_pairs={{0,16},{2,18},{16,0},{18,2},{1,17},{3,19},{17,1},{19,3},{4,20},{6,... | collective-permute-start | bytes 589832 | tf_op jit(solution)/shard_map/ppermute | solution.py:423
  71.4 23.6 %collective-permute-start.17 = (bf16[2,2,64,384]{3,2,1,0:T(8,128)(2,1)S(1)}, bf16[2,2,64,384]{3,2,1,0:T(8,128)(2,1)S(1)}, u32[]{:S(2)}, u32[]{:S(2)}) collective-permute-start(bf16[2,2,64,384]{3,2,1,0:T(8,128)(2,1)S(1)} %get-tuple-element.62), channel_id=1, source_target_pairs={{0,18},{2,16},{16,2},{18,0},{1,19},{3,17},{17,3},{19,1},{4,22},{6,... | collective-permute-start | bytes 589832 | tf_op jit(solution)/shard_map/ppermute | solution.py:423
  95.0 1.1 %copy-start.10 = (bf16[2,16,64,384]{3,2,1,0:T(8,128)(2,1)}, bf16[2,16,64,384]{3,2,1,0:T(8,128)(2,1)S(1)}, u32[]{:S(2)}) copy-start(bf16[2,16,64,384]{3,2,1,0:T(8,128)(2,1)S(1)} %constant_dynamic-update-slice_fusion) | copy-start | bytes 4718596
